TPU v7x, 128 devices: a whole 4x4x4 slice. The times are simulated.
128 devices in a mesh: section: 4 (over x), seq: 16 (over z_lo, y, core), head: 2 (over z_hi).
Axes of the slice: x: 4, y: 4, z: 4 (z_hi: 2, z_lo: 2; z = z_hi * 2 + z_lo), core: 2. Of those that a mesh axis runs over, the one named last changes fastest.
Arguments:
- notes: bfloat16 [4, 4096, 2048], P('section', 'seq'), may hold values from -18 to 18
- frames: bfloat16 [4, 16384, 2048], P('section', 'seq'), may hold values from -18 to 18
- w_query: bfloat16 [2048, 2048], P(None, 'head'), may hold values from -0.125 to 0.125
- w_key: bfloat16 [2048, 2048], P(None, 'head'), may hold values from -0.125 to 0.125
- w_value: bfloat16 [2048, 2048], P(None, 'head'), may hold values from -0.125 to 0.125
- w_out: bfloat16 [2048, 2048], P('head'), may hold values from -0.125 to 0.125
- band_blocks: int32 [4, 2, 128], P('section', None, 'seq'), may hold values from 0 to 31, as said below
- grad_mixed: bfloat16 [4, 16384, 2048], P('section', 'seq'), may hold values from -6 to 6
Outputs:
- frame_grad: bfloat16 [4, 16384, 2048], P('section', 'seq', 'head')
- note_grad: bfloat16 [4, 4096, 2048], P('section', 'seq', 'head')
Inputs may be any that keep to these rules, and one draw needn't show every extreme that they name: band_blocks[m, 0, b] <= band_blocks[m, 1, b]; both lie among the note blocks of seq shards b // 8 - 1 to b // 8 + 1.
All inputs are finite; a program needn't handle non-finite values.
Results may differ from a plain program's by a relative error of at most 0.017.
The roundings to bfloat16 on the way count: a program that leaves them out, or rounds other values in their place, can miss the bound.
Values may be sent and summed in bfloat16 or wider, within the bound.
No kernel may reach another device: no remote copies, remote signals or barrier semaphores. Data moves between devices by JAX's collectives and lax.ppermute only.
A program may use at most 192 MiB of HBM per device.

v0:
```python
import jax
import jax.numpy as jnp
from jax import lax
from jax.sharding import PartitionSpec as P

D = 2048
HEADS = 16
BLK = 128


def shifted(block, axis, distance):
    devices = range(lax.axis_size(axis))
    route = [(i - distance, i) for i in devices if i - distance in devices]
    return lax.ppermute(block, axis, route)


def from_behind(block, axis, distance):
    devices = range(lax.axis_size(axis))
    route = [((i - distance) % len(devices), i) for i in devices]
    return lax.ppermute(block, axis, route)


def extended(cells, sides, width):
    for axis, dim in sides:
        count = lax.axis_size(axis)
        ends = count - 1
        head = lax.slice_in_dim(cells, 0, width, axis=dim)
        tail = lax.slice_in_dim(cells, cells.shape[dim] - width, cells.shape[dim], axis=dim)
        cells = jnp.concatenate(
            [
                lax.ppermute(tail, axis, [(i, (i + 1) % count) for i in range(ends)]),
                cells,
                lax.ppermute(head, axis, [((i + 1) % count, i) for i in range(ends)]),
            ],
            axis=dim,
        )
    return cells


def collect_rims(window_grads):
    rim_width = window_grads.shape[1] // 3
    summed_grads = window_grads[:, rim_width : 2 * rim_width]
    for offset, begin in ((1, 2 * rim_width), (-1, 0)):
        summed_grads = summed_grads + shifted(
            window_grads[:, begin : begin + rim_width], "seq", offset
        )
    return summed_grads


def per_device(notes, frames, w_query, w_key, w_value, w_out, band_blocks, grad_mixed):
    head_size = D // HEADS
    local_heads = w_query.shape[1] // head_size
    score_scale = head_size ** (-0.5)
    frame_rows = frames.shape[1]
    note_rows = notes.shape[1]
    key_rows = jnp.dot(notes[0], w_key, preferred_element_type=jnp.float32).astype(jnp.bfloat16)
    value_rows = jnp.dot(notes[0], w_value, preferred_element_type=jnp.float32).astype(jnp.bfloat16)
    key_values = from_behind(jnp.stack([key_rows, value_rows]), "section", 1)
    window = extended(key_values, (("seq", 1),), note_rows)
    key_win = window[0].reshape(3 * note_rows, local_heads, head_size)
    value_win = window[1].reshape(3 * note_rows, local_heads, head_size)
    queries = jnp.dot(frames[0], w_query, preferred_element_type=jnp.float32).astype(jnp.bfloat16)
    grad_ctx = lax.dot_general(
        grad_mixed[0], w_out, (((1,), (1,)), ((), ())), preferred_element_type=jnp.float32
    ).astype(jnp.bfloat16)
    shard = lax.axis_index("seq")
    window_blocks = (shard - 1) * (note_rows // BLK) + jnp.arange(
        3 * note_rows, dtype=jnp.int32
    ) // BLK
    first_rows = jnp.broadcast_to(band_blocks[0, 0][:, None], (frame_rows // BLK, BLK)).reshape(
        frame_rows
    )
    last_rows = jnp.broadcast_to(band_blocks[0, 1][:, None], (frame_rows // BLK, BLK)).reshape(
        frame_rows
    )
    block_rows = min(512, frame_rows)
    block_count = frame_rows // block_rows
    inputs = (
        queries.reshape(block_count, block_rows, local_heads, head_size),
        grad_ctx.reshape(block_count, block_rows, local_heads, head_size),
        first_rows.reshape(block_count, block_rows),
        last_rows.reshape(block_count, block_rows),
    )

    def one_block(carry, pieces):
        key_acc, value_acc = carry
        query_blk, grad_blk, first_blk, last_blk = pieces
        scores = (
            jnp.einsum("rhd,nhd->hrn", query_blk, key_win, preferred_element_type=jnp.float32)
            * score_scale
        )
        allowed = (window_blocks[None, :] >= first_blk[:, None]) & (
            window_blocks[None, :] <= last_blk[:, None]
        )
        scores = jnp.where(allowed[None], scores, -jnp.inf)
        peak = jnp.max(scores, axis=-1, keepdims=True)
        expos = jnp.exp(scores - peak)
        probs = expos / jnp.sum(expos, axis=-1, keepdims=True)
        grad_probs = jnp.einsum(
            "rhd,nhd->hrn", grad_blk, value_win, preferred_element_type=jnp.float32
        )
        probs_low = probs.astype(jnp.bfloat16)
        value_acc = value_acc + jnp.einsum(
            "hrn,rhd->nhd", probs_low, grad_blk, preferred_element_type=jnp.float32
        )
        delta = jnp.sum(probs * grad_probs, axis=-1, keepdims=True)
        grad_scores = (probs * (grad_probs - delta) * score_scale).astype(jnp.bfloat16)
        grad_query_blk = jnp.einsum(
            "hrn,nhd->rhd", grad_scores, key_win, preferred_element_type=jnp.float32
        ).astype(jnp.bfloat16)
        key_acc = key_acc + jnp.einsum(
            "hrn,rhd->nhd", grad_scores, query_blk, preferred_element_type=jnp.float32
        )
        return ((key_acc, value_acc), grad_query_blk)

    empty = jnp.zeros((3 * note_rows, local_heads, head_size), jnp.float32)
    (key_acc, value_acc), grad_query_blocks = lax.scan(one_block, (empty, empty), inputs)
    grad_queries = grad_query_blocks.reshape(frame_rows, local_heads * head_size)
    window_grads = jnp.stack(
        [key_acc.reshape(3 * note_rows, -1), value_acc.reshape(3 * note_rows, -1)]
    )
    summed_grads = collect_rims(window_grads).astype(jnp.bfloat16)
    owned_grads = from_behind(summed_grads, "section", -1)
    contract = (((1,), (1,)), ((), ()))
    frame_term = lax.dot_general(
        grad_queries, w_query, contract, preferred_element_type=jnp.float32
    )
    note_term = lax.dot_general(
        owned_grads[0], w_key, contract, preferred_element_type=jnp.float32
    ) + lax.dot_general(owned_grads[1], w_value, contract, preferred_element_type=jnp.float32)
    frame_sum, note_sum = (
        lax.psum_scatter(
            frame_term.astype(jnp.bfloat16), "head", scatter_dimension=1, tiled=True
        ).astype(jnp.float32),
        lax.psum_scatter(
            note_term.astype(jnp.bfloat16), "head", scatter_dimension=1, tiled=True
        ).astype(jnp.float32),
    )
    return (frame_sum.astype(jnp.bfloat16)[None], note_sum.astype(jnp.bfloat16)[None])


def solution(mesh):
    placed = (
        P("section", "seq", None),
        P("section", "seq", None),
        P(None, "head"),
        P(None, "head"),
        P(None, "head"),
        P("head", None),
        P("section", None, "seq"),
        P("section", "seq", None),
    )
    return jax.shard_map(
        per_device,
        mesh=mesh,
        in_specs=placed,
        out_specs=(P("section", "seq", "head"), P("section", "seq", "head")),
        check_vma=False,
    )
```

profile of v0, /device:TPU:1, one launch (start us, length us, event | category | flops | bytes accessed | tf_op | source)
XLA Modules:
  0.0 426.2 jit_solution(8190955085347428320)
XLA Ops:
  7.2 1.2 copy-done
  8.4 3.6 fusion.59
  12.0 1.3 fusion.60
  13.5 2.1 collective-permute-start
  15.6 4.7 %convert_bitcast_fusion.1 = bf16[128,8,8,128]{3,1,2,0:T(8,128)(2,1)S(1)} fusion(bf16[2048,1024]{1,0:T(8,128)(2,1)S(1)} %copy-done.12, bf16[1,1024,2048]{2,1,0:T(8,128)(2,1)S(1)} %copy-done.6), kind=kOutput, calls=%fused_computation.66 | convolution fusion | flops 4296015872 | bytes 10485760 | tf_op jit(solution)/shard_map/dot_general | solution.py:62
  20.3 19.0 %collective-permute-done = bf16[2,256,1024]{2,1,0:T(8,128)(2,1)S(1)} collective-permute-done((bf16[2,256,1024]{2,1,0:T(8,128)(2,1)S(1)}, bf16[2,256,1024]{2,1,0:T(8,128)(2,1)S(1)}, u32[]{:S(2)}, u32[]{:S(2)}) %collective-permute-start) | collective-permute-done | bytes 1048608 | tf_op jit(solution)/shard_map/ppermute | solution.py:20
  39.3 5.0 %collective-permute-start.1 = (bf16[2,256,1024]{2,1,0:T(8,128)(2,1)S(1)}, bf16[2,256,1024]{2,1,0:T(8,128)(2,1)}, u32[]{:S(2)}, u32[]{:S(2)}) collective-permute-start(bf16[2,256,1024]{2,1,0:T(8,128)(2,1)S(1)} %collective-permute-done), channel_id=1, source_target_pairs={{0,2},{2,4},{4,6},{6,8},{8,10},{10,12},{12,14},{14,16},{16,18},{18... | collective-permute-start | bytes 3145736 | tf_op jit(solution)/shard_map/ppermute | solution.py:31
  44.2 5.8 %convert_bitcast_fusion = bf16[128,8,8,128]{3,1,2,0:T(8,128)(2,1)} fusion(bf16[1024,2048]{1,0:T(8,128)(2,1)S(1)} %copy-done.7, bf16[1,1024,2048]{2,1,0:T(8,128)(2,1)S(1)} %copy-done.8), kind=kOutput, calls=%fused_computation.65 | convolution fusion | flops 4296015872 | bytes 10485760 | tf_op jit(solution)/shard_map/dot_general | solution.py:63
  50.1 1.9 collective-permute-start.2
  52.2 1.9 copy.29
  54.1 2.0 copy.33
  56.2 1.3 constant_dynamic-update-slice_fusion.2
  57.6 8.7 %collective-permute-done.2 = bf16[2,256,1024]{2,1,0:T(8,128)(2,1)} collective-permute-done((bf16[2,256,1024]{2,1,0:T(8,128)(2,1)S(1)}, bf16[2,256,1024]{2,1,0:T(8,128)(2,1)}, u32[]{:S(2)}, u32[]{:S(2)}) %collective-permute-start.2) | collective-permute-done | bytes 1048608 | tf_op jit(solution)/shard_map/ppermute | solution.py:33
  66.3 1.3 constant_dynamic-update-slice_fusion
  67.6 0.7 slice_bitcast_fusion
  68.3 0.4 copy.32
  68.7 1.4 copy.19
  70.2 0.4 copy.34
  70.8 199.5 %while.15 = (s32[]{:T(128)}, f32[768,8,128]{0,2,1:T(8,128)}, f32[768,8,128]{0,2,1:T(8,128)}, bf16[2,512,8,128]{3,2,1,0:T(8,128)(2,1)}, bf16[2,512,8,128]{3,2,1,0...) while((s32[]{:T(128)}, f32[768,8,128]{0,2,1:T(8,128)}, ...), condition=%wide.region_4.5_spmd.clone, body=%wide.region_0.4_spmd.clone.sunk | while | flops 4094313472 | bytes 117787280 | solution.py:117
  71.0 0.4 compare_and_fusion.2
  71.4 2.7 constant_dynamic-slice_fusion.6
  74.1 10.7 %fusion.94 = (f32[8,512]{1,0:T(8,128)S(1)}, f32[8,512,768]{2,1,0:T(8,128)}) fusion(pred[512,768]{1,0:T(8,128)(4,1)S(1)} %compare_and_fusion.2, bf16[768,8,128]{2,0,1:T(8,128)(2,1)} %get-tuple-element.273, bf16[1,512,8,128]{3,2,1,0:T(8,128)(2,1)} %get-tuple-element.235), kind=kOutput, calls=%fused_computation.88.clone.1 | convolution fusion | flops 817890048 | bytes 15613952 | tf_op jit(solution)/shard_map/while/body/eval_jaxpr/sub | solution.py:97
  84.8 6.3 %fusion.92 = f32[8,512,768]{2,1,0:T(8,128)} fusion(bf16[768,8,128]{2,0,1:T(8,128)(2,1)S(1)} %get-tuple-element.275, bf16[1,512,8,128]{3,2,1,0:T(8,128)(2,1)S(1)} %get-tuple-element.234), kind=kOutput, calls=%fused_computation.26.clone.1 | convolution fusion | flops 805306368 | bytes 15204352 | tf_op jit(solution)/shard_map/while/body/eval_jaxpr/rhd,nhd->hrn/dot_general | solution.py:99
  91.1 33.1 %fusion.95 = bf16[1,512,8,128]{3,1,2,0:T(8,128)(2,1)} fusion(bf16[768,8,128]{2,0,1:T(8,128)(2,1)} %get-tuple-element.273, f32[8,512,768]{2,1,0:T(8,128)} %fusion.92, f32[8,512,768]{2,1,0:T(8,128)} %get-tuple-element.238, f32[8,512]{1,0:T(8,128)S(1)} %get-tuple-element.239), kind=kOutput, calls=%fused_computation.21.clone.1 | convolution fusion | flops 827855616 | bytes 27803648 | tf_op jit(solution)/shard_map/while/body/eval_jaxpr/hrn,nhd->rhd/dot_general | solution.py:108
  124.2 2.9 copy_dynamic-update-slice_fusion.2
  127.0 7.8 %bitcast_add_fusion.5 = f32[768,8,128]{0,2,1:T(8,128)} fusion(f32[768,8,128]{0,2,1:T(8,128)} %get-tuple-element.255, pred[]{:T(512)S(6)} %compare.5, bf16[1,512,8,128]{3,2,1,0:T(8,128)(2,1)S(1)} %get-tuple-element.234, f32[8,512,768]{2,1,0:T(8,128)} %get-tuple-element.238, f32[8,512]{1,0:T(8,128)S(1)} %get-tuple-element.239), kind=kOutput, calls=%fused_computation.17.clone.1 | convolution fusion | flops 813170688 | bytes 19939328 | tf_op jit(solution)/shard_map/while/body/eval_jaxpr/hrn,rhd->nhd/dot_general | solution.py:103
  134.8 35.0 %bitcast_add_fusion.4 = f32[768,8,128]{0,2,1:T(8,128)} fusion(f32[768,8,128]{0,2,1:T(8,128)} %get-tuple-element.254, f32[8,512,768]{2,1,0:T(8,128)} %fusion.92, pred[]{:T(512)S(6)} %compare.5, bf16[1,512,8,128]{3,2,1,0:T(8,128)(2,1)} %get-tuple-element.235, f32[8,512,768]{2,1,0:T(8,128)} %get-tuple-element.238, f32[8,512]{1,0:T(8,128)S(1)} %get-tuple-element.239), kind=kOutput, calls=%fused_computation.18.clone.1 | convolution fusion | flops 828904192 | bytes 32522240 | tf_op jit(solution)/shard_map/while/body/eval_jaxpr/hrn,rhd->nhd/dot_general | solution.py:111
  169.8 0.4 compare_and_fusion.2
  170.2 2.7 constant_dynamic-slice_fusion.6
  172.8 10.7 %fusion.94 = (f32[8,512]{1,0:T(8,128)S(1)}, f32[8,512,768]{2,1,0:T(8,128)}) fusion(pred[512,768]{1,0:T(8,128)(4,1)S(1)} %compare_and_fusion.2, bf16[768,8,128]{2,0,1:T(8,128)(2,1)} %get-tuple-element.273, bf16[1,512,8,128]{3,2,1,0:T(8,128)(2,1)} %get-tuple-element.235), kind=kOutput, calls=%fused_computation.88.clone.1 | convolution fusion | flops 817890048 | bytes 15613952 | tf_op jit(solution)/shard_map/while/body/eval_jaxpr/sub | solution.py:97
  183.5 6.3 %fusion.92 = f32[8,512,768]{2,1,0:T(8,128)} fusion(bf16[768,8,128]{2,0,1:T(8,128)(2,1)S(1)} %get-tuple-element.275, bf16[1,512,8,128]{3,2,1,0:T(8,128)(2,1)S(1)} %get-tuple-element.234), kind=kOutput, calls=%fused_computation.26.clone.1 | convolution fusion | flops 805306368 | bytes 15204352 | tf_op jit(solution)/shard_map/while/body/eval_jaxpr/rhd,nhd->hrn/dot_general | solution.py:99
  189.8 33.1 %fusion.95 = bf16[1,512,8,128]{3,1,2,0:T(8,128)(2,1)} fusion(bf16[768,8,128]{2,0,1:T(8,128)(2,1)} %get-tuple-element.273, f32[8,512,768]{2,1,0:T(8,128)} %fusion.92, f32[8,512,768]{2,1,0:T(8,128)} %get-tuple-element.238, f32[8,512]{1,0:T(8,128)S(1)} %get-tuple-element.239), kind=kOutput, calls=%fused_computation.21.clone.1 | convolution fusion | flops 827855616 | bytes 27803648 | tf_op jit(solution)/shard_map/while/body/eval_jaxpr/hrn,nhd->rhd/dot_general | solution.py:108
  222.9 2.9 copy_dynamic-update-slice_fusion.2
  225.8 8.7 %bitcast_add_fusion.5 = f32[768,8,128]{0,2,1:T(8,128)} fusion(f32[768,8,128]{0,2,1:T(8,128)} %get-tuple-element.255, pred[]{:T(512)S(6)} %compare.5, bf16[1,512,8,128]{3,2,1,0:T(8,128)(2,1)S(1)} %get-tuple-element.234, f32[8,512,768]{2,1,0:T(8,128)} %get-tuple-element.238, f32[8,512]{1,0:T(8,128)S(1)} %get-tuple-element.239), kind=kOutput, calls=%fused_computation.17.clone.1 | convolution fusion | flops 813170688 | bytes 19939328 | tf_op jit(solution)/shard_map/while/body/eval_jaxpr/hrn,rhd->nhd/dot_general | solution.py:103
  234.4 35.9 %bitcast_add_fusion.4 = f32[768,8,128]{0,2,1:T(8,128)} fusion(f32[768,8,128]{0,2,1:T(8,128)} %get-tuple-element.254, f32[8,512,768]{2,1,0:T(8,128)} %fusion.92, pred[]{:T(512)S(6)} %compare.5, bf16[1,512,8,128]{3,2,1,0:T(8,128)(2,1)} %get-tuple-element.235, f32[8,512,768]{2,1,0:T(8,128)} %get-tuple-element.238, f32[8,512]{1,0:T(8,128)S(1)} %get-tuple-element.239), kind=kOutput, calls=%fused_computation.18.clone.1 | convolution fusion | flops 828904192 | bytes 32522240 | tf_op jit(solution)/shard_map/while/body/eval_jaxpr/hrn,rhd->nhd/dot_general | solution.py:111
  270.3 2.7 fusion.48
  273.0 2.1 collective-permute-start.3
  275.1 2.8 collective-permute-start.4
  277.9 20.1 %collective-permute-done.3 = f32[2,256,1024]{1,2,0:T(8,128)S(1)} collective-permute-done((f32[2,256,1024]{1,2,0:T(8,128)S(1)}, f32[2,256,1024]{1,2,0:T(8,128)S(1)}, u32[]{:S(2)}, u32[]{:S(2)}) %collective-permute-start.3) | collective-permute-done | bytes 2097184 | tf_op jit(solution)/shard_map/ppermute | solution.py:14
  298.0 4.7 %collective-permute-done.4 = f32[2,256,1024]{1,2,0:T(8,128)S(1)} collective-permute-done((f32[2,256,1024]{1,2,0:T(8,128)S(1)}, f32[2,256,1024]{1,2,0:T(8,128)S(1)}, u32[]{:S(2)}, u32[]{:S(2)}) %collective-permute-start.4) | collective-permute-done | bytes 2097184 | tf_op jit(solution)/shard_map/ppermute | solution.py:14
  302.7 0.5 fusion.52
  303.2 1.3 collective-permute-start.5
  304.5 12.4 %collective-permute-done.5 = bf16[2,256,1024]{1,2,0:T(8,128)(2,1)S(1)} collective-permute-done((bf16[2,256,1024]{1,2,0:T(8,128)(2,1)S(1)}, bf16[2,256,1024]{1,2,0:T(8,128)(2,1)S(1)}, u32[]{:S(2)}, u32[]{:S(2)}) %collective-permute-start.5) | collective-permute-done | bytes 1048608 | tf_op jit(solution)/shard_map/ppermute | solution.py:20
  316.9 1.3 fusion.63
  318.2 2.3 fusion.47
  320.6 8.4 %convolution_convert_fusion = bf16[1024,2048]{1,0:T(8,128)(2,1)} fusion(bf16[2048,1024]{1,0:T(8,128)(2,1)} %param.12, bf16[128,8,8,128]{3,2,1,0:T(8,128)(2,1)S(1)} %bitcast.130), kind=kOutput, calls=%fused_computation.54 | convolution fusion | flops 4297064448 | bytes 10485760 | tf_op jit(solution)/shard_map/dot_general | solution.py:125
  329.0 29.5 %reduce-scatter.5.cloned.1.call-done = bf16[256,1024]{1,0:T(8,128)(2,1)} async-done(((bf16[256,2048]{1,0:T(8,128)(2,1)}), bf16[256,1024]{1,0:T(8,128)(2,1)}) %reduce-scatter.5.cloned.1.call-update) | async-done | bytes 524304 | tf_op jit(solution)/shard_map/reduce_scatter | solution.py:135
  358.6 60.8 %reduce-scatter.3.cloned.1.call-done = bf16[1024,1024]{1,0:T(8,128)(2,1)} async-done(((bf16[1024,2048]{1,0:T(8,128)(2,1)}), bf16[1024,1024]{1,0:T(8,128)(2,1)}) %reduce-scatter.3.cloned.1.call-update) | async-done | bytes 2097168 | tf_op jit(solution)/shard_map/reduce_scatter | solution.py:132
  (48 shorter events, 0.9 us)
Async XLA Ops:
  7.2 1.2 copy-start
  7.2 351.4 %reduce-scatter.5.cloned.1.call-start = ((), (), s32[]{:S(2)}) async-start(), calls=%async_computation.3 | async-start | bytes 1572864 | tf_op jit(solution)/shard_map/reduce_scatter | solution.py:135
  8.4 3.6 copy-start.9
  12.0 3.6 copy-start.6
  12.0 3.6 copy-start.12
  13.4 30.8 %copy-start.7 = (bf16[1024,2048]{1,0:T(8,128)(2,1)S(1)}, bf16[1024,2048]{1,0:T(8,128)(2,1)}, u32[]{:S(2)}) copy-start(bf16[1024,2048]{1,0:T(8,128)(2,1)} %param.15) | copy-start | bytes 12582916
  13.4 30.8 %copy-start.8 = (bf16[1,1024,2048]{2,1,0:T(8,128)(2,1)S(1)}, bf16[1,1024,2048]{2,1,0:T(8,128)(2,1)}, u32[]{:S(2)}) copy-start(bf16[1,1024,2048]{2,1,0:T(8,128)(2,1)} %param.17) | copy-start | bytes 12582916
  13.5 25.8 %collective-permute-start = (bf16[2,256,1024]{2,1,0:T(8,128)(2,1)S(1)}, bf16[2,256,1024]{2,1,0:T(8,128)(2,1)S(1)}, u32[]{:S(2)}, u32[]{:S(2)}) collective-permute-start(bf16[2,256,1024]{2,1,0:T(8,128)(2,1)S(1)} %pad_maximum_fusion.1), channel_id=1, source_target_pairs={{96,0},{0,32},{32,64},{64,96},{97,1},{1,33},{33,65},{65,97},{98,2}... | collective-permute-start | bytes 3145736 | tf_op jit(solution)/shard_map/ppermute | solution.py:20
  20.3 31.7 %copy-start.5 = (s32[1,2,8]{2,1,0:T(2,128)S(1)}, s32[1,2,8]{2,1,0:T(2,128)}, u32[]{:S(2)}) copy-start(s32[1,2,8]{2,1,0:T(2,128)} %param.16) | copy-start | bytes 196
  39.3 17.0 %collective-permute-start.1 = (bf16[2,256,1024]{2,1,0:T(8,128)(2,1)S(1)}, bf16[2,256,1024]{2,1,0:T(8,128)(2,1)}, u32[]{:S(2)}, u32[]{:S(2)}) collective-permute-start(bf16[2,256,1024]{2,1,0:T(8,128)(2,1)S(1)} %collective-permute-done), channel_id=1, source_target_pairs={{0,2},{2,4},{4,6},{6,8},{8,10},{10,12},{12,14},{14,16},{16,18},{18... | collective-permute-start | bytes 3145736 | tf_op jit(solution)/shard_map/ppermute | solution.py:31
  50.1 16.2 %collective-permute-start.2 = (bf16[2,256,1024]{2,1,0:T(8,128)(2,1)S(1)}, bf16[2,256,1024]{2,1,0:T(8,128)(2,1)}, u32[]{:S(2)}, u32[]{:S(2)}) collective-permute-start(bf16[2,256,1024]{2,1,0:T(8,128)(2,1)S(1)} %collective-permute-done), channel_id=1, source_target_pairs={{2,0},{4,2},{6,4},{8,6},{10,8},{12,10},{14,12},{16,14},{18,16},{20... | collective-permute-start | bytes 3145736 | tf_op jit(solution)/shard_map/ppermute | solution.py:33
  52.2 1.9 copy-start.4
  270.3 32.4 %copy-start.2 = (f32[768,8,128]{0,2,1:T(8,128)S(1)}, f32[768,8,128]{0,2,1:T(8,128)}, u32[]{:S(2)}) copy-start(f32[768,8,128]{0,2,1:T(8,128)} %get-tuple-element.62) | copy-start | bytes 9437188
  270.3 32.4 %copy-start.3 = (f32[768,8,128]{0,2,1:T(8,128)S(1)}, f32[768,8,128]{0,2,1:T(8,128)}, u32[]{:S(2)}) copy-start(f32[768,8,128]{0,2,1:T(8,128)} %get-tuple-element.63) | copy-start | bytes 9437188
  273.0 25.0 %collective-permute-start.3 = (f32[2,256,1024]{1,2,0:T(8,128)S(1)}, f32[2,256,1024]{1,2,0:T(8,128)S(1)}, u32[]{:S(2)}, u32[]{:S(2)}) collective-permute-start(f32[2,256,1024]{1,2,0:T(8,128)S(1)} %get-tuple-element.155), channel_id=1, source_target_pairs={{0,2},{2,4},{4,6},{6,8},{8,10},{10,12},{12,14},{14,16},{16,18},{18... | collective-permute-start | bytes 6291464 | tf_op jit(solution)/shard_map/ppermute | solution.py:14
  275.1 41.8 %copy-start.10 = (bf16[2048,1024]{1,0:T(8,128)(2,1)S(1)}, bf16[2048,1024]{1,0:T(8,128)(2,1)}, u32[]{:S(2)}) copy-start(bf16[2048,1024]{1,0:T(8,128)(2,1)} %param.14) | copy-start | bytes 12582916
  275.1 27.6 %collective-permute-start.4 = (f32[2,256,1024]{1,2,0:T(8,128)S(1)}, f32[2,256,1024]{1,2,0:T(8,128)S(1)}, u32[]{:S(2)}, u32[]{:S(2)}) collective-permute-start(f32[2,256,1024]{1,2,0:T(8,128)S(1)} %get-tuple-element.156), channel_id=1, source_target_pairs={{2,0},{4,2},{6,4},{8,6},{10,8},{12,10},{14,12},{16,14},{18,16},{20... | collective-permute-start | bytes 6291464 | tf_op jit(solution)/shard_map/ppermute | solution.py:14
  303.2 15.0 %copy-start.11 = (bf16[2048,1024]{1,0:T(8,128)(2,1)S(1)}, bf16[2048,1024]{1,0:T(8,128)(2,1)}, u32[]{:S(2)}) copy-start(bf16[2048,1024]{1,0:T(8,128)(2,1)} %param.13) | copy-start | bytes 12582916
  303.2 13.7 %collective-permute-start.5 = (bf16[2,256,1024]{1,2,0:T(8,128)(2,1)S(1)}, bf16[2,256,1024]{1,2,0:T(8,128)(2,1)S(1)}, u32[]{:S(2)}, u32[]{:S(2)}) collective-permute-start(bf16[2,256,1024]{1,2,0:T(8,128)(2,1)S(1)} %fusion.52), channel_id=1, source_target_pairs={{32,0},{64,32},{96,64},{0,96},{33,1},{65,33},{97,65},{1,97},{34,2}... | collective-permute-start | bytes 3145736 | tf_op jit(solution)/shard_map/ppermute | solution.py:20
  318.2 2.4 copy-start.13
  320.5 98.8 %reduce-scatter.3.cloned.1.call-start = ((), (), s32[]{:S(2)}) async-start(), calls=%async_computation.2 | async-start | bytes 6291456 | tf_op jit(solution)/shard_map/reduce_scatter | solution.py:132
  320.6 98.8 %copy-start.1 = (bf16[1,256,2048]{2,1,0:T(8,128)(2,1)S(1)}, bf16[1,256,2048]{2,1,0:T(8,128)(2,1)}, u32[]{:S(2)}) copy-start(bf16[1,256,2048]{2,1,0:T(8,128)(2,1)} %param.10) | copy-start | bytes 3145732
Sparse Core Ops, SparseCore 0:
  320.6 37.8 reduce-scatter.4
  361.7 57.6 reduce-scatter.2
where the time goes:
time: 427 us; the launch traced here: 426 us
  matrix products  215 us (50%)
  waiting for transfers between devices  155 us (36%)
  local copies, waits for them, and re-layouts  22.4 us (5%)
  starting transfers between devices  15.2 us (4%)
  between operations  14.3 us (3%)
    dot_general x2, matrix products, one_block(): jnp.einsum('hrn,rhd->nhd', grad_scores, query_blk, preferred_element_type...  70.9 us
    dot_general x2, matrix products, one_block(): jnp.einsum('hrn,nhd->rhd', grad_scores, key_win, preferred_element_type=j...  66.1 us
    reduce_scatter x1, waiting for transfers between devices, per_device(): lax.psum_scatter(frame_term.astype(jnp.bfloat16), 'head', scatter_dimensi...  60.8 us
    ppermute x2, waiting for transfers between devices, from_behind(): return lax.ppermute(block, axis, route)  31.4 us
    reduce_scatter x1, waiting for transfers between devices, per_device(): lax.psum_scatter(note_term.astype(jnp.bfloat16), 'head', scatter_dimensio...  29.5 us
    ppermute x2, waiting for transfers between devices, shifted(): return lax.ppermute(block, axis, route)  24.8 us
    sub x2, matrix products, one_block(): expos = jnp.exp(scores - peak)  21.3 us
    dot_general x2, matrix products, one_block(): jnp.einsum('hrn,rhd->nhd', probs_low, grad_blk, preferred_element_type=jn...  16.4 us
  transfers between devices with their start and end apart: 8, of which 7 were waited for; matrix products, arithmetic and copies ran while one was open for 6% of the time, Pallas kernels for 0%

commit v1 on v0

v1 whole, which is shorter than its diff:
```python
import jax
import jax.numpy as jnp
from jax import lax
from jax.experimental import pallas as pl
from jax.experimental.pallas import tpu as pltpu
from jax.sharding import PartitionSpec as P

D = 2048
HEADS = 16
BLK = 128
HD = D // HEADS
SCALE = HD**-0.5
LOG2E = 1.4426950408889634
CHUNKS = ((0, 2), (2, 2), (4, 4))
MIB = 2**20

F32 = jnp.float32
BF16 = jnp.bfloat16
NN = (((1,), (0,)), ((), ()))
NT = (((1,), (1,)), ((), ()))
TN = (((0,), (0,)), ((), ()))


def dot(a, b, dims):
    return lax.dot_general(a, b, dims, preferred_element_type=F32)


def section_shift(block, distance):
    count = lax.axis_size("section")
    return lax.ppermute(
        block, "section", [(i, (i + distance) % count) for i in range(count)]
    )


def seq_shift(block, distance):
    count = lax.axis_size("seq")
    return lax.ppermute(
        block, "seq", [(i, i + distance) for i in range(count) if 0 <= i + distance < count]
    )


def seq_flip(block, mask):
    count = lax.axis_size("seq")
    return lax.ppermute(block, "seq", [(i, i ^ mask) for i in range(count)])


def head_swap(block):
    return lax.ppermute(block, "head", [(0, 1), (1, 0)])


def across(block, mask):
    count = lax.axis_size("seq")
    route = [(2 * i + g, 2 * (i ^ mask) + 1 - g) for i in range(count) for g in range(2)]
    return lax.ppermute(block, ("seq", "head"), route)


def key_value_body(notes_ref, wk_ref, wv_ref, out_ref):
    rows = notes_ref[...]
    out_ref[0] = dot(rows, wk_ref[...], NN).astype(BF16)
    out_ref[1] = dot(rows, wv_ref[...], NN).astype(BF16)


def key_values(notes, w_key, w_value, h0, hc):
    rows = notes.shape[0]
    wide = 2 * HD
    base = h0 * HD // wide
    weight = pl.BlockSpec((D, wide), lambda j: (0, base + j))
    return pl.pallas_call(
        key_value_body,
        grid=(hc * HD // wide,),
        in_specs=[pl.BlockSpec((rows, D), lambda j: (0, 0)), weight, weight],
        out_specs=pl.BlockSpec((2, rows, wide), lambda j: (0, 0, j)),
        out_shape=jax.ShapeDtypeStruct((2, rows, hc * HD), BF16),
        compiler_params=pltpu.CompilerParams(vmem_limit_bytes=16 * MIB),
        cost_estimate=pl.CostEstimate(
            flops=4 * rows * D * hc * HD,
            bytes_accessed=2 * (rows * D + 2 * D * hc * HD + 2 * rows * hc * HD),
            transcendentals=0,
        ),
        name="key_values",
    )(notes, w_key, w_value)


def attention_body(
    bias_ref, q_ref, g_ref, kvl_ref, kvo_ref, kvr_ref, dq_ref, own_ref, left_ref, right_ref,
    p_scr, ds_scr,
):
    scale2 = SCALE * LOG2E
    frames = q_ref.shape[0]
    nt = kvo_ref.shape[1]
    step = 256
    blocks = 3 * nt // BLK
    keys = jnp.concatenate([kvl_ref[0], kvo_ref[0], kvr_ref[0]], axis=0)
    values = jnp.concatenate([kvl_ref[1], kvo_ref[1], kvr_ref[1]], axis=0)
    for f in range(frames // step):
        cols = slice(f * step, (f + 1) * step)
        s = dot(keys, q_ref[cols, :], NT)
        gp = dot(values, g_ref[cols, :], NT)
        rows = [slice(j * BLK, (j + 1) * BLK) for j in range(blocks)]
        bias = [bias_ref[j : j + 1, cols] for j in range(blocks)]
        peak = None
        for j in range(blocks):
            top = jnp.max(s[rows[j]], axis=0, keepdims=True) + bias[j]
            peak = top if peak is None else jnp.maximum(peak, top)
        expos = []
        total = jnp.zeros((1, step), F32)
        mixed = jnp.zeros((1, step), F32)
        for j in range(blocks):
            e = jnp.exp2(s[rows[j]] * scale2 + (bias[j] - peak) * scale2)
            expos.append(e)
            total = total + jnp.sum(e, axis=0, keepdims=True)
            mixed = mixed + jnp.sum(e * gp[rows[j]], axis=0, keepdims=True)
        inv = 1.0 / total
        delta = mixed * inv
        for j in range(blocks):
            p = expos[j] * inv
            p_scr[rows[j], cols] = p.astype(BF16)
            ds_scr[rows[j], cols] = (p * (gp[rows[j]] - delta)).astype(BF16)
    dq_ref[...] = (dot(ds_scr[...], keys, TN) * SCALE).astype(BF16)
    dv = dot(p_scr[...], g_ref[...], NN)
    dk = dot(ds_scr[...], q_ref[...], NN) * SCALE
    for i, grad in enumerate((dk, dv)):
        left_ref[i] = grad[:nt].astype(BF16)
        own_ref[i] = grad[nt : 2 * nt]
        right_ref[i] = grad[2 * nt :].astype(BF16)


def attention(bias, queries, grad_ctx, kv_left, kv_own, kv_right, h0, hc):
    frames = queries.shape[0]
    nt = kv_own.shape[1]
    frame_in = pl.BlockSpec((frames, HD), lambda h: (0, h0 + h))
    note_io = pl.BlockSpec((2, nt, HD), lambda h: (0, 0, h))
    pairs = frames * 3 * nt * hc
    return pl.pallas_call(
        attention_body,
        grid=(hc,),
        in_specs=[
            pl.BlockSpec(bias.shape, lambda h: (0, 0)), frame_in, frame_in, note_io, note_io, note_io,
        ],
        out_specs=[pl.BlockSpec((frames, HD), lambda h: (0, h)), note_io, note_io, note_io],
        out_shape=[
            jax.ShapeDtypeStruct((frames, hc * HD), BF16),
            jax.ShapeDtypeStruct((2, nt, hc * HD), F32),
            jax.ShapeDtypeStruct((2, nt, hc * HD), BF16),
            jax.ShapeDtypeStruct((2, nt, hc * HD), BF16),
        ],
        scratch_shapes=[pltpu.VMEM((3 * nt, frames), BF16), pltpu.VMEM((3 * nt, frames), BF16)],
        compiler_params=pltpu.CompilerParams(vmem_limit_bytes=32 * MIB),
        cost_estimate=pl.CostEstimate(
            flops=20 * pairs * HD,
            bytes_accessed=hc * HD * (6 * frames + 32 * nt),
            transcendentals=pairs,
        ),
        name="attention",
    )(bias, queries, grad_ctx, kv_left, kv_own, kv_right)


def per_device(notes, frames, w_query, w_key, w_value, w_out, band_blocks, grad_mixed):
    nt = notes.shape[1]
    fr = frames.shape[1]
    cols = w_query.shape[1]
    half = D // 2
    shard = lax.axis_index("seq")
    group = lax.axis_index("head")
    core = shard % 2

    block_ids = (shard - 1) * (nt // BLK) + jnp.arange(8, dtype=jnp.int32)
    inside = (block_ids[:, None] >= band_blocks[0, 0][None]) & (
        block_ids[:, None] <= band_blocks[0, 1][None]
    )
    bias = jnp.repeat(jnp.where(inside, 0.0, -jnp.inf).astype(F32), BLK, axis=1)

    moved = []
    for h0, hc in CHUNKS:
        moved.append(section_shift(key_values(notes[0], w_key, w_value, h0, hc), 1))

    quarter = half // 2
    give = lax.dynamic_slice_in_dim(w_query, (1 - group) * half + core * quarter, quarter, 0)
    mine = across(give, 8)
    theirs = seq_flip(mine, 1)
    w_other = jnp.where(
        core == 0, jnp.concatenate([mine, theirs]), jnp.concatenate([theirs, mine])
    )
    w_own = lax.dynamic_slice_in_dim(w_query, group * half, half, 0)

    queries = dot(frames[0], w_query, NN).astype(BF16)
    grad_ctx = dot(grad_mixed[0], w_out, NT).astype(BF16)

    grad_q = []
    grad_q_other = []
    note_cols = []
    for (h0, hc), kv in zip(CHUNKS, moved):
        kv_left = seq_shift(kv, 1)
        kv_right = seq_shift(kv, -1)
        dq, own, left, right = attention(bias, queries, grad_ctx, kv_left, kv, kv_right, h0, hc)
        grad_q.append(dq)
        grad_q_other.append(head_swap(dq))
        summed = own + seq_shift(right, 1).astype(F32) + seq_shift(left, -1).astype(F32)
        note_cols.append(section_shift(summed.astype(BF16), -1))

    frame_sum = None
    for weight, grads in ((w_own, grad_q), (w_other, grad_q_other)):
        for (h0, hc), grad in zip(CHUNKS, grads):
            term = dot(grad, weight[:, h0 * HD : (h0 + hc) * HD], NT)
            frame_sum = term if frame_sum is None else frame_sum + term

    note_term = None
    for (h0, hc), grad in zip(CHUNKS, note_cols):
        part = slice(h0 * HD, (h0 + hc) * HD)
        term = dot(grad[0], w_key[:, part], NT) + dot(grad[1], w_value[:, part], NT)
        note_term = term if note_term is None else note_term + term
    note_term = note_term.astype(BF16)
    give_notes = lax.dynamic_slice_in_dim(note_term, (1 - group) * half, half, 1)
    keep_notes = lax.dynamic_slice_in_dim(note_term, group * half, half, 1)
    note_sum = keep_notes.astype(F32) + head_swap(give_notes).astype(F32)
    return (frame_sum.astype(BF16)[None], note_sum.astype(BF16)[None])


def solution(mesh):
    placed = (
        P("section", "seq", None),
        P("section", "seq", None),
        P(None, "head"),
        P(None, "head"),
        P(None, "head"),
        P("head", None),
        P("section", None, "seq"),
        P("section", "seq", None),
    )
    return jax.shard_map(
        per_device,
        mesh=mesh,
        in_specs=placed,
        out_specs=(P("section", "seq", "head"), P("section", "seq", "head")),
        check_vma=False,
    )
```

time: 427 us -> 160 us (0.37)
  matrix products: 215 us -> 29.5 us
  waiting for transfers between devices: 155 us -> 30.9 us
  starting transfers between devices: 15.2 us -> 52.2 us
  Pallas kernels: 0 us -> 29.2 us
  between operations: 14.3 us -> 1.06 us
  local copies, waits for them, and re-layouts: 22.4 us -> 12 us
    dot_general x15 -> x14, matrix products: 193 us -> 29.5 us  [dot(): return lax.dot_general(a, b, dims, preferred_element_type=F32)]
    reduce_scatter x2 -> x0, waiting for transfers between devices: 90.4 us -> none  [the longest x1 60.8 us: per_device(): lax.psum_scatter(frame_term.astype(jnp.bfloat16), 'head', scatter_dimensi...]
    ppermute x6 -> x24, starting transfers between devices: 15.2 us -> 52.2 us  [the longest x12 32.6 us: seq_shift(): lax.ppermute(block, 'seq', [(i, i + distance) for i in range(count) if 0...]
    ppermute x6 -> x24, waiting for transfers between devices: 64.8 us -> 30.9 us  [the longest x4 16.6 us: head_swap(): return lax.ppermute(block, 'head', [(0, 1), (1, 0)])]
    pallas_call x0 -> x6, Pallas kernels: none -> 29.2 us  [the longest x3 25.7 us: attention(): pl.pallas_call(attention_body, grid=(hc,), in_specs=[pl.BlockSpec(bias.sh...]
    sub x2 -> x0, matrix products: 21.3 us -> none  [one_block(): expos = jnp.exp(scores - peak)]
    dynamic_update_slice x2 -> x0, local copies, waits for them, and re-layouts: 5.74 us -> none  [per_device(): lax.scan(one_block, (empty, empty), inputs)]
    unnamed x39 -> x20, local copies, waits for them, and re-layouts: 9.85 us -> 8.8 us
  transfers between devices with their start and end apart: 8 -> 24, of which waited for: 7 -> 5; matrix products, arithmetic and copies ran while one was open for 6% -> 22% of each run, Pallas kernels for 0% -> 18%
where the time goes in v1:
time: 160 us; the launch traced here: 158 us
  starting transfers between devices  52.2 us (33%)
  waiting for transfers between devices  30.9 us (19%)
  matrix products  29.5 us (18%)
  Pallas kernels  29.2 us (18%)
  local copies, waits for them, and re-layouts  12 us (8%)
  other arithmetic  3.52 us (2%)
    ppermute x12, starting transfers between devices, seq_shift(): lax.ppermute(block, 'seq', [(i, i + distance) for i in range(count) if 0...  32.6 us
    dot_general x14, matrix products, dot(): return lax.dot_general(a, b, dims, preferred_element_type=F32)  29.5 us
    pallas_call x3, Pallas kernels, attention(): pl.pallas_call(attention_body, grid=(hc,), in_specs=[pl.BlockSpec(bias.sh...  25.7 us
    ppermute x4, waiting for transfers between devices, head_swap(): return lax.ppermute(block, 'head', [(0, 1), (1, 0)])  16.6 us
    ppermute x6, waiting for transfers between devices, section_shift(): lax.ppermute(block, 'section', [(i, (i + distance) % count) for i in rang...  12.8 us
    unnamed x20, local copies, waits for them, and re-layouts  8.8 us
    ppermute x6, starting transfers between devices, section_shift(): lax.ppermute(block, 'section', [(i, (i + distance) % count) for i in rang...  7.92 us
    ppermute x4, starting transfers between devices, head_swap(): return lax.ppermute(block, 'head', [(0, 1), (1, 0)])  7.87 us
  transfers between devices with their start and end apart: 24, of which 5 were waited for; matrix products, arithmetic and copies ran while one was open for 22% of the time, Pallas kernels for 18%

profile of v1, /device:TPU:1, one launch (start us, length us, event | category | flops | bytes accessed | tf_op | source)
XLA Modules:
  0.0 158.3 jit_solution(17167819238695019313)
XLA Ops:
  0.6 2.2 %copy-done = bf16[2048,1024]{1,0:T(8,128)(2,1)S(1)} copy-done((bf16[2048,1024]{1,0:T(8,128)(2,1)S(1)}, bf16[2048,1024]{1,0:T(8,128)(2,1)}, u32[]{:S(2)}) %copy-start) | copy-done | bytes 4194328
  2.8 2.2 %copy-done.2 = bf16[2048,1024]{1,0:T(8,128)(2,1)S(1)} copy-done((bf16[2048,1024]{1,0:T(8,128)(2,1)S(1)}, bf16[2048,1024]{1,0:T(8,128)(2,1)}, u32[]{:S(2)}) %copy-start.2) | copy-done | bytes 4194328
  5.0 1.2 copy-done.4
  7.0 2.1 %collective-permute-start = (bf16[2,256,256]{2,1,0:T(8,128)(2,1)S(1)}, bf16[2,256,256]{2,1,0:T(8,128)(2,1)S(1)}, u32[]{:S(2)}, u32[]{:S(2)}) collective-permute-start(bf16[2,256,256]{2,1,0:T(8,128)(2,1)S(1)} %key_values.3), channel_id=1, source_target_pairs={{0,32},{32,64},{64,96},{96,0},{1,33},{33,65},{65,97},{97,1},{2,34}... | collective-permute-start | bytes 786440 | tf_op jit(solution)/shard_map/ppermute | solution.py:30
  9.8 1.3 collective-permute-start.3
  11.1 2.0 %key_values.5 = bf16[2,256,512]{2,1,0:T(8,128)(2,1)S(1)} custom-call(bf16[256,2048]{1,0:T(8,128)(2,1)S(1)} %bitcast.49, bf16[2048,1024]{1,0:T(8,128)(2,1)S(1)} %copy-done.2, bf16[2048,1024]{1,0:T(8,128)(2,1)S(1)} %copy-done), custom_call_target="tpu_custom_call" | custom-call | flops 1073741824 | bytes 5767168 | tf_op jit(solution)/shard_map/key_values/pallas_call | solution.py:68
  13.1 1.0 collective-permute-start.6
  14.1 2.3 %constant_dynamic-slice_fusion.1 = bf16[512,1024]{1,0:T(8,128)(2,1)} fusion(bf16[2048,1024]{1,0:T(8,128)(2,1)} %param.10, s32[]{:T(128)S(6)} %select_n.33), kind=kLoop, calls=%fused_computation.51 | loop fusion | bytes 2097156 | tf_op jit(solution)/shard_map/dynamic_slice | solution.py:178
  16.4 3.8 %collective-permute-start.10 = (bf16[512,1024]{1,0:T(8,128)(2,1)}, bf16[512,1024]{1,0:T(8,128)(2,1)S(1)}, u32[]{:S(2)}, u32[]{:S(2)}) collective-permute-start(bf16[512,1024]{1,0:T(8,128)(2,1)} %constant_dynamic-slice_fusion.1), channel_id=1, source_target_pairs={{0,17},{1,16},{2,19},{3,18},{4,21},{5,20},{6,23},{7,22},{8,25},{9,... | collective-permute-start | bytes 3145736 | tf_op jit(solution)/shard_map/ppermute | solution.py:54
  20.2 9.4 %fusion.11.q_ref = bf16[1024,1024]{1,0:T(8,128)(2,1)} fusion(bf16[2048,1024]{1,0:T(8,128)(2,1)} %param.10, bf16[1,1024,2048]{2,1,0:T(8,128)(2,1)} %param.9), kind=kOutput, calls=%fused_computation.16 | convolution fusion | flops 4296015872 | bytes 10485760 | tf_op jit(solution)/shard_map/dot_general | solution.py:25
  29.6 5.8 %fusion.14.g_ref = bf16[1024,1024]{1,0:T(8,128)(2,1)} fusion(bf16[1024,2048]{1,0:T(8,128)(2,1)S(1)} %copy-done.8, bf16[1,1024,2048]{2,1,0:T(8,128)(2,1)S(1)} %copy-done.9), kind=kOutput, calls=%fused_computation.17 | convolution fusion | flops 4296015872 | bytes 10485760 | tf_op jit(solution)/shard_map/dot_general | solution.py:25
  35.5 3.7 %collective-permute-start.2 = (bf16[2,256,256]{2,1,0:T(8,128)(2,1)S(1)}, bf16[2,256,256]{2,1,0:T(8,128)(2,1)S(1)}, u32[]{:S(2)}, u32[]{:S(2)}) collective-permute-start(bf16[2,256,256]{2,1,0:T(8,128)(2,1)S(1)} %collective-permute-done.kvo_ref), channel_id=1, source_target_pairs={{2,0},{4,2},{6,4},{8,6},{10,8},{12,10},{14,12},{16,14},{18,16},{20... | collective-permute-start | bytes 786440 | tf_op jit(solution)/shard_map/ppermute | solution.py:37
  39.2 3.1 %collective-permute-start.1 = (bf16[2,256,256]{2,1,0:T(8,128)(2,1)S(1)}, bf16[2,256,256]{2,1,0:T(8,128)(2,1)S(1)}, u32[]{:S(2)}, u32[]{:S(2)}) collective-permute-start(bf16[2,256,256]{2,1,0:T(8,128)(2,1)S(1)} %collective-permute-done.kvo_ref), channel_id=1, source_target_pairs={{0,2},{2,4},{4,6},{6,8},{8,10},{10,12},{12,14},{14,16},{16,18},{18... | collective-permute-start | bytes 786440 | tf_op jit(solution)/shard_map/ppermute | solution.py:37
  42.4 1.9 %collective-permute-start.5 = (bf16[2,256,256]{2,1,0:T(8,128)(2,1)S(1)}, bf16[2,256,256]{2,1,0:T(8,128)(2,1)S(1)}, u32[]{:S(2)}, u32[]{:S(2)}) collective-permute-start(bf16[2,256,256]{2,1,0:T(8,128)(2,1)S(1)} %collective-permute-done.3.kvo_ref), channel_id=1, source_target_pairs={{2,0},{4,2},{6,4},{8,6},{10,8},{12,10},{14,12},{16,14},{18,16},{20... | collective-permute-start | bytes 786440 | tf_op jit(solution)/shard_map/ppermute | solution.py:37
  44.4 3.6 %collective-permute-start.4 = (bf16[2,256,256]{2,1,0:T(8,128)(2,1)S(1)}, bf16[2,256,256]{2,1,0:T(8,128)(2,1)S(1)}, u32[]{:S(2)}, u32[]{:S(2)}) collective-permute-start(bf16[2,256,256]{2,1,0:T(8,128)(2,1)S(1)} %collective-permute-done.3.kvo_ref), channel_id=1, source_target_pairs={{0,2},{2,4},{4,6},{6,8},{8,10},{10,12},{12,14},{14,16},{16,18},{18... | collective-permute-start | bytes 786440 | tf_op jit(solution)/shard_map/ppermute | solution.py:37
  48.0 1.6 copy-done.5
  49.6 1.6 %copy-done.6 = bf16[1024,1024]{1,0:T(8,128)(2,1)S(1)} copy-done((bf16[1024,1024]{1,0:T(8,128)(2,1)S(1)}, bf16[1024,1024]{1,0:T(8,128)(2,1)}, u32[]{:S(2)}) %copy-start.6) | copy-done | bytes 2097176
  51.2 6.4 %attention.3 = (bf16[1024,256]{1,0:T(8,128)(2,1)S(1)}, f32[2,256,256]{2,1,0:T(8,128)S(1)}, bf16[2,256,256]{2,1,0:T(8,128)(2,1)S(1)}, bf16[2,256,256]{2,1,0:T(8,128)(2,1)S(1)}) custom-call(f32[8,1024]{1,0:T(8,128)S(1)} %broadcast_bitcast_fusion.bias_ref, bf16[1024,1024]{1,0:T(8,128)(2,1)S(1)} %copy-done.5, bf16[1024,1024]{1,0:T(8,128)(2,1)S(1)} %copy-done.6, ...), custom_call_target="tpu_custom_call" | custom-call | flops 4026531840 | bytes 3670016 | tf_op jit(solution)/shard_map/attention/pallas_call | solution.py:134
  57.6 2.4 %collective-permute-start.14 = (bf16[2,256,256]{2,1,0:T(8,128)(2,1)S(1)}, bf16[2,256,256]{2,1,0:T(8,128)(2,1)S(1)}, u32[]{:S(2)}, u32[]{:S(2)}) collective-permute-start(bf16[2,256,256]{2,1,0:T(8,128)(2,1)S(1)} %get-tuple-element.18), channel_id=1, source_target_pairs={{0,2},{2,4},{4,6},{6,8},{8,10},{10,12},{12,14},{14,16},{16,18},{18... | collective-permute-start | bytes 786440 | tf_op jit(solution)/shard_map/ppermute | solution.py:37
  60.0 1.8 %fusion.36 = f32[1024,1024]{1,0:T(8,128)S(1)} fusion(bf16[1024,256]{1,0:T(8,128)(2,1)S(1)} %get-tuple-element.14, bf16[2048,1024]{1,0:T(8,128)(2,1)} %param.10, s32[]{:T(128)S(6)} %select_n.30), kind=kOutput, calls=%fused_computation.37 | convolution fusion | flops 536870912 | bytes 5242884 | tf_op jit(solution)/shard_map/dot_general | solution.py:25
  61.8 2.2 %collective-permute-start.15 = (bf16[2,256,256]{2,1,0:T(8,128)(2,1)S(1)}, bf16[2,256,256]{2,1,0:T(8,128)(2,1)S(1)}, u32[]{:S(2)}, u32[]{:S(2)}) collective-permute-start(bf16[2,256,256]{2,1,0:T(8,128)(2,1)S(1)} %get-tuple-element.19), channel_id=1, source_target_pairs={{2,0},{4,2},{6,4},{8,6},{10,8},{12,10},{14,12},{16,14},{18,16},{20... | collective-permute-start | bytes 786440 | tf_op jit(solution)/shard_map/ppermute | solution.py:37
  64.0 1.9 %collective-permute-start.8 = (bf16[2,256,512]{2,1,0:T(8,128)(2,1)S(1)}, bf16[2,256,512]{2,1,0:T(8,128)(2,1)S(1)}, u32[]{:S(2)}, u32[]{:S(2)}) collective-permute-start(bf16[2,256,512]{2,1,0:T(8,128)(2,1)S(1)} %collective-permute-done.6.kvo_ref), channel_id=1, source_target_pairs={{2,0},{4,2},{6,4},{8,6},{10,8},{12,10},{14,12},{16,14},{18,16},{20... | collective-permute-start | bytes 1572872 | tf_op jit(solution)/shard_map/ppermute | solution.py:37
  65.9 3.6 %collective-permute-start.7 = (bf16[2,256,512]{2,1,0:T(8,128)(2,1)S(1)}, bf16[2,256,512]{2,1,0:T(8,128)(2,1)S(1)}, u32[]{:S(2)}, u32[]{:S(2)}) collective-permute-start(bf16[2,256,512]{2,1,0:T(8,128)(2,1)S(1)} %collective-permute-done.6.kvo_ref), channel_id=1, source_target_pairs={{0,2},{2,4},{4,6},{6,8},{8,10},{10,12},{12,14},{14,16},{16,18},{18... | collective-permute-start | bytes 1572872 | tf_op jit(solution)/shard_map/ppermute | solution.py:37
  69.6 6.4 %attention.4 = (bf16[1024,256]{1,0:T(8,128)(2,1)S(1)}, f32[2,256,256]{2,1,0:T(8,128)S(1)}, bf16[2,256,256]{2,1,0:T(8,128)(2,1)S(1)}, bf16[2,256,256]{2,1,0:T(8,128)(2,1)S(1)}) custom-call(f32[8,1024]{1,0:T(8,128)S(1)} %broadcast_bitcast_fusion.bias_ref, bf16[1024,1024]{1,0:T(8,128)(2,1)S(1)} %copy-done.5, bf16[1024,1024]{1,0:T(8,128)(2,1)S(1)} %copy-done.6, ...), custom_call_target="tpu_custom_call" | custom-call | flops 4026531840 | bytes 3670016 | tf_op jit(solution)/shard_map/attention/pallas_call | solution.py:134
  76.0 1.8 %fusion.34 = f32[1024,1024]{1,0:T(8,128)S(1)} fusion(bf16[1024,256]{1,0:T(8,128)(2,1)S(1)} %get-tuple-element.15, bf16[2048,1024]{1,0:T(8,128)(2,1)} %param.10, s32[]{:T(128)S(6)} %select_n.30, s32[]{:T(128)S(6)} %add.103), kind=kOutput, calls=%fused_computation.35 | convolution fusion | flops 536870912 | bytes 5242888 | tf_op jit(solution)/shard_map/dot_general | solution.py:25
  77.9 2.2 %collective-permute-start.17 = (bf16[2,256,256]{2,1,0:T(8,128)(2,1)S(1)}, bf16[2,256,256]{2,1,0:T(8,128)(2,1)S(1)}, u32[]{:S(2)}, u32[]{:S(2)}) collective-permute-start(bf16[2,256,256]{2,1,0:T(8,128)(2,1)S(1)} %get-tuple-element.21), channel_id=1, source_target_pairs={{0,2},{2,4},{4,6},{6,8},{8,10},{10,12},{12,14},{14,16},{16,18},{18... | collective-permute-start | bytes 786440 | tf_op jit(solution)/shard_map/ppermute | solution.py:37
  80.2 2.4 %collective-permute-start.18 = (bf16[2,256,256]{2,1,0:T(8,128)(2,1)S(1)}, bf16[2,256,256]{2,1,0:T(8,128)(2,1)S(1)}, u32[]{:S(2)}, u32[]{:S(2)}) collective-permute-start(bf16[2,256,256]{2,1,0:T(8,128)(2,1)S(1)} %get-tuple-element.22), channel_id=1, source_target_pairs={{2,0},{4,2},{6,4},{8,6},{10,8},{12,10},{14,12},{16,14},{18,16},{20... | collective-permute-start | bytes 786440 | tf_op jit(solution)/shard_map/ppermute | solution.py:37
  82.6 1.8 %collective-permute-start.16 = (bf16[2,256,256]{2,1,0:T(8,128)(2,1)S(1)}, bf16[2,256,256]{2,1,0:T(8,128)(2,1)S(1)}, u32[]{:S(2)}, u32[]{:S(2)}) collective-permute-start(bf16[2,256,256]{2,1,0:T(8,128)(2,1)S(1)} %add_convert_fusion.4), channel_id=1, source_target_pairs={{0,96},{32,0},{64,32},{96,64},{1,97},{33,1},{65,33},{97,65},{2,98}... | collective-permute-start | bytes 786440 | tf_op jit(solution)/shard_map/ppermute | solution.py:30
  84.4 12.9 %attention.5 = (bf16[1024,512]{1,0:T(8,128)(2,1)S(1)}, f32[2,256,512]{2,1,0:T(8,128)S(1)}, bf16[2,256,512]{2,1,0:T(8,128)(2,1)S(1)}, bf16[2,256,512]{2,1,0:T(8,128)(2,1)S(1)}) custom-call(f32[8,1024]{1,0:T(8,128)S(1)} %broadcast_bitcast_fusion.bias_ref, bf16[1024,1024]{1,0:T(8,128)(2,1)S(1)} %copy-done.5, bf16[1024,1024]{1,0:T(8,128)(2,1)S(1)} %copy-done.6, ...), custom_call_target="tpu_custom_call" | custom-call | flops 8053063680 | bytes 7340032 | tf_op jit(solution)/shard_map/attention/pallas_call | solution.py:134
  97.3 3.7 %collective-permute-start.20 = (bf16[2,256,512]{2,1,0:T(8,128)(2,1)S(1)}, bf16[2,256,512]{2,1,0:T(8,128)(2,1)S(1)}, u32[]{:S(2)}, u32[]{:S(2)}) collective-permute-start(bf16[2,256,512]{2,1,0:T(8,128)(2,1)S(1)} %get-tuple-element.24), channel_id=1, source_target_pairs={{0,2},{2,4},{4,6},{6,8},{8,10},{10,12},{12,14},{14,16},{16,18},{18... | collective-permute-start | bytes 1572872 | tf_op jit(solution)/shard_map/ppermute | solution.py:37
  101.0 1.9 %collective-permute-start.21 = (bf16[2,256,512]{2,1,0:T(8,128)(2,1)S(1)}, bf16[2,256,512]{2,1,0:T(8,128)(2,1)S(1)}, u32[]{:S(2)}, u32[]{:S(2)}) collective-permute-start(bf16[2,256,512]{2,1,0:T(8,128)(2,1)S(1)} %get-tuple-element.25), channel_id=1, source_target_pairs={{2,0},{4,2},{6,4},{8,6},{10,8},{12,10},{14,12},{16,14},{18,16},{20... | collective-permute-start | bytes 1572872 | tf_op jit(solution)/shard_map/ppermute | solution.py:37
  103.1 3.3 %collective-permute-start.9 = (bf16[1024,256]{1,0:T(8,128)(2,1)S(1)}, bf16[1024,256]{1,0:T(8,128)(2,1)S(1)}, u32[]{:S(2)}, u32[]{:S(2)}) collective-permute-start(bf16[1024,256]{1,0:T(8,128)(2,1)S(1)} %get-tuple-element.14), channel_id=1, source_target_pairs={{0,1},{1,0},{2,3},{3,2},{4,5},{5,4},{6,7},{7,6},{8,9},{9,8},{10,11... | collective-permute-start | bytes 1572872 | tf_op jit(solution)/shard_map/ppermute | solution.py:48
  107.1 3.2 %collective-permute-start.13 = (bf16[1024,512]{1,0:T(8,128)(2,1)S(1)}, bf16[1024,512]{1,0:T(8,128)(2,1)S(1)}, u32[]{:S(2)}, u32[]{:S(2)}) collective-permute-start(bf16[1024,512]{1,0:T(8,128)(2,1)S(1)} %get-tuple-element.16), channel_id=1, source_target_pairs={{0,1},{1,0},{2,3},{3,2},{4,5},{5,4},{6,7},{7,6},{8,9},{9,8},{10,11... | collective-permute-start | bytes 3145736 | tf_op jit(solution)/shard_map/ppermute | solution.py:48
  110.3 1.5 collective-permute-done.21
  112.1 1.8 %collective-permute-done.19 = bf16[2,256,256]{2,1,0:T(8,128)(2,1)S(1)} collective-permute-done((bf16[2,256,256]{2,1,0:T(8,128)(2,1)S(1)}, bf16[2,256,256]{2,1,0:T(8,128)(2,1)S(1)}, u32[]{:S(2)}, u32[]{:S(2)}) %collective-permute-start.19) | collective-permute-done | bytes 262176 | tf_op jit(solution)/shard_map/ppermute | solution.py:30
  113.9 1.5 collective-permute-start.22
  116.3 11.0 %collective-permute-done.22 = bf16[2,256,512]{2,1,0:T(8,128)(2,1)S(1)} collective-permute-done((bf16[2,256,512]{2,1,0:T(8,128)(2,1)S(1)}, bf16[2,256,512]{2,1,0:T(8,128)(2,1)S(1)}, u32[]{:S(2)}, u32[]{:S(2)}) %collective-permute-start.22) | collective-permute-done | bytes 524320 | tf_op jit(solution)/shard_map/ppermute | solution.py:30
  127.3 0.8 fusion.8
  128.1 0.8 convolution_add_fusion
  129.5 0.8 constant_dynamic-slice_fusion
  130.4 1.3 collective-permute-start.23
  131.7 1.0 maximum_select_fusion
  132.7 0.7 fusion.32
  133.5 13.7 %collective-permute-done.13 = bf16[1024,512]{1,0:T(8,128)(2,1)S(1)} collective-permute-done((bf16[1024,512]{1,0:T(8,128)(2,1)S(1)}, bf16[1024,512]{1,0:T(8,128)(2,1)S(1)}, u32[]{:S(2)}, u32[]{:S(2)}) %collective-permute-start.13) | collective-permute-done | bytes 1048608 | tf_op jit(solution)/shard_map/ppermute | solution.py:48
  147.1 1.3 fusion.17
  149.2 4.2 %fusion.7 = bf16[1,1024,1024]{2,1,0:T(8,128)(2,1)} fusion(f32[1024,1024]{1,0:T(8,128)S(1)} %fusion.17, f32[1024,1024]{1,0:T(8,128)S(1)} %fusion.30, f32[1024,1024]{1,0:T(8,128)S(1)} %fusion.32, f32[1024,1024]{1,0:T(8,128)S(1)} %fusion.36, f32[1024,1024]{1,0:T(8,128)S(1)} %fusion.34, bf16[1024,512]{1,0:T(8,128)(2,1)S(1)} %get-tuple-element.16, ...), kind=kOutput, calls=%fused_computation.11 | convolution fusion | flops 1080033280 | bytes 25165832 | tf_op jit(solution)/shard_map/dot_general | solution.py:25
  153.4 2.9 %collective-permute-done.23 = bf16[256,1024]{1,0:T(8,128)(2,1)} collective-permute-done((bf16[256,1024]{1,0:T(8,128)(2,1)}, bf16[256,1024]{1,0:T(8,128)(2,1)}, u32[]{:S(2)}, u32[]{:S(2)}) %collective-permute-start.23) | collective-permute-done | bytes 524320 | tf_op jit(solution)/shard_map/ppermute | solution.py:48
  156.3 2.0 %fusion.29 = bf16[1,256,1024]{2,1,0:T(8,128)(2,1)} fusion(bf16[256,1024]{1,0:T(8,128)(2,1)} %collective-permute-done.23, bf16[256,2048]{1,0:T(8,128)(2,1)S(1)} %fusion.6, s32[]{:T(128)S(6)} %select_n.30), kind=kLoop, calls=%fused_computation.30 | loop fusion | flops 1048576 | bytes 1572868 | tf_op jit(solution)/shard_map/broadcast_in_dim | solution.py:216
  (51 shorter events, 5.3 us)
Async XLA Ops:
  0.6 2.2 %copy-start = (bf16[2048,1024]{1,0:T(8,128)(2,1)S(1)}, bf16[2048,1024]{1,0:T(8,128)(2,1)}, u32[]{:S(2)}) copy-start(bf16[2048,1024]{1,0:T(8,128)(2,1)} %wv_ref.5) | copy-start | bytes 12582916
  2.8 2.2 %copy-start.2 = (bf16[2048,1024]{1,0:T(8,128)(2,1)S(1)}, bf16[2048,1024]{1,0:T(8,128)(2,1)}, u32[]{:S(2)}) copy-start(bf16[2048,1024]{1,0:T(8,128)(2,1)} %wk_ref.5) | copy-start | bytes 12582916
  5.0 1.2 copy-start.4
  7.0 28.5 %collective-permute-start = (bf16[2,256,256]{2,1,0:T(8,128)(2,1)S(1)}, bf16[2,256,256]{2,1,0:T(8,128)(2,1)S(1)}, u32[]{:S(2)}, u32[]{:S(2)}) collective-permute-start(bf16[2,256,256]{2,1,0:T(8,128)(2,1)S(1)} %key_values.3), channel_id=1, source_target_pairs={{0,32},{32,64},{64,96},{96,0},{1,33},{33,65},{65,97},{97,1},{2,34}... | collective-permute-start | bytes 786440 | tf_op jit(solution)/shard_map/ppermute | solution.py:30
  9.8 32.6 %collective-permute-start.3 = (bf16[2,256,256]{2,1,0:T(8,128)(2,1)S(1)}, bf16[2,256,256]{2,1,0:T(8,128)(2,1)S(1)}, u32[]{:S(2)}, u32[]{:S(2)}) collective-permute-start(bf16[2,256,256]{2,1,0:T(8,128)(2,1)S(1)} %key_values.4), channel_id=1, source_target_pairs={{0,32},{32,64},{64,96},{96,0},{1,33},{33,65},{65,97},{97,1},{2,34}... | collective-permute-start | bytes 786440 | tf_op jit(solution)/shard_map/ppermute | solution.py:30
  13.1 50.8 %collective-permute-start.6 = (bf16[2,256,512]{2,1,0:T(8,128)(2,1)S(1)}, bf16[2,256,512]{2,1,0:T(8,128)(2,1)S(1)}, u32[]{:S(2)}, u32[]{:S(2)}) collective-permute-start(bf16[2,256,512]{2,1,0:T(8,128)(2,1)S(1)} %key_values.5), channel_id=1, source_target_pairs={{0,32},{32,64},{64,96},{96,0},{1,33},{33,65},{65,97},{97,1},{2,34}... | collective-permute-start | bytes 1572872 | tf_op jit(solution)/shard_map/ppermute | solution.py:30
  16.4 90.4 %collective-permute-start.10 = (bf16[512,1024]{1,0:T(8,128)(2,1)}, bf16[512,1024]{1,0:T(8,128)(2,1)S(1)}, u32[]{:S(2)}, u32[]{:S(2)}) collective-permute-start(bf16[512,1024]{1,0:T(8,128)(2,1)} %constant_dynamic-slice_fusion.1), channel_id=1, source_target_pairs={{0,17},{1,16},{2,19},{3,18},{4,21},{5,20},{6,23},{7,22},{8,25},{9,... | collective-permute-start | bytes 3145736 | tf_op jit(solution)/shard_map/ppermute | solution.py:54
  20.2 9.4 %copy-start.8 = (bf16[1024,2048]{1,0:T(8,128)(2,1)S(1)}, bf16[1024,2048]{1,0:T(8,128)(2,1)}, u32[]{:S(2)}) copy-start(bf16[1024,2048]{1,0:T(8,128)(2,1)} %param.13) | copy-start | bytes 12582916
  20.2 9.4 %copy-start.9 = (bf16[1,1024,2048]{2,1,0:T(8,128)(2,1)S(1)}, bf16[1,1024,2048]{2,1,0:T(8,128)(2,1)}, u32[]{:S(2)}) copy-start(bf16[1,1024,2048]{2,1,0:T(8,128)(2,1)} %param.15) | copy-start | bytes 12582916
  29.6 5.9 %copy-start.7 = (s32[1,2,8]{2,1,0:T(2,128)S(1)}, s32[1,2,8]{2,1,0:T(2,128)}, u32[]{:S(2)}) copy-start(s32[1,2,8]{2,1,0:T(2,128)} %param.14) | copy-start | bytes 196
  35.5 8.9 %collective-permute-start.2 = (bf16[2,256,256]{2,1,0:T(8,128)(2,1)S(1)}, bf16[2,256,256]{2,1,0:T(8,128)(2,1)S(1)}, u32[]{:S(2)}, u32[]{:S(2)}) collective-permute-start(bf16[2,256,256]{2,1,0:T(8,128)(2,1)S(1)} %collective-permute-done.kvo_ref), channel_id=1, source_target_pairs={{2,0},{4,2},{6,4},{8,6},{10,8},{12,10},{14,12},{16,14},{18,16},{20... | collective-permute-start | bytes 786440 | tf_op jit(solution)/shard_map/ppermute | solution.py:37
  39.2 8.8 %collective-permute-start.1 = (bf16[2,256,256]{2,1,0:T(8,128)(2,1)S(1)}, bf16[2,256,256]{2,1,0:T(8,128)(2,1)S(1)}, u32[]{:S(2)}, u32[]{:S(2)}) collective-permute-start(bf16[2,256,256]{2,1,0:T(8,128)(2,1)S(1)} %collective-permute-done.kvo_ref), channel_id=1, source_target_pairs={{0,2},{2,4},{4,6},{6,8},{8,10},{10,12},{12,14},{14,16},{16,18},{18... | collective-permute-start | bytes 786440 | tf_op jit(solution)/shard_map/ppermute | solution.py:37
  42.4 19.3 %collective-permute-start.5 = (bf16[2,256,256]{2,1,0:T(8,128)(2,1)S(1)}, bf16[2,256,256]{2,1,0:T(8,128)(2,1)S(1)}, u32[]{:S(2)}, u32[]{:S(2)}) collective-permute-start(bf16[2,256,256]{2,1,0:T(8,128)(2,1)S(1)} %collective-permute-done.3.kvo_ref), channel_id=1, source_target_pairs={{2,0},{4,2},{6,4},{8,6},{10,8},{12,10},{14,12},{16,14},{18,16},{20... | collective-permute-start | bytes 786440 | tf_op jit(solution)/shard_map/ppermute | solution.py:37
  44.4 21.5 %collective-permute-start.4 = (bf16[2,256,256]{2,1,0:T(8,128)(2,1)S(1)}, bf16[2,256,256]{2,1,0:T(8,128)(2,1)S(1)}, u32[]{:S(2)}, u32[]{:S(2)}) collective-permute-start(bf16[2,256,256]{2,1,0:T(8,128)(2,1)S(1)} %collective-permute-done.3.kvo_ref), channel_id=1, source_target_pairs={{0,2},{2,4},{4,6},{6,8},{8,10},{10,12},{12,14},{14,16},{16,18},{18... | collective-permute-start | bytes 786440 | tf_op jit(solution)/shard_map/ppermute | solution.py:37
  48.0 1.6 %copy-start.5 = (bf16[1024,1024]{1,0:T(8,128)(2,1)S(1)}, bf16[1024,1024]{1,0:T(8,128)(2,1)}, u32[]{:S(2)}) copy-start(bf16[1024,1024]{1,0:T(8,128)(2,1)} %fusion.11.q_ref) | copy-start | bytes 6291460
  49.6 1.6 %copy-start.6 = (bf16[1024,1024]{1,0:T(8,128)(2,1)S(1)}, bf16[1024,1024]{1,0:T(8,128)(2,1)}, u32[]{:S(2)}) copy-start(bf16[1024,1024]{1,0:T(8,128)(2,1)} %fusion.14.g_ref) | copy-start | bytes 6291460
  57.6 20.2 %collective-permute-start.14 = (bf16[2,256,256]{2,1,0:T(8,128)(2,1)S(1)}, bf16[2,256,256]{2,1,0:T(8,128)(2,1)S(1)}, u32[]{:S(2)}, u32[]{:S(2)}) collective-permute-start(bf16[2,256,256]{2,1,0:T(8,128)(2,1)S(1)} %get-tuple-element.18), channel_id=1, source_target_pairs={{0,2},{2,4},{4,6},{6,8},{8,10},{10,12},{12,14},{14,16},{16,18},{18... | collective-permute-start | bytes 786440 | tf_op jit(solution)/shard_map/ppermute | solution.py:37
  61.8 16.1 %collective-permute-start.15 = (bf16[2,256,256]{2,1,0:T(8,128)(2,1)S(1)}, bf16[2,256,256]{2,1,0:T(8,128)(2,1)S(1)}, u32[]{:S(2)}, u32[]{:S(2)}) collective-permute-start(bf16[2,256,256]{2,1,0:T(8,128)(2,1)S(1)} %get-tuple-element.19), channel_id=1, source_target_pairs={{2,0},{4,2},{6,4},{8,6},{10,8},{12,10},{14,12},{16,14},{18,16},{20... | collective-permute-start | bytes 786440 | tf_op jit(solution)/shard_map/ppermute | solution.py:37
  64.0 16.2 %collective-permute-start.8 = (bf16[2,256,512]{2,1,0:T(8,128)(2,1)S(1)}, bf16[2,256,512]{2,1,0:T(8,128)(2,1)S(1)}, u32[]{:S(2)}, u32[]{:S(2)}) collective-permute-start(bf16[2,256,512]{2,1,0:T(8,128)(2,1)S(1)} %collective-permute-done.6.kvo_ref), channel_id=1, source_target_pairs={{2,0},{4,2},{6,4},{8,6},{10,8},{12,10},{14,12},{16,14},{18,16},{20... | collective-permute-start | bytes 1572872 | tf_op jit(solution)/shard_map/ppermute | solution.py:37
  65.9 16.7 %collective-permute-start.7 = (bf16[2,256,512]{2,1,0:T(8,128)(2,1)S(1)}, bf16[2,256,512]{2,1,0:T(8,128)(2,1)S(1)}, u32[]{:S(2)}, u32[]{:S(2)}) collective-permute-start(bf16[2,256,512]{2,1,0:T(8,128)(2,1)S(1)} %collective-permute-done.6.kvo_ref), channel_id=1, source_target_pairs={{0,2},{2,4},{4,6},{6,8},{8,10},{10,12},{12,14},{14,16},{16,18},{18... | collective-permute-start | bytes 1572872 | tf_op jit(solution)/shard_map/ppermute | solution.py:37
  77.8 70.6 %collective-permute-start.12 = (bf16[1024,256]{1,0:T(8,128)(2,1)S(1)}, bf16[1024,256]{1,0:T(8,128)(2,1)S(1)}, u32[]{:S(2)}, u32[]{:S(2)}) collective-permute-start(bf16[1024,256]{1,0:T(8,128)(2,1)S(1)} %get-tuple-element.15), channel_id=1, source_target_pairs={{0,1},{1,0},{2,3},{3,2},{4,5},{5,4},{6,7},{7,6},{8,9},{9,8},{10,11... | collective-permute-start | bytes 1572872 | tf_op jit(solution)/shard_map/ppermute | solution.py:48
  77.9 19.4 %collective-permute-start.17 = (bf16[2,256,256]{2,1,0:T(8,128)(2,1)S(1)}, bf16[2,256,256]{2,1,0:T(8,128)(2,1)S(1)}, u32[]{:S(2)}, u32[]{:S(2)}) collective-permute-start(bf16[2,256,256]{2,1,0:T(8,128)(2,1)S(1)} %get-tuple-element.21), channel_id=1, source_target_pairs={{0,2},{2,4},{4,6},{6,8},{8,10},{10,12},{12,14},{14,16},{16,18},{18... | collective-permute-start | bytes 786440 | tf_op jit(solution)/shard_map/ppermute | solution.py:37
  80.2 26.2 %copy-start.1 = (bf16[2048,1024]{1,0:T(8,128)(2,1)S(1)}, bf16[2048,1024]{1,0:T(8,128)(2,1)}, u32[]{:S(2)}) copy-start(bf16[2048,1024]{1,0:T(8,128)(2,1)} %wv_ref.5) | copy-start | bytes 12582916
  80.2 20.8 %collective-permute-start.18 = (bf16[2,256,256]{2,1,0:T(8,128)(2,1)S(1)}, bf16[2,256,256]{2,1,0:T(8,128)(2,1)S(1)}, u32[]{:S(2)}, u32[]{:S(2)}) collective-permute-start(bf16[2,256,256]{2,1,0:T(8,128)(2,1)S(1)} %get-tuple-element.22), channel_id=1, source_target_pairs={{2,0},{4,2},{6,4},{8,6},{10,8},{12,10},{14,12},{16,14},{18,16},{20... | collective-permute-start | bytes 786440 | tf_op jit(solution)/shard_map/ppermute | solution.py:37
  82.6 20.4 %collective-permute-start.16 = (bf16[2,256,256]{2,1,0:T(8,128)(2,1)S(1)}, bf16[2,256,256]{2,1,0:T(8,128)(2,1)S(1)}, u32[]{:S(2)}, u32[]{:S(2)}) collective-permute-start(bf16[2,256,256]{2,1,0:T(8,128)(2,1)S(1)} %add_convert_fusion.4), channel_id=1, source_target_pairs={{0,96},{32,0},{64,32},{96,64},{1,97},{33,1},{65,33},{97,65},{2,98}... | collective-permute-start | bytes 786440 | tf_op jit(solution)/shard_map/ppermute | solution.py:30
  97.3 9.8 %collective-permute-start.20 = (bf16[2,256,512]{2,1,0:T(8,128)(2,1)S(1)}, bf16[2,256,512]{2,1,0:T(8,128)(2,1)S(1)}, u32[]{:S(2)}, u32[]{:S(2)}) collective-permute-start(bf16[2,256,512]{2,1,0:T(8,128)(2,1)S(1)} %get-tuple-element.24), channel_id=1, source_target_pairs={{0,2},{2,4},{4,6},{6,8},{8,10},{10,12},{12,14},{14,16},{16,18},{18... | collective-permute-start | bytes 1572872 | tf_op jit(solution)/shard_map/ppermute | solution.py:37
  101.0 10.8 %collective-permute-start.21 = (bf16[2,256,512]{2,1,0:T(8,128)(2,1)S(1)}, bf16[2,256,512]{2,1,0:T(8,128)(2,1)S(1)}, u32[]{:S(2)}, u32[]{:S(2)}) collective-permute-start(bf16[2,256,512]{2,1,0:T(8,128)(2,1)S(1)} %get-tuple-element.25), channel_id=1, source_target_pairs={{2,0},{4,2},{6,4},{8,6},{10,8},{12,10},{14,12},{16,14},{18,16},{20... | collective-permute-start | bytes 1572872 | tf_op jit(solution)/shard_map/ppermute | solution.py:37
  103.0 12.8 %copy-start.3 = (bf16[2048,1024]{1,0:T(8,128)(2,1)S(1)}, bf16[2048,1024]{1,0:T(8,128)(2,1)}, u32[]{:S(2)}) copy-start(bf16[2048,1024]{1,0:T(8,128)(2,1)} %wk_ref.5) | copy-start | bytes 12582916
  103.1 29.6 %collective-permute-start.9 = (bf16[1024,256]{1,0:T(8,128)(2,1)S(1)}, bf16[1024,256]{1,0:T(8,128)(2,1)S(1)}, u32[]{:S(2)}, u32[]{:S(2)}) collective-permute-start(bf16[1024,256]{1,0:T(8,128)(2,1)S(1)} %get-tuple-element.14), channel_id=1, source_target_pairs={{0,1},{1,0},{2,3},{3,2},{4,5},{5,4},{6,7},{7,6},{8,9},{9,8},{10,11... | collective-permute-start | bytes 1572872 | tf_op jit(solution)/shard_map/ppermute | solution.py:48
  106.9 7.0 %collective-permute-start.19 = (bf16[2,256,256]{2,1,0:T(8,128)(2,1)S(1)}, bf16[2,256,256]{2,1,0:T(8,128)(2,1)S(1)}, u32[]{:S(2)}, u32[]{:S(2)}) collective-permute-start(bf16[2,256,256]{2,1,0:T(8,128)(2,1)S(1)} %add_convert_fusion.3), channel_id=1, source_target_pairs={{0,96},{32,0},{64,32},{96,64},{1,97},{33,1},{65,33},{97,65},{2,98}... | collective-permute-start | bytes 786440 | tf_op jit(solution)/shard_map/ppermute | solution.py:30
  107.1 40.0 %collective-permute-start.13 = (bf16[1024,512]{1,0:T(8,128)(2,1)S(1)}, bf16[1024,512]{1,0:T(8,128)(2,1)S(1)}, u32[]{:S(2)}, u32[]{:S(2)}) collective-permute-start(bf16[1024,512]{1,0:T(8,128)(2,1)S(1)} %get-tuple-element.16), channel_id=1, source_target_pairs={{0,1},{1,0},{2,3},{3,2},{4,5},{5,4},{6,7},{7,6},{8,9},{9,8},{10,11... | collective-permute-start | bytes 3145736 | tf_op jit(solution)/shard_map/ppermute | solution.py:48
  111.8 19.9 %collective-permute-start.11 = (bf16[512,1024]{1,0:T(8,128)(2,1)S(1)}, bf16[512,1024]{1,0:T(8,128)(2,1)S(1)}, u32[]{:S(2)}, u32[]{:S(2)}) collective-permute-start(bf16[512,1024]{1,0:T(8,128)(2,1)S(1)} %collective-permute-done.10), channel_id=1, source_target_pairs={{0,2},{2,0},{4,6},{6,4},{8,10},{10,8},{12,14},{14,12},{16,18},{18,... | collective-permute-start | bytes 3145736 | tf_op jit(solution)/shard_map/ppermute | solution.py:44
  113.9 13.4 %collective-permute-start.22 = (bf16[2,256,512]{2,1,0:T(8,128)(2,1)S(1)}, bf16[2,256,512]{2,1,0:T(8,128)(2,1)S(1)}, u32[]{:S(2)}, u32[]{:S(2)}) collective-permute-start(bf16[2,256,512]{2,1,0:T(8,128)(2,1)S(1)} %add_convert_fusion.2), channel_id=1, source_target_pairs={{0,96},{32,0},{64,32},{96,64},{1,97},{33,1},{65,33},{97,65},{2,98}... | collective-permute-start | bytes 1572872 | tf_op jit(solution)/shard_map/ppermute | solution.py:30
  130.4 25.9 %collective-permute-start.23 = (bf16[256,1024]{1,0:T(8,128)(2,1)}, bf16[256,1024]{1,0:T(8,128)(2,1)}, u32[]{:S(2)}, u32[]{:S(2)}) collective-permute-start(bf16[256,1024]{1,0:T(8,128)(2,1)} %constant_dynamic-slice_fusion), channel_id=1, source_target_pairs={{0,1},{1,0},{2,3},{3,2},{4,5},{5,4},{6,7},{7,6},{8,9},{9,8},{10,11... | collective-permute-start | bytes 1572872 | tf_op jit(solution)/shard_map/ppermute | solution.py:48

commit v2 on v1

v2 whole, which is shorter than its diff:
```python
import jax
import jax.numpy as jnp
from jax import lax
from jax.experimental import pallas as pl
from jax.experimental.pallas import tpu as pltpu
from jax.sharding import PartitionSpec as P

D = 2048
HEADS = 16
BLK = 128
HD = D // HEADS
SCALE = HD**-0.5
LOG2E = 1.4426950408889634
CHUNKS = ((0, 2), (2, 3), (5, 3))
MIB = 2**20

F32 = jnp.float32
BF16 = jnp.bfloat16
NN = (((1,), (0,)), ((), ()))
NT = (((1,), (1,)), ((), ()))
TN = (((0,), (0,)), ((), ()))


def dot(a, b, dims):
    return lax.dot_general(a, b, dims, preferred_element_type=F32)


def section_shift(block, distance):
    count = lax.axis_size("section")
    return lax.ppermute(
        block, "section", [(i, (i + distance) % count) for i in range(count)]
    )


def near_swap(block):
    count = lax.axis_size("seq")
    return lax.ppermute(block, "seq", [(i, i ^ 1) for i in range(count)])


def far_swap(block):
    count = lax.axis_size("seq")
    pairs = [(i, i + 1) for i in range(1, count - 1, 2)]
    return lax.ppermute(block, "seq", pairs + [(j, i) for i, j in pairs])


def head_swap(block):
    return lax.ppermute(block, "head", [(0, 1), (1, 0)])


def other_columns(give):
    count = lax.axis_size("seq")
    quads = [
        [2 * i, 2 * i + 2, 2 * (i ^ 8) + 1, 2 * (i ^ 8) + 3] for i in range(0, count, 2)
    ]
    return lax.all_gather(give, ("seq", "head"), axis_index_groups=quads)


def in_hbm(shape):
    return pltpu.HBM(shape.shape, shape.dtype)


def call(body, grid, in_specs, out_specs, out_shape, args, name, after=(), scalars=0, scratch=(), flops=0):
    first = scalars + len(in_specs)
    unread = len(after)

    def reads(*refs):
        body(*refs[:first], *refs[first + unread :])

    in_specs = list(in_specs) + [pl.BlockSpec(memory_space=pl.ANY)] * unread
    return pl.pallas_call(
        reads,
        grid_spec=pltpu.PrefetchScalarGridSpec(
            num_scalar_prefetch=scalars,
            grid=grid,
            in_specs=in_specs,
            out_specs=out_specs,
            scratch_shapes=scratch,
        ),
        out_shape=jax.tree.map(in_hbm, out_shape),
        compiler_params=pltpu.CompilerParams(vmem_limit_bytes=64 * MIB - 64 * 1024),
        cost_estimate=pl.CostEstimate(flops=flops, bytes_accessed=0, transcendentals=0),
        name=name,
    )(*args, *after)


def key_value_body(notes_ref, wk_ref, wv_ref, out_ref):
    weights = jnp.concatenate([wk_ref[...], wv_ref[...]], axis=1)
    both = dot(notes_ref[...], weights, NN).astype(BF16)
    out_ref[0] = both[:, :HD]
    out_ref[1] = both[:, HD:]


def key_values(notes, w_key, w_value, h0, hc, after):
    rows = notes.shape[0]
    weight = pl.BlockSpec((D, HD), lambda h: (0, h0 + h))
    return call(
        key_value_body,
        (hc,),
        [pl.BlockSpec((rows, D), lambda h: (0, 0)), weight, weight],
        pl.BlockSpec((2, rows, HD), lambda h: (0, 0, h)),
        jax.ShapeDtypeStruct((2, rows, hc * HD), BF16),
        (notes, w_key, w_value),
        "key_values",
        after,
    )


def project(rows, weight, transposed, name, after):
    count, depth = rows.shape
    width = weight.shape[0 if transposed else 1]
    step = 256
    dims = NT if transposed else NN

    def body(a_ref, w_ref, out_ref):
        out_ref[...] = dot(a_ref[...], w_ref[...], dims).astype(BF16)

    if transposed:
        weight_in = pl.BlockSpec((step, depth), lambda n: (n, 0))
    else:
        weight_in = pl.BlockSpec((depth, step), lambda n: (0, n))
    return call(
        body,
        (width // step,),
        [pl.BlockSpec((count, depth), lambda n: (0, 0)), weight_in],
        pl.BlockSpec((count, step), lambda n: (0, n)),
        jax.ShapeDtypeStruct((count, width), BF16),
        (rows, weight),
        name,
        after,
    )


def give_body(scalars_ref, w_ref, out_ref):
    out_ref[...] = w_ref[...]


def give_columns(scalars, w_query, after):
    cols = w_query.shape[1]
    rows = D // 4
    step = rows // 2
    return call(
        give_body,
        (2,),
        [pl.BlockSpec((step, cols), lambda n, s: (4 * (1 - s[0]) + 2 * s[1] + n, 0))],
        pl.BlockSpec((step, cols), lambda n, s: (n, 0)),
        jax.ShapeDtypeStruct((rows, cols), BF16),
        (scalars, w_query),
        "give_columns",
        after,
        scalars=1,
    )


def frame_sum_own(scalars, grads, grads_other, w_query, w_other, chunks_other, after):
    rows = grads[0].shape[0]
    half = D // 2
    cols = w_query.shape[1]
    step = 256
    nother = len(grads_other)
    other_width = sum(hc for _, hc in chunks_other) * HD

    def body(s_ref, *refs):
        own = refs[: len(grads)]
        other = refs[len(grads) : len(grads) + nother]
        w_ref, wo_ref, out_ref = refs[len(grads) + nother :]
        left = jnp.concatenate([r[...] for r in own], axis=1)
        total = dot(left, w_ref[...], NT)
        right = jnp.concatenate([r[...] for r in other], axis=1)
        out_ref[...] = total + dot(right, wo_ref[0, :, :other_width], NT)

    whole = lambda g: pl.BlockSpec(g.shape, lambda n, s: (0, 0))
    return call(
        body,
        (half // step,),
        [whole(g) for g in grads]
        + [whole(g) for g in grads_other]
        + [
            pl.BlockSpec((step, cols), lambda n, s: (4 * s[0] + n, 0)),
            pl.BlockSpec((1, step, cols), lambda n, s: (2 * (1 - s[0]) + n // 2, n % 2, 0)),
        ],
        pl.BlockSpec((rows, step), lambda n, s: (0, n)),
        jax.ShapeDtypeStruct((rows, half), F32),
        (scalars, *grads, *grads_other, w_query, w_other),
        "frame_sum_own",
        after,
        scalars=1,
    )


def frame_sum_last(scalars, total, grad, w_other, h0, hc, after):
    rows, half = total.shape
    step = 256

    def body(s_ref, t_ref, g_ref, *refs):
        weight = jnp.concatenate([r[0] for r in refs[:hc]], axis=1)
        refs[hc][...] = (t_ref[...] + dot(g_ref[...], weight, NT)).astype(BF16)

    def weight_in(k):
        return pl.BlockSpec((1, step, HD), lambda n, s: (2 * (1 - s[0]) + n // 2, n % 2, h0 + k))

    return call(
        body,
        (half // step,),
        [
            pl.BlockSpec((rows, step), lambda n, s: (0, n)),
            pl.BlockSpec(grad.shape, lambda n, s: (0, 0)),
        ]
        + [weight_in(k) for k in range(hc)],
        pl.BlockSpec((rows, step), lambda n, s: (0, n)),
        jax.ShapeDtypeStruct((rows, half), BF16),
        (scalars, total, grad) + (w_other,) * hc,
        "frame_sum_last",
        after,
        scalars=1,
    )


def note_product(scalars, grads, chunks, w_key, w_value, after, before=None):
    nt = grads[0].shape[1]
    half = D // 2
    heads = [h for h0, hc in chunks for h in range(h0, h0 + hc)]
    hc = len(heads)
    last = before is not None

    def body(s_ref, *refs):
        grad_refs, refs = refs[: len(grads)], refs[len(grads) :]
        wk = jnp.concatenate([r[...] for r in refs[:hc]], axis=1)
        wv = jnp.concatenate([r[...] for r in refs[hc : 2 * hc]], axis=1)
        gk = jnp.concatenate([r[0] for r in grad_refs], axis=1)
        gv = jnp.concatenate([r[1] for r in grad_refs], axis=1)
        total = dot(gk, wk, NT) + dot(gv, wv, NT)
        if last:
            total = total + refs[2 * hc][0]
        out_ref = refs[-1]
        out_ref[0] = total.astype(out_ref.dtype)

    def weight_in(h):
        return pl.BlockSpec((half, HD), lambda n, s: (jnp.where(n == 0, 1 - s[0], s[0]), h))

    half_io = pl.BlockSpec((1, nt, half), lambda n, s: (n, 0, 0))
    return call(
        body,
        (2,),
        [pl.BlockSpec(g.shape, lambda n, s: (0, 0, 0)) for g in grads]
        + [weight_in(h) for h in heads] * 2
        + ([half_io] if last else []),
        half_io,
        jax.ShapeDtypeStruct((2, nt, half), BF16 if last else F32),
        (scalars, *grads) + (w_key,) * hc + (w_value,) * hc + ((before,) if last else ()),
        "note_product",
        after,
        scalars=1,
    )


def attention_body(
    bias_ref, q_ref, g_ref, kvo_ref, kvn_ref, kvf_ref, dq_ref, own_ref, near_ref, far_ref,
    p_scr, ds_scr,
):
    scale2 = SCALE * LOG2E
    frames = q_ref.shape[0]
    nt = kvo_ref.shape[1]
    step = 256
    blocks = 3 * nt // BLK
    keys = jnp.concatenate([kvo_ref[0], kvn_ref[0], kvf_ref[0]], axis=0)
    values = jnp.concatenate([kvo_ref[1], kvn_ref[1], kvf_ref[1]], axis=0)
    for f in range(frames // step):
        cols = slice(f * step, (f + 1) * step)
        s = dot(keys, q_ref[cols, :], NT)
        gp = dot(values, g_ref[cols, :], NT)
        rows = [slice(j * BLK, (j + 1) * BLK) for j in range(blocks)]
        bias = [bias_ref[j : j + 1, cols] for j in range(blocks)]
        peak = None
        for j in range(blocks):
            top = jnp.max(s[rows[j]], axis=0, keepdims=True) + bias[j]
            peak = top if peak is None else jnp.maximum(peak, top)
        expos = []
        total = jnp.zeros((1, step), F32)
        mixed = jnp.zeros((1, step), F32)
        for j in range(blocks):
            e = jnp.exp2(s[rows[j]] * scale2 + (bias[j] - peak) * scale2)
            expos.append(e)
            total = total + jnp.sum(e, axis=0, keepdims=True)
            mixed = mixed + jnp.sum(e * gp[rows[j]], axis=0, keepdims=True)
        inv = 1.0 / total
        delta = mixed * inv
        for j in range(blocks):
            p = expos[j] * inv
            p_scr[rows[j], cols] = p.astype(BF16)
            ds_scr[rows[j], cols] = (p * (gp[rows[j]] - delta)).astype(BF16)
    dq_ref[...] = (dot(ds_scr[...], keys, TN) * SCALE).astype(BF16)
    dv = dot(p_scr[...], g_ref[...], NN)
    dk = dot(ds_scr[...], q_ref[...], NN) * SCALE
    for i, grad in enumerate((dk, dv)):
        own_ref[i] = grad[:nt]
        near_ref[i] = grad[nt : 2 * nt].astype(BF16)
        far_ref[i] = grad[2 * nt :].astype(BF16)


def attention(bias, queries, grad_ctx, kv_own, kv_near, kv_far, h0, hc, after):
    frames = queries.shape[0]
    nt = kv_own.shape[1]
    frame_in = pl.BlockSpec((frames, HD), lambda h: (0, h0 + h))
    note_io = pl.BlockSpec((2, nt, HD), lambda h: (0, 0, h))
    notes_out = jax.ShapeDtypeStruct((2, nt, hc * HD), BF16)
    return call(
        attention_body,
        (hc,),
        [pl.BlockSpec(bias.shape, lambda h: (0, 0)), frame_in, frame_in, note_io, note_io, note_io],
        [pl.BlockSpec((frames, HD), lambda h: (0, h)), note_io, note_io, note_io],
        [
            jax.ShapeDtypeStruct((frames, hc * HD), BF16),
            jax.ShapeDtypeStruct((2, nt, hc * HD), F32),
            notes_out,
            notes_out,
        ],
        (bias, queries, grad_ctx, kv_own, kv_near, kv_far),
        "attention",
        after,
        scratch=[pltpu.VMEM((3 * nt, frames), BF16), pltpu.VMEM((3 * nt, frames), BF16)],
        flops=90 * frames * nt * hc * HD,
    )


def per_device(notes, frames, w_query, w_key, w_value, w_out, band_blocks, grad_mixed):
    nt = notes.shape[1]
    shard = lax.axis_index("seq")
    group = lax.axis_index("head")
    core = shard % 2
    scalars = jnp.stack([group, core]).astype(jnp.int32)

    made = []
    moved = []
    for h0, hc in CHUNKS:
        made.append(key_values(notes[0], w_key, w_value, h0, hc, made[-1:]))
        moved.append(section_shift(made[-1], 1))
    given = give_columns(scalars, w_query, made[-1:])
    w_other = other_columns(given)

    far_shard = jnp.where(core == 0, shard - 1, shard + 1)
    shards = jnp.stack([shard, shard ^ 1, far_shard, shard])
    per_shard = nt // BLK
    block_ids = (shards[:, None] * per_shard + jnp.arange(per_shard, dtype=jnp.int32)).reshape(-1)
    inside = (block_ids[:, None] >= band_blocks[0, 0][None]) & (
        block_ids[:, None] <= band_blocks[0, 1][None]
    )
    bias = jnp.repeat(jnp.where(inside, 0.0, -jnp.inf).astype(F32), BLK, axis=1)

    queries = project(frames[0], w_query, False, "queries", (given,))
    moved[0], queries = lax.optimization_barrier((moved[0], queries))
    grad_ctx = project(grad_mixed[0], w_out, True, "grad_ctx", (queries, moved[0]))

    grad_q = []
    grad_q_other = []
    note_cols = []
    summed_all = []

    def send_back(own, near, far, also=None):
        near = near_swap(near)
        far = far_swap(far)
        if also:
            near, also[-1] = lax.optimization_barrier((near, also[-1]))
        summed_all.append((own + near.astype(F32) + far.astype(F32)).astype(BF16))
        note_cols.append(section_shift(summed_all[-1], -1))

    for step, (h0, hc) in enumerate(CHUNKS):
        kv = moved[step]
        after = grad_q[-1:]
        kv_near, kv_far = near_swap(kv), far_swap(kv)
        if step == 1:
            near, far, kv_near, kv_far = lax.optimization_barrier((near, far, kv_near, kv_far))
            send_back(own, near, far)
        if step == 2:
            after = after + [grad_q_other[0], summed_all[0]]
        dq, own, near, far = attention(
            bias, queries, grad_ctx, kv, kv_near, kv_far, h0, hc, after
        )
        if step == 0:
            moved[2], dq = lax.optimization_barrier((moved[2], dq))
        grad_q.append(dq)
        grad_q_other.append(head_swap(dq))
        if step == 1:
            send_back(own, near, far, grad_q_other)
    near, far, note_cols[0] = lax.optimization_barrier((near, far, note_cols[0]))
    send_back(own, near, far)

    total = frame_sum_own(
        scalars, grad_q, grad_q_other[:-1], w_query, w_other, CHUNKS[:-1], ()
    )
    before = note_product(scalars, note_cols[:-1], CHUNKS[:-1], w_key, w_value, (total,))
    frame_sum = frame_sum_last(
        scalars, total, grad_q_other[-1], w_other, *CHUNKS[-1], (before,)
    )
    halves = note_product(
        scalars, note_cols[-1:], CHUNKS[-1:], w_key, w_value, (frame_sum,), before
    )
    give_notes = head_swap(halves[0])
    note_sum = halves[1].astype(F32) + give_notes.astype(F32)
    return (frame_sum[None], note_sum.astype(BF16)[None])


def solution(mesh):
    placed = (
        P("section", "seq", None),
        P("section", "seq", None),
        P(None, "head"),
        P(None, "head"),
        P(None, "head"),
        P("head", None),
        P("section", None, "seq"),
        P("section", "seq", None),
    )
    return jax.shard_map(
        per_device,
        mesh=mesh,
        in_specs=placed,
        out_specs=(P("section", "seq", "head"), P("section", "seq", "head")),
        check_vma=False,
    )
```

time: 160 us -> 170 us (1.062)
  Pallas kernels: 29.2 us -> 88 us
  matrix products: 29.5 us -> 0 us
  waiting for transfers between devices: 30.9 us -> 12.3 us
  between operations: 1.06 us -> 14.2 us
  starting transfers between devices: 52.2 us -> 41.4 us
  local copies, waits for them, and re-layouts: 12 us -> 3.23 us
  other arithmetic: 3.52 us -> 9.63 us
    pallas_call x6 -> x13, Pallas kernels: 29.2 us -> 88 us  [call(): pl.pallas_call(reads, grid_spec=pltpu.PrefetchScalarGridSpec(num_scalar_p...]
    dot_general x14 -> x0, matrix products: 29.5 us -> none  [dot(): return lax.dot_general(a, b, dims, preferred_element_type=F32)]
    ppermute x14 -> x12, starting transfers between devices: 36.4 us -> 22.8 us  [the longest x6 20.9 us: far_swap(): return lax.ppermute(block, 'seq', pairs + [(j, i) for i, j in pairs])]
    ppermute x6, waiting for transfers between devices: 12.8 us -> 0.02 us  [section_shift(): lax.ppermute(block, 'section', [(i, (i + distance) % count) for i in rang...]
    unnamed x20 -> x0, local copies, waits for them, and re-layouts: 8.8 us -> none
    convert_element_type x3, other arithmetic: 0.41 us -> 6.25 us  [send_back(): summed_all.append((own + near.astype(F32) + far.astype(F32)).astype(BF16))]
    ppermute x4, waiting for transfers between devices: 16.6 us -> 12.3 us  [head_swap(): return lax.ppermute(block, 'head', [(0, 1), (1, 0)])]
    dynamic_slice x2 -> x0, local copies, waits for them, and re-layouts: 3.13 us -> none  [the longest x1 2.29 us: per_device(): lax.dynamic_slice_in_dim(w_query, (1 - group) * half + core * quarter, qu...]
  transfers between devices with their start and end apart: 24 -> 23, of which waited for: 5 -> 1; matrix products, arithmetic and copies ran while one was open for 22% -> 5% of each run, Pallas kernels for 18% -> 40%
where the time goes in v2:
time: 170 us; the launch traced here: 169 us
  Pallas kernels  88 us (52%)
  starting transfers between devices  41.4 us (24%)
  between operations  14.2 us (8%)
  waiting for transfers between devices  12.3 us (7%)
  other arithmetic  9.63 us (6%)
  local copies, waits for them, and re-layouts  3.23 us (2%)
    pallas_call x13, Pallas kernels, call(): pl.pallas_call(reads, grid_spec=pltpu.PrefetchScalarGridSpec(num_scalar_p...  88 us
    ppermute x6, starting transfers between devices, far_swap(): return lax.ppermute(block, 'seq', pairs + [(j, i) for i, j in pairs])  20.9 us
    ppermute x4, waiting for transfers between devices, head_swap(): return lax.ppermute(block, 'head', [(0, 1), (1, 0)])  12.3 us
    ppermute x4, starting transfers between devices, head_swap(): return lax.ppermute(block, 'head', [(0, 1), (1, 0)])  10 us
    ppermute x6, starting transfers between devices, section_shift(): lax.ppermute(block, 'section', [(i, (i + distance) % count) for i in rang...  8.58 us
    convert_element_type x3, other arithmetic, send_back(): summed_all.append((own + near.astype(F32) + far.astype(F32)).astype(BF16))  6.25 us
  transfers between devices with their start and end apart: 23, of which 1 were waited for; matrix products, arithmetic and copies ran while one was open for 5% of the time, Pallas kernels for 40%

profile of v2, /device:TPU:1, one launch (start us, length us, event | category | flops | bytes accessed | tf_op | source)
XLA Modules:
  0.0 168.8 jit_solution(5799566982547738227)
XLA Ops:
  7.2 0.0 all-gather.3.cloned.1.call-start
  7.2 3.3 %key_values.3.refs_3_ = bf16[2,256,256]{2,1,0:T(8,128)(2,1)} custom-call(bf16[256,2048]{1,0:T(8,128)(2,1)} %bitcast.29, bf16[2048,1024]{1,0:T(8,128)(2,1)} %refs_4_.3, bf16[2048,1024]{1,0:T(8,128)(2,1)} %refs_7_.3), custom_call_target="tpu_custom_call" | custom-call | tf_op jit(solution)/shard_map/key_values/pallas_call | solution.py:70
  10.6 4.4 %key_values.4.refs_3_ = bf16[2,256,384]{2,1,0:T(8,128)(2,1)} custom-call(bf16[256,2048]{1,0:T(8,128)(2,1)} %bitcast.30, bf16[2048,1024]{1,0:T(8,128)(2,1)} %refs_4_.3, bf16[2048,1024]{1,0:T(8,128)(2,1)} %refs_7_.3, bf16[2,256,256]{2,1,0:T(8,128)(2,1)} %key_values.3.refs_3_), custom_call_target="tpu_custom_call" | custom-call | tf_op jit(solution)/shard_map/key_values/pallas_call | solution.py:70
  15.0 4.4 %key_values.5.refs_2_ = bf16[2,256,384]{2,1,0:T(8,128)(2,1)} custom-call(bf16[256,2048]{1,0:T(8,128)(2,1)} %bitcast.31, bf16[2048,1024]{1,0:T(8,128)(2,1)} %refs_4_.3, bf16[2048,1024]{1,0:T(8,128)(2,1)} %refs_7_.3, bf16[2,256,384]{2,1,0:T(8,128)(2,1)} %key_values.4.refs_3_), custom_call_target="tpu_custom_call" | custom-call | tf_op jit(solution)/shard_map/key_values/pallas_call | solution.py:70
  19.4 0.6 pad_add_fusion.refs_0_
  20.0 2.7 %give_columns.1.refs_2_ = bf16[512,1024]{1,0:T(8,128)(2,1)} custom-call(s32[2]{0:T(128)} %pad_add_fusion.refs_0_, bf16[2048,1024]{1,0:T(8,128)(2,1)} %refs_6_.3, bf16[2,256,384]{2,1,0:T(8,128)(2,1)} %key_values.5.refs_2_), custom_call_target="tpu_custom_call" | custom-call | tf_op jit(solution)/shard_map/give_columns/pallas_call | solution.py:70
  22.7 0.0 all-gather.3.cloned.1.call-update
  22.7 2.1 %collective-permute-start.1 = (bf16[2,256,256]{2,1,0:T(8,128)(2,1)}, bf16[2,256,256]{2,1,0:T(8,128)(2,1)}, u32[]{:S(2)}, u32[]{:S(2)}) collective-permute-start(bf16[2,256,256]{2,1,0:T(8,128)(2,1)} %key_values.3.refs_3_), channel_id=1, source_target_pairs={{0,32},{32,64},{64,96},{96,0},{1,33},{33,65},{65,97},{97,1},{2,34}... | collective-permute-start | bytes 786440 | tf_op jit(solution)/shard_map/ppermute | solution.py:30
  24.8 1.2 collective-permute-start.4
  26.1 0.9 collective-permute-start
  27.0 0.1 add_multiply_fusion
  27.1 0.6 iota_add_fusion
  27.7 8.6 %queries.1.refs_2_.refs_1_ = bf16[1024,1024]{1,0:T(8,128)(2,1)} custom-call(bf16[1024,2048]{1,0:T(8,128)(2,1)} %bitcast.34, bf16[2048,1024]{1,0:T(8,128)(2,1)} %refs_6_.3, bf16[512,1024]{1,0:T(8,128)(2,1)} %give_columns.1.refs_2_), custom_call_target="tpu_custom_call" | custom-call | tf_op jit(solution)/shard_map/queries/pallas_call | solution.py:70
  36.2 0.7 add.54
  36.9 0.8 slice_bitcast_fusion.3
  37.7 1.6 collective-permute-start.2
  39.3 3.1 %collective-permute-start.3 = (bf16[2,256,256]{2,1,0:T(8,128)(2,1)}, bf16[2,256,256]{2,1,0:T(8,128)(2,1)}, u32[]{:S(2)}, u32[]{:S(2)}) collective-permute-start(bf16[2,256,256]{2,1,0:T(8,128)(2,1)} %collective-permute-done.1.refs_3_), channel_id=1, source_target_pairs={{2,4},{6,8},{10,12},{14,16},{18,20},{22,24},{26,28},{4,2},{8,6},{1... | collective-permute-start | bytes 786440 | tf_op jit(solution)/shard_map/ppermute | solution.py:43
  42.4 0.1 and_select_fusion
  42.5 0.7 broadcast_bitcast_fusion.refs_0_
  43.2 8.7 %grad_ctx.1.refs_2_ = bf16[1024,1024]{1,0:T(8,128)(2,1)} custom-call(bf16[1024,2048]{1,0:T(8,128)(2,1)} %bitcast.33, bf16[1024,2048]{1,0:T(8,128)(2,1)} %refs_1_.11, bf16[1024,1024]{1,0:T(8,128)(2,1)} %queries.1.refs_2_.refs_1_, bf16[2,256,256]{2,1,0:T(8,128)(2,1)} %collective-permute-done.1.refs_3_), custom_call_target="tpu_custom_call" | custom-call | tf_op jit(solution)/shard_map/grad_ctx/pallas_call | solution.py:70
  51.9 3.6 %collective-permute-start.6 = (bf16[2,256,384]{2,1,0:T(8,128)(2,1)}, bf16[2,256,384]{2,1,0:T(8,128)(2,1)}, u32[]{:S(2)}, u32[]{:S(2)}) collective-permute-start(bf16[2,256,384]{2,1,0:T(8,128)(2,1)} %collective-permute-done.4.refs_3_), channel_id=1, source_target_pairs={{2,4},{6,8},{10,12},{14,16},{18,20},{22,24},{26,28},{4,2},{8,6},{1... | collective-permute-start | bytes 1179656 | tf_op jit(solution)/shard_map/ppermute | solution.py:43
  55.5 7.9 %attention.3 = (bf16[1024,256]{1,0:T(8,128)(2,1)}, f32[2,256,256]{2,1,0:T(8,128)}, bf16[2,256,256]{2,1,0:T(8,128)(2,1)}, bf16[2,256,256]{2,1,0:T(8,128)(2,1)}) custom-call(f32[8,1024]{1,0:T(8,128)} %broadcast_bitcast_fusion.refs_0_, bf16[1024,1024]{1,0:T(8,128)(2,1)} %queries.1.refs_2_.refs_1_, bf16[1024,1024]{1,0:T(8,128)(2,1)} %grad_ctx.1.refs_2_, ...), custom_call_target="tpu_custom_call" | custom-call | flops 6039797760 | tf_op jit(solution)/shard_map/attention/pallas_call | solution.py:70
  63.4 0.1 collective-permute-start.7
  63.4 3.3 %collective-permute-start.8 = (bf16[2,256,384]{2,1,0:T(8,128)(2,1)}, bf16[2,256,384]{2,1,0:T(8,128)(2,1)}, u32[]{:S(2)}, u32[]{:S(2)}) collective-permute-start(bf16[2,256,384]{2,1,0:T(8,128)(2,1)} %collective-permute-done.refs_3_), channel_id=1, source_target_pairs={{2,4},{6,8},{10,12},{14,16},{18,20},{22,24},{26,28},{4,2},{8,6},{1... | collective-permute-start | bytes 1179656 | tf_op jit(solution)/shard_map/ppermute | solution.py:43
  66.7 3.8 %collective-permute-start.9 = (bf16[1024,256]{1,0:T(8,128)(2,1)}, bf16[1024,256]{1,0:T(8,128)(2,1)}, u32[]{:S(2)}, u32[]{:S(2)}) collective-permute-start(bf16[1024,256]{1,0:T(8,128)(2,1)} %get-tuple-element.30.refs_6_.refs_1_), channel_id=1, source_target_pairs={{0,1},{1,0},{2,3},{3,2},{4,5},{5,4},{6,7},{7,6},{8,9},{9,8},{10,11... | collective-permute-start | bytes 1572872 | tf_op jit(solution)/shard_map/ppermute | solution.py:47
  70.5 3.3 %collective-permute-start.11 = (bf16[2,256,256]{2,1,0:T(8,128)(2,1)}, bf16[2,256,256]{2,1,0:T(8,128)(2,1)}, u32[]{:S(2)}, u32[]{:S(2)}) collective-permute-start(bf16[2,256,256]{2,1,0:T(8,128)(2,1)} %get-tuple-element.39), channel_id=1, source_target_pairs={{2,4},{6,8},{10,12},{14,16},{18,20},{22,24},{26,28},{4,2},{8,6},{1... | collective-permute-start | bytes 786440 | tf_op jit(solution)/shard_map/ppermute | solution.py:43
  73.8 10.8 %attention.4 = (bf16[1024,384]{1,0:T(8,128)(2,1)}, f32[2,256,384]{2,1,0:T(8,128)}, bf16[2,256,384]{2,1,0:T(8,128)(2,1)}, bf16[2,256,384]{2,1,0:T(8,128)(2,1)}) custom-call(f32[8,1024]{1,0:T(8,128)} %broadcast_bitcast_fusion.refs_0_, bf16[1024,1024]{1,0:T(8,128)(2,1)} %queries.1.refs_2_.refs_1_, bf16[1024,1024]{1,0:T(8,128)(2,1)} %grad_ctx.1.refs_2_, ...), custom_call_target="tpu_custom_call" | custom-call | flops 9059696640 | tf_op jit(solution)/shard_map/attention/pallas_call | solution.py:70
  84.6 0.2 collective-permute-start.13
  84.8 0.2 collective-permute-start.12
  85.0 2.0 %add_convert_fusion.2.refs_8_ = bf16[2,256,256]{2,1,0:T(8,128)(2,1)} fusion(bf16[2,256,256]{2,1,0:T(8,128)(2,1)} %collective-permute-done.11, f32[2,256,256]{2,1,0:T(8,128)} %get-tuple-element.37, bf16[2,256,256]{2,1,0:T(8,128)(2,1)} %collective-permute-done.10), kind=kLoop, calls=%fused_computation.7 | loop fusion | flops 655360 | bytes 1310720 | tf_op jit(solution)/shard_map/convert_element_type | solution.py:363
  87.0 4.9 %collective-permute-start.16 = (bf16[2,256,384]{2,1,0:T(8,128)(2,1)}, bf16[2,256,384]{2,1,0:T(8,128)(2,1)}, u32[]{:S(2)}, u32[]{:S(2)}) collective-permute-start(bf16[2,256,384]{2,1,0:T(8,128)(2,1)} %get-tuple-element.48), channel_id=1, source_target_pairs={{2,4},{6,8},{10,12},{14,16},{18,20},{22,24},{26,28},{4,2},{8,6},{1... | collective-permute-start | bytes 1179656 | tf_op jit(solution)/shard_map/ppermute | solution.py:43
  91.9 1.8 %collective-permute-start.15 = (bf16[2,256,256]{2,1,0:T(8,128)(2,1)}, bf16[2,256,256]{2,1,0:T(8,128)(2,1)}, u32[]{:S(2)}, u32[]{:S(2)}) collective-permute-start(bf16[2,256,256]{2,1,0:T(8,128)(2,1)} %add_convert_fusion.2.refs_8_), channel_id=1, source_target_pairs={{0,96},{32,0},{64,32},{96,64},{1,97},{33,1},{65,33},{97,65},{2,98}... | collective-permute-start | bytes 786440 | tf_op jit(solution)/shard_map/ppermute | solution.py:30
  93.7 10.8 %attention.5 = (bf16[1024,384]{1,0:T(8,128)(2,1)}, f32[2,256,384]{2,1,0:T(8,128)}, bf16[2,256,384]{2,1,0:T(8,128)(2,1)}, bf16[2,256,384]{2,1,0:T(8,128)(2,1)}) custom-call(f32[8,1024]{1,0:T(8,128)} %broadcast_bitcast_fusion.refs_0_, bf16[1024,1024]{1,0:T(8,128)(2,1)} %queries.1.refs_2_.refs_1_, bf16[1024,1024]{1,0:T(8,128)(2,1)} %grad_ctx.1.refs_2_, ...), custom_call_target="tpu_custom_call" | custom-call | flops 9059696640 | tf_op jit(solution)/shard_map/attention/pallas_call | solution.py:70
  104.5 0.1 collective-permute-start.18
  104.6 2.8 %collective-permute-start.19 = (bf16[2,256,384]{2,1,0:T(8,128)(2,1)}, bf16[2,256,384]{2,1,0:T(8,128)(2,1)S(1)}, u32[]{:S(2)}, u32[]{:S(2)}) collective-permute-start(bf16[2,256,384]{2,1,0:T(8,128)(2,1)} %get-tuple-element.51), channel_id=1, source_target_pairs={{2,4},{6,8},{10,12},{14,16},{18,20},{22,24},{26,28},{4,2},{8,6},{1... | collective-permute-start | bytes 1179656 | tf_op jit(solution)/shard_map/ppermute | solution.py:43
  107.4 2.8 %collective-permute-start.14 = (bf16[1024,384]{1,0:T(8,128)(2,1)}, bf16[1024,384]{1,0:T(8,128)(2,1)}, u32[]{:S(2)}, u32[]{:S(2)}) collective-permute-start(bf16[1024,384]{1,0:T(8,128)(2,1)} %get-tuple-element.40.refs_3_), channel_id=1, source_target_pairs={{0,1},{1,0},{2,3},{3,2},{4,5},{5,4},{6,7},{7,6},{8,9},{9,8},{10,11... | collective-permute-start | bytes 2359304 | tf_op jit(solution)/shard_map/ppermute | solution.py:47
  110.2 2.2 %add_convert_fusion.1 = bf16[2,256,384]{2,1,0:T(8,128)(2,1)} fusion(bf16[2,256,384]{2,1,0:T(8,128)(2,1)} %collective-permute-done.16, f32[2,256,384]{2,1,0:T(8,128)} %get-tuple-element.46, bf16[2,256,384]{2,1,0:T(8,128)(2,1)} %collective-permute-done.12), kind=kLoop, calls=%fused_computation.3 | loop fusion | flops 983040 | bytes 1966080 | tf_op jit(solution)/shard_map/convert_element_type | solution.py:363
  112.4 2.3 %collective-permute-start.17 = (bf16[2,256,384]{2,1,0:T(8,128)(2,1)}, bf16[2,256,384]{2,1,0:T(8,128)(2,1)}, u32[]{:S(2)}, u32[]{:S(2)}) collective-permute-start(bf16[2,256,384]{2,1,0:T(8,128)(2,1)} %add_convert_fusion.1), channel_id=1, source_target_pairs={{0,96},{32,0},{64,32},{96,64},{1,97},{33,1},{65,33},{97,65},{2,98}... | collective-permute-start | bytes 1179656 | tf_op jit(solution)/shard_map/ppermute | solution.py:30
  114.7 2.0 %add_convert_fusion = bf16[2,256,384]{2,1,0:T(8,128)(2,1)} fusion(bf16[2,256,384]{2,1,0:T(8,128)(2,1)S(1)} %collective-permute-done.19, f32[2,256,384]{2,1,0:T(8,128)} %get-tuple-element.49, bf16[2,256,384]{2,1,0:T(8,128)(2,1)S(1)} %collective-permute-done.18), kind=kLoop, calls=%fused_computation.2 | loop fusion | flops 983040 | bytes 1966080 | tf_op jit(solution)/shard_map/convert_element_type | solution.py:363
  116.7 0.3 collective-permute-start.20
  117.0 9.1 %frame_sum_own.1.refs_13_.refs_1_ = f32[1024,1024]{1,0:T(8,128)} custom-call(s32[2]{0:T(128)} %pad_add_fusion.refs_0_, bf16[1024,256]{1,0:T(8,128)(2,1)} %get-tuple-element.30.refs_6_.refs_1_, bf16[1024,384]{1,0:T(8,128)(2,1)} %get-tuple-element.35.refs_6_.refs_2_, bf16[1024,384]{1,0:T(8,128)(2,1)} %get-tuple-element.40.refs_3_, ...), custom_call_target="tpu_custom_call" | custom-call | tf_op jit(solution)/shard_map/frame_sum_own/pallas_call | solution.py:70
  126.1 5.9 %note_product.2.refs_6_.refs_8_ = f32[2,256,1024]{2,1,0:T(8,128)} custom-call(s32[2]{0:T(128)} %pad_add_fusion.refs_0_, bf16[2,256,256]{2,1,0:T(8,128)(2,1)} %collective-permute-done.15.refs_1_, bf16[2,256,384]{2,1,0:T(8,128)(2,1)} %collective-permute-done.17.refs_2_, bf16[2048,1024]{1,0:T(8,128)(2,1)} %refs_4_.3, bf16[2048,1024]{1,0:T(8,128)(2,1)} %refs_4_.3, ...), custom_call_target="tpu_custom_call" | custom-call | tf_op jit(solution)/shard_map/note_product/pallas_call | solution.py:70
  132.0 6.1 %frame_sum_last.1.refs_9_ = bf16[1024,1024]{1,0:T(8,128)(2,1)} custom-call(s32[2]{0:T(128)} %pad_add_fusion.refs_0_, f32[1024,1024]{1,0:T(8,128)} %frame_sum_own.1.refs_13_.refs_1_, bf16[1024,384]{1,0:T(8,128)(2,1)} %collective-permute-done.14.refs_2_, bf16[4,512,1024]{2,1,0:T(8,128)(2,1)} %bitcast.26, bf16[4,512,1024]{2,1,0:T(8,128)(2,1)} %bitcast.27, ...), custom_call_target="tpu_custom_call" | custom-call | tf_op jit(solution)/shard_map/frame_sum_last/pallas_call | solution.py:70
  138.1 5.2 %note_product.3 = bf16[2,256,1024]{2,1,0:T(8,128)(2,1)} custom-call(s32[2]{0:T(128)} %pad_add_fusion.refs_0_, bf16[2,256,384]{2,1,0:T(8,128)(2,1)} %collective-permute-done.20.refs_1_, bf16[2048,1024]{1,0:T(8,128)(2,1)} %refs_4_.3, bf16[2048,1024]{1,0:T(8,128)(2,1)} %refs_4_.3, bf16[2048,1024]{1,0:T(8,128)(2,1)} %refs_4_.3, bf16[2048,1024]{1,0:T(8,128)(2,1)} %refs_7_.3, ...), custom_call_target="tpu_custom_call" | custom-call | tf_op jit(solution)/shard_map/note_product/pallas_call | solution.py:70
  143.3 1.1 slice_bitcast_fusion
  144.4 3.3 %collective-permute-start.21 = (bf16[256,1024]{1,0:T(8,128)(2,1)S(1)}, bf16[256,1024]{1,0:T(8,128)(2,1)S(1)}, u32[]{:S(2)}, u32[]{:S(2)}) collective-permute-start(bf16[256,1024]{1,0:T(8,128)(2,1)S(1)} %slice_bitcast_fusion), channel_id=1, source_target_pairs={{0,1},{1,0},{2,3},{3,2},{4,5},{5,4},{6,7},{7,6},{8,9},{9,8},{10,11... | collective-permute-start | bytes 1572872 | tf_op jit(solution)/shard_map/ppermute | solution.py:47
  147.7 12.3 %collective-permute-done.21 = bf16[256,1024]{1,0:T(8,128)(2,1)S(1)} collective-permute-done((bf16[256,1024]{1,0:T(8,128)(2,1)S(1)}, bf16[256,1024]{1,0:T(8,128)(2,1)S(1)}, u32[]{:S(2)}, u32[]{:S(2)}) %collective-permute-start.21) | collective-permute-done | bytes 524320 | tf_op jit(solution)/shard_map/ppermute | solution.py:47
  159.9 2.0 %fusion.1 = bf16[1,256,1024]{2,1,0:T(8,128)(2,1)} fusion(bf16[256,1024]{1,0:T(8,128)(2,1)S(1)} %collective-permute-done.21, bf16[2,256,1024]{2,1,0:T(8,128)(2,1)} %note_product.3), kind=kLoop, calls=%fused_computation.4 | loop fusion | flops 1048576 | bytes 1572864 | tf_op jit(solution)/shard_map/broadcast_in_dim | solution.py:399
  (24 shorter events, 0.1 us)
Async XLA Ops:
  7.2 109.8 %all-gather.3.cloned.1.call-start = ((), (), s32[]{:S(2)}) async-start(), calls=%async_computation | async-start | bytes 5242880 | tf_op jit(solution)/shard_map/all_gather | solution.py:55
  22.7 15.0 %collective-permute-start.1 = (bf16[2,256,256]{2,1,0:T(8,128)(2,1)}, bf16[2,256,256]{2,1,0:T(8,128)(2,1)}, u32[]{:S(2)}, u32[]{:S(2)}) collective-permute-start(bf16[2,256,256]{2,1,0:T(8,128)(2,1)} %key_values.3.refs_3_), channel_id=1, source_target_pairs={{0,32},{32,64},{64,96},{96,0},{1,33},{33,65},{65,97},{97,1},{2,34}... | collective-permute-start | bytes 786440 | tf_op jit(solution)/shard_map/ppermute | solution.py:30
  24.8 27.0 %collective-permute-start.4 = (bf16[2,256,384]{2,1,0:T(8,128)(2,1)}, bf16[2,256,384]{2,1,0:T(8,128)(2,1)}, u32[]{:S(2)}, u32[]{:S(2)}) collective-permute-start(bf16[2,256,384]{2,1,0:T(8,128)(2,1)} %key_values.4.refs_3_), channel_id=1, source_target_pairs={{0,32},{32,64},{64,96},{96,0},{1,33},{33,65},{65,97},{97,1},{2,34}... | collective-permute-start | bytes 1179656 | tf_op jit(solution)/shard_map/ppermute | solution.py:30
  26.1 37.3 %collective-permute-start = (bf16[2,256,384]{2,1,0:T(8,128)(2,1)}, bf16[2,256,384]{2,1,0:T(8,128)(2,1)}, u32[]{:S(2)}, u32[]{:S(2)}) collective-permute-start(bf16[2,256,384]{2,1,0:T(8,128)(2,1)} %key_values.5.refs_2_), channel_id=1, source_target_pairs={{0,32},{32,64},{64,96},{96,0},{1,33},{33,65},{65,97},{97,1},{2,34}... | collective-permute-start | bytes 1179656 | tf_op jit(solution)/shard_map/ppermute | solution.py:30
  37.7 17.8 %collective-permute-start.2 = (bf16[2,256,256]{2,1,0:T(8,128)(2,1)}, bf16[2,256,256]{2,1,0:T(8,128)(2,1)}, u32[]{:S(2)}, u32[]{:S(2)}) collective-permute-start(bf16[2,256,256]{2,1,0:T(8,128)(2,1)} %collective-permute-done.1.refs_3_), channel_id=1, source_target_pairs={{0,2},{2,0},{4,6},{6,4},{8,10},{10,8},{12,14},{14,12},{16,18},{18,... | collective-permute-start | bytes 786440 | tf_op jit(solution)/shard_map/ppermute | solution.py:37
  39.3 16.2 %collective-permute-start.3 = (bf16[2,256,256]{2,1,0:T(8,128)(2,1)}, bf16[2,256,256]{2,1,0:T(8,128)(2,1)}, u32[]{:S(2)}, u32[]{:S(2)}) collective-permute-start(bf16[2,256,256]{2,1,0:T(8,128)(2,1)} %collective-permute-done.1.refs_3_), channel_id=1, source_target_pairs={{2,4},{6,8},{10,12},{14,16},{18,20},{22,24},{26,28},{4,2},{8,6},{1... | collective-permute-start | bytes 786440 | tf_op jit(solution)/shard_map/ppermute | solution.py:43
  51.9 18.6 %collective-permute-start.5 = (bf16[2,256,384]{2,1,0:T(8,128)(2,1)}, bf16[2,256,384]{2,1,0:T(8,128)(2,1)}, u32[]{:S(2)}, u32[]{:S(2)}) collective-permute-start(bf16[2,256,384]{2,1,0:T(8,128)(2,1)} %collective-permute-done.4.refs_3_), channel_id=1, source_target_pairs={{0,2},{2,0},{4,6},{6,4},{8,10},{10,8},{12,14},{14,12},{16,18},{18,... | collective-permute-start | bytes 1179656 | tf_op jit(solution)/shard_map/ppermute | solution.py:37
  51.9 18.6 %collective-permute-start.6 = (bf16[2,256,384]{2,1,0:T(8,128)(2,1)}, bf16[2,256,384]{2,1,0:T(8,128)(2,1)}, u32[]{:S(2)}, u32[]{:S(2)}) collective-permute-start(bf16[2,256,384]{2,1,0:T(8,128)(2,1)} %collective-permute-done.4.refs_3_), channel_id=1, source_target_pairs={{2,4},{6,8},{10,12},{14,16},{18,20},{22,24},{26,28},{4,2},{8,6},{1... | collective-permute-start | bytes 1179656 | tf_op jit(solution)/shard_map/ppermute | solution.py:43
  63.4 23.7 %collective-permute-start.7 = (bf16[2,256,384]{2,1,0:T(8,128)(2,1)}, bf16[2,256,384]{2,1,0:T(8,128)(2,1)}, u32[]{:S(2)}, u32[]{:S(2)}) collective-permute-start(bf16[2,256,384]{2,1,0:T(8,128)(2,1)} %collective-permute-done.refs_3_), channel_id=1, source_target_pairs={{0,2},{2,0},{4,6},{6,4},{8,10},{10,8},{12,14},{14,12},{16,18},{18,... | collective-permute-start | bytes 1179656 | tf_op jit(solution)/shard_map/ppermute | solution.py:37
  63.4 28.5 %collective-permute-start.8 = (bf16[2,256,384]{2,1,0:T(8,128)(2,1)}, bf16[2,256,384]{2,1,0:T(8,128)(2,1)}, u32[]{:S(2)}, u32[]{:S(2)}) collective-permute-start(bf16[2,256,384]{2,1,0:T(8,128)(2,1)} %collective-permute-done.refs_3_), channel_id=1, source_target_pairs={{2,4},{6,8},{10,12},{14,16},{18,20},{22,24},{26,28},{4,2},{8,6},{1... | collective-permute-start | bytes 1179656 | tf_op jit(solution)/shard_map/ppermute | solution.py:43
  66.7 27.0 %collective-permute-start.9 = (bf16[1024,256]{1,0:T(8,128)(2,1)}, bf16[1024,256]{1,0:T(8,128)(2,1)}, u32[]{:S(2)}, u32[]{:S(2)}) collective-permute-start(bf16[1024,256]{1,0:T(8,128)(2,1)} %get-tuple-element.30.refs_6_.refs_1_), channel_id=1, source_target_pairs={{0,1},{1,0},{2,3},{3,2},{4,5},{5,4},{6,7},{7,6},{8,9},{9,8},{10,11... | collective-permute-start | bytes 1572872 | tf_op jit(solution)/shard_map/ppermute | solution.py:47
  70.5 14.1 %collective-permute-start.10 = (bf16[2,256,256]{2,1,0:T(8,128)(2,1)}, bf16[2,256,256]{2,1,0:T(8,128)(2,1)}, u32[]{:S(2)}, u32[]{:S(2)}) collective-permute-start(bf16[2,256,256]{2,1,0:T(8,128)(2,1)} %get-tuple-element.38), channel_id=1, source_target_pairs={{0,2},{2,0},{4,6},{6,4},{8,10},{10,8},{12,14},{14,12},{16,18},{18,... | collective-permute-start | bytes 786440 | tf_op jit(solution)/shard_map/ppermute | solution.py:37
  70.5 14.3 %collective-permute-start.11 = (bf16[2,256,256]{2,1,0:T(8,128)(2,1)}, bf16[2,256,256]{2,1,0:T(8,128)(2,1)}, u32[]{:S(2)}, u32[]{:S(2)}) collective-permute-start(bf16[2,256,256]{2,1,0:T(8,128)(2,1)} %get-tuple-element.39), channel_id=1, source_target_pairs={{2,4},{6,8},{10,12},{14,16},{18,20},{22,24},{26,28},{4,2},{8,6},{1... | collective-permute-start | bytes 786440 | tf_op jit(solution)/shard_map/ppermute | solution.py:43
  84.6 25.5 %collective-permute-start.13 = (bf16[1024,384]{1,0:T(8,128)(2,1)}, bf16[1024,384]{1,0:T(8,128)(2,1)}, u32[]{:S(2)}, u32[]{:S(2)}) collective-permute-start(bf16[1024,384]{1,0:T(8,128)(2,1)} %get-tuple-element.35.refs_6_.refs_2_), channel_id=1, source_target_pairs={{0,1},{1,0},{2,3},{3,2},{4,5},{5,4},{6,7},{7,6},{8,9},{9,8},{10,11... | collective-permute-start | bytes 2359304 | tf_op jit(solution)/shard_map/ppermute | solution.py:47
  84.8 22.5 %collective-permute-start.12 = (bf16[2,256,384]{2,1,0:T(8,128)(2,1)}, bf16[2,256,384]{2,1,0:T(8,128)(2,1)}, u32[]{:S(2)}, u32[]{:S(2)}) collective-permute-start(bf16[2,256,384]{2,1,0:T(8,128)(2,1)} %get-tuple-element.41), channel_id=1, source_target_pairs={{0,2},{2,0},{4,6},{6,4},{8,10},{10,8},{12,14},{14,12},{16,18},{18,... | collective-permute-start | bytes 1179656 | tf_op jit(solution)/shard_map/ppermute | solution.py:37
  87.0 23.2 %collective-permute-start.16 = (bf16[2,256,384]{2,1,0:T(8,128)(2,1)}, bf16[2,256,384]{2,1,0:T(8,128)(2,1)}, u32[]{:S(2)}, u32[]{:S(2)}) collective-permute-start(bf16[2,256,384]{2,1,0:T(8,128)(2,1)} %get-tuple-element.48), channel_id=1, source_target_pairs={{2,4},{6,8},{10,12},{14,16},{18,20},{22,24},{26,28},{4,2},{8,6},{1... | collective-permute-start | bytes 1179656 | tf_op jit(solution)/shard_map/ppermute | solution.py:43
  91.9 12.6 %collective-permute-start.15 = (bf16[2,256,256]{2,1,0:T(8,128)(2,1)}, bf16[2,256,256]{2,1,0:T(8,128)(2,1)}, u32[]{:S(2)}, u32[]{:S(2)}) collective-permute-start(bf16[2,256,256]{2,1,0:T(8,128)(2,1)} %add_convert_fusion.2.refs_8_), channel_id=1, source_target_pairs={{0,96},{32,0},{64,32},{96,64},{1,97},{33,1},{65,33},{97,65},{2,98}... | collective-permute-start | bytes 786440 | tf_op jit(solution)/shard_map/ppermute | solution.py:30
  104.5 10.1 %collective-permute-start.18 = (bf16[2,256,384]{2,1,0:T(8,128)(2,1)}, bf16[2,256,384]{2,1,0:T(8,128)(2,1)S(1)}, u32[]{:S(2)}, u32[]{:S(2)}) collective-permute-start(bf16[2,256,384]{2,1,0:T(8,128)(2,1)} %get-tuple-element.50), channel_id=1, source_target_pairs={{0,2},{2,0},{4,6},{6,4},{8,10},{10,8},{12,14},{14,12},{16,18},{18,... | collective-permute-start | bytes 1179656 | tf_op jit(solution)/shard_map/ppermute | solution.py:37
  104.6 10.1 %collective-permute-start.19 = (bf16[2,256,384]{2,1,0:T(8,128)(2,1)}, bf16[2,256,384]{2,1,0:T(8,128)(2,1)S(1)}, u32[]{:S(2)}, u32[]{:S(2)}) collective-permute-start(bf16[2,256,384]{2,1,0:T(8,128)(2,1)} %get-tuple-element.51), channel_id=1, source_target_pairs={{2,4},{6,8},{10,12},{14,16},{18,20},{22,24},{26,28},{4,2},{8,6},{1... | collective-permute-start | bytes 1179656 | tf_op jit(solution)/shard_map/ppermute | solution.py:43
  107.4 24.6 %collective-permute-start.14 = (bf16[1024,384]{1,0:T(8,128)(2,1)}, bf16[1024,384]{1,0:T(8,128)(2,1)}, u32[]{:S(2)}, u32[]{:S(2)}) collective-permute-start(bf16[1024,384]{1,0:T(8,128)(2,1)} %get-tuple-element.40.refs_3_), channel_id=1, source_target_pairs={{0,1},{1,0},{2,3},{3,2},{4,5},{5,4},{6,7},{7,6},{8,9},{9,8},{10,11... | collective-permute-start | bytes 2359304 | tf_op jit(solution)/shard_map/ppermute | solution.py:47
  112.4 13.7 %collective-permute-start.17 = (bf16[2,256,384]{2,1,0:T(8,128)(2,1)}, bf16[2,256,384]{2,1,0:T(8,128)(2,1)}, u32[]{:S(2)}, u32[]{:S(2)}) collective-permute-start(bf16[2,256,384]{2,1,0:T(8,128)(2,1)} %add_convert_fusion.1), channel_id=1, source_target_pairs={{0,96},{32,0},{64,32},{96,64},{1,97},{33,1},{65,33},{97,65},{2,98}... | collective-permute-start | bytes 1179656 | tf_op jit(solution)/shard_map/ppermute | solution.py:30
  116.7 21.4 %collective-permute-start.20 = (bf16[2,256,384]{2,1,0:T(8,128)(2,1)}, bf16[2,256,384]{2,1,0:T(8,128)(2,1)}, u32[]{:S(2)}, u32[]{:S(2)}) collective-permute-start(bf16[2,256,384]{2,1,0:T(8,128)(2,1)} %add_convert_fusion), channel_id=1, source_target_pairs={{0,96},{32,0},{64,32},{96,64},{1,97},{33,1},{65,33},{97,65},{2,98}... | collective-permute-start | bytes 1179656 | tf_op jit(solution)/shard_map/ppermute | solution.py:30
  144.4 15.5 %collective-permute-start.21 = (bf16[256,1024]{1,0:T(8,128)(2,1)S(1)}, bf16[256,1024]{1,0:T(8,128)(2,1)S(1)}, u32[]{:S(2)}, u32[]{:S(2)}) collective-permute-start(bf16[256,1024]{1,0:T(8,128)(2,1)S(1)} %slice_bitcast_fusion), channel_id=1, source_target_pairs={{0,1},{1,0},{2,3},{3,2},{4,5},{5,4},{6,7},{7,6},{8,9},{9,8},{10,11... | collective-permute-start | bytes 1572872 | tf_op jit(solution)/shard_map/ppermute | solution.py:47
Sparse Core Ops, SparseCore 0:
  22.9 56.0 all-gather.2

commit v3 on v2

--- a/solution.py
+++ b/solution.py
@@ -12,7 +12,7 @@
 SCALE = HD**-0.5
 LOG2E = 1.4426950408889634
 CHUNKS = ((0, 2), (2, 3), (5, 3))
-MIB = 2**20
+VMEM = 64 * 2**20 - 2**16
 
 F32 = jnp.float32
 BF16 = jnp.bfloat16
@@ -55,11 +55,10 @@
     return lax.all_gather(give, ("seq", "head"), axis_index_groups=quads)
 
 
-def in_hbm(shape):
-    return pltpu.HBM(shape.shape, shape.dtype)
-
-
-def call(body, grid, in_specs, out_specs, out_shape, args, name, after=(), scalars=0, scratch=(), flops=0):
+def call(
+    body, grid, in_specs, out_specs, out_shape, args, name, after=(), scalars=0, scratch=(),
+    flops=0,
+):
     first = scalars + len(in_specs)
     unread = len(after)
 
@@ -76,78 +75,141 @@
             out_specs=out_specs,
             scratch_shapes=scratch,
         ),
-        out_shape=jax.tree.map(in_hbm, out_shape),
-        compiler_params=pltpu.CompilerParams(vmem_limit_bytes=64 * MIB - 64 * 1024),
+        out_shape=out_shape,
+        compiler_params=pltpu.CompilerParams(vmem_limit_bytes=VMEM),
         cost_estimate=pl.CostEstimate(flops=flops, bytes_accessed=0, transcendentals=0),
         name=name,
     )(*args, *after)
 
 
-def key_value_body(notes_ref, wk_ref, wv_ref, out_ref):
-    weights = jnp.concatenate([wk_ref[...], wv_ref[...]], axis=1)
-    both = dot(notes_ref[...], weights, NN).astype(BF16)
-    out_ref[0] = both[:, :HD]
-    out_ref[1] = both[:, HD:]
-
-
-def key_values(notes, w_key, w_value, h0, hc, after):
+def key_values(scalars, notes, w_key, w_value, w_query):
     rows = notes.shape[0]
-    weight = pl.BlockSpec((D, HD), lambda h: (0, h0 + h))
-    return call(
-        key_value_body,
-        (hc,),
-        [pl.BlockSpec((rows, D), lambda h: (0, 0)), weight, weight],
-        pl.BlockSpec((2, rows, HD), lambda h: (0, 0, h)),
-        jax.ShapeDtypeStruct((2, rows, hc * HD), BF16),
-        (notes, w_key, w_value),
+    cols = w_key.shape[1]
+    wide = 2 * HD
+    pieces = cols // wide
+    quarter = D // 4
+
+    def body(s_ref, notes_ref, wk_ref, wv_ref, wq_ref, *refs):
+        outs = refs[: len(CHUNKS)]
+        give_ref, wk_scr, wv_scr, *made_scr, sems, out_sems, give_sem = refs[len(CHUNKS) :]
+        copies = []
+        for p in range(pieces):
+            part = slice(p * wide, (p + 1) * wide)
+            for i, (src, dst) in enumerate(((wk_ref, wk_scr), (wv_ref, wv_scr))):
+                copy = pltpu.make_async_copy(src.at[:, part], dst.at[:, part], sems.at[p, i])
+                copy.start()
+                copies.append(copy)
+        offset = pl.multiple_of((1 - s_ref[0]) * (2 * quarter) + s_ref[1] * quarter, quarter)
+        give = pltpu.make_async_copy(wq_ref.at[pl.ds(offset, quarter), :], give_ref, give_sem)
+        give.start()
+        left = notes_ref[...]
+        sent = []
+        for p in range(pieces):
+            part = slice(p * wide, (p + 1) * wide)
+            for i, scr in enumerate((wk_scr, wv_scr)):
+                copies[2 * p + i].wait()
+                made = dot(left, scr[:, part], NN).astype(BF16)
+                for k in range(2):
+                    head = 2 * p + k
+                    for c, (h0, hc) in enumerate(CHUNKS):
+                        if h0 <= head < h0 + hc:
+                            at = (head - h0) * HD
+                            made_scr[c][i, :, at : at + HD] = made[:, k * HD : (k + 1) * HD]
+                        if i == 1 and head == h0 + hc - 1:
+                            out = pltpu.make_async_copy(made_scr[c], outs[c], out_sems.at[c])
+                            out.start()
+                            sent.append(out)
+        for copy in sent + [give]:
+            copy.wait()
+
+    far = pl.BlockSpec(memory_space=pl.ANY)
+    here = pl.BlockSpec(memory_space=pltpu.VMEM)
+    return call(
+        body,
+        (),
+        [here, far, far, far],
+        [far] * (len(CHUNKS) + 1),
+        [jax.ShapeDtypeStruct((2, rows, hc * HD), BF16) for _, hc in CHUNKS]
+        + [jax.ShapeDtypeStruct((quarter, cols), BF16)],
+        (scalars, notes, w_key, w_value, w_query),
         "key_values",
+        scalars=1,
+        scratch=[
+            pltpu.VMEM((D, cols), BF16),
+            pltpu.VMEM((D, cols), BF16),
+            *[pltpu.VMEM((2, rows, hc * HD), BF16) for _, hc in CHUNKS],
+            pltpu.SemaphoreType.DMA((pieces, 2)),
+            pltpu.SemaphoreType.DMA((len(CHUNKS),)),
+            pltpu.SemaphoreType.DMA,
+        ],
+    )
+
+
+def project(frames, w_query, grad_mixed, w_out, after):
+    rows, depth = frames.shape
+    width = w_query.shape[1]
+    step = 256
+    steps = rows // step
+    parts = 4
+
+    def body(a_ref, w_ref, b_ref, v_ref, q_ref, g_ref, a_scr, w_scr, b_scr, v_scr, q_scr, g_scr,
+             w_sems, row_sems, out_sems):
+        waits = []
+        for i, (rows_ref, rows_scr, weight_ref, weight_scr) in enumerate(
+            ((a_ref, a_scr, w_ref, w_scr), (b_ref, b_scr, v_ref, v_scr))
+        ):
+            size = weight_ref.shape[0] // parts
+            weight_copies = []
+            row_copies = []
+            for p in range(parts):
+                at = slice(p * size, (p + 1) * size)
+                copy = pltpu.make_async_copy(weight_ref.at[at], weight_scr.at[at], w_sems.at[i, p])
+                copy.start()
+                weight_copies.append(copy)
+            for m in range(steps):
+                at = slice(m * step, (m + 1) * step)
+                copy = pltpu.make_async_copy(rows_ref.at[at], rows_scr.at[at], row_sems.at[i, m])
+                copy.start()
+                row_copies.append(copy)
+            waits.append((weight_copies, row_copies))
+        sent = []
+        for i, (rows_scr, weight_scr, out_scr, out_ref, dims) in enumerate(
+            ((a_scr, w_scr, q_scr, q_ref, NN), (b_scr, v_scr, g_scr, g_ref, NT))
+        ):
+            for copy in waits[i][0]:
+                copy.wait()
+            for m in range(steps):
+                at = slice(m * step, (m + 1) * step)
+                waits[i][1][m].wait()
+                out_scr[at, :] = dot(rows_scr[at, :], weight_scr[...], dims).astype(BF16)
+                copy = pltpu.make_async_copy(out_scr.at[at], out_ref.at[at], out_sems.at[i, m])
+                copy.start()
+                sent.append(copy)
+        for copy in sent:
+            copy.wait()
+
+    far = pl.BlockSpec(memory_space=pl.ANY)
+    out = jax.ShapeDtypeStruct((rows, width), BF16)
+    return call(
+        body,
+        (),
+        [far] * 4,
+        [far] * 2,
+        [out, out],
+        (frames, w_query, grad_mixed, w_out),
+        "queries_and_grad_ctx",
         after,
-    )
-
-
-def project(rows, weight, transposed, name, after):
-    count, depth = rows.shape
-    width = weight.shape[0 if transposed else 1]
-    step = 256
-    dims = NT if transposed else NN
-
-    def body(a_ref, w_ref, out_ref):
-        out_ref[...] = dot(a_ref[...], w_ref[...], dims).astype(BF16)
-
-    if transposed:
-        weight_in = pl.BlockSpec((step, depth), lambda n: (n, 0))
-    else:
-        weight_in = pl.BlockSpec((depth, step), lambda n: (0, n))
-    return call(
-        body,
-        (width // step,),
-        [pl.BlockSpec((count, depth), lambda n: (0, 0)), weight_in],
-        pl.BlockSpec((count, step), lambda n: (0, n)),
-        jax.ShapeDtypeStruct((count, width), BF16),
-        (rows, weight),
-        name,
-        after,
-    )
-
-
-def give_body(scalars_ref, w_ref, out_ref):
-    out_ref[...] = w_ref[...]
-
-
-def give_columns(scalars, w_query, after):
-    cols = w_query.shape[1]
-    rows = D // 4
-    step = rows // 2
-    return call(
-        give_body,
-        (2,),
-        [pl.BlockSpec((step, cols), lambda n, s: (4 * (1 - s[0]) + 2 * s[1] + n, 0))],
-        pl.BlockSpec((step, cols), lambda n, s: (n, 0)),
-        jax.ShapeDtypeStruct((rows, cols), BF16),
-        (scalars, w_query),
-        "give_columns",
-        after,
-        scalars=1,
+        scratch=[
+            pltpu.VMEM(frames.shape, BF16),
+            pltpu.VMEM(w_query.shape, BF16),
+            pltpu.VMEM(grad_mixed.shape, BF16),
+            pltpu.VMEM(w_out.shape, BF16),
+            pltpu.VMEM((rows, width), BF16),
+            pltpu.VMEM((rows, width), BF16),
+            pltpu.SemaphoreType.DMA((2, parts)),
+            pltpu.SemaphoreType.DMA((2, steps)),
+            pltpu.SemaphoreType.DMA((2, steps)),
+        ],
     )
 
 
@@ -215,12 +277,13 @@
     )
 
 
-def note_product(scalars, grads, chunks, w_key, w_value, after, before=None):
+def note_product(scalars, grads, chunks, w_key, w_value, after, before=None, which=(0, 1)):
     nt = grads[0].shape[1]
     half = D // 2
     heads = [h for h0, hc in chunks for h in range(h0, h0 + hc)]
     hc = len(heads)
     last = before is not None
+    start = which[0]
 
     def body(s_ref, *refs):
         grad_refs, refs = refs[: len(grads)], refs[len(grads) :]
@@ -235,17 +298,18 @@
         out_ref[0] = total.astype(out_ref.dtype)
 
     def weight_in(h):
-        return pl.BlockSpec((half, HD), lambda n, s: (jnp.where(n == 0, 1 - s[0], s[0]), h))
-
-    half_io = pl.BlockSpec((1, nt, half), lambda n, s: (n, 0, 0))
+        return pl.BlockSpec(
+            (half, HD), lambda n, s: (jnp.where(n + start == 0, 1 - s[0], s[0]), h)
+        )
+
     return call(
         body,
-        (2,),
+        (len(which),),
         [pl.BlockSpec(g.shape, lambda n, s: (0, 0, 0)) for g in grads]
         + [weight_in(h) for h in heads] * 2
-        + ([half_io] if last else []),
-        half_io,
-        jax.ShapeDtypeStruct((2, nt, half), BF16 if last else F32),
+        + ([pl.BlockSpec((1, nt, half), lambda n, s: (n + start, 0, 0))] if last else []),
+        pl.BlockSpec((1, nt, half), lambda n, s: (n, 0, 0)),
+        jax.ShapeDtypeStruct((len(which), nt, half), BF16 if last else F32),
         (scalars, *grads) + (w_key,) * hc + (w_value,) * hc + ((before,) if last else ()),
         "note_product",
         after,
@@ -254,9 +318,19 @@
 
 
 def attention_body(
-    bias_ref, q_ref, g_ref, kvo_ref, kvn_ref, kvf_ref, dq_ref, own_ref, near_ref, far_ref,
-    p_scr, ds_scr,
+    s_ref, band_ref, q_ref, g_ref, kvo_ref, kvn_ref, kvf_ref, dq_ref, own_ref, near_ref, far_ref,
+    p_scr, ds_scr, bias_ref,
 ):
+    @pl.when(pl.program_id(0) == 0)
+    def _():
+        row = lax.broadcasted_iota(jnp.int32, (8, BLK), 0)
+        shard = s_ref[2]
+        far = shard - 1 + 2 * s_ref[1]
+        block = jnp.where(row < 2, 2 * shard, jnp.where(row < 4, 2 * (shard ^ 1), 2 * far)) + row % 2
+        for b in range(q_ref.shape[0] // BLK):
+            inside = (block >= band_ref[0, b]) & (block <= band_ref[1, b])
+            bias_ref[:, b * BLK : (b + 1) * BLK] = jnp.where(inside, 0.0, -jnp.inf)
+
     scale2 = SCALE * LOG2E
     frames = q_ref.shape[0]
     nt = kvo_ref.shape[1]
@@ -297,58 +371,48 @@
         far_ref[i] = grad[2 * nt :].astype(BF16)
 
 
-def attention(bias, queries, grad_ctx, kv_own, kv_near, kv_far, h0, hc, after):
+def attention(scalars, band, queries, grad_ctx, kv_own, kv_near, kv_far, h0, hc, after):
     frames = queries.shape[0]
     nt = kv_own.shape[1]
-    frame_in = pl.BlockSpec((frames, HD), lambda h: (0, h0 + h))
-    note_io = pl.BlockSpec((2, nt, HD), lambda h: (0, 0, h))
+    frame_in = pl.BlockSpec((frames, HD), lambda h, s, b: (0, h0 + h))
+    note_io = pl.BlockSpec((2, nt, HD), lambda h, s, b: (0, 0, h))
     notes_out = jax.ShapeDtypeStruct((2, nt, hc * HD), BF16)
     return call(
         attention_body,
         (hc,),
-        [pl.BlockSpec(bias.shape, lambda h: (0, 0)), frame_in, frame_in, note_io, note_io, note_io],
-        [pl.BlockSpec((frames, HD), lambda h: (0, h)), note_io, note_io, note_io],
+        [frame_in, frame_in, note_io, note_io, note_io],
+        [pl.BlockSpec((frames, HD), lambda h, s, b: (0, h)), note_io, note_io, note_io],
         [
             jax.ShapeDtypeStruct((frames, hc * HD), BF16),
             jax.ShapeDtypeStruct((2, nt, hc * HD), F32),
             notes_out,
             notes_out,
         ],
-        (bias, queries, grad_ctx, kv_own, kv_near, kv_far),
+        (scalars, band, queries, grad_ctx, kv_own, kv_near, kv_far),
         "attention",
         after,
-        scratch=[pltpu.VMEM((3 * nt, frames), BF16), pltpu.VMEM((3 * nt, frames), BF16)],
-        flops=90 * frames * nt * hc * HD,
+        scalars=2,
+        scratch=[
+            pltpu.VMEM((3 * nt, frames), BF16),
+            pltpu.VMEM((3 * nt, frames), BF16),
+            pltpu.VMEM((8, frames), F32),
+        ],
+        flops=90 * frames * nt * hc * HD if h0 else 0,
     )
 
 
 def per_device(notes, frames, w_query, w_key, w_value, w_out, band_blocks, grad_mixed):
-    nt = notes.shape[1]
     shard = lax.axis_index("seq")
     group = lax.axis_index("head")
     core = shard % 2
-    scalars = jnp.stack([group, core]).astype(jnp.int32)
-
-    made = []
-    moved = []
-    for h0, hc in CHUNKS:
-        made.append(key_values(notes[0], w_key, w_value, h0, hc, made[-1:]))
-        moved.append(section_shift(made[-1], 1))
-    given = give_columns(scalars, w_query, made[-1:])
+    scalars = jnp.stack([group, core, shard]).astype(jnp.int32)
+    band = band_blocks[0]
+
+    *made, given = key_values(scalars, notes[0], w_key, w_value, w_query)
+    moved = [section_shift(kv, 1) for kv in made]
     w_other = other_columns(given)
-
-    far_shard = jnp.where(core == 0, shard - 1, shard + 1)
-    shards = jnp.stack([shard, shard ^ 1, far_shard, shard])
-    per_shard = nt // BLK
-    block_ids = (shards[:, None] * per_shard + jnp.arange(per_shard, dtype=jnp.int32)).reshape(-1)
-    inside = (block_ids[:, None] >= band_blocks[0, 0][None]) & (
-        block_ids[:, None] <= band_blocks[0, 1][None]
-    )
-    bias = jnp.repeat(jnp.where(inside, 0.0, -jnp.inf).astype(F32), BLK, axis=1)
-
-    queries = project(frames[0], w_query, False, "queries", (given,))
+    queries, grad_ctx = project(frames[0], w_query, grad_mixed[0], w_out, (given,))
     moved[0], queries = lax.optimization_barrier((moved[0], queries))
-    grad_ctx = project(grad_mixed[0], w_out, True, "grad_ctx", (queries, moved[0]))
 
     grad_q = []
     grad_q_other = []
@@ -367,13 +431,15 @@
         kv = moved[step]
         after = grad_q[-1:]
         kv_near, kv_far = near_swap(kv), far_swap(kv)
+        if step == 0:
+            kv_far, moved[1] = lax.optimization_barrier((kv_far, moved[1]))
         if step == 1:
             near, far, kv_near, kv_far = lax.optimization_barrier((near, far, kv_near, kv_far))
             send_back(own, near, far)
         if step == 2:
             after = after + [grad_q_other[0], summed_all[0]]
         dq, own, near, far = attention(
-            bias, queries, grad_ctx, kv, kv_near, kv_far, h0, hc, after
+            scalars, band, queries, grad_ctx, kv, kv_near, kv_far, h0, hc, after
         )
         if step == 0:
             moved[2], dq = lax.optimization_barrier((moved[2], dq))
@@ -387,15 +453,15 @@
     total = frame_sum_own(
         scalars, grad_q, grad_q_other[:-1], w_query, w_other, CHUNKS[:-1], ()
     )
-    before = note_product(scalars, note_cols[:-1], CHUNKS[:-1], w_key, w_value, (total,))
+    before = note_product(scalars, note_cols[:-1], CHUNKS[:-1], w_key, w_value, (total, grad_q_other[-1]))
+    last = (scalars, note_cols[-1:], CHUNKS[-1:], w_key, w_value)
+    give_notes = note_product(*last, (), before, (0,))
+    notes_other = head_swap(give_notes)
+    keep_notes = note_product(*last, (give_notes,), before, (1,))
     frame_sum = frame_sum_last(
-        scalars, total, grad_q_other[-1], w_other, *CHUNKS[-1], (before,)
-    )
-    halves = note_product(
-        scalars, note_cols[-1:], CHUNKS[-1:], w_key, w_value, (frame_sum,), before
-    )
-    give_notes = head_swap(halves[0])
-    note_sum = halves[1].astype(F32) + give_notes.astype(F32)
+        scalars, total, grad_q_other[-1], w_other, *CHUNKS[-1], (keep_notes,)
+    )
+    note_sum = keep_notes[0].astype(F32) + notes_other[0].astype(F32)
     return (frame_sum[None], note_sum.astype(BF16)[None])
 
 

time: 170 us -> 187 us (1.10)
  Pallas kernels: 88 us -> 110 us
  local copies, waits for them, and re-layouts: 3.23 us -> 0 us
    pallas_call x13 -> x10, Pallas kernels: 88 us -> 110 us  [call(): pl.pallas_call(reads, grid_spec=pltpu.PrefetchScalarGridSpec(num_scalar_p...]
    ppermute x4, waiting for transfers between devices: 12.3 us -> 6.84 us  [head_swap(): return lax.ppermute(block, 'head', [(0, 1), (1, 0)])]
    ppermute x6, waiting for transfers between devices: 0.02 us -> 4.3 us  [far_swap(): return lax.ppermute(block, 'seq', pairs + [(j, i) for i, j in pairs])]
    ppermute x6, starting transfers between devices: 20.9 us -> 23.5 us  [far_swap(): return lax.ppermute(block, 'seq', pairs + [(j, i) for i, j in pairs])]
    convert_element_type x0 -> x1, other arithmetic: none -> 2.19 us  [per_device(): return (frame_sum[None], note_sum.astype(BF16)[None])]
    broadcast_in_dim x1 -> x0, other arithmetic: 2.03 us -> none  [per_device(): return (frame_sum[None], note_sum.astype(BF16)[None])]
  transfers between devices with their start and end apart: 23 -> 23, of which waited for: 1 -> 5; matrix products, arithmetic and copies ran while one was open for 5% -> 3% of each run, Pallas kernels for 40% -> 38%
where the time goes in v3:
time: 187 us
  Pallas kernels  110 us (59%)
  starting transfers between devices  40.6 us (22%)
  between operations  14.2 us (8%)
  waiting for transfers between devices  13 us (7%)
  other arithmetic  9.04 us (5%)
    pallas_call x10, Pallas kernels, call(): pl.pallas_call(reads, grid_spec=pltpu.PrefetchScalarGridSpec(num_scalar_p...  110 us
    ppermute x6, starting transfers between devices, far_swap(): return lax.ppermute(block, 'seq', pairs + [(j, i) for i, j in pairs])  23.5 us
    ppermute x4, starting transfers between devices, head_swap(): return lax.ppermute(block, 'head', [(0, 1), (1, 0)])  9.76 us
    ppermute x4, waiting for transfers between devices, head_swap(): return lax.ppermute(block, 'head', [(0, 1), (1, 0)])  6.84 us
    ppermute x6, starting transfers between devices, section_shift(): lax.ppermute(block, 'section', [(i, (i + distance) % count) for i in rang...  6.76 us
    convert_element_type x3, other arithmetic, send_back(): summed_all.append((own + near.astype(F32) + far.astype(F32)).astype(BF16))  6.21 us
    ppermute x6, waiting for transfers between devices, far_swap(): return lax.ppermute(block, 'seq', pairs + [(j, i) for i, j in pairs])  4.3 us
  transfers between devices with their start and end apart: 23, of which 5 were waited for; matrix products, arithmetic and copies ran while one was open for 3% of the time, Pallas kernels for 38%

profile of v3, /device:TPU:1, one launch (start us, length us, event | category | flops | bytes accessed | tf_op | source)
XLA Modules:
  0.0 186.6 jit_solution(9554762586918198706)
XLA Ops:
  7.2 0.0 all-gather.3.cloned.1.call-start
  7.2 0.6 pad_add_fusion.refs_0_
  7.9 34.9 %key_values.1 = (bf16[2,256,256]{2,1,0:T(8,128)(2,1)}, bf16[2,256,384]{2,1,0:T(8,128)(2,1)}, bf16[2,256,384]{2,1,0:T(8,128)(2,1)}, bf16[512,1024]{1,0:T(8,128)(2,1)}) custom-call(s32[3]{0:T(128)} %pad_add_fusion.refs_0_, bf16[256,2048]{1,0:T(8,128)(2,1)} %bitcast.16, bf16[2048,1024]{1,0:T(8,128)(2,1)} %refs_4_.7, bf16[2048,1024]{1,0:T(8,128)(2,1)} %refs_7_.5, ...), custom_call_target="tpu_custom_call" | custom-call | tf_op jit(solution)/shard_map/key_values/pallas_call | solution.py:69
  42.7 0.0 all-gather.3.cloned.1.call-update
  42.8 2.1 %collective-permute-start.1 = (bf16[2,256,256]{2,1,0:T(8,128)(2,1)}, bf16[2,256,256]{2,1,0:T(8,128)(2,1)}, u32[]{:S(2)}, u32[]{:S(2)}) collective-permute-start(bf16[2,256,256]{2,1,0:T(8,128)(2,1)} %get-tuple-element.36), channel_id=1, source_target_pairs={{0,32},{32,64},{64,96},{96,0},{1,33},{33,65},{65,97},{97,1},{2,34}... | collective-permute-start | bytes 786440 | tf_op jit(solution)/shard_map/ppermute | solution.py:30
  44.9 1.2 collective-permute-start.4
  46.1 14.3 %queries_and_grad_ctx.1 = (bf16[1024,1024]{1,0:T(8,128)(2,1)}, bf16[1024,1024]{1,0:T(8,128)(2,1)}) custom-call(bf16[1024,2048]{1,0:T(8,128)(2,1)} %bitcast.13, bf16[2048,1024]{1,0:T(8,128)(2,1)} %refs_6_.4, bf16[1024,2048]{1,0:T(8,128)(2,1)} %bitcast.14, bf16[1024,2048]{1,0:T(8,128)(2,1)} %refs_3_.6, bf16[512,1024]{1,0:T(8,128)(2,1)} %get-tuple-element.37.refs_4_), custom_call_target="tpu_custom_call" | custom-call | tf_op jit(solution)/shard_map/queries_and_grad_ctx/pallas_call | solution.py:69
  60.4 0.0 collective-permute-done.1.refs_4_
  60.4 4.3 %collective-permute-start.3 = (bf16[2,256,256]{2,1,0:T(8,128)(2,1)}, bf16[2,256,256]{2,1,0:T(8,128)(2,1)}, u32[]{:S(2)}, u32[]{:S(2)}) collective-permute-start(bf16[2,256,256]{2,1,0:T(8,128)(2,1)} %collective-permute-done.1.refs_4_), channel_id=1, source_target_pairs={{2,4},{6,8},{10,12},{14,16},{18,20},{22,24},{26,28},{4,2},{8,6},{1... | collective-permute-start | bytes 786440 | tf_op jit(solution)/shard_map/ppermute | solution.py:43
  64.7 1.0 collective-permute-start
  65.7 0.0 collective-permute-done.4.refs_4_
  65.7 3.7 %collective-permute-done.3.refs_6_ = bf16[2,256,256]{2,1,0:T(8,128)(2,1)} collective-permute-done((bf16[2,256,256]{2,1,0:T(8,128)(2,1)}, bf16[2,256,256]{2,1,0:T(8,128)(2,1)}, u32[]{:S(2)}, u32[]{:S(2)}) %collective-permute-start.3) | collective-permute-done | bytes 262176 | tf_op jit(solution)/shard_map/ppermute | solution.py:43
  69.3 0.0 collective-permute-start.5
  69.3 3.6 %collective-permute-start.6 = (bf16[2,256,384]{2,1,0:T(8,128)(2,1)}, bf16[2,256,384]{2,1,0:T(8,128)(2,1)}, u32[]{:S(2)}, u32[]{:S(2)}) collective-permute-start(bf16[2,256,384]{2,1,0:T(8,128)(2,1)} %collective-permute-done.4.refs_4_), channel_id=1, source_target_pairs={{2,4},{6,8},{10,12},{14,16},{18,20},{22,24},{26,28},{4,2},{8,6},{1... | collective-permute-start | bytes 1179656 | tf_op jit(solution)/shard_map/ppermute | solution.py:43
  72.9 0.3 collective-permute-start.2
  73.2 1.9 collective-permute-done.2.refs_5_
  75.1 8.4 %attention.3 = (bf16[1024,256]{1,0:T(8,128)(2,1)}, f32[2,256,256]{2,1,0:T(8,128)}, bf16[2,256,256]{2,1,0:T(8,128)(2,1)}, bf16[2,256,256]{2,1,0:T(8,128)(2,1)}) custom-call(s32[3]{0:T(128)} %pad_add_fusion.refs_0_, s32[2,8]{1,0:T(2,128)} %bitcast.17, bf16[1024,1024]{1,0:T(8,128)(2,1)} %get-tuple-element.39.refs_2_, ...), custom_call_target="tpu_custom_call" | custom-call | tf_op jit(solution)/shard_map/attention/pallas_call | solution.py:69
  83.5 0.0 collective-permute-done.refs_4_
  83.5 0.2 collective-permute-start.7
  83.7 3.2 %collective-permute-start.8 = (bf16[2,256,384]{2,1,0:T(8,128)(2,1)}, bf16[2,256,384]{2,1,0:T(8,128)(2,1)}, u32[]{:S(2)}, u32[]{:S(2)}) collective-permute-start(bf16[2,256,384]{2,1,0:T(8,128)(2,1)} %collective-permute-done.refs_4_), channel_id=1, source_target_pairs={{2,4},{6,8},{10,12},{14,16},{18,20},{22,24},{26,28},{4,2},{8,6},{1... | collective-permute-start | bytes 1179656 | tf_op jit(solution)/shard_map/ppermute | solution.py:43
  86.9 3.7 %collective-permute-start.9 = (bf16[1024,256]{1,0:T(8,128)(2,1)}, bf16[1024,256]{1,0:T(8,128)(2,1)}, u32[]{:S(2)}, u32[]{:S(2)}) collective-permute-start(bf16[1024,256]{1,0:T(8,128)(2,1)} %get-tuple-element.45.refs_7_.refs_1_), channel_id=1, source_target_pairs={{0,1},{1,0},{2,3},{3,2},{4,5},{5,4},{6,7},{7,6},{8,9},{9,8},{10,11... | collective-permute-start | bytes 1572872 | tf_op jit(solution)/shard_map/ppermute | solution.py:47
  90.7 4.6 %collective-permute-start.11 = (bf16[2,256,256]{2,1,0:T(8,128)(2,1)}, bf16[2,256,256]{2,1,0:T(8,128)(2,1)}, u32[]{:S(2)}, u32[]{:S(2)}) collective-permute-start(bf16[2,256,256]{2,1,0:T(8,128)(2,1)} %get-tuple-element.55), channel_id=1, source_target_pairs={{2,4},{6,8},{10,12},{14,16},{18,20},{22,24},{26,28},{4,2},{8,6},{1... | collective-permute-start | bytes 786440 | tf_op jit(solution)/shard_map/ppermute | solution.py:43
  95.3 11.5 %attention.4 = (bf16[1024,384]{1,0:T(8,128)(2,1)}, f32[2,256,384]{2,1,0:T(8,128)}, bf16[2,256,384]{2,1,0:T(8,128)(2,1)}, bf16[2,256,384]{2,1,0:T(8,128)(2,1)}) custom-call(s32[3]{0:T(128)} %pad_add_fusion.refs_0_, s32[2,8]{1,0:T(2,128)} %bitcast.18, bf16[1024,1024]{1,0:T(8,128)(2,1)} %get-tuple-element.39.refs_2_, ...), custom_call_target="tpu_custom_call" | custom-call | flops 9059696640 | tf_op jit(solution)/shard_map/attention/pallas_call | solution.py:69
  106.8 0.2 collective-permute-start.13
  107.0 0.0 collective-permute-done.11
  107.0 0.0 collective-permute-start.12
  107.0 2.0 %add_convert_fusion.3.refs_9_ = bf16[2,256,256]{2,1,0:T(8,128)(2,1)} fusion(bf16[2,256,256]{2,1,0:T(8,128)(2,1)} %collective-permute-done.11, f32[2,256,256]{2,1,0:T(8,128)} %get-tuple-element.53, bf16[2,256,256]{2,1,0:T(8,128)(2,1)} %collective-permute-done.10), kind=kLoop, calls=%fused_computation.3 | loop fusion | flops 655360 | bytes 1310720 | tf_op jit(solution)/shard_map/convert_element_type | solution.py:427
  109.0 4.0 %collective-permute-start.19 = (bf16[2,256,384]{2,1,0:T(8,128)(2,1)}, bf16[2,256,384]{2,1,0:T(8,128)(2,1)}, u32[]{:S(2)}, u32[]{:S(2)}) collective-permute-start(bf16[2,256,384]{2,1,0:T(8,128)(2,1)} %get-tuple-element.67), channel_id=1, source_target_pairs={{2,4},{6,8},{10,12},{14,16},{18,20},{22,24},{26,28},{4,2},{8,6},{1... | collective-permute-start | bytes 1179656 | tf_op jit(solution)/shard_map/ppermute | solution.py:43
  113.0 0.0 collective-permute-done.8.refs_6_
  113.0 1.5 collective-permute-start.15
  114.6 11.4 %attention.5 = (bf16[1024,384]{1,0:T(8,128)(2,1)}, f32[2,256,384]{2,1,0:T(8,128)}, bf16[2,256,384]{2,1,0:T(8,128)(2,1)}, bf16[2,256,384]{2,1,0:T(8,128)(2,1)}) custom-call(s32[3]{0:T(128)} %pad_add_fusion.refs_0_, s32[2,8]{1,0:T(2,128)} %bitcast.19, bf16[1024,1024]{1,0:T(8,128)(2,1)} %get-tuple-element.39.refs_2_, ...), custom_call_target="tpu_custom_call" | custom-call | flops 9059696640 | tf_op jit(solution)/shard_map/attention/pallas_call | solution.py:69
  126.0 0.1 collective-permute-start.16
  126.1 3.7 %collective-permute-start.17 = (bf16[2,256,384]{2,1,0:T(8,128)(2,1)}, bf16[2,256,384]{2,1,0:T(8,128)(2,1)S(1)}, u32[]{:S(2)}, u32[]{:S(2)}) collective-permute-start(bf16[2,256,384]{2,1,0:T(8,128)(2,1)} %get-tuple-element.63), channel_id=1, source_target_pairs={{2,4},{6,8},{10,12},{14,16},{18,20},{22,24},{26,28},{4,2},{8,6},{1... | collective-permute-start | bytes 1179656 | tf_op jit(solution)/shard_map/ppermute | solution.py:43
  129.8 3.0 %collective-permute-start.14 = (bf16[1024,384]{1,0:T(8,128)(2,1)}, bf16[1024,384]{1,0:T(8,128)(2,1)}, u32[]{:S(2)}, u32[]{:S(2)}) collective-permute-start(bf16[1024,384]{1,0:T(8,128)(2,1)} %get-tuple-element.56.refs_3_), channel_id=1, source_target_pairs={{0,1},{1,0},{2,3},{3,2},{4,5},{5,4},{6,7},{7,6},{8,9},{9,8},{10,11... | collective-permute-start | bytes 2359304 | tf_op jit(solution)/shard_map/ppermute | solution.py:47
  132.8 2.2 %add_convert_fusion.1 = bf16[2,256,384]{2,1,0:T(8,128)(2,1)} fusion(bf16[2,256,384]{2,1,0:T(8,128)(2,1)} %collective-permute-done.19, f32[2,256,384]{2,1,0:T(8,128)} %get-tuple-element.65, bf16[2,256,384]{2,1,0:T(8,128)(2,1)} %collective-permute-done.12), kind=kLoop, calls=%fused_computation.1 | loop fusion | flops 983040 | bytes 1966080 | tf_op jit(solution)/shard_map/convert_element_type | solution.py:427
  135.0 0.2 collective-permute-start.20
  135.3 0.6 collective-permute-done.17
  135.9 2.0 %add_convert_fusion.2 = bf16[2,256,384]{2,1,0:T(8,128)(2,1)} fusion(bf16[2,256,384]{2,1,0:T(8,128)(2,1)S(1)} %collective-permute-done.17, f32[2,256,384]{2,1,0:T(8,128)} %get-tuple-element.59, bf16[2,256,384]{2,1,0:T(8,128)(2,1)S(1)} %collective-permute-done.16), kind=kLoop, calls=%fused_computation.2 | loop fusion | flops 983040 | bytes 1966080 | tf_op jit(solution)/shard_map/convert_element_type | solution.py:427
  137.9 0.7 collective-permute-start.18
  138.5 9.1 %frame_sum_own.1.refs_13_.refs_1_ = f32[1024,1024]{1,0:T(8,128)} custom-call(s32[3]{0:T(128)} %pad_add_fusion.refs_0_, bf16[1024,256]{1,0:T(8,128)(2,1)} %get-tuple-element.45.refs_7_.refs_1_, bf16[1024,384]{1,0:T(8,128)(2,1)} %get-tuple-element.51.refs_7_.refs_2_, bf16[1024,384]{1,0:T(8,128)(2,1)} %get-tuple-element.56.refs_3_, ...), custom_call_target="tpu_custom_call" | custom-call | tf_op jit(solution)/shard_map/frame_sum_own/pallas_call | solution.py:69
  147.6 5.5 %collective-permute-done.14.refs_14_.refs_2_ = bf16[1024,384]{1,0:T(8,128)(2,1)} collective-permute-done((bf16[1024,384]{1,0:T(8,128)(2,1)}, bf16[1024,384]{1,0:T(8,128)(2,1)}, u32[]{:S(2)}, u32[]{:S(2)}) %collective-permute-start.14) | collective-permute-done | bytes 786464 | tf_op jit(solution)/shard_map/ppermute | solution.py:47
  153.1 5.9 %note_product.3.refs_8_ = f32[2,256,1024]{2,1,0:T(8,128)} custom-call(s32[3]{0:T(128)} %pad_add_fusion.refs_0_, bf16[2,256,256]{2,1,0:T(8,128)(2,1)} %collective-permute-done.15.refs_1_, bf16[2,256,384]{2,1,0:T(8,128)(2,1)} %collective-permute-done.20.refs_2_, bf16[2048,1024]{1,0:T(8,128)(2,1)} %refs_4_.7, bf16[2048,1024]{1,0:T(8,128)(2,1)} %refs_4_.7, ...), custom_call_target="tpu_custom_call" | custom-call | tf_op jit(solution)/shard_map/note_product/pallas_call | solution.py:69
  159.0 4.1 %note_product.4.refs_9_ = bf16[1,256,1024]{2,1,0:T(8,128)(2,1)} custom-call(s32[3]{0:T(128)} %pad_add_fusion.refs_0_, bf16[2,256,384]{2,1,0:T(8,128)(2,1)} %collective-permute-done.18.refs_1_, bf16[2048,1024]{1,0:T(8,128)(2,1)} %refs_4_.7, bf16[2048,1024]{1,0:T(8,128)(2,1)} %refs_4_.7, bf16[2048,1024]{1,0:T(8,128)(2,1)} %refs_4_.7, ...), custom_call_target="tpu_custom_call" | custom-call | tf_op jit(solution)/shard_map/note_product/pallas_call | solution.py:69
  163.1 2.9 %collective-permute-start.21 = (bf16[1,256,1024]{2,1,0:T(8,128)(2,1)}, bf16[1,256,1024]{2,1,0:T(8,128)(2,1)}, u32[]{:S(2)}, u32[]{:S(2)}) collective-permute-start(bf16[1,256,1024]{2,1,0:T(8,128)(2,1)} %note_product.4.refs_9_), channel_id=1, source_target_pairs={{0,1},{1,0},{2,3},{3,2},{4,5},{5,4},{6,7},{7,6},{8,9},{9,8},{10,11... | collective-permute-start | bytes 1572872 | tf_op jit(solution)/shard_map/ppermute | solution.py:47
  166.0 4.1 %note_product.5.refs_6_ = bf16[1,256,1024]{2,1,0:T(8,128)(2,1)} custom-call(s32[3]{0:T(128)} %pad_add_fusion.refs_0_, bf16[2,256,384]{2,1,0:T(8,128)(2,1)} %collective-permute-done.18.refs_1_, bf16[2048,1024]{1,0:T(8,128)(2,1)} %refs_4_.7, bf16[2048,1024]{1,0:T(8,128)(2,1)} %refs_4_.7, bf16[2048,1024]{1,0:T(8,128)(2,1)} %refs_4_.7, ...), custom_call_target="tpu_custom_call" | custom-call | tf_op jit(solution)/shard_map/note_product/pallas_call | solution.py:69
  170.1 6.1 %frame_sum_last.1 = bf16[1024,1024]{1,0:T(8,128)(2,1)} custom-call(s32[3]{0:T(128)} %pad_add_fusion.refs_0_, f32[1024,1024]{1,0:T(8,128)} %frame_sum_own.1.refs_13_.refs_1_, bf16[1024,384]{1,0:T(8,128)(2,1)} %collective-permute-done.14.refs_14_.refs_2_, bf16[4,512,1024]{2,1,0:T(8,128)(2,1)} %bitcast.10, bf16[4,512,1024]{2,1,0:T(8,128)(2,1)} %bitcast.11, ...), custom_call_target="tpu_custom_call" | custom-call | tf_op jit(solution)/shard_map/frame_sum_last/pallas_call | solution.py:69
  176.2 1.3 collective-permute-done.21
  177.6 2.2 %add_convert_fusion = bf16[1,256,1024]{2,1,0:T(8,128)(2,1)} fusion(bf16[1,256,1024]{2,1,0:T(8,128)(2,1)} %collective-permute-done.21, bf16[1,256,1024]{2,1,0:T(8,128)(2,1)} %note_product.5.refs_6_), kind=kLoop, calls=%fused_computation | loop fusion | flops 1048576 | bytes 1572864 | tf_op jit(solution)/shard_map/convert_element_type | solution.py:465
  (14 shorter events, 0.0 us)
Async XLA Ops:
  7.2 131.4 %all-gather.3.cloned.1.call-start = ((), (), s32[]{:S(2)}) async-start(), calls=%async_computation | async-start | bytes 5242880 | tf_op jit(solution)/shard_map/all_gather | solution.py:55
  42.8 17.6 %collective-permute-start.1 = (bf16[2,256,256]{2,1,0:T(8,128)(2,1)}, bf16[2,256,256]{2,1,0:T(8,128)(2,1)}, u32[]{:S(2)}, u32[]{:S(2)}) collective-permute-start(bf16[2,256,256]{2,1,0:T(8,128)(2,1)} %get-tuple-element.36), channel_id=1, source_target_pairs={{0,32},{32,64},{64,96},{96,0},{1,33},{33,65},{65,97},{97,1},{2,34}... | collective-permute-start | bytes 786440 | tf_op jit(solution)/shard_map/ppermute | solution.py:30
  44.9 20.8 %collective-permute-start.4 = (bf16[2,256,384]{2,1,0:T(8,128)(2,1)}, bf16[2,256,384]{2,1,0:T(8,128)(2,1)}, u32[]{:S(2)}, u32[]{:S(2)}) collective-permute-start(bf16[2,256,384]{2,1,0:T(8,128)(2,1)} %get-tuple-element.42), channel_id=1, source_target_pairs={{0,32},{32,64},{64,96},{96,0},{1,33},{33,65},{65,97},{97,1},{2,34}... | collective-permute-start | bytes 1179656 | tf_op jit(solution)/shard_map/ppermute | solution.py:30
  60.4 9.0 %collective-permute-start.3 = (bf16[2,256,256]{2,1,0:T(8,128)(2,1)}, bf16[2,256,256]{2,1,0:T(8,128)(2,1)}, u32[]{:S(2)}, u32[]{:S(2)}) collective-permute-start(bf16[2,256,256]{2,1,0:T(8,128)(2,1)} %collective-permute-done.1.refs_4_), channel_id=1, source_target_pairs={{2,4},{6,8},{10,12},{14,16},{18,20},{22,24},{26,28},{4,2},{8,6},{1... | collective-permute-start | bytes 786440 | tf_op jit(solution)/shard_map/ppermute | solution.py:43
  64.7 18.8 %collective-permute-start = (bf16[2,256,384]{2,1,0:T(8,128)(2,1)}, bf16[2,256,384]{2,1,0:T(8,128)(2,1)}, u32[]{:S(2)}, u32[]{:S(2)}) collective-permute-start(bf16[2,256,384]{2,1,0:T(8,128)(2,1)} %get-tuple-element.35), channel_id=1, source_target_pairs={{0,32},{32,64},{64,96},{96,0},{1,33},{33,65},{65,97},{97,1},{2,34}... | collective-permute-start | bytes 1179656 | tf_op jit(solution)/shard_map/ppermute | solution.py:30
  69.3 21.3 %collective-permute-start.5 = (bf16[2,256,384]{2,1,0:T(8,128)(2,1)}, bf16[2,256,384]{2,1,0:T(8,128)(2,1)}, u32[]{:S(2)}, u32[]{:S(2)}) collective-permute-start(bf16[2,256,384]{2,1,0:T(8,128)(2,1)} %collective-permute-done.4.refs_4_), channel_id=1, source_target_pairs={{0,2},{2,0},{4,6},{6,4},{8,10},{10,8},{12,14},{14,12},{16,18},{18,... | collective-permute-start | bytes 1179656 | tf_op jit(solution)/shard_map/ppermute | solution.py:37
  69.3 21.3 %collective-permute-start.6 = (bf16[2,256,384]{2,1,0:T(8,128)(2,1)}, bf16[2,256,384]{2,1,0:T(8,128)(2,1)}, u32[]{:S(2)}, u32[]{:S(2)}) collective-permute-start(bf16[2,256,384]{2,1,0:T(8,128)(2,1)} %collective-permute-done.4.refs_4_), channel_id=1, source_target_pairs={{2,4},{6,8},{10,12},{14,16},{18,20},{22,24},{26,28},{4,2},{8,6},{1... | collective-permute-start | bytes 1179656 | tf_op jit(solution)/shard_map/ppermute | solution.py:43
  72.9 2.1 %collective-permute-start.2 = (bf16[2,256,256]{2,1,0:T(8,128)(2,1)}, bf16[2,256,256]{2,1,0:T(8,128)(2,1)}, u32[]{:S(2)}, u32[]{:S(2)}) collective-permute-start(bf16[2,256,256]{2,1,0:T(8,128)(2,1)} %collective-permute-done.1.refs_4_), channel_id=1, source_target_pairs={{0,2},{2,0},{4,6},{6,4},{8,10},{10,8},{12,14},{14,12},{16,18},{18,... | collective-permute-start | bytes 786440 | tf_op jit(solution)/shard_map/ppermute | solution.py:37
  83.5 25.5 %collective-permute-start.7 = (bf16[2,256,384]{2,1,0:T(8,128)(2,1)}, bf16[2,256,384]{2,1,0:T(8,128)(2,1)}, u32[]{:S(2)}, u32[]{:S(2)}) collective-permute-start(bf16[2,256,384]{2,1,0:T(8,128)(2,1)} %collective-permute-done.refs_4_), channel_id=1, source_target_pairs={{0,2},{2,0},{4,6},{6,4},{8,10},{10,8},{12,14},{14,12},{16,18},{18,... | collective-permute-start | bytes 1179656 | tf_op jit(solution)/shard_map/ppermute | solution.py:37
  83.7 29.3 %collective-permute-start.8 = (bf16[2,256,384]{2,1,0:T(8,128)(2,1)}, bf16[2,256,384]{2,1,0:T(8,128)(2,1)}, u32[]{:S(2)}, u32[]{:S(2)}) collective-permute-start(bf16[2,256,384]{2,1,0:T(8,128)(2,1)} %collective-permute-done.refs_4_), channel_id=1, source_target_pairs={{2,4},{6,8},{10,12},{14,16},{18,20},{22,24},{26,28},{4,2},{8,6},{1... | collective-permute-start | bytes 1179656 | tf_op jit(solution)/shard_map/ppermute | solution.py:43
  86.9 27.7 %collective-permute-start.9 = (bf16[1024,256]{1,0:T(8,128)(2,1)}, bf16[1024,256]{1,0:T(8,128)(2,1)}, u32[]{:S(2)}, u32[]{:S(2)}) collective-permute-start(bf16[1024,256]{1,0:T(8,128)(2,1)} %get-tuple-element.45.refs_7_.refs_1_), channel_id=1, source_target_pairs={{0,1},{1,0},{2,3},{3,2},{4,5},{5,4},{6,7},{7,6},{8,9},{9,8},{10,11... | collective-permute-start | bytes 1572872 | tf_op jit(solution)/shard_map/ppermute | solution.py:47
  90.7 16.1 %collective-permute-start.10 = (bf16[2,256,256]{2,1,0:T(8,128)(2,1)}, bf16[2,256,256]{2,1,0:T(8,128)(2,1)}, u32[]{:S(2)}, u32[]{:S(2)}) collective-permute-start(bf16[2,256,256]{2,1,0:T(8,128)(2,1)} %get-tuple-element.54), channel_id=1, source_target_pairs={{0,2},{2,0},{4,6},{6,4},{8,10},{10,8},{12,14},{14,12},{16,18},{18,... | collective-permute-start | bytes 786440 | tf_op jit(solution)/shard_map/ppermute | solution.py:37
  90.7 16.3 %collective-permute-start.11 = (bf16[2,256,256]{2,1,0:T(8,128)(2,1)}, bf16[2,256,256]{2,1,0:T(8,128)(2,1)}, u32[]{:S(2)}, u32[]{:S(2)}) collective-permute-start(bf16[2,256,256]{2,1,0:T(8,128)(2,1)} %get-tuple-element.55), channel_id=1, source_target_pairs={{2,4},{6,8},{10,12},{14,16},{18,20},{22,24},{26,28},{4,2},{8,6},{1... | collective-permute-start | bytes 786440 | tf_op jit(solution)/shard_map/ppermute | solution.py:43
  106.8 26.0 %collective-permute-start.13 = (bf16[1024,384]{1,0:T(8,128)(2,1)}, bf16[1024,384]{1,0:T(8,128)(2,1)}, u32[]{:S(2)}, u32[]{:S(2)}) collective-permute-start(bf16[1024,384]{1,0:T(8,128)(2,1)} %get-tuple-element.51.refs_7_.refs_2_), channel_id=1, source_target_pairs={{0,1},{1,0},{2,3},{3,2},{4,5},{5,4},{6,7},{7,6},{8,9},{9,8},{10,11... | collective-permute-start | bytes 2359304 | tf_op jit(solution)/shard_map/ppermute | solution.py:47
  107.0 22.8 %collective-permute-start.12 = (bf16[2,256,384]{2,1,0:T(8,128)(2,1)}, bf16[2,256,384]{2,1,0:T(8,128)(2,1)}, u32[]{:S(2)}, u32[]{:S(2)}) collective-permute-start(bf16[2,256,384]{2,1,0:T(8,128)(2,1)} %get-tuple-element.57), channel_id=1, source_target_pairs={{0,2},{2,0},{4,6},{6,4},{8,10},{10,8},{12,14},{14,12},{16,18},{18,... | collective-permute-start | bytes 1179656 | tf_op jit(solution)/shard_map/ppermute | solution.py:37
  109.0 23.8 %collective-permute-start.19 = (bf16[2,256,384]{2,1,0:T(8,128)(2,1)}, bf16[2,256,384]{2,1,0:T(8,128)(2,1)}, u32[]{:S(2)}, u32[]{:S(2)}) collective-permute-start(bf16[2,256,384]{2,1,0:T(8,128)(2,1)} %get-tuple-element.67), channel_id=1, source_target_pairs={{2,4},{6,8},{10,12},{14,16},{18,20},{22,24},{26,28},{4,2},{8,6},{1... | collective-permute-start | bytes 1179656 | tf_op jit(solution)/shard_map/ppermute | solution.py:43
  113.0 13.0 %collective-permute-start.15 = (bf16[2,256,256]{2,1,0:T(8,128)(2,1)}, bf16[2,256,256]{2,1,0:T(8,128)(2,1)}, u32[]{:S(2)}, u32[]{:S(2)}) collective-permute-start(bf16[2,256,256]{2,1,0:T(8,128)(2,1)} %add_convert_fusion.3.refs_9_), channel_id=1, source_target_pairs={{0,96},{32,0},{64,32},{96,64},{1,97},{33,1},{65,33},{97,65},{2,98}... | collective-permute-start | bytes 786440 | tf_op jit(solution)/shard_map/ppermute | solution.py:30
  126.0 9.3 %collective-permute-start.16 = (bf16[2,256,384]{2,1,0:T(8,128)(2,1)}, bf16[2,256,384]{2,1,0:T(8,128)(2,1)S(1)}, u32[]{:S(2)}, u32[]{:S(2)}) collective-permute-start(bf16[2,256,384]{2,1,0:T(8,128)(2,1)} %get-tuple-element.62), channel_id=1, source_target_pairs={{0,2},{2,0},{4,6},{6,4},{8,10},{10,8},{12,14},{14,12},{16,18},{18,... | collective-permute-start | bytes 1179656 | tf_op jit(solution)/shard_map/ppermute | solution.py:37
  126.1 9.8 %collective-permute-start.17 = (bf16[2,256,384]{2,1,0:T(8,128)(2,1)}, bf16[2,256,384]{2,1,0:T(8,128)(2,1)S(1)}, u32[]{:S(2)}, u32[]{:S(2)}) collective-permute-start(bf16[2,256,384]{2,1,0:T(8,128)(2,1)} %get-tuple-element.63), channel_id=1, source_target_pairs={{2,4},{6,8},{10,12},{14,16},{18,20},{22,24},{26,28},{4,2},{8,6},{1... | collective-permute-start | bytes 1179656 | tf_op jit(solution)/shard_map/ppermute | solution.py:43
  129.8 23.3 %collective-permute-start.14 = (bf16[1024,384]{1,0:T(8,128)(2,1)}, bf16[1024,384]{1,0:T(8,128)(2,1)}, u32[]{:S(2)}, u32[]{:S(2)}) collective-permute-start(bf16[1024,384]{1,0:T(8,128)(2,1)} %get-tuple-element.56.refs_3_), channel_id=1, source_target_pairs={{0,1},{1,0},{2,3},{3,2},{4,5},{5,4},{6,7},{7,6},{8,9},{9,8},{10,11... | collective-permute-start | bytes 2359304 | tf_op jit(solution)/shard_map/ppermute | solution.py:47
  135.0 18.1 %collective-permute-start.20 = (bf16[2,256,384]{2,1,0:T(8,128)(2,1)}, bf16[2,256,384]{2,1,0:T(8,128)(2,1)}, u32[]{:S(2)}, u32[]{:S(2)}) collective-permute-start(bf16[2,256,384]{2,1,0:T(8,128)(2,1)} %add_convert_fusion.1), channel_id=1, source_target_pairs={{0,96},{32,0},{64,32},{96,64},{1,97},{33,1},{65,33},{97,65},{2,98}... | collective-permute-start | bytes 1179656 | tf_op jit(solution)/shard_map/ppermute | solution.py:30
  137.9 21.1 %collective-permute-start.18 = (bf16[2,256,384]{2,1,0:T(8,128)(2,1)}, bf16[2,256,384]{2,1,0:T(8,128)(2,1)}, u32[]{:S(2)}, u32[]{:S(2)}) collective-permute-start(bf16[2,256,384]{2,1,0:T(8,128)(2,1)} %add_convert_fusion.2), channel_id=1, source_target_pairs={{0,96},{32,0},{64,32},{96,64},{1,97},{33,1},{65,33},{97,65},{2,98}... | collective-permute-start | bytes 1179656 | tf_op jit(solution)/shard_map/ppermute | solution.py:30
  163.1 14.5 %collective-permute-start.21 = (bf16[1,256,1024]{2,1,0:T(8,128)(2,1)}, bf16[1,256,1024]{2,1,0:T(8,128)(2,1)}, u32[]{:S(2)}, u32[]{:S(2)}) collective-permute-start(bf16[1,256,1024]{2,1,0:T(8,128)(2,1)} %note_product.4.refs_9_), channel_id=1, source_target_pairs={{0,1},{1,0},{2,3},{3,2},{4,5},{5,4},{6,7},{7,6},{8,9},{9,8},{10,11... | collective-permute-start | bytes 1572872 | tf_op jit(solution)/shard_map/ppermute | solution.py:47
Sparse Core Ops, SparseCore 0:
  42.9 57.6 all-gather.2

commit v4 on v3

--- a/solution.py
+++ b/solution.py
@@ -11,7 +11,7 @@
 HD = D // HEADS
 SCALE = HD**-0.5
 LOG2E = 1.4426950408889634
-CHUNKS = ((0, 2), (2, 3), (5, 3))
+CHUNKS = ((0, 4), (4, 4))
 VMEM = 64 * 2**20 - 2**16
 
 F32 = jnp.float32
@@ -91,7 +91,7 @@
 
     def body(s_ref, notes_ref, wk_ref, wv_ref, wq_ref, *refs):
         outs = refs[: len(CHUNKS)]
-        give_ref, wk_scr, wv_scr, *made_scr, sems, out_sems, give_sem = refs[len(CHUNKS) :]
+        give_ref, wk_scr, wv_scr, wq_scr, *made_scr, sems, out_sems, give_sems = refs[len(CHUNKS) :]
         copies = []
         for p in range(pieces):
             part = slice(p * wide, (p + 1) * wide)
@@ -100,8 +100,8 @@
                 copy.start()
                 copies.append(copy)
         offset = pl.multiple_of((1 - s_ref[0]) * (2 * quarter) + s_ref[1] * quarter, quarter)
-        give = pltpu.make_async_copy(wq_ref.at[pl.ds(offset, quarter), :], give_ref, give_sem)
-        give.start()
+        take = pltpu.make_async_copy(wq_ref.at[pl.ds(offset, quarter), :], wq_scr, give_sems.at[0])
+        take.start()
         left = notes_ref[...]
         sent = []
         for p in range(pieces):
@@ -119,6 +119,9 @@
                             out = pltpu.make_async_copy(made_scr[c], outs[c], out_sems.at[c])
                             out.start()
                             sent.append(out)
+        take.wait()
+        give = pltpu.make_async_copy(wq_scr, give_ref, give_sems.at[1])
+        give.start()
         for copy in sent + [give]:
             copy.wait()
 
@@ -137,10 +140,11 @@
         scratch=[
             pltpu.VMEM((D, cols), BF16),
             pltpu.VMEM((D, cols), BF16),
+            pltpu.VMEM((quarter, cols), BF16),
             *[pltpu.VMEM((2, rows, hc * HD), BF16) for _, hc in CHUNKS],
             pltpu.SemaphoreType.DMA((pieces, 2)),
             pltpu.SemaphoreType.DMA((len(CHUNKS),)),
-            pltpu.SemaphoreType.DMA,
+            pltpu.SemaphoreType.DMA((2,)),
         ],
     )
 
@@ -213,67 +217,81 @@
     )
 
 
-def frame_sum_own(scalars, grads, grads_other, w_query, w_other, chunks_other, after):
+def frame_sum(scalars, grads, grads_other, w_query, w_other, after):
     rows = grads[0].shape[0]
     half = D // 2
     cols = w_query.shape[1]
+    quarter = half // 2
     step = 256
-    nother = len(grads_other)
-    other_width = sum(hc for _, hc in chunks_other) * HD
+    steps = rows // step
+    terms = len(grads) * 2
+    widths = [g.shape[1] for g in grads] * 2
 
     def body(s_ref, *refs):
-        own = refs[: len(grads)]
-        other = refs[len(grads) : len(grads) + nother]
-        w_ref, wo_ref, out_ref = refs[len(grads) + nother :]
-        left = jnp.concatenate([r[...] for r in own], axis=1)
-        total = dot(left, w_ref[...], NT)
-        right = jnp.concatenate([r[...] for r in other], axis=1)
-        out_ref[...] = total + dot(right, wo_ref[0, :, :other_width], NT)
-
-    whole = lambda g: pl.BlockSpec(g.shape, lambda n, s: (0, 0))
+        grad_refs, refs = refs[:terms], refs[terms:]
+        wq_ref, wo_ref, out_ref, w_scr, o_scr, *refs = refs
+        grad_scrs, refs = refs[:terms], refs[terms:]
+        w_sems, grad_sems, out_sems = refs
+        weight_copies = []
+        for p in range(2):
+            at = pl.ds(pl.multiple_of(s_ref[0] * half + p * quarter, quarter), quarter)
+            to = slice(p * quarter, (p + 1) * quarter)
+            weight_copies.append(
+                pltpu.make_async_copy(wq_ref.at[at], w_scr.at[0, to], w_sems.at[0, p])
+            )
+            weight_copies.append(
+                pltpu.make_async_copy(wo_ref.at[2 * (1 - s_ref[0]) + p], w_scr.at[1, to], w_sems.at[1, p])
+            )
+        for copy in weight_copies:
+            copy.start()
+        grad_copies = []
+        for m in range(steps):
+            at = slice(m * step, (m + 1) * step)
+            for t in range(terms):
+                copy = pltpu.make_async_copy(grad_refs[t].at[at], grad_scrs[t].at[at], grad_sems.at[m, t])
+                copy.start()
+                grad_copies.append(copy)
+        for copy in weight_copies:
+            copy.wait()
+        sent = []
+        for m in range(steps):
+            at = slice(m * step, (m + 1) * step)
+            total = None
+            for group in range(2):
+                first = group * len(grads)
+                for t in range(first, first + len(grads)):
+                    grad_copies[m * terms + t].wait()
+                left = jnp.concatenate(
+                    [grad_scrs[t][at, :] for t in range(first, first + len(grads))], axis=1
+                )
+                term = dot(left, w_scr[group], NT)
+                total = term if total is None else total + term
+            o_scr[at, :] = total.astype(BF16)
+            copy = pltpu.make_async_copy(o_scr.at[at], out_ref.at[at], out_sems.at[m])
+            copy.start()
+            sent.append(copy)
+        for copy in sent:
+            copy.wait()
+
+    far = pl.BlockSpec(memory_space=pl.ANY)
     return call(
         body,
-        (half // step,),
-        [whole(g) for g in grads]
-        + [whole(g) for g in grads_other]
-        + [
-            pl.BlockSpec((step, cols), lambda n, s: (4 * s[0] + n, 0)),
-            pl.BlockSpec((1, step, cols), lambda n, s: (2 * (1 - s[0]) + n // 2, n % 2, 0)),
-        ],
-        pl.BlockSpec((rows, step), lambda n, s: (0, n)),
-        jax.ShapeDtypeStruct((rows, half), F32),
+        (),
+        [far] * (terms + 2),
+        far,
+        jax.ShapeDtypeStruct((rows, half), BF16),
         (scalars, *grads, *grads_other, w_query, w_other),
-        "frame_sum_own",
+        "frame_sum",
         after,
         scalars=1,
-    )
-
-
-def frame_sum_last(scalars, total, grad, w_other, h0, hc, after):
-    rows, half = total.shape
-    step = 256
-
-    def body(s_ref, t_ref, g_ref, *refs):
-        weight = jnp.concatenate([r[0] for r in refs[:hc]], axis=1)
-        refs[hc][...] = (t_ref[...] + dot(g_ref[...], weight, NT)).astype(BF16)
-
-    def weight_in(k):
-        return pl.BlockSpec((1, step, HD), lambda n, s: (2 * (1 - s[0]) + n // 2, n % 2, h0 + k))
-
-    return call(
-        body,
-        (half // step,),
-        [
-            pl.BlockSpec((rows, step), lambda n, s: (0, n)),
-            pl.BlockSpec(grad.shape, lambda n, s: (0, 0)),
-        ]
-        + [weight_in(k) for k in range(hc)],
-        pl.BlockSpec((rows, step), lambda n, s: (0, n)),
-        jax.ShapeDtypeStruct((rows, half), BF16),
-        (scalars, total, grad) + (w_other,) * hc,
-        "frame_sum_last",
-        after,
-        scalars=1,
+        scratch=[
+            pltpu.VMEM((2, half, cols), BF16),
+            pltpu.VMEM((rows, half), BF16),
+            *[pltpu.VMEM((rows, width), BF16) for width in widths],
+            pltpu.SemaphoreType.DMA((2, 2)),
+            pltpu.SemaphoreType.DMA((steps, terms)),
+            pltpu.SemaphoreType.DMA((steps,)),
+        ],
     )
 
 
@@ -414,55 +432,42 @@
     queries, grad_ctx = project(frames[0], w_query, grad_mixed[0], w_out, (given,))
     moved[0], queries = lax.optimization_barrier((moved[0], queries))
 
-    grad_q = []
-    grad_q_other = []
-    note_cols = []
-    summed_all = []
-
-    def send_back(own, near, far, also=None):
-        near = near_swap(near)
-        far = far_swap(far)
-        if also:
-            near, also[-1] = lax.optimization_barrier((near, also[-1]))
-        summed_all.append((own + near.astype(F32) + far.astype(F32)).astype(BF16))
-        note_cols.append(section_shift(summed_all[-1], -1))
-
-    for step, (h0, hc) in enumerate(CHUNKS):
-        kv = moved[step]
-        after = grad_q[-1:]
-        kv_near, kv_far = near_swap(kv), far_swap(kv)
-        if step == 0:
-            kv_far, moved[1] = lax.optimization_barrier((kv_far, moved[1]))
-        if step == 1:
-            near, far, kv_near, kv_far = lax.optimization_barrier((near, far, kv_near, kv_far))
-            send_back(own, near, far)
-        if step == 2:
-            after = after + [grad_q_other[0], summed_all[0]]
-        dq, own, near, far = attention(
-            scalars, band, queries, grad_ctx, kv, kv_near, kv_far, h0, hc, after
+    def attend(step, near, far, after):
+        return attention(
+            scalars, band, queries, grad_ctx, moved[step], near, far, *CHUNKS[step], after
         )
-        if step == 0:
-            moved[2], dq = lax.optimization_barrier((moved[2], dq))
-        grad_q.append(dq)
-        grad_q_other.append(head_swap(dq))
-        if step == 1:
-            send_back(own, near, far, grad_q_other)
-    near, far, note_cols[0] = lax.optimization_barrier((near, far, note_cols[0]))
-    send_back(own, near, far)
-
-    total = frame_sum_own(
-        scalars, grad_q, grad_q_other[:-1], w_query, w_other, CHUNKS[:-1], ()
-    )
-    before = note_product(scalars, note_cols[:-1], CHUNKS[:-1], w_key, w_value, (total, grad_q_other[-1]))
-    last = (scalars, note_cols[-1:], CHUNKS[-1:], w_key, w_value)
-    give_notes = note_product(*last, (), before, (0,))
+
+    def note_sum_of(own, near, far):
+        return (own + near.astype(F32) + far.astype(F32)).astype(BF16)
+
+    near0, far0 = near_swap(moved[0]), far_swap(moved[0])
+    far0, moved[1] = lax.optimization_barrier((far0, moved[1]))
+    near1, far1 = near_swap(moved[1]), far_swap(moved[1])
+    dq0, own0, rim_near0, rim_far0 = attend(0, near0, far0, ())
+    dq0_other = head_swap(dq0)
+    rim_near0, rim_far0, near1, far1 = lax.optimization_barrier((rim_near0, rim_far0, near1, far1))
+    in_near0, in_far0 = near_swap(rim_near0), far_swap(rim_far0)
+    dq1, own1, rim_near1, rim_far1 = attend(1, near1, far1, (dq0,))
+    dq1_other = head_swap(dq1)
+    in_near0, in_far0, rim_near1, rim_far1 = lax.optimization_barrier(
+        (in_near0, in_far0, rim_near1, rim_far1)
+    )
+    in_near1, in_far1 = near_swap(rim_near1), far_swap(rim_far1)
+    notes0 = section_shift(note_sum_of(own0, in_near0, in_far0), -1)
+    in_near1, dq0_other = lax.optimization_barrier((in_near1, dq0_other))
+    notes1 = section_shift(note_sum_of(own1, in_near1, in_far1), -1)
+
+    before = note_product(scalars, [notes0], CHUNKS[:1], w_key, w_value, ())
+    last = (scalars, [notes1], CHUNKS[1:], w_key, w_value)
+    give_notes = note_product(*last, (dq1_other,), before, (0,))
     notes_other = head_swap(give_notes)
     keep_notes = note_product(*last, (give_notes,), before, (1,))
-    frame_sum = frame_sum_last(
-        scalars, total, grad_q_other[-1], w_other, *CHUNKS[-1], (keep_notes,)
-    )
-    note_sum = keep_notes[0].astype(F32) + notes_other[0].astype(F32)
-    return (frame_sum[None], note_sum.astype(BF16)[None])
+    frame_out = frame_sum(
+        scalars, [dq0, dq1], [dq0_other, dq1_other], w_query, w_other, (keep_notes,)
+    )
+    notes_other, frame_out = lax.optimization_barrier((notes_other, frame_out))
+    note_out = keep_notes[0].astype(F32) + notes_other[0].astype(F32)
+    return (frame_out[None], note_out.astype(BF16)[None])
 
 
 def solution(mesh):

time: 187 us -> 157 us (0.84)
  Pallas kernels: 110 us -> 77.7 us
  waiting for transfers between devices: 13 us -> 28.2 us
  starting transfers between devices: 40.6 us -> 29.7 us
  other arithmetic: 9.04 us -> 6.79 us
    pallas_call x10 -> x8, Pallas kernels: 110 us -> 77.7 us  [call(): pl.pallas_call(reads, grid_spec=pltpu.PrefetchScalarGridSpec(num_scalar_p...]
    ppermute x4 -> x3, waiting for transfers between devices: 6.84 us -> 20.8 us  [head_swap(): return lax.ppermute(block, 'head', [(0, 1), (1, 0)])]
    ppermute x6 -> x4, starting transfers between devices: 23.5 us -> 16.1 us  [far_swap(): return lax.ppermute(block, 'seq', pairs + [(j, i) for i, j in pairs])]
    ppermute x6 -> x4, waiting for transfers between devices: 0.02 us -> 4.11 us  [section_shift(): lax.ppermute(block, 'section', [(i, (i + distance) % count) for i in rang...]
    ppermute x4 -> x3, starting transfers between devices: 9.76 us -> 7.02 us  [head_swap(): return lax.ppermute(block, 'head', [(0, 1), (1, 0)])]
    convert_element_type x4 -> x3, other arithmetic: 8.4 us -> 6.15 us  [the longest x2 3.96 us: note_sum_of(): return (own + near.astype(F32) + far.astype(F32)).astype(BF16)]
    ppermute x6 -> x4, waiting for transfers between devices: 4.3 us -> 3.27 us  [far_swap(): return lax.ppermute(block, 'seq', pairs + [(j, i) for i, j in pairs])]
    ppermute x6 -> x4, starting transfers between devices: 6.76 us -> 6.38 us  [section_shift(): lax.ppermute(block, 'section', [(i, (i + distance) % count) for i in rang...]
  transfers between devices with their start and end apart: 23 -> 16, of which waited for: 5 -> 4; matrix products, arithmetic and copies ran while one was open for 3% -> 3% of each run, Pallas kernels for 38% -> 43%
where the time goes in v4:
time: 157 us
  Pallas kernels  77.7 us (49%)
  starting transfers between devices  29.7 us (19%)
  waiting for transfers between devices  28.2 us (18%)
  between operations  14.2 us (9%)
  other arithmetic  6.79 us (4%)
    pallas_call x8, Pallas kernels, call(): pl.pallas_call(reads, grid_spec=pltpu.PrefetchScalarGridSpec(num_scalar_p...  77.7 us
    ppermute x3, waiting for transfers between devices, head_swap(): return lax.ppermute(block, 'head', [(0, 1), (1, 0)])  20.8 us
    ppermute x4, starting transfers between devices, far_swap(): return lax.ppermute(block, 'seq', pairs + [(j, i) for i, j in pairs])  16.1 us
    ppermute x3, starting transfers between devices, head_swap(): return lax.ppermute(block, 'head', [(0, 1), (1, 0)])  7.02 us
    ppermute x4, starting transfers between devices, section_shift(): lax.ppermute(block, 'section', [(i, (i + distance) % count) for i in rang...  6.38 us
    ppermute x4, waiting for transfers between devices, section_shift(): lax.ppermute(block, 'section', [(i, (i + distance) % count) for i in rang...  4.11 us
    convert_element_type x2, other arithmetic, note_sum_of(): return (own + near.astype(F32) + far.astype(F32)).astype(BF16)  3.96 us
    ppermute x4, waiting for transfers between devices, far_swap(): return lax.ppermute(block, 'seq', pairs + [(j, i) for i, j in pairs])  3.27 us
  transfers between devices with their start and end apart: 16, of which 4 were waited for; matrix products, arithmetic and copies ran while one was open for 3% of the time, Pallas kernels for 43%

profile of v4, /device:TPU:1, one launch (start us, length us, event | category | flops | bytes accessed | tf_op | source)
XLA Modules:
  0.0 156.5 jit_solution(9909226422043776429)
XLA Ops:
  7.2 0.0 all-gather.3.cloned.1.call-start
  7.2 0.6 pad_add_fusion.refs_0_
  7.9 9.9 %key_values.1 = (bf16[2,256,512]{2,1,0:T(8,128)(2,1)}, bf16[2,256,512]{2,1,0:T(8,128)(2,1)}, bf16[512,1024]{1,0:T(8,128)(2,1)}) custom-call(s32[3]{0:T(128)} %pad_add_fusion.refs_0_, bf16[256,2048]{1,0:T(8,128)(2,1)} %bitcast.13, bf16[2048,1024]{1,0:T(8,128)(2,1)} %refs_5_.6, bf16[2048,1024]{1,0:T(8,128)(2,1)} %refs_9_.5, bf16[2048,1024]{1,0:T(8,128)(2,1)} %refs_5_.7), custom_call_target="tpu_custom_call" | custom-call | tf_op jit(solution)/shard_map/key_values/pallas_call | solution.py:69
  17.8 0.0 all-gather.3.cloned.1.call-update
  17.8 2.1 %collective-permute-start = (bf16[2,256,512]{2,1,0:T(8,128)(2,1)}, bf16[2,256,512]{2,1,0:T(8,128)(2,1)}, u32[]{:S(2)}, u32[]{:S(2)}) collective-permute-start(bf16[2,256,512]{2,1,0:T(8,128)(2,1)} %get-tuple-element.31), channel_id=1, source_target_pairs={{0,32},{32,64},{64,96},{96,0},{1,33},{33,65},{65,97},{97,1},{2,34}... | collective-permute-start | bytes 1572872 | tf_op jit(solution)/shard_map/ppermute | solution.py:30
  19.9 1.2 collective-permute-start.2
  21.1 14.3 %queries_and_grad_ctx.1 = (bf16[1024,1024]{1,0:T(8,128)(2,1)}, bf16[1024,1024]{1,0:T(8,128)(2,1)}) custom-call(bf16[1024,2048]{1,0:T(8,128)(2,1)} %bitcast.9, bf16[2048,1024]{1,0:T(8,128)(2,1)} %refs_5_.7, bf16[1024,2048]{1,0:T(8,128)(2,1)} %bitcast.10, bf16[1024,2048]{1,0:T(8,128)(2,1)} %refs_3_.6, bf16[512,1024]{1,0:T(8,128)(2,1)} %get-tuple-element.32.refs_4_), custom_call_target="tpu_custom_call" | custom-call | tf_op jit(solution)/shard_map/queries_and_grad_ctx/pallas_call | solution.py:69
  35.4 0.0 collective-permute-done.refs_4_
  35.4 4.3 %collective-permute-start.1 = (bf16[2,256,512]{2,1,0:T(8,128)(2,1)}, bf16[2,256,512]{2,1,0:T(8,128)(2,1)}, u32[]{:S(2)}, u32[]{:S(2)}) collective-permute-start(bf16[2,256,512]{2,1,0:T(8,128)(2,1)} %collective-permute-done.refs_4_), channel_id=1, source_target_pairs={{2,4},{6,8},{10,12},{14,16},{18,20},{22,24},{26,28},{4,2},{8,6},{1... | collective-permute-start | bytes 1572872 | tf_op jit(solution)/shard_map/ppermute | solution.py:43
  39.7 0.1 collective-permute-start.3
  39.8 4.1 %collective-permute-done.2.refs_4_ = bf16[2,256,512]{2,1,0:T(8,128)(2,1)} collective-permute-done((bf16[2,256,512]{2,1,0:T(8,128)(2,1)}, bf16[2,256,512]{2,1,0:T(8,128)(2,1)}, u32[]{:S(2)}, u32[]{:S(2)}) %collective-permute-start.2) | collective-permute-done | bytes 524320 | tf_op jit(solution)/shard_map/ppermute | solution.py:30
  43.9 3.3 %collective-permute-done.1.refs_6_ = bf16[2,256,512]{2,1,0:T(8,128)(2,1)} collective-permute-done((bf16[2,256,512]{2,1,0:T(8,128)(2,1)}, bf16[2,256,512]{2,1,0:T(8,128)(2,1)}, u32[]{:S(2)}, u32[]{:S(2)}) %collective-permute-start.1) | collective-permute-done | bytes 524320 | tf_op jit(solution)/shard_map/ppermute | solution.py:43
  47.2 0.0 collective-permute-start.4
  47.2 3.8 %collective-permute-start.5 = (bf16[2,256,512]{2,1,0:T(8,128)(2,1)}, bf16[2,256,512]{2,1,0:T(8,128)(2,1)}, u32[]{:S(2)}, u32[]{:S(2)}) collective-permute-start(bf16[2,256,512]{2,1,0:T(8,128)(2,1)} %collective-permute-done.2.refs_4_), channel_id=1, source_target_pairs={{2,4},{6,8},{10,12},{14,16},{18,20},{22,24},{26,28},{4,2},{8,6},{1... | collective-permute-start | bytes 1572872 | tf_op jit(solution)/shard_map/ppermute | solution.py:43
  51.0 0.0 collective-permute-done.3.refs_5_
  51.0 14.2 %attention.2 = (bf16[1024,512]{1,0:T(8,128)(2,1)}, f32[2,256,512]{2,1,0:T(8,128)}, bf16[2,256,512]{2,1,0:T(8,128)(2,1)}, bf16[2,256,512]{2,1,0:T(8,128)(2,1)}) custom-call(s32[3]{0:T(128)} %pad_add_fusion.refs_0_, s32[2,8]{1,0:T(2,128)} %bitcast.14, bf16[1024,1024]{1,0:T(8,128)(2,1)} %get-tuple-element.34.refs_2_, ...), custom_call_target="tpu_custom_call" | custom-call | tf_op jit(solution)/shard_map/attention/pallas_call | solution.py:69
  65.2 3.6 %collective-permute-start.9 = (bf16[1024,512]{1,0:T(8,128)(2,1)}, bf16[1024,512]{1,0:T(8,128)(2,1)}, u32[]{:S(2)}, u32[]{:S(2)}) collective-permute-start(bf16[1024,512]{1,0:T(8,128)(2,1)} %get-tuple-element.44.refs_7_.refs_1_), channel_id=1, source_target_pairs={{0,1},{1,0},{2,3},{3,2},{4,5},{5,4},{6,7},{7,6},{8,9},{9,8},{10,11... | collective-permute-start | bytes 3145736 | tf_op jit(solution)/shard_map/ppermute | solution.py:47
  68.9 0.0 collective-permute-done.4.refs_5_
  68.9 0.0 collective-permute-done.5.refs_6_
  68.9 0.0 collective-permute-start.6
  68.9 3.3 %collective-permute-start.7 = (bf16[2,256,512]{2,1,0:T(8,128)(2,1)}, bf16[2,256,512]{2,1,0:T(8,128)(2,1)}, u32[]{:S(2)}, u32[]{:S(2)}) collective-permute-start(bf16[2,256,512]{2,1,0:T(8,128)(2,1)} %get-tuple-element.47), channel_id=1, source_target_pairs={{2,4},{6,8},{10,12},{14,16},{18,20},{22,24},{26,28},{4,2},{8,6},{1... | collective-permute-start | bytes 1572872 | tf_op jit(solution)/shard_map/ppermute | solution.py:43
  72.2 14.4 %attention.3 = (bf16[1024,512]{1,0:T(8,128)(2,1)}, f32[2,256,512]{2,1,0:T(8,128)}, bf16[2,256,512]{2,1,0:T(8,128)(2,1)}, bf16[2,256,512]{2,1,0:T(8,128)(2,1)}) custom-call(s32[3]{0:T(128)} %pad_add_fusion.refs_0_, s32[2,8]{1,0:T(2,128)} %bitcast.15, bf16[1024,1024]{1,0:T(8,128)(2,1)} %get-tuple-element.34.refs_2_, ...), custom_call_target="tpu_custom_call" | custom-call | flops 12079595520 | tf_op jit(solution)/shard_map/attention/pallas_call | solution.py:69
  86.7 0.0 collective-permute-done.6
  86.7 0.0 collective-permute-done.7
  86.7 0.1 collective-permute-start.8
  86.8 4.6 %collective-permute-start.10 = (bf16[2,256,512]{2,1,0:T(8,128)(2,1)}, bf16[2,256,512]{2,1,0:T(8,128)(2,1)S(1)}, u32[]{:S(2)}, u32[]{:S(2)}) collective-permute-start(bf16[2,256,512]{2,1,0:T(8,128)(2,1)} %get-tuple-element.52), channel_id=1, source_target_pairs={{2,4},{6,8},{10,12},{14,16},{18,20},{22,24},{26,28},{4,2},{8,6},{1... | collective-permute-start | bytes 1572872 | tf_op jit(solution)/shard_map/ppermute | solution.py:43
  91.4 0.2 collective-permute-start.13
  91.6 1.7 %add_convert_fusion.1 = bf16[2,256,512]{2,1,0:T(8,128)(2,1)S(1)} fusion(bf16[2,256,512]{2,1,0:T(8,128)(2,1)} %collective-permute-done.7, f32[2,256,512]{2,1,0:T(8,128)} %get-tuple-element.53, bf16[2,256,512]{2,1,0:T(8,128)(2,1)} %collective-permute-done.6), kind=kLoop, calls=%fused_computation.1 | loop fusion | flops 1310720 | bytes 2621440 | tf_op jit(solution)/shard_map/convert_element_type | solution.py:441
  93.3 1.5 collective-permute-start.12
  94.9 9.3 %collective-permute-done.9.refs_3_ = bf16[1024,512]{1,0:T(8,128)(2,1)} collective-permute-done((bf16[1024,512]{1,0:T(8,128)(2,1)}, bf16[1024,512]{1,0:T(8,128)(2,1)}, u32[]{:S(2)}, u32[]{:S(2)}) %collective-permute-start.9) | collective-permute-done | bytes 1048608 | tf_op jit(solution)/shard_map/ppermute | solution.py:47
  104.2 0.0 collective-permute-done.8
  104.2 0.0 collective-permute-done.10
  104.2 2.2 %add_convert_fusion.2 = bf16[2,256,512]{2,1,0:T(8,128)(2,1)} fusion(bf16[2,256,512]{2,1,0:T(8,128)(2,1)S(1)} %collective-permute-done.10, f32[2,256,512]{2,1,0:T(8,128)} %get-tuple-element.45, bf16[2,256,512]{2,1,0:T(8,128)(2,1)S(1)} %collective-permute-done.8), kind=kLoop, calls=%fused_computation.2 | loop fusion | flops 1310720 | bytes 2621440 | tf_op jit(solution)/shard_map/convert_element_type | solution.py:441
  106.4 1.5 collective-permute-start.11
  107.9 0.0 collective-permute-done.12.refs_1_
  107.9 5.3 %note_product.3.refs_10_ = f32[2,256,1024]{2,1,0:T(8,128)} custom-call(s32[3]{0:T(128)} %pad_add_fusion.refs_0_, bf16[2,256,512]{2,1,0:T(8,128)(2,1)} %collective-permute-done.12.refs_1_, bf16[2048,1024]{1,0:T(8,128)(2,1)} %refs_5_.6, bf16[2048,1024]{1,0:T(8,128)(2,1)} %refs_5_.6, bf16[2048,1024]{1,0:T(8,128)(2,1)} %refs_5_.6, bf16[2048,1024]{1,0:T(8,128)(2,1)} %refs_5_.6, ...), custom_call_target="tpu_custom_call" | custom-call | tf_op jit(solution)/shard_map/note_product/pallas_call | solution.py:69
  113.3 11.5 %collective-permute-done.13.refs_11_.refs_4_ = bf16[1024,512]{1,0:T(8,128)(2,1)} collective-permute-done((bf16[1024,512]{1,0:T(8,128)(2,1)}, bf16[1024,512]{1,0:T(8,128)(2,1)}, u32[]{:S(2)}, u32[]{:S(2)}) %collective-permute-start.13) | collective-permute-done | bytes 1048608 | tf_op jit(solution)/shard_map/ppermute | solution.py:47
  124.7 0.0 collective-permute-done.11.refs_1_
  124.7 4.3 %note_product.4.refs_11_ = bf16[1,256,1024]{2,1,0:T(8,128)(2,1)} custom-call(s32[3]{0:T(128)} %pad_add_fusion.refs_0_, bf16[2,256,512]{2,1,0:T(8,128)(2,1)} %collective-permute-done.11.refs_1_, bf16[2048,1024]{1,0:T(8,128)(2,1)} %refs_5_.6, bf16[2048,1024]{1,0:T(8,128)(2,1)} %refs_5_.6, bf16[2048,1024]{1,0:T(8,128)(2,1)} %refs_5_.6, ...), custom_call_target="tpu_custom_call" | custom-call | tf_op jit(solution)/shard_map/note_product/pallas_call | solution.py:69
  129.0 3.2 %collective-permute-start.14 = (bf16[1,256,1024]{2,1,0:T(8,128)(2,1)}, bf16[1,256,1024]{2,1,0:T(8,128)(2,1)}, u32[]{:S(2)}, u32[]{:S(2)}) collective-permute-start(bf16[1,256,1024]{2,1,0:T(8,128)(2,1)} %note_product.4.refs_11_), channel_id=1, source_target_pairs={{0,1},{1,0},{2,3},{3,2},{4,5},{5,4},{6,7},{7,6},{8,9},{9,8},{10,11... | collective-permute-start | bytes 1572872 | tf_op jit(solution)/shard_map/ppermute | solution.py:47
  132.2 4.3 %note_product.5.refs_7_ = bf16[1,256,1024]{2,1,0:T(8,128)(2,1)} custom-call(s32[3]{0:T(128)} %pad_add_fusion.refs_0_, bf16[2,256,512]{2,1,0:T(8,128)(2,1)} %collective-permute-done.11.refs_1_, bf16[2048,1024]{1,0:T(8,128)(2,1)} %refs_5_.6, bf16[2048,1024]{1,0:T(8,128)(2,1)} %refs_5_.6, bf16[2048,1024]{1,0:T(8,128)(2,1)} %refs_5_.6, ...), custom_call_target="tpu_custom_call" | custom-call | tf_op jit(solution)/shard_map/note_product/pallas_call | solution.py:69
  136.5 0.0 all-gather.3.cloned.1.call-done
  136.5 10.9 %frame_sum.1 = bf16[1024,1024]{1,0:T(8,128)(2,1)} custom-call(s32[3]{0:T(128)} %pad_add_fusion.refs_0_, bf16[1024,512]{1,0:T(8,128)(2,1)} %get-tuple-element.44.refs_7_.refs_1_, bf16[1024,512]{1,0:T(8,128)(2,1)} %get-tuple-element.56.refs_2_, bf16[1024,512]{1,0:T(8,128)(2,1)} %collective-permute-done.9.refs_3_, ...), custom_call_target="tpu_custom_call" | custom-call | tf_op jit(solution)/shard_map/frame_sum/pallas_call | solution.py:69
  147.5 0.0 collective-permute-done.14
  147.5 2.2 %add_convert_fusion = bf16[1,256,1024]{2,1,0:T(8,128)(2,1)} fusion(bf16[1,256,1024]{2,1,0:T(8,128)(2,1)} %collective-permute-done.14, bf16[1,256,1024]{2,1,0:T(8,128)(2,1)} %note_product.5.refs_7_), kind=kLoop, calls=%fused_computation | loop fusion | flops 1048576 | bytes 1572864 | tf_op jit(solution)/shard_map/convert_element_type | solution.py:470
Async XLA Ops:
  7.2 129.4 %all-gather.3.cloned.1.call-start = ((), (), s32[]{:S(2)}) async-start(), calls=%async_computation | async-start | bytes 5242880 | tf_op jit(solution)/shard_map/all_gather | solution.py:55
  17.8 17.6 %collective-permute-start = (bf16[2,256,512]{2,1,0:T(8,128)(2,1)}, bf16[2,256,512]{2,1,0:T(8,128)(2,1)}, u32[]{:S(2)}, u32[]{:S(2)}) collective-permute-start(bf16[2,256,512]{2,1,0:T(8,128)(2,1)} %get-tuple-element.31), channel_id=1, source_target_pairs={{0,32},{32,64},{64,96},{96,0},{1,33},{33,65},{65,97},{97,1},{2,34}... | collective-permute-start | bytes 1572872 | tf_op jit(solution)/shard_map/ppermute | solution.py:30
  19.9 24.0 %collective-permute-start.2 = (bf16[2,256,512]{2,1,0:T(8,128)(2,1)}, bf16[2,256,512]{2,1,0:T(8,128)(2,1)}, u32[]{:S(2)}, u32[]{:S(2)}) collective-permute-start(bf16[2,256,512]{2,1,0:T(8,128)(2,1)} %get-tuple-element.37), channel_id=1, source_target_pairs={{0,32},{32,64},{64,96},{96,0},{1,33},{33,65},{65,97},{97,1},{2,34}... | collective-permute-start | bytes 1572872 | tf_op jit(solution)/shard_map/ppermute | solution.py:30
  35.4 11.8 %collective-permute-start.1 = (bf16[2,256,512]{2,1,0:T(8,128)(2,1)}, bf16[2,256,512]{2,1,0:T(8,128)(2,1)}, u32[]{:S(2)}, u32[]{:S(2)}) collective-permute-start(bf16[2,256,512]{2,1,0:T(8,128)(2,1)} %collective-permute-done.refs_4_), channel_id=1, source_target_pairs={{2,4},{6,8},{10,12},{14,16},{18,20},{22,24},{26,28},{4,2},{8,6},{1... | collective-permute-start | bytes 1572872 | tf_op jit(solution)/shard_map/ppermute | solution.py:43
  39.7 11.2 %collective-permute-start.3 = (bf16[2,256,512]{2,1,0:T(8,128)(2,1)}, bf16[2,256,512]{2,1,0:T(8,128)(2,1)}, u32[]{:S(2)}, u32[]{:S(2)}) collective-permute-start(bf16[2,256,512]{2,1,0:T(8,128)(2,1)} %collective-permute-done.refs_4_), channel_id=1, source_target_pairs={{0,2},{2,0},{4,6},{6,4},{8,10},{10,8},{12,14},{14,12},{16,18},{18,... | collective-permute-start | bytes 1572872 | tf_op jit(solution)/shard_map/ppermute | solution.py:37
  47.2 21.7 %collective-permute-start.4 = (bf16[2,256,512]{2,1,0:T(8,128)(2,1)}, bf16[2,256,512]{2,1,0:T(8,128)(2,1)}, u32[]{:S(2)}, u32[]{:S(2)}) collective-permute-start(bf16[2,256,512]{2,1,0:T(8,128)(2,1)} %collective-permute-done.2.refs_4_), channel_id=1, source_target_pairs={{0,2},{2,0},{4,6},{6,4},{8,10},{10,8},{12,14},{14,12},{16,18},{18,... | collective-permute-start | bytes 1572872 | tf_op jit(solution)/shard_map/ppermute | solution.py:37
  47.2 21.7 %collective-permute-start.5 = (bf16[2,256,512]{2,1,0:T(8,128)(2,1)}, bf16[2,256,512]{2,1,0:T(8,128)(2,1)}, u32[]{:S(2)}, u32[]{:S(2)}) collective-permute-start(bf16[2,256,512]{2,1,0:T(8,128)(2,1)} %collective-permute-done.2.refs_4_), channel_id=1, source_target_pairs={{2,4},{6,8},{10,12},{14,16},{18,20},{22,24},{26,28},{4,2},{8,6},{1... | collective-permute-start | bytes 1572872 | tf_op jit(solution)/shard_map/ppermute | solution.py:43
  65.2 39.0 %collective-permute-start.9 = (bf16[1024,512]{1,0:T(8,128)(2,1)}, bf16[1024,512]{1,0:T(8,128)(2,1)}, u32[]{:S(2)}, u32[]{:S(2)}) collective-permute-start(bf16[1024,512]{1,0:T(8,128)(2,1)} %get-tuple-element.44.refs_7_.refs_1_), channel_id=1, source_target_pairs={{0,1},{1,0},{2,3},{3,2},{4,5},{5,4},{6,7},{7,6},{8,9},{9,8},{10,11... | collective-permute-start | bytes 3145736 | tf_op jit(solution)/shard_map/ppermute | solution.py:47
  68.9 17.8 %collective-permute-start.6 = (bf16[2,256,512]{2,1,0:T(8,128)(2,1)}, bf16[2,256,512]{2,1,0:T(8,128)(2,1)}, u32[]{:S(2)}, u32[]{:S(2)}) collective-permute-start(bf16[2,256,512]{2,1,0:T(8,128)(2,1)} %get-tuple-element.46), channel_id=1, source_target_pairs={{0,2},{2,0},{4,6},{6,4},{8,10},{10,8},{12,14},{14,12},{16,18},{18,... | collective-permute-start | bytes 1572872 | tf_op jit(solution)/shard_map/ppermute | solution.py:37
  68.9 17.8 %collective-permute-start.7 = (bf16[2,256,512]{2,1,0:T(8,128)(2,1)}, bf16[2,256,512]{2,1,0:T(8,128)(2,1)}, u32[]{:S(2)}, u32[]{:S(2)}) collective-permute-start(bf16[2,256,512]{2,1,0:T(8,128)(2,1)} %get-tuple-element.47), channel_id=1, source_target_pairs={{2,4},{6,8},{10,12},{14,16},{18,20},{22,24},{26,28},{4,2},{8,6},{1... | collective-permute-start | bytes 1572872 | tf_op jit(solution)/shard_map/ppermute | solution.py:43
  86.7 17.5 %collective-permute-start.8 = (bf16[2,256,512]{2,1,0:T(8,128)(2,1)}, bf16[2,256,512]{2,1,0:T(8,128)(2,1)S(1)}, u32[]{:S(2)}, u32[]{:S(2)}) collective-permute-start(bf16[2,256,512]{2,1,0:T(8,128)(2,1)} %get-tuple-element.50), channel_id=1, source_target_pairs={{0,2},{2,0},{4,6},{6,4},{8,10},{10,8},{12,14},{14,12},{16,18},{18,... | collective-permute-start | bytes 1572872 | tf_op jit(solution)/shard_map/ppermute | solution.py:37
  86.8 17.4 %collective-permute-start.10 = (bf16[2,256,512]{2,1,0:T(8,128)(2,1)}, bf16[2,256,512]{2,1,0:T(8,128)(2,1)S(1)}, u32[]{:S(2)}, u32[]{:S(2)}) collective-permute-start(bf16[2,256,512]{2,1,0:T(8,128)(2,1)} %get-tuple-element.52), channel_id=1, source_target_pairs={{2,4},{6,8},{10,12},{14,16},{18,20},{22,24},{26,28},{4,2},{8,6},{1... | collective-permute-start | bytes 1572872 | tf_op jit(solution)/shard_map/ppermute | solution.py:43
  91.4 33.3 %collective-permute-start.13 = (bf16[1024,512]{1,0:T(8,128)(2,1)}, bf16[1024,512]{1,0:T(8,128)(2,1)}, u32[]{:S(2)}, u32[]{:S(2)}) collective-permute-start(bf16[1024,512]{1,0:T(8,128)(2,1)} %get-tuple-element.56.refs_2_), channel_id=1, source_target_pairs={{0,1},{1,0},{2,3},{3,2},{4,5},{5,4},{6,7},{7,6},{8,9},{9,8},{10,11... | collective-permute-start | bytes 3145736 | tf_op jit(solution)/shard_map/ppermute | solution.py:47
  93.3 14.6 %collective-permute-start.12 = (bf16[2,256,512]{2,1,0:T(8,128)(2,1)S(1)}, bf16[2,256,512]{2,1,0:T(8,128)(2,1)}, u32[]{:S(2)}, u32[]{:S(2)}) collective-permute-start(bf16[2,256,512]{2,1,0:T(8,128)(2,1)S(1)} %add_convert_fusion.1), channel_id=1, source_target_pairs={{0,96},{32,0},{64,32},{96,64},{1,97},{33,1},{65,33},{97,65},{2,98}... | collective-permute-start | bytes 1572872 | tf_op jit(solution)/shard_map/ppermute | solution.py:30
  106.4 18.3 %collective-permute-start.11 = (bf16[2,256,512]{2,1,0:T(8,128)(2,1)}, bf16[2,256,512]{2,1,0:T(8,128)(2,1)}, u32[]{:S(2)}, u32[]{:S(2)}) collective-permute-start(bf16[2,256,512]{2,1,0:T(8,128)(2,1)} %add_convert_fusion.2), channel_id=1, source_target_pairs={{0,96},{32,0},{64,32},{96,64},{1,97},{33,1},{65,33},{97,65},{2,98}... | collective-permute-start | bytes 1572872 | tf_op jit(solution)/shard_map/ppermute | solution.py:30
  129.0 18.5 %collective-permute-start.14 = (bf16[1,256,1024]{2,1,0:T(8,128)(2,1)}, bf16[1,256,1024]{2,1,0:T(8,128)(2,1)}, u32[]{:S(2)}, u32[]{:S(2)}) collective-permute-start(bf16[1,256,1024]{2,1,0:T(8,128)(2,1)} %note_product.4.refs_11_), channel_id=1, source_target_pairs={{0,1},{1,0},{2,3},{3,2},{4,5},{5,4},{6,7},{7,6},{8,9},{9,8},{10,11... | collective-permute-start | bytes 1572872 | tf_op jit(solution)/shard_map/ppermute | solution.py:47
Sparse Core Ops, SparseCore 0:
  17.9 61.5 all-gather.2

commit v5 on v4

--- a/solution.py
+++ b/solution.py
@@ -47,12 +47,10 @@
     return lax.ppermute(block, "head", [(0, 1), (1, 0)])
 
 
-def other_columns(give):
+def across(block):
     count = lax.axis_size("seq")
-    quads = [
-        [2 * i, 2 * i + 2, 2 * (i ^ 8) + 1, 2 * (i ^ 8) + 3] for i in range(0, count, 2)
-    ]
-    return lax.all_gather(give, ("seq", "head"), axis_index_groups=quads)
+    route = [(2 * i + g, 2 * (i ^ 8) + 1 - g) for i in range(count) for g in range(2)]
+    return lax.ppermute(block, ("seq", "head"), route)
 
 
 def call(
@@ -82,70 +80,69 @@
     )(*args, *after)
 
 
-def key_values(scalars, notes, w_key, w_value, w_query):
+def key_values(scalars, notes, w_key, w_value, w_query, h0, hc, give, after):
     rows = notes.shape[0]
-    cols = w_key.shape[1]
+    cols = w_query.shape[1]
     wide = 2 * HD
-    pieces = cols // wide
+    pieces = hc * HD // wide
     quarter = D // 4
 
     def body(s_ref, notes_ref, wk_ref, wv_ref, wq_ref, *refs):
-        outs = refs[: len(CHUNKS)]
-        give_ref, wk_scr, wv_scr, wq_scr, *made_scr, sems, out_sems, give_sems = refs[len(CHUNKS) :]
+        if give:
+            out_ref, give_ref, wk_scr, wv_scr, out_scr, sems, out_sem, wq_scr, give_sems = refs
+        else:
+            out_ref, wk_scr, wv_scr, out_scr, sems, out_sem = refs
         copies = []
         for p in range(pieces):
-            part = slice(p * wide, (p + 1) * wide)
+            part = slice(h0 * HD + p * wide, h0 * HD + (p + 1) * wide)
+            to = slice(p * wide, (p + 1) * wide)
             for i, (src, dst) in enumerate(((wk_ref, wk_scr), (wv_ref, wv_scr))):
-                copy = pltpu.make_async_copy(src.at[:, part], dst.at[:, part], sems.at[p, i])
+                copy = pltpu.make_async_copy(src.at[:, part], dst.at[:, to], sems.at[p, i])
                 copy.start()
                 copies.append(copy)
-        offset = pl.multiple_of((1 - s_ref[0]) * (2 * quarter) + s_ref[1] * quarter, quarter)
-        take = pltpu.make_async_copy(wq_ref.at[pl.ds(offset, quarter), :], wq_scr, give_sems.at[0])
-        take.start()
+        if give:
+            offset = pl.multiple_of((1 - s_ref[0]) * (2 * quarter) + s_ref[1] * quarter, quarter)
+            take = pltpu.make_async_copy(
+                wq_ref.at[pl.ds(offset, quarter), :], wq_scr, give_sems.at[0]
+            )
+            take.start()
         left = notes_ref[...]
-        sent = []
         for p in range(pieces):
-            part = slice(p * wide, (p + 1) * wide)
+            to = slice(p * wide, (p + 1) * wide)
             for i, scr in enumerate((wk_scr, wv_scr)):
                 copies[2 * p + i].wait()
-                made = dot(left, scr[:, part], NN).astype(BF16)
-                for k in range(2):
-                    head = 2 * p + k
-                    for c, (h0, hc) in enumerate(CHUNKS):
-                        if h0 <= head < h0 + hc:
-                            at = (head - h0) * HD
-                            made_scr[c][i, :, at : at + HD] = made[:, k * HD : (k + 1) * HD]
-                        if i == 1 and head == h0 + hc - 1:
-                            out = pltpu.make_async_copy(made_scr[c], outs[c], out_sems.at[c])
-                            out.start()
-                            sent.append(out)
-        take.wait()
-        give = pltpu.make_async_copy(wq_scr, give_ref, give_sems.at[1])
-        give.start()
-        for copy in sent + [give]:
+                out_scr[i, :, to] = dot(left, scr[:, to], NN).astype(BF16)
+        sent = [pltpu.make_async_copy(out_scr, out_ref, out_sem)]
+        if give:
+            take.wait()
+            sent.append(pltpu.make_async_copy(wq_scr, give_ref, give_sems.at[1]))
+        for copy in sent:
+            copy.start()
+        for copy in sent:
             copy.wait()
 
     far = pl.BlockSpec(memory_space=pl.ANY)
     here = pl.BlockSpec(memory_space=pltpu.VMEM)
+    out = jax.ShapeDtypeStruct((2, rows, hc * HD), BF16)
+    given = jax.ShapeDtypeStruct((quarter, cols), BF16)
     return call(
         body,
         (),
         [here, far, far, far],
-        [far] * (len(CHUNKS) + 1),
-        [jax.ShapeDtypeStruct((2, rows, hc * HD), BF16) for _, hc in CHUNKS]
-        + [jax.ShapeDtypeStruct((quarter, cols), BF16)],
+        [far, far] if give else far,
+        [out, given] if give else out,
         (scalars, notes, w_key, w_value, w_query),
         "key_values",
+        after,
         scalars=1,
         scratch=[
-            pltpu.VMEM((D, cols), BF16),
-            pltpu.VMEM((D, cols), BF16),
-            pltpu.VMEM((quarter, cols), BF16),
-            *[pltpu.VMEM((2, rows, hc * HD), BF16) for _, hc in CHUNKS],
+            pltpu.VMEM((D, hc * HD), BF16),
+            pltpu.VMEM((D, hc * HD), BF16),
+            pltpu.VMEM((2, rows, hc * HD), BF16),
             pltpu.SemaphoreType.DMA((pieces, 2)),
-            pltpu.SemaphoreType.DMA((len(CHUNKS),)),
-            pltpu.SemaphoreType.DMA((2,)),
-        ],
+            pltpu.SemaphoreType.DMA,
+        ]
+        + ([pltpu.VMEM((quarter, cols), BF16), pltpu.SemaphoreType.DMA((2,))] if give else []),
     )
 
 
@@ -217,7 +214,7 @@
     )
 
 
-def frame_sum(scalars, grads, grads_other, w_query, w_other, after):
+def frame_sum(scalars, grads, grads_other, w_query, w_mine, w_theirs, after):
     rows = grads[0].shape[0]
     half = D // 2
     cols = w_query.shape[1]
@@ -229,7 +226,7 @@
 
     def body(s_ref, *refs):
         grad_refs, refs = refs[:terms], refs[terms:]
-        wq_ref, wo_ref, out_ref, w_scr, o_scr, *refs = refs
+        wq_ref, mine_ref, theirs_ref, out_ref, w_scr, o_scr, *refs = refs
         grad_scrs, refs = refs[:terms], refs[terms:]
         w_sems, grad_sems, out_sems = refs
         weight_copies = []
@@ -239,9 +236,9 @@
             weight_copies.append(
                 pltpu.make_async_copy(wq_ref.at[at], w_scr.at[0, to], w_sems.at[0, p])
             )
-            weight_copies.append(
-                pltpu.make_async_copy(wo_ref.at[2 * (1 - s_ref[0]) + p], w_scr.at[1, to], w_sems.at[1, p])
-            )
+            src, core = (mine_ref, s_ref[1]) if p == 0 else (theirs_ref, 1 - s_ref[1])
+            to = pl.ds(pl.multiple_of(core * quarter, quarter), quarter)
+            weight_copies.append(pltpu.make_async_copy(src, w_scr.at[1, to], w_sems.at[1, p]))
         for copy in weight_copies:
             copy.start()
         grad_copies = []
@@ -277,10 +274,10 @@
     return call(
         body,
         (),
-        [far] * (terms + 2),
+        [far] * (terms + 3),
         far,
         jax.ShapeDtypeStruct((rows, half), BF16),
-        (scalars, *grads, *grads_other, w_query, w_other),
+        (scalars, *grads, *grads_other, w_query, w_mine, w_theirs),
         "frame_sum",
         after,
         scalars=1,
@@ -426,9 +423,11 @@
     scalars = jnp.stack([group, core, shard]).astype(jnp.int32)
     band = band_blocks[0]
 
-    *made, given = key_values(scalars, notes[0], w_key, w_value, w_query)
-    moved = [section_shift(kv, 1) for kv in made]
-    w_other = other_columns(given)
+    arrays = (scalars, notes[0], w_key, w_value, w_query)
+    made0 = key_values(*arrays, *CHUNKS[0], False, ())
+    made1, given = key_values(*arrays, *CHUNKS[1], True, (made0,))
+    moved = [section_shift(made0, 1), section_shift(made1, 1)]
+    w_mine = across(given)
     queries, grad_ctx = project(frames[0], w_query, grad_mixed[0], w_out, (given,))
     moved[0], queries = lax.optimization_barrier((moved[0], queries))
 
@@ -445,6 +444,8 @@
     near1, far1 = near_swap(moved[1]), far_swap(moved[1])
     dq0, own0, rim_near0, rim_far0 = attend(0, near0, far0, ())
     dq0_other = head_swap(dq0)
+    w_mine, dq0 = lax.optimization_barrier((w_mine, dq0))
+    w_theirs = near_swap(w_mine)
     rim_near0, rim_far0, near1, far1 = lax.optimization_barrier((rim_near0, rim_far0, near1, far1))
     in_near0, in_far0 = near_swap(rim_near0), far_swap(rim_far0)
     dq1, own1, rim_near1, rim_far1 = attend(1, near1, far1, (dq0,))
@@ -463,7 +464,7 @@
     notes_other = head_swap(give_notes)
     keep_notes = note_product(*last, (give_notes,), before, (1,))
     frame_out = frame_sum(
-        scalars, [dq0, dq1], [dq0_other, dq1_other], w_query, w_other, (keep_notes,)
+        scalars, [dq0, dq1], [dq0_other, dq1_other], w_query, w_mine, w_theirs, (keep_notes,)
     )
     notes_other, frame_out = lax.optimization_barrier((notes_other, frame_out))
     note_out = keep_notes[0].astype(F32) + notes_other[0].astype(F32)

time: 157 us -> 149 us (0.949)
  between operations: 14.2 us -> 0.79 us
  Pallas kernels: 77.7 us -> 81.6 us
    ppermute x4, waiting for transfers between devices: 4.11 us -> 8.66 us  [section_shift(): lax.ppermute(block, 'section', [(i, (i + distance) % count) for i in rang...]
    ppermute x3, waiting for transfers between devices: 20.8 us -> 16.3 us  [head_swap(): return lax.ppermute(block, 'head', [(0, 1), (1, 0)])]
    pallas_call x8 -> x9, Pallas kernels: 77.7 us -> 81.6 us  [call(): pl.pallas_call(reads, grid_spec=pltpu.PrefetchScalarGridSpec(num_scalar_p...]
    ppermute x0 -> x1, starting transfers between devices: none -> 3.83 us  [across(): return lax.ppermute(block, ('seq', 'head'), route)]
    ppermute x4, starting transfers between devices: 16.1 us -> 14 us  [far_swap(): return lax.ppermute(block, 'seq', pairs + [(j, i) for i, j in pairs])]
    ppermute x4 -> x5, starting transfers between devices: 0.18 us -> 2.1 us  [near_swap(): return lax.ppermute(block, 'seq', [(i, i ^ 1) for i in range(count)])]
  transfers between devices with their start and end apart: 16 -> 17, of which waited for: 4 -> 5; matrix products, arithmetic and copies ran while one was open for 3% -> 3% of each run, Pallas kernels for 43% -> 51%
where the time goes in v5:
time: 149 us; the launch traced here: 148 us
  Pallas kernels  81.6 us (55%)
  starting transfers between devices  30.8 us (21%)
  waiting for transfers between devices  27.8 us (19%)
  other arithmetic  6.75 us (5%)
    pallas_call x9, Pallas kernels, call(): pl.pallas_call(reads, grid_spec=pltpu.PrefetchScalarGridSpec(num_scalar_p...  81.6 us
    ppermute x3, waiting for transfers between devices, head_swap(): return lax.ppermute(block, 'head', [(0, 1), (1, 0)])  16.3 us
    ppermute x4, starting transfers between devices, far_swap(): return lax.ppermute(block, 'seq', pairs + [(j, i) for i, j in pairs])  14 us
    ppermute x4, waiting for transfers between devices, section_shift(): lax.ppermute(block, 'section', [(i, (i + distance) % count) for i in rang...  8.66 us
    ppermute x3, starting transfers between devices, head_swap(): return lax.ppermute(block, 'head', [(0, 1), (1, 0)])  5.71 us
    ppermute x4, starting transfers between devices, section_shift(): lax.ppermute(block, 'section', [(i, (i + distance) % count) for i in rang...  5.09 us
    convert_element_type x2, other arithmetic, note_sum_of(): return (own + near.astype(F32) + far.astype(F32)).astype(BF16)  3.96 us
    ppermute x1, starting transfers between devices, across(): return lax.ppermute(block, ('seq', 'head'), route)  3.83 us
  transfers between devices with their start and end apart: 17, of which 5 were waited for; matrix products, arithmetic and copies ran while one was open for 3% of the time, Pallas kernels for 51%

profile of v5, /device:TPU:1, one launch (start us, length us, event | category | flops | bytes accessed | tf_op | source)
XLA Modules:
  0.0 147.7 jit_solution(14175235110062763193)
XLA Ops:
  0.6 0.6 pad_add_fusion.refs_0_
  1.2 6.7 %key_values.2.refs_5_ = bf16[2,256,512]{2,1,0:T(8,128)(2,1)} custom-call(s32[3]{0:T(128)} %pad_add_fusion.refs_0_, bf16[256,2048]{1,0:T(8,128)(2,1)} %bitcast.10, bf16[2048,1024]{1,0:T(8,128)(2,1)} %refs_5_.6, bf16[2048,1024]{1,0:T(8,128)(2,1)} %refs_9_.5, bf16[2048,1024]{1,0:T(8,128)(2,1)} %refs_5_.7), custom_call_target="tpu_custom_call" | custom-call | tf_op jit(solution)/shard_map/key_values/pallas_call | solution.py:67
  7.9 2.1 %collective-permute-start = (bf16[2,256,512]{2,1,0:T(8,128)(2,1)}, bf16[2,256,512]{2,1,0:T(8,128)(2,1)}, u32[]{:S(2)}, u32[]{:S(2)}) collective-permute-start(bf16[2,256,512]{2,1,0:T(8,128)(2,1)} %key_values.2.refs_5_), channel_id=1, source_target_pairs={{0,32},{32,64},{64,96},{96,0},{1,33},{33,65},{65,97},{97,1},{2,34}... | collective-permute-start | bytes 1572872 | tf_op jit(solution)/shard_map/ppermute | solution.py:30
  10.1 7.2 %key_values.3 = (bf16[2,256,512]{2,1,0:T(8,128)(2,1)}, bf16[512,1024]{1,0:T(8,128)(2,1)}) custom-call(s32[3]{0:T(128)} %pad_add_fusion.refs_0_, bf16[256,2048]{1,0:T(8,128)(2,1)} %bitcast.11, bf16[2048,1024]{1,0:T(8,128)(2,1)} %refs_5_.6, bf16[2048,1024]{1,0:T(8,128)(2,1)} %refs_9_.5, bf16[2048,1024]{1,0:T(8,128)(2,1)} %refs_5_.7, ...), custom_call_target="tpu_custom_call" | custom-call | tf_op jit(solution)/shard_map/key_values/pallas_call | solution.py:67
  17.2 1.3 collective-permute-start.2
  18.5 14.3 %queries_and_grad_ctx.1 = (bf16[1024,1024]{1,0:T(8,128)(2,1)}, bf16[1024,1024]{1,0:T(8,128)(2,1)}) custom-call(bf16[1024,2048]{1,0:T(8,128)(2,1)} %bitcast.8, bf16[2048,1024]{1,0:T(8,128)(2,1)} %refs_5_.7, bf16[1024,2048]{1,0:T(8,128)(2,1)} %bitcast.9, bf16[1024,2048]{1,0:T(8,128)(2,1)} %refs_3_.8, bf16[512,1024]{1,0:T(8,128)(2,1)} %get-tuple-element.32.refs_4_), custom_call_target="tpu_custom_call" | custom-call | tf_op jit(solution)/shard_map/queries_and_grad_ctx/pallas_call | solution.py:67
  32.8 0.0 collective-permute-done.refs_4_
  32.8 4.3 %collective-permute-start.1 = (bf16[2,256,512]{2,1,0:T(8,128)(2,1)}, bf16[2,256,512]{2,1,0:T(8,128)(2,1)}, u32[]{:S(2)}, u32[]{:S(2)}) collective-permute-start(bf16[2,256,512]{2,1,0:T(8,128)(2,1)} %collective-permute-done.refs_4_), channel_id=1, source_target_pairs={{2,4},{6,8},{10,12},{14,16},{18,20},{22,24},{26,28},{4,2},{8,6},{1... | collective-permute-start | bytes 1572872 | tf_op jit(solution)/shard_map/ppermute | solution.py:43
  37.1 3.8 %collective-permute-start.6 = (bf16[512,1024]{1,0:T(8,128)(2,1)}, bf16[512,1024]{1,0:T(8,128)(2,1)}, u32[]{:S(2)}, u32[]{:S(2)}) collective-permute-start(bf16[512,1024]{1,0:T(8,128)(2,1)} %get-tuple-element.32.refs_4_), channel_id=1, source_target_pairs={{0,17},{1,16},{2,19},{3,18},{4,21},{5,20},{6,23},{7,22},{8,25},{9,... | collective-permute-start | bytes 3145736 | tf_op jit(solution)/shard_map/ppermute | solution.py:53
  41.0 0.8 collective-permute-start.3
  41.8 0.0 collective-permute-done.2.refs_4_
  41.8 2.8 %collective-permute-done.1.refs_6_ = bf16[2,256,512]{2,1,0:T(8,128)(2,1)} collective-permute-done((bf16[2,256,512]{2,1,0:T(8,128)(2,1)}, bf16[2,256,512]{2,1,0:T(8,128)(2,1)}, u32[]{:S(2)}, u32[]{:S(2)}) %collective-permute-start.1) | collective-permute-done | bytes 524320 | tf_op jit(solution)/shard_map/ppermute | solution.py:43
  44.6 3.3 %collective-permute-start.5 = (bf16[2,256,512]{2,1,0:T(8,128)(2,1)}, bf16[2,256,512]{2,1,0:T(8,128)(2,1)}, u32[]{:S(2)}, u32[]{:S(2)}) collective-permute-start(bf16[2,256,512]{2,1,0:T(8,128)(2,1)} %collective-permute-done.2.refs_4_), channel_id=1, source_target_pairs={{2,4},{6,8},{10,12},{14,16},{18,20},{22,24},{26,28},{4,2},{8,6},{1... | collective-permute-start | bytes 1572872 | tf_op jit(solution)/shard_map/ppermute | solution.py:43
  48.0 0.3 collective-permute-start.4
  48.2 0.0 collective-permute-done.3.refs_5_
  48.2 14.2 %attention.2 = (bf16[1024,512]{1,0:T(8,128)(2,1)}, f32[2,256,512]{2,1,0:T(8,128)}, bf16[2,256,512]{2,1,0:T(8,128)(2,1)}, bf16[2,256,512]{2,1,0:T(8,128)(2,1)}) custom-call(s32[3]{0:T(128)} %pad_add_fusion.refs_0_, s32[2,8]{1,0:T(2,128)} %bitcast.13, bf16[1024,1024]{1,0:T(8,128)(2,1)} %get-tuple-element.34.refs_2_, ...), custom_call_target="tpu_custom_call" | custom-call | tf_op jit(solution)/shard_map/attention/pallas_call | solution.py:67
  62.5 3.7 %collective-permute-start.10 = (bf16[1024,512]{1,0:T(8,128)(2,1)}, bf16[1024,512]{1,0:T(8,128)(2,1)}, u32[]{:S(2)}, u32[]{:S(2)}) collective-permute-start(bf16[1024,512]{1,0:T(8,128)(2,1)} %get-tuple-element.45.refs_7_.refs_1_), channel_id=1, source_target_pairs={{0,1},{1,0},{2,3},{3,2},{4,5},{5,4},{6,7},{7,6},{8,9},{9,8},{10,11... | collective-permute-start | bytes 3145736 | tf_op jit(solution)/shard_map/ppermute | solution.py:47
  66.2 0.0 collective-permute-done.6.refs_6_
  66.2 0.0 collective-permute-done.5.refs_6_
  66.2 0.0 collective-permute-done.4.refs_5_
  66.2 0.8 collective-permute-start.7
  67.0 3.1 %collective-permute-start.8 = (bf16[2,256,512]{2,1,0:T(8,128)(2,1)}, bf16[2,256,512]{2,1,0:T(8,128)(2,1)}, u32[]{:S(2)}, u32[]{:S(2)}) collective-permute-start(bf16[2,256,512]{2,1,0:T(8,128)(2,1)} %get-tuple-element.48), channel_id=1, source_target_pairs={{2,4},{6,8},{10,12},{14,16},{18,20},{22,24},{26,28},{4,2},{8,6},{1... | collective-permute-start | bytes 1572872 | tf_op jit(solution)/shard_map/ppermute | solution.py:43
  70.1 14.4 %attention.3 = (bf16[1024,512]{1,0:T(8,128)(2,1)}, f32[2,256,512]{2,1,0:T(8,128)}, bf16[2,256,512]{2,1,0:T(8,128)(2,1)}, bf16[2,256,512]{2,1,0:T(8,128)(2,1)}) custom-call(s32[3]{0:T(128)} %pad_add_fusion.refs_0_, s32[2,8]{1,0:T(2,128)} %bitcast.14, bf16[1024,1024]{1,0:T(8,128)(2,1)} %get-tuple-element.34.refs_2_, ...), custom_call_target="tpu_custom_call" | custom-call | flops 12079595520 | tf_op jit(solution)/shard_map/attention/pallas_call | solution.py:67
  84.5 0.0 collective-permute-done.7
  84.5 0.0 collective-permute-done.8
  84.5 0.1 collective-permute-start.9
  84.6 3.3 %collective-permute-start.11 = (bf16[2,256,512]{2,1,0:T(8,128)(2,1)}, bf16[2,256,512]{2,1,0:T(8,128)(2,1)S(1)}, u32[]{:S(2)}, u32[]{:S(2)}) collective-permute-start(bf16[2,256,512]{2,1,0:T(8,128)(2,1)} %get-tuple-element.53), channel_id=1, source_target_pairs={{2,4},{6,8},{10,12},{14,16},{18,20},{22,24},{26,28},{4,2},{8,6},{1... | collective-permute-start | bytes 1572872 | tf_op jit(solution)/shard_map/ppermute | solution.py:43
  87.9 0.1 collective-permute-start.16
  88.0 0.1 collective-permute-start.14
  88.1 1.7 %add_convert_fusion.1 = bf16[2,256,512]{2,1,0:T(8,128)(2,1)S(1)} fusion(bf16[2,256,512]{2,1,0:T(8,128)(2,1)} %collective-permute-done.8, f32[2,256,512]{2,1,0:T(8,128)} %get-tuple-element.54, bf16[2,256,512]{2,1,0:T(8,128)(2,1)} %collective-permute-done.7), kind=kLoop, calls=%fused_computation.1 | loop fusion | flops 1310720 | bytes 2621440 | tf_op jit(solution)/shard_map/convert_element_type | solution.py:440
  89.8 11.0 %collective-permute-done.10.refs_3_ = bf16[1024,512]{1,0:T(8,128)(2,1)} collective-permute-done((bf16[1024,512]{1,0:T(8,128)(2,1)}, bf16[1024,512]{1,0:T(8,128)(2,1)}, u32[]{:S(2)}, u32[]{:S(2)}) %collective-permute-start.10) | collective-permute-done | bytes 1048608 | tf_op jit(solution)/shard_map/ppermute | solution.py:47
  100.8 1.5 collective-permute-start.13
  102.3 0.0 collective-permute-done.9
  102.3 0.0 collective-permute-done.11
  102.3 2.2 %add_convert_fusion.2 = bf16[2,256,512]{2,1,0:T(8,128)(2,1)} fusion(bf16[2,256,512]{2,1,0:T(8,128)(2,1)S(1)} %collective-permute-done.11, f32[2,256,512]{2,1,0:T(8,128)} %get-tuple-element.46, bf16[2,256,512]{2,1,0:T(8,128)(2,1)S(1)} %collective-permute-done.9), kind=kLoop, calls=%fused_computation.2 | loop fusion | flops 1310720 | bytes 2621440 | tf_op jit(solution)/shard_map/convert_element_type | solution.py:440
  104.5 0.2 collective-permute-start.12
  104.8 8.0 %collective-permute-done.13.refs_1_ = bf16[2,256,512]{2,1,0:T(8,128)(2,1)} collective-permute-done((bf16[2,256,512]{2,1,0:T(8,128)(2,1)S(1)}, bf16[2,256,512]{2,1,0:T(8,128)(2,1)}, u32[]{:S(2)}, u32[]{:S(2)}) %collective-permute-start.13) | collective-permute-done | bytes 524320 | tf_op jit(solution)/shard_map/ppermute | solution.py:30
  112.7 5.3 %note_product.3.refs_10_ = f32[2,256,1024]{2,1,0:T(8,128)} custom-call(s32[3]{0:T(128)} %pad_add_fusion.refs_0_, bf16[2,256,512]{2,1,0:T(8,128)(2,1)} %collective-permute-done.13.refs_1_, bf16[2048,1024]{1,0:T(8,128)(2,1)} %refs_5_.6, bf16[2048,1024]{1,0:T(8,128)(2,1)} %refs_5_.6, bf16[2048,1024]{1,0:T(8,128)(2,1)} %refs_5_.6, bf16[2048,1024]{1,0:T(8,128)(2,1)} %refs_5_.6, ...), custom_call_target="tpu_custom_call" | custom-call | tf_op jit(solution)/shard_map/note_product/pallas_call | solution.py:67
  118.0 5.3 %collective-permute-done.14.refs_11_.refs_4_ = bf16[1024,512]{1,0:T(8,128)(2,1)} collective-permute-done((bf16[1024,512]{1,0:T(8,128)(2,1)}, bf16[1024,512]{1,0:T(8,128)(2,1)}, u32[]{:S(2)}, u32[]{:S(2)}) %collective-permute-start.14) | collective-permute-done | bytes 1048608 | tf_op jit(solution)/shard_map/ppermute | solution.py:47
  123.3 0.7 collective-permute-done.12.refs_1_
  124.0 4.3 %note_product.4.refs_11_ = bf16[1,256,1024]{2,1,0:T(8,128)(2,1)} custom-call(s32[3]{0:T(128)} %pad_add_fusion.refs_0_, bf16[2,256,512]{2,1,0:T(8,128)(2,1)} %collective-permute-done.12.refs_1_, bf16[2048,1024]{1,0:T(8,128)(2,1)} %refs_5_.6, bf16[2048,1024]{1,0:T(8,128)(2,1)} %refs_5_.6, bf16[2048,1024]{1,0:T(8,128)(2,1)} %refs_5_.6, ...), custom_call_target="tpu_custom_call" | custom-call | tf_op jit(solution)/shard_map/note_product/pallas_call | solution.py:67
  128.3 2.0 %collective-permute-start.15 = (bf16[1,256,1024]{2,1,0:T(8,128)(2,1)}, bf16[1,256,1024]{2,1,0:T(8,128)(2,1)}, u32[]{:S(2)}, u32[]{:S(2)}) collective-permute-start(bf16[1,256,1024]{2,1,0:T(8,128)(2,1)} %note_product.4.refs_11_), channel_id=1, source_target_pairs={{0,1},{1,0},{2,3},{3,2},{4,5},{5,4},{6,7},{7,6},{8,9},{9,8},{10,11... | collective-permute-start | bytes 1572872 | tf_op jit(solution)/shard_map/ppermute | solution.py:47
  130.2 4.3 %note_product.5.refs_8_ = bf16[1,256,1024]{2,1,0:T(8,128)(2,1)} custom-call(s32[3]{0:T(128)} %pad_add_fusion.refs_0_, bf16[2,256,512]{2,1,0:T(8,128)(2,1)} %collective-permute-done.12.refs_1_, bf16[2048,1024]{1,0:T(8,128)(2,1)} %refs_5_.6, bf16[2048,1024]{1,0:T(8,128)(2,1)} %refs_5_.6, bf16[2048,1024]{1,0:T(8,128)(2,1)} %refs_5_.6, ...), custom_call_target="tpu_custom_call" | custom-call | tf_op jit(solution)/shard_map/note_product/pallas_call | solution.py:67
  134.5 0.0 collective-permute-done.16.refs_7_
  134.5 10.9 %frame_sum.1 = bf16[1024,1024]{1,0:T(8,128)(2,1)} custom-call(s32[3]{0:T(128)} %pad_add_fusion.refs_0_, bf16[1024,512]{1,0:T(8,128)(2,1)} %get-tuple-element.45.refs_7_.refs_1_, bf16[1024,512]{1,0:T(8,128)(2,1)} %get-tuple-element.57.refs_2_, bf16[1024,512]{1,0:T(8,128)(2,1)} %collective-permute-done.10.refs_3_, ...), custom_call_target="tpu_custom_call" | custom-call | tf_op jit(solution)/shard_map/frame_sum/pallas_call | solution.py:67
  145.5 0.0 collective-permute-done.15
  145.5 2.2 %add_convert_fusion = bf16[1,256,1024]{2,1,0:T(8,128)(2,1)} fusion(bf16[1,256,1024]{2,1,0:T(8,128)(2,1)} %collective-permute-done.15, bf16[1,256,1024]{2,1,0:T(8,128)(2,1)} %note_product.5.refs_8_), kind=kLoop, calls=%fused_computation | loop fusion | flops 1048576 | bytes 1572864 | tf_op jit(solution)/shard_map/convert_element_type | solution.py:471
Async XLA Ops:
  7.9 24.9 %collective-permute-start = (bf16[2,256,512]{2,1,0:T(8,128)(2,1)}, bf16[2,256,512]{2,1,0:T(8,128)(2,1)}, u32[]{:S(2)}, u32[]{:S(2)}) collective-permute-start(bf16[2,256,512]{2,1,0:T(8,128)(2,1)} %key_values.2.refs_5_), channel_id=1, source_target_pairs={{0,32},{32,64},{64,96},{96,0},{1,33},{33,65},{65,97},{97,1},{2,34}... | collective-permute-start | bytes 1572872 | tf_op jit(solution)/shard_map/ppermute | solution.py:30
  17.2 24.6 %collective-permute-start.2 = (bf16[2,256,512]{2,1,0:T(8,128)(2,1)}, bf16[2,256,512]{2,1,0:T(8,128)(2,1)}, u32[]{:S(2)}, u32[]{:S(2)}) collective-permute-start(bf16[2,256,512]{2,1,0:T(8,128)(2,1)} %get-tuple-element.37), channel_id=1, source_target_pairs={{0,32},{32,64},{64,96},{96,0},{1,33},{33,65},{65,97},{97,1},{2,34}... | collective-permute-start | bytes 1572872 | tf_op jit(solution)/shard_map/ppermute | solution.py:30
  32.8 11.8 %collective-permute-start.1 = (bf16[2,256,512]{2,1,0:T(8,128)(2,1)}, bf16[2,256,512]{2,1,0:T(8,128)(2,1)}, u32[]{:S(2)}, u32[]{:S(2)}) collective-permute-start(bf16[2,256,512]{2,1,0:T(8,128)(2,1)} %collective-permute-done.refs_4_), channel_id=1, source_target_pairs={{2,4},{6,8},{10,12},{14,16},{18,20},{22,24},{26,28},{4,2},{8,6},{1... | collective-permute-start | bytes 1572872 | tf_op jit(solution)/shard_map/ppermute | solution.py:43
  37.1 29.0 %collective-permute-start.6 = (bf16[512,1024]{1,0:T(8,128)(2,1)}, bf16[512,1024]{1,0:T(8,128)(2,1)}, u32[]{:S(2)}, u32[]{:S(2)}) collective-permute-start(bf16[512,1024]{1,0:T(8,128)(2,1)} %get-tuple-element.32.refs_4_), channel_id=1, source_target_pairs={{0,17},{1,16},{2,19},{3,18},{4,21},{5,20},{6,23},{7,22},{8,25},{9,... | collective-permute-start | bytes 3145736 | tf_op jit(solution)/shard_map/ppermute | solution.py:53
  41.0 7.2 %collective-permute-start.3 = (bf16[2,256,512]{2,1,0:T(8,128)(2,1)}, bf16[2,256,512]{2,1,0:T(8,128)(2,1)}, u32[]{:S(2)}, u32[]{:S(2)}) collective-permute-start(bf16[2,256,512]{2,1,0:T(8,128)(2,1)} %collective-permute-done.refs_4_), channel_id=1, source_target_pairs={{0,2},{2,0},{4,6},{6,4},{8,10},{10,8},{12,14},{14,12},{16,18},{18,... | collective-permute-start | bytes 1572872 | tf_op jit(solution)/shard_map/ppermute | solution.py:37
  44.6 21.5 %collective-permute-start.5 = (bf16[2,256,512]{2,1,0:T(8,128)(2,1)}, bf16[2,256,512]{2,1,0:T(8,128)(2,1)}, u32[]{:S(2)}, u32[]{:S(2)}) collective-permute-start(bf16[2,256,512]{2,1,0:T(8,128)(2,1)} %collective-permute-done.2.refs_4_), channel_id=1, source_target_pairs={{2,4},{6,8},{10,12},{14,16},{18,20},{22,24},{26,28},{4,2},{8,6},{1... | collective-permute-start | bytes 1572872 | tf_op jit(solution)/shard_map/ppermute | solution.py:43
  48.0 18.2 %collective-permute-start.4 = (bf16[2,256,512]{2,1,0:T(8,128)(2,1)}, bf16[2,256,512]{2,1,0:T(8,128)(2,1)}, u32[]{:S(2)}, u32[]{:S(2)}) collective-permute-start(bf16[2,256,512]{2,1,0:T(8,128)(2,1)} %collective-permute-done.2.refs_4_), channel_id=1, source_target_pairs={{0,2},{2,0},{4,6},{6,4},{8,10},{10,8},{12,14},{14,12},{16,18},{18,... | collective-permute-start | bytes 1572872 | tf_op jit(solution)/shard_map/ppermute | solution.py:37
  62.5 38.3 %collective-permute-start.10 = (bf16[1024,512]{1,0:T(8,128)(2,1)}, bf16[1024,512]{1,0:T(8,128)(2,1)}, u32[]{:S(2)}, u32[]{:S(2)}) collective-permute-start(bf16[1024,512]{1,0:T(8,128)(2,1)} %get-tuple-element.45.refs_7_.refs_1_), channel_id=1, source_target_pairs={{0,1},{1,0},{2,3},{3,2},{4,5},{5,4},{6,7},{7,6},{8,9},{9,8},{10,11... | collective-permute-start | bytes 3145736 | tf_op jit(solution)/shard_map/ppermute | solution.py:47
  66.2 18.3 %collective-permute-start.7 = (bf16[2,256,512]{2,1,0:T(8,128)(2,1)}, bf16[2,256,512]{2,1,0:T(8,128)(2,1)}, u32[]{:S(2)}, u32[]{:S(2)}) collective-permute-start(bf16[2,256,512]{2,1,0:T(8,128)(2,1)} %get-tuple-element.47), channel_id=1, source_target_pairs={{0,2},{2,0},{4,6},{6,4},{8,10},{10,8},{12,14},{14,12},{16,18},{18,... | collective-permute-start | bytes 1572872 | tf_op jit(solution)/shard_map/ppermute | solution.py:37
  67.0 17.5 %collective-permute-start.8 = (bf16[2,256,512]{2,1,0:T(8,128)(2,1)}, bf16[2,256,512]{2,1,0:T(8,128)(2,1)}, u32[]{:S(2)}, u32[]{:S(2)}) collective-permute-start(bf16[2,256,512]{2,1,0:T(8,128)(2,1)} %get-tuple-element.48), channel_id=1, source_target_pairs={{2,4},{6,8},{10,12},{14,16},{18,20},{22,24},{26,28},{4,2},{8,6},{1... | collective-permute-start | bytes 1572872 | tf_op jit(solution)/shard_map/ppermute | solution.py:43
  84.5 17.8 %collective-permute-start.9 = (bf16[2,256,512]{2,1,0:T(8,128)(2,1)}, bf16[2,256,512]{2,1,0:T(8,128)(2,1)S(1)}, u32[]{:S(2)}, u32[]{:S(2)}) collective-permute-start(bf16[2,256,512]{2,1,0:T(8,128)(2,1)} %get-tuple-element.51), channel_id=1, source_target_pairs={{0,2},{2,0},{4,6},{6,4},{8,10},{10,8},{12,14},{14,12},{16,18},{18,... | collective-permute-start | bytes 1572872 | tf_op jit(solution)/shard_map/ppermute | solution.py:37
  84.6 17.7 %collective-permute-start.11 = (bf16[2,256,512]{2,1,0:T(8,128)(2,1)}, bf16[2,256,512]{2,1,0:T(8,128)(2,1)S(1)}, u32[]{:S(2)}, u32[]{:S(2)}) collective-permute-start(bf16[2,256,512]{2,1,0:T(8,128)(2,1)} %get-tuple-element.53), channel_id=1, source_target_pairs={{2,4},{6,8},{10,12},{14,16},{18,20},{22,24},{26,28},{4,2},{8,6},{1... | collective-permute-start | bytes 1572872 | tf_op jit(solution)/shard_map/ppermute | solution.py:43
  87.9 46.7 %collective-permute-start.16 = (bf16[512,1024]{1,0:T(8,128)(2,1)}, bf16[512,1024]{1,0:T(8,128)(2,1)}, u32[]{:S(2)}, u32[]{:S(2)}) collective-permute-start(bf16[512,1024]{1,0:T(8,128)(2,1)} %collective-permute-done.6.refs_6_), channel_id=1, source_target_pairs={{0,2},{2,0},{4,6},{6,4},{8,10},{10,8},{12,14},{14,12},{16,18},{18,... | collective-permute-start | bytes 3145736 | tf_op jit(solution)/shard_map/ppermute | solution.py:37
  88.0 35.3 %collective-permute-start.14 = (bf16[1024,512]{1,0:T(8,128)(2,1)}, bf16[1024,512]{1,0:T(8,128)(2,1)}, u32[]{:S(2)}, u32[]{:S(2)}) collective-permute-start(bf16[1024,512]{1,0:T(8,128)(2,1)} %get-tuple-element.57.refs_2_), channel_id=1, source_target_pairs={{0,1},{1,0},{2,3},{3,2},{4,5},{5,4},{6,7},{7,6},{8,9},{9,8},{10,11... | collective-permute-start | bytes 3145736 | tf_op jit(solution)/shard_map/ppermute | solution.py:47
  100.8 11.9 %collective-permute-start.13 = (bf16[2,256,512]{2,1,0:T(8,128)(2,1)S(1)}, bf16[2,256,512]{2,1,0:T(8,128)(2,1)}, u32[]{:S(2)}, u32[]{:S(2)}) collective-permute-start(bf16[2,256,512]{2,1,0:T(8,128)(2,1)S(1)} %add_convert_fusion.1), channel_id=1, source_target_pairs={{0,96},{32,0},{64,32},{96,64},{1,97},{33,1},{65,33},{97,65},{2,98}... | collective-permute-start | bytes 1572872 | tf_op jit(solution)/shard_map/ppermute | solution.py:30
  104.5 19.5 %collective-permute-start.12 = (bf16[2,256,512]{2,1,0:T(8,128)(2,1)}, bf16[2,256,512]{2,1,0:T(8,128)(2,1)}, u32[]{:S(2)}, u32[]{:S(2)}) collective-permute-start(bf16[2,256,512]{2,1,0:T(8,128)(2,1)} %add_convert_fusion.2), channel_id=1, source_target_pairs={{0,96},{32,0},{64,32},{96,64},{1,97},{33,1},{65,33},{97,65},{2,98}... | collective-permute-start | bytes 1572872 | tf_op jit(solution)/shard_map/ppermute | solution.py:30
  128.3 17.2 %collective-permute-start.15 = (bf16[1,256,1024]{2,1,0:T(8,128)(2,1)}, bf16[1,256,1024]{2,1,0:T(8,128)(2,1)}, u32[]{:S(2)}, u32[]{:S(2)}) collective-permute-start(bf16[1,256,1024]{2,1,0:T(8,128)(2,1)} %note_product.4.refs_11_), channel_id=1, source_target_pairs={{0,1},{1,0},{2,3},{3,2},{4,5},{5,4},{6,7},{7,6},{8,9},{9,8},{10,11... | collective-permute-start | bytes 1572872 | tf_op jit(solution)/shard_map/ppermute | solution.py:47

commit v6 on v5

--- a/solution.py
+++ b/solution.py
@@ -89,9 +89,11 @@
 
     def body(s_ref, notes_ref, wk_ref, wv_ref, wq_ref, *refs):
         if give:
-            out_ref, give_ref, wk_scr, wv_scr, out_scr, sems, out_sem, wq_scr, give_sems = refs
+            out_ref, give_ref, n_scr, wk_scr, wv_scr, out_scr, sems, out_sems, wq_scr, give_sems = refs
         else:
-            out_ref, wk_scr, wv_scr, out_scr, sems, out_sem = refs
+            out_ref, n_scr, wk_scr, wv_scr, out_scr, sems, out_sems = refs
+        notes_in = pltpu.make_async_copy(notes_ref, n_scr, out_sems.at[1])
+        notes_in.start()
         copies = []
         for p in range(pieces):
             part = slice(h0 * HD + p * wide, h0 * HD + (p + 1) * wide)
@@ -106,13 +108,14 @@
                 wq_ref.at[pl.ds(offset, quarter), :], wq_scr, give_sems.at[0]
             )
             take.start()
-        left = notes_ref[...]
+        notes_in.wait()
+        left = n_scr[...]
         for p in range(pieces):
             to = slice(p * wide, (p + 1) * wide)
             for i, scr in enumerate((wk_scr, wv_scr)):
                 copies[2 * p + i].wait()
                 out_scr[i, :, to] = dot(left, scr[:, to], NN).astype(BF16)
-        sent = [pltpu.make_async_copy(out_scr, out_ref, out_sem)]
+        sent = [pltpu.make_async_copy(out_scr, out_ref, out_sems.at[0])]
         if give:
             take.wait()
             sent.append(pltpu.make_async_copy(wq_scr, give_ref, give_sems.at[1]))
@@ -122,13 +125,12 @@
             copy.wait()
 
     far = pl.BlockSpec(memory_space=pl.ANY)
-    here = pl.BlockSpec(memory_space=pltpu.VMEM)
     out = jax.ShapeDtypeStruct((2, rows, hc * HD), BF16)
     given = jax.ShapeDtypeStruct((quarter, cols), BF16)
     return call(
         body,
         (),
-        [here, far, far, far],
+        [far] * 4,
         [far, far] if give else far,
         [out, given] if give else out,
         (scalars, notes, w_key, w_value, w_query),
@@ -136,133 +138,115 @@
         after,
         scalars=1,
         scratch=[
+            pltpu.VMEM((rows, D), BF16),
             pltpu.VMEM((D, hc * HD), BF16),
             pltpu.VMEM((D, hc * HD), BF16),
             pltpu.VMEM((2, rows, hc * HD), BF16),
             pltpu.SemaphoreType.DMA((pieces, 2)),
-            pltpu.SemaphoreType.DMA,
+            pltpu.SemaphoreType.DMA((2,)),
         ]
         + ([pltpu.VMEM((quarter, cols), BF16), pltpu.SemaphoreType.DMA((2,))] if give else []),
     )
 
 
-def project(frames, w_query, grad_mixed, w_out, after):
-    rows, depth = frames.shape
-    width = w_query.shape[1]
+def project(rows_in, weight, dims, name, after):
+    rows = rows_in.shape[0]
+    width = D // 2
     step = 256
     steps = rows // step
     parts = 4
 
-    def body(a_ref, w_ref, b_ref, v_ref, q_ref, g_ref, a_scr, w_scr, b_scr, v_scr, q_scr, g_scr,
-             w_sems, row_sems, out_sems):
-        waits = []
-        for i, (rows_ref, rows_scr, weight_ref, weight_scr) in enumerate(
-            ((a_ref, a_scr, w_ref, w_scr), (b_ref, b_scr, v_ref, v_scr))
-        ):
-            size = weight_ref.shape[0] // parts
-            weight_copies = []
-            row_copies = []
-            for p in range(parts):
-                at = slice(p * size, (p + 1) * size)
-                copy = pltpu.make_async_copy(weight_ref.at[at], weight_scr.at[at], w_sems.at[i, p])
-                copy.start()
-                weight_copies.append(copy)
-            for m in range(steps):
-                at = slice(m * step, (m + 1) * step)
-                copy = pltpu.make_async_copy(rows_ref.at[at], rows_scr.at[at], row_sems.at[i, m])
-                copy.start()
-                row_copies.append(copy)
-            waits.append((weight_copies, row_copies))
-        sent = []
-        for i, (rows_scr, weight_scr, out_scr, out_ref, dims) in enumerate(
-            ((a_scr, w_scr, q_scr, q_ref, NN), (b_scr, v_scr, g_scr, g_ref, NT))
-        ):
-            for copy in waits[i][0]:
-                copy.wait()
-            for m in range(steps):
-                at = slice(m * step, (m + 1) * step)
-                waits[i][1][m].wait()
-                out_scr[at, :] = dot(rows_scr[at, :], weight_scr[...], dims).astype(BF16)
-                copy = pltpu.make_async_copy(out_scr.at[at], out_ref.at[at], out_sems.at[i, m])
-                copy.start()
-                sent.append(copy)
-        for copy in sent:
-            copy.wait()
-
-    far = pl.BlockSpec(memory_space=pl.ANY)
-    out = jax.ShapeDtypeStruct((rows, width), BF16)
-    return call(
-        body,
-        (),
-        [far] * 4,
-        [far] * 2,
-        [out, out],
-        (frames, w_query, grad_mixed, w_out),
-        "queries_and_grad_ctx",
-        after,
-        scratch=[
-            pltpu.VMEM(frames.shape, BF16),
-            pltpu.VMEM(w_query.shape, BF16),
-            pltpu.VMEM(grad_mixed.shape, BF16),
-            pltpu.VMEM(w_out.shape, BF16),
-            pltpu.VMEM((rows, width), BF16),
-            pltpu.VMEM((rows, width), BF16),
-            pltpu.SemaphoreType.DMA((2, parts)),
-            pltpu.SemaphoreType.DMA((2, steps)),
-            pltpu.SemaphoreType.DMA((2, steps)),
-        ],
-    )
-
-
-def frame_sum(scalars, grads, grads_other, w_query, w_mine, w_theirs, after):
-    rows = grads[0].shape[0]
-    half = D // 2
-    cols = w_query.shape[1]
-    quarter = half // 2
-    step = 256
-    steps = rows // step
-    terms = len(grads) * 2
-    widths = [g.shape[1] for g in grads] * 2
-
-    def body(s_ref, *refs):
-        grad_refs, refs = refs[:terms], refs[terms:]
-        wq_ref, mine_ref, theirs_ref, out_ref, w_scr, o_scr, *refs = refs
-        grad_scrs, refs = refs[:terms], refs[terms:]
-        w_sems, grad_sems, out_sems = refs
+    def body(a_ref, w_ref, out_ref, a_scr, w_scr, o_scr, w_sems, row_sems, out_sems):
+        size = w_ref.shape[0] // parts
         weight_copies = []
-        for p in range(2):
-            at = pl.ds(pl.multiple_of(s_ref[0] * half + p * quarter, quarter), quarter)
-            to = slice(p * quarter, (p + 1) * quarter)
-            weight_copies.append(
-                pltpu.make_async_copy(wq_ref.at[at], w_scr.at[0, to], w_sems.at[0, p])
-            )
-            src, core = (mine_ref, s_ref[1]) if p == 0 else (theirs_ref, 1 - s_ref[1])
-            to = pl.ds(pl.multiple_of(core * quarter, quarter), quarter)
-            weight_copies.append(pltpu.make_async_copy(src, w_scr.at[1, to], w_sems.at[1, p]))
-        for copy in weight_copies:
-            copy.start()
-        grad_copies = []
+        row_copies = []
+        for p in range(parts):
+            at = slice(p * size, (p + 1) * size)
+            weight_copies.append(pltpu.make_async_copy(w_ref.at[at], w_scr.at[at], w_sems.at[p]))
         for m in range(steps):
             at = slice(m * step, (m + 1) * step)
-            for t in range(terms):
-                copy = pltpu.make_async_copy(grad_refs[t].at[at], grad_scrs[t].at[at], grad_sems.at[m, t])
-                copy.start()
-                grad_copies.append(copy)
+            row_copies.append(pltpu.make_async_copy(a_ref.at[at], a_scr.at[at], row_sems.at[m]))
+        for copy in row_copies[:1] + weight_copies + row_copies[1:]:
+            copy.start()
         for copy in weight_copies:
             copy.wait()
         sent = []
         for m in range(steps):
             at = slice(m * step, (m + 1) * step)
-            total = None
-            for group in range(2):
-                first = group * len(grads)
-                for t in range(first, first + len(grads)):
-                    grad_copies[m * terms + t].wait()
-                left = jnp.concatenate(
-                    [grad_scrs[t][at, :] for t in range(first, first + len(grads))], axis=1
-                )
-                term = dot(left, w_scr[group], NT)
-                total = term if total is None else total + term
+            row_copies[m].wait()
+            o_scr[at, :] = dot(a_scr[at, :], w_scr[...], dims).astype(BF16)
+            copy = pltpu.make_async_copy(o_scr.at[at], out_ref.at[at], out_sems.at[m])
+            copy.start()
+            sent.append(copy)
+        for copy in sent:
+            copy.wait()
+
+    far = pl.BlockSpec(memory_space=pl.ANY)
+    return call(
+        body,
+        (),
+        [far] * 2,
+        far,
+        jax.ShapeDtypeStruct((rows, width), BF16),
+        (rows_in, weight),
+        name,
+        after,
+        scratch=[
+            pltpu.VMEM(rows_in.shape, BF16),
+            pltpu.VMEM(weight.shape, BF16),
+            pltpu.VMEM((rows, width), BF16),
+            pltpu.SemaphoreType.DMA((parts,)),
+            pltpu.SemaphoreType.DMA((steps,)),
+            pltpu.SemaphoreType.DMA((steps,)),
+        ],
+    )
+
+
+def frame_part(scalars, grads, weights, own, name, after):
+    rows = grads[0].shape[0]
+    half = D // 2
+    cols = sum(g.shape[1] for g in grads)
+    quarter = half // 2
+    step = 256
+    steps = rows // step
+    terms = list(grads) + ([] if own is None else [own])
+    count = len(terms)
+
+    def body(s_ref, *refs):
+        term_refs, refs = refs[:count], refs[count:]
+        weight_refs, refs = refs[: len(weights)], refs[len(weights) :]
+        out_ref, w_scr, o_scr, *refs = refs
+        term_scrs, (w_sems, term_sems, out_sems) = refs[:count], refs[count:]
+        weight_copies = []
+        for p in range(2):
+            if own is None:
+                at = pl.ds(pl.multiple_of(s_ref[0] * half + p * quarter, quarter), quarter)
+                src, dst = weight_refs[0].at[at], w_scr.at[p * quarter : (p + 1) * quarter]
+            else:
+                core = s_ref[1] if p == 0 else 1 - s_ref[1]
+                to = pl.ds(pl.multiple_of(core * quarter, quarter), quarter)
+                src, dst = weight_refs[p], w_scr.at[to]
+            weight_copies.append(pltpu.make_async_copy(src, dst, w_sems.at[p]))
+        for copy in weight_copies:
+            copy.start()
+        term_copies = []
+        for m in range(steps):
+            at = slice(m * step, (m + 1) * step)
+            for t in range(count):
+                copy = pltpu.make_async_copy(term_refs[t].at[at], term_scrs[t].at[at], term_sems.at[m, t])
+                copy.start()
+                term_copies.append(copy)
+        for copy in weight_copies:
+            copy.wait()
+        sent = []
+        for m in range(steps):
+            at = slice(m * step, (m + 1) * step)
+            for t in range(count):
+                term_copies[m * count + t].wait()
+            left = jnp.concatenate([scr[at, :] for scr in term_scrs[: len(grads)]], axis=1)
+            total = dot(left, w_scr[...], NT)
+            if own is not None:
+                total = total + term_scrs[-1][at, :].astype(F32)
             o_scr[at, :] = total.astype(BF16)
             copy = pltpu.make_async_copy(o_scr.at[at], out_ref.at[at], out_sems.at[m])
             copy.start()
@@ -274,19 +258,19 @@
     return call(
         body,
         (),
-        [far] * (terms + 3),
+        [far] * (count + len(weights)),
         far,
         jax.ShapeDtypeStruct((rows, half), BF16),
-        (scalars, *grads, *grads_other, w_query, w_mine, w_theirs),
-        "frame_sum",
+        (scalars, *terms, *weights),
+        name,
         after,
         scalars=1,
         scratch=[
-            pltpu.VMEM((2, half, cols), BF16),
+            pltpu.VMEM((half, cols), BF16),
             pltpu.VMEM((rows, half), BF16),
-            *[pltpu.VMEM((rows, width), BF16) for width in widths],
-            pltpu.SemaphoreType.DMA((2, 2)),
-            pltpu.SemaphoreType.DMA((steps, terms)),
+            *[pltpu.VMEM(term.shape, BF16) for term in terms],
+            pltpu.SemaphoreType.DMA((2,)),
+            pltpu.SemaphoreType.DMA((steps, count)),
             pltpu.SemaphoreType.DMA((steps,)),
         ],
     )
@@ -428,8 +412,11 @@
     made1, given = key_values(*arrays, *CHUNKS[1], True, (made0,))
     moved = [section_shift(made0, 1), section_shift(made1, 1)]
     w_mine = across(given)
-    queries, grad_ctx = project(frames[0], w_query, grad_mixed[0], w_out, (given,))
+    queries = project(frames[0], w_query, NN, "queries", (given,))
     moved[0], queries = lax.optimization_barrier((moved[0], queries))
+    near0, far0 = near_swap(moved[0]), far_swap(moved[0])
+    grad_ctx = project(grad_mixed[0], w_out, NT, "grad_ctx", (queries, moved[0]))
+    moved[1], grad_ctx = lax.optimization_barrier((moved[1], grad_ctx))
 
     def attend(step, near, far, after):
         return attention(
@@ -439,8 +426,6 @@
     def note_sum_of(own, near, far):
         return (own + near.astype(F32) + far.astype(F32)).astype(BF16)
 
-    near0, far0 = near_swap(moved[0]), far_swap(moved[0])
-    far0, moved[1] = lax.optimization_barrier((far0, moved[1]))
     near1, far1 = near_swap(moved[1]), far_swap(moved[1])
     dq0, own0, rim_near0, rim_far0 = attend(0, near0, far0, ())
     dq0_other = head_swap(dq0)
@@ -455,16 +440,18 @@
     )
     in_near1, in_far1 = near_swap(rim_near1), far_swap(rim_far1)
     notes0 = section_shift(note_sum_of(own0, in_near0, in_far0), -1)
-    in_near1, dq0_other = lax.optimization_barrier((in_near1, dq0_other))
-    notes1 = section_shift(note_sum_of(own1, in_near1, in_far1), -1)
-
-    before = note_product(scalars, [notes0], CHUNKS[:1], w_key, w_value, ())
+    owned1 = note_sum_of(own1, in_near1, in_far1)
+    owned1, dq0_other = lax.optimization_barrier((owned1, dq0_other))
+    notes1 = section_shift(owned1, -1)
+
+    own_part = frame_part(scalars, [dq0, dq1], [w_query], None, "frame_own", (owned1,))
+    before = note_product(scalars, [notes0], CHUNKS[:1], w_key, w_value, (own_part,))
     last = (scalars, [notes1], CHUNKS[1:], w_key, w_value)
-    give_notes = note_product(*last, (dq1_other,), before, (0,))
+    give_notes = note_product(*last, (), before, (0,))
     notes_other = head_swap(give_notes)
     keep_notes = note_product(*last, (give_notes,), before, (1,))
-    frame_out = frame_sum(
-        scalars, [dq0, dq1], [dq0_other, dq1_other], w_query, w_mine, w_theirs, (keep_notes,)
+    frame_out = frame_part(
+        scalars, [dq0_other, dq1_other], [w_mine, w_theirs], own_part, "frame_sum", (keep_notes,)
     )
     notes_other, frame_out = lax.optimization_barrier((notes_other, frame_out))
     note_out = keep_notes[0].astype(F32) + notes_other[0].astype(F32)

time: 149 us -> 138 us (0.926)
  the two profiles are of different devices: /device:TPU:1 before, /device:TPU:38 now
where the time goes in v6:
time: 138 us
  Pallas kernels  88.2 us (64%)
  starting transfers between devices  26 us (19%)
  waiting for transfers between devices  15.3 us (11%)
  other arithmetic  7.61 us (6%)
    pallas_call x11, Pallas kernels, call(): pl.pallas_call(reads, grid_spec=pltpu.PrefetchScalarGridSpec(num_scalar_p...  88.2 us
    ppermute x4, starting transfers between devices, far_swap(): return lax.ppermute(block, 'seq', pairs + [(j, i) for i, j in pairs])  16.3 us
    ppermute x4, waiting for transfers between devices, section_shift(): lax.ppermute(block, 'section', [(i, (i + distance) % count) for i in rang...  8.56 us
    convert_element_type x2, other arithmetic, note_sum_of(): return (own + near.astype(F32) + far.astype(F32)).astype(BF16)  4.75 us
    ppermute x3, starting transfers between devices, head_swap(): return lax.ppermute(block, 'head', [(0, 1), (1, 0)])  3.83 us
    ppermute x3, waiting for transfers between devices, head_swap(): return lax.ppermute(block, 'head', [(0, 1), (1, 0)])  3.44 us
    ppermute x4, waiting for transfers between devices, far_swap(): return lax.ppermute(block, 'seq', pairs + [(j, i) for i, j in pairs])  3.25 us
    ppermute x4, starting transfers between devices, section_shift(): lax.ppermute(block, 'section', [(i, (i + distance) % count) for i in rang...  3.16 us
  transfers between devices with their start and end apart: 17, of which 4 were waited for; matrix products, arithmetic and copies ran while one was open for 3% of the time, Pallas kernels for 59%

profile of v6, /device:TPU:38, one launch (start us, length us, event | category | flops | bytes accessed | tf_op | source)
XLA Modules:
  0.0 137.9 jit_solution(5558226882478038430)
XLA Ops:
  0.6 0.7 pad_add_fusion.refs_0_
  1.3 6.5 %key_values.2.refs_5_ = bf16[2,256,512]{2,1,0:T(8,128)(2,1)} custom-call(s32[3]{0:T(128)} %pad_add_fusion.refs_0_, bf16[256,2048]{1,0:T(8,128)(2,1)} %bitcast.10, bf16[2048,1024]{1,0:T(8,128)(2,1)} %refs_5_.5, bf16[2048,1024]{1,0:T(8,128)(2,1)} %refs_9_.5, bf16[2048,1024]{1,0:T(8,128)(2,1)} %refs_3_.8), custom_call_target="tpu_custom_call" | custom-call | tf_op jit(solution)/shard_map/key_values/pallas_call | solution.py:67
  7.9 0.5 collective-permute-start
  8.4 6.9 %key_values.3 = (bf16[2,256,512]{2,1,0:T(8,128)(2,1)}, bf16[512,1024]{1,0:T(8,128)(2,1)}) custom-call(s32[3]{0:T(128)} %pad_add_fusion.refs_0_, bf16[256,2048]{1,0:T(8,128)(2,1)} %bitcast.11, bf16[2048,1024]{1,0:T(8,128)(2,1)} %refs_5_.5, bf16[2048,1024]{1,0:T(8,128)(2,1)} %refs_9_.5, bf16[2048,1024]{1,0:T(8,128)(2,1)} %refs_3_.8, ...), custom_call_target="tpu_custom_call" | custom-call | tf_op jit(solution)/shard_map/key_values/pallas_call | solution.py:67
  15.4 1.6 %collective-permute-start.1 = (bf16[2,256,512]{2,1,0:T(8,128)(2,1)}, bf16[2,256,512]{2,1,0:T(8,128)(2,1)}, u32[]{:S(2)}, u32[]{:S(2)}) collective-permute-start(bf16[2,256,512]{2,1,0:T(8,128)(2,1)} %get-tuple-element.32), channel_id=1, source_target_pairs={{0,32},{32,64},{64,96},{96,0},{1,33},{33,65},{65,97},{97,1},{2,34}... | collective-permute-start | bytes 1572872 | tf_op jit(solution)/shard_map/ppermute | solution.py:30
  16.9 1.9 %collective-permute-start.6 = (bf16[512,1024]{1,0:T(8,128)(2,1)}, bf16[512,1024]{1,0:T(8,128)(2,1)}, u32[]{:S(2)}, u32[]{:S(2)}) collective-permute-start(bf16[512,1024]{1,0:T(8,128)(2,1)} %get-tuple-element.30.refs_2_), channel_id=1, source_target_pairs={{0,17},{1,16},{2,19},{3,18},{4,21},{5,20},{6,23},{7,22},{8,25},{9,... | collective-permute-start | bytes 3145736 | tf_op jit(solution)/shard_map/ppermute | solution.py:53
  18.8 9.0 %queries.1.refs_2_ = bf16[1024,1024]{1,0:T(8,128)(2,1)} custom-call(bf16[1024,2048]{1,0:T(8,128)(2,1)} %bitcast.9, bf16[2048,1024]{1,0:T(8,128)(2,1)} %refs_3_.8, bf16[512,1024]{1,0:T(8,128)(2,1)} %get-tuple-element.30.refs_2_), custom_call_target="tpu_custom_call" | custom-call | tf_op jit(solution)/shard_map/queries/pallas_call | solution.py:67
  27.9 0.0 collective-permute-done.refs_3_.refs_4_
  27.9 5.2 %collective-permute-start.3 = (bf16[2,256,512]{2,1,0:T(8,128)(2,1)}, bf16[2,256,512]{2,1,0:T(8,128)(2,1)}, u32[]{:S(2)}, u32[]{:S(2)}) collective-permute-start(bf16[2,256,512]{2,1,0:T(8,128)(2,1)} %collective-permute-done.refs_3_.refs_4_), channel_id=1, source_target_pairs={{2,4},{6,8},{10,12},{14,16},{18,20},{22,24},{26,28},{4,2},{8,6},{1... | collective-permute-start | bytes 1572872 | tf_op jit(solution)/shard_map/ppermute | solution.py:43
  33.1 0.1 collective-permute-start.2
  33.1 9.2 %grad_ctx.1.refs_3_ = bf16[1024,1024]{1,0:T(8,128)(2,1)} custom-call(bf16[1024,2048]{1,0:T(8,128)(2,1)} %bitcast.8, bf16[1024,2048]{1,0:T(8,128)(2,1)} %refs_1_.3, bf16[1024,1024]{1,0:T(8,128)(2,1)} %queries.1.refs_2_, bf16[2,256,512]{2,1,0:T(8,128)(2,1)} %collective-permute-done.refs_3_.refs_4_), custom_call_target="tpu_custom_call" | custom-call | tf_op jit(solution)/shard_map/grad_ctx/pallas_call | solution.py:67
  42.3 0.0 collective-permute-done.1.refs_4_
  42.3 3.4 %collective-permute-start.5 = (bf16[2,256,512]{2,1,0:T(8,128)(2,1)}, bf16[2,256,512]{2,1,0:T(8,128)(2,1)}, u32[]{:S(2)}, u32[]{:S(2)}) collective-permute-start(bf16[2,256,512]{2,1,0:T(8,128)(2,1)} %collective-permute-done.1.refs_4_), channel_id=1, source_target_pairs={{2,4},{6,8},{10,12},{14,16},{18,20},{22,24},{26,28},{4,2},{8,6},{1... | collective-permute-start | bytes 1572872 | tf_op jit(solution)/shard_map/ppermute | solution.py:43
  45.8 0.3 collective-permute-start.4
  46.0 0.0 collective-permute-done.3.refs_6_
  46.1 0.0 collective-permute-done.2.refs_5_
  46.1 14.3 %attention.2 = (bf16[1024,512]{1,0:T(8,128)(2,1)}, f32[2,256,512]{2,1,0:T(8,128)}, bf16[2,256,512]{2,1,0:T(8,128)(2,1)}, bf16[2,256,512]{2,1,0:T(8,128)(2,1)}) custom-call(s32[3]{0:T(128)} %pad_add_fusion.refs_0_, s32[2,8]{1,0:T(2,128)} %bitcast.13, bf16[1024,1024]{1,0:T(8,128)(2,1)} %queries.1.refs_2_, bf16[1024,1024]{1,0:T(8,128)(2,1)} %grad_ctx.1.refs_3_, ...), custom_call_target="tpu_custom_call" | custom-call | tf_op jit(solution)/shard_map/attention/pallas_call | solution.py:67
  60.3 0.0 collective-permute-done.5.refs_6_
  60.3 0.0 collective-permute-done.4.refs_5_
  60.4 0.2 collective-permute-start.11
  60.6 0.0 collective-permute-done.6.refs_4_
  60.6 0.4 collective-permute-start.7
  61.0 4.3 %collective-permute-start.8 = (bf16[2,256,512]{2,1,0:T(8,128)(2,1)}, bf16[2,256,512]{2,1,0:T(8,128)(2,1)}, u32[]{:S(2)}, u32[]{:S(2)}) collective-permute-start(bf16[2,256,512]{2,1,0:T(8,128)(2,1)} %get-tuple-element.44), channel_id=1, source_target_pairs={{2,4},{6,8},{10,12},{14,16},{18,20},{22,24},{26,28},{4,2},{8,6},{1... | collective-permute-start | bytes 1572872 | tf_op jit(solution)/shard_map/ppermute | solution.py:43
  65.3 14.4 %attention.3 = (bf16[1024,512]{1,0:T(8,128)(2,1)}, f32[2,256,512]{2,1,0:T(8,128)}, bf16[2,256,512]{2,1,0:T(8,128)(2,1)}, bf16[2,256,512]{2,1,0:T(8,128)(2,1)}) custom-call(s32[3]{0:T(128)} %pad_add_fusion.refs_0_, s32[2,8]{1,0:T(2,128)} %bitcast.14, bf16[1024,1024]{1,0:T(8,128)(2,1)} %queries.1.refs_2_, bf16[1024,1024]{1,0:T(8,128)(2,1)} %grad_ctx.1.refs_3_, ...), custom_call_target="tpu_custom_call" | custom-call | flops 12079595520 | tf_op jit(solution)/shard_map/attention/pallas_call | solution.py:67
  79.7 0.0 collective-permute-done.7
  79.7 0.0 collective-permute-done.8
  79.7 0.1 collective-permute-start.9
  79.8 3.4 %collective-permute-start.10 = (bf16[2,256,512]{2,1,0:T(8,128)(2,1)}, bf16[2,256,512]{2,1,0:T(8,128)(2,1)S(1)}, u32[]{:S(2)}, u32[]{:S(2)}) collective-permute-start(bf16[2,256,512]{2,1,0:T(8,128)(2,1)} %get-tuple-element.48), channel_id=1, source_target_pairs={{2,4},{6,8},{10,12},{14,16},{18,20},{22,24},{26,28},{4,2},{8,6},{1... | collective-permute-start | bytes 1572872 | tf_op jit(solution)/shard_map/ppermute | solution.py:43
  83.2 3.2 %collective-permute-start.15 = (bf16[1024,512]{1,0:T(8,128)(2,1)}, bf16[1024,512]{1,0:T(8,128)(2,1)}, u32[]{:S(2)}, u32[]{:S(2)}) collective-permute-start(bf16[1024,512]{1,0:T(8,128)(2,1)} %get-tuple-element.53.refs_2_), channel_id=1, source_target_pairs={{0,1},{1,0},{2,3},{3,2},{4,5},{5,4},{6,7},{7,6},{8,9},{9,8},{10,11... | collective-permute-start | bytes 3145736 | tf_op jit(solution)/shard_map/ppermute | solution.py:47
  86.4 0.0 collective-permute-start.16
  86.4 2.5 %add_convert_fusion.1 = bf16[2,256,512]{2,1,0:T(8,128)(2,1)} fusion(bf16[2,256,512]{2,1,0:T(8,128)(2,1)} %collective-permute-done.8, f32[2,256,512]{2,1,0:T(8,128)} %get-tuple-element.50, bf16[2,256,512]{2,1,0:T(8,128)(2,1)} %collective-permute-done.7), kind=kLoop, calls=%fused_computation.1 | loop fusion | flops 1310720 | bytes 2621440 | tf_op jit(solution)/shard_map/convert_element_type | solution.py:427
  88.9 0.0 collective-permute-done.9
  88.9 0.5 collective-permute-start.13
  89.5 3.2 %collective-permute-done.10 = bf16[2,256,512]{2,1,0:T(8,128)(2,1)S(1)} collective-permute-done((bf16[2,256,512]{2,1,0:T(8,128)(2,1)}, bf16[2,256,512]{2,1,0:T(8,128)(2,1)S(1)}, u32[]{:S(2)}, u32[]{:S(2)}) %collective-permute-start.10) | collective-permute-done | bytes 524320 | tf_op jit(solution)/shard_map/ppermute | solution.py:43
  92.7 2.2 %add_convert_fusion.2.refs_4_ = bf16[2,256,512]{2,1,0:T(8,128)(2,1)} fusion(bf16[2,256,512]{2,1,0:T(8,128)(2,1)S(1)} %collective-permute-done.10, f32[2,256,512]{2,1,0:T(8,128)} %get-tuple-element.42, bf16[2,256,512]{2,1,0:T(8,128)(2,1)S(1)} %collective-permute-done.9), kind=kLoop, calls=%fused_computation.2 | loop fusion | flops 1310720 | bytes 2621440 | tf_op jit(solution)/shard_map/convert_element_type | solution.py:427
  94.9 0.5 collective-permute-start.12
  95.5 6.7 %frame_own.1.refs_10_.refs_3_ = bf16[1024,1024]{1,0:T(8,128)(2,1)} custom-call(s32[3]{0:T(128)} %pad_add_fusion.refs_0_, bf16[1024,512]{1,0:T(8,128)(2,1)} %get-tuple-element.41.refs_7_.refs_1_, bf16[1024,512]{1,0:T(8,128)(2,1)} %get-tuple-element.53.refs_2_, bf16[2048,1024]{1,0:T(8,128)(2,1)} %refs_3_.8, bf16[2,256,512]{2,1,0:T(8,128)(2,1)} %add_convert_fusion.2.refs_4_), custom_call_target="tpu_custom_call" | custom-call | tf_op jit(solution)/shard_map/frame_own/pallas_call | solution.py:67
  102.2 3.0 %collective-permute-done.13.refs_1_ = bf16[2,256,512]{2,1,0:T(8,128)(2,1)} collective-permute-done((bf16[2,256,512]{2,1,0:T(8,128)(2,1)}, bf16[2,256,512]{2,1,0:T(8,128)(2,1)}, u32[]{:S(2)}, u32[]{:S(2)}) %collective-permute-start.13) | collective-permute-done | bytes 524320 | tf_op jit(solution)/shard_map/ppermute | solution.py:30
  105.2 5.3 %note_product.3.refs_10_ = f32[2,256,1024]{2,1,0:T(8,128)} custom-call(s32[3]{0:T(128)} %pad_add_fusion.refs_0_, bf16[2,256,512]{2,1,0:T(8,128)(2,1)} %collective-permute-done.13.refs_1_, bf16[2048,1024]{1,0:T(8,128)(2,1)} %refs_5_.5, bf16[2048,1024]{1,0:T(8,128)(2,1)} %refs_5_.5, bf16[2048,1024]{1,0:T(8,128)(2,1)} %refs_5_.5, bf16[2048,1024]{1,0:T(8,128)(2,1)} %refs_5_.5, ...), custom_call_target="tpu_custom_call" | custom-call | tf_op jit(solution)/shard_map/note_product/pallas_call | solution.py:67
  110.5 5.5 %collective-permute-done.12.refs_1_ = bf16[2,256,512]{2,1,0:T(8,128)(2,1)} collective-permute-done((bf16[2,256,512]{2,1,0:T(8,128)(2,1)}, bf16[2,256,512]{2,1,0:T(8,128)(2,1)}, u32[]{:S(2)}, u32[]{:S(2)}) %collective-permute-start.12) | collective-permute-done | bytes 524320 | tf_op jit(solution)/shard_map/ppermute | solution.py:30
  116.0 4.3 %note_product.4.refs_11_ = bf16[1,256,1024]{2,1,0:T(8,128)(2,1)} custom-call(s32[3]{0:T(128)} %pad_add_fusion.refs_0_, bf16[2,256,512]{2,1,0:T(8,128)(2,1)} %collective-permute-done.12.refs_1_, bf16[2048,1024]{1,0:T(8,128)(2,1)} %refs_5_.5, bf16[2048,1024]{1,0:T(8,128)(2,1)} %refs_5_.5, bf16[2048,1024]{1,0:T(8,128)(2,1)} %refs_5_.5, ...), custom_call_target="tpu_custom_call" | custom-call | tf_op jit(solution)/shard_map/note_product/pallas_call | solution.py:67
  120.3 0.4 collective-permute-start.14
  120.7 4.3 %note_product.5.refs_6_ = bf16[1,256,1024]{2,1,0:T(8,128)(2,1)} custom-call(s32[3]{0:T(128)} %pad_add_fusion.refs_0_, bf16[2,256,512]{2,1,0:T(8,128)(2,1)} %collective-permute-done.12.refs_1_, bf16[2048,1024]{1,0:T(8,128)(2,1)} %refs_5_.5, bf16[2048,1024]{1,0:T(8,128)(2,1)} %refs_5_.5, bf16[2048,1024]{1,0:T(8,128)(2,1)} %refs_5_.5, ...), custom_call_target="tpu_custom_call" | custom-call | tf_op jit(solution)/shard_map/note_product/pallas_call | solution.py:67
  125.0 0.0 collective-permute-done.15.refs_2_
  125.0 0.0 collective-permute-done.16.refs_5_
  125.0 7.3 %frame_sum.1 = bf16[1024,1024]{1,0:T(8,128)(2,1)} custom-call(s32[3]{0:T(128)} %pad_add_fusion.refs_0_, bf16[1024,512]{1,0:T(8,128)(2,1)} %collective-permute-done.11.refs_1_, bf16[1024,512]{1,0:T(8,128)(2,1)} %collective-permute-done.15.refs_2_, bf16[1024,1024]{1,0:T(8,128)(2,1)} %frame_own.1.refs_10_.refs_3_, ...), custom_call_target="tpu_custom_call" | custom-call | tf_op jit(solution)/shard_map/frame_sum/pallas_call | solution.py:67
  132.3 3.4 %collective-permute-done.14 = bf16[1,256,1024]{2,1,0:T(8,128)(2,1)} collective-permute-done((bf16[1,256,1024]{2,1,0:T(8,128)(2,1)}, bf16[1,256,1024]{2,1,0:T(8,128)(2,1)}, u32[]{:S(2)}, u32[]{:S(2)}) %collective-permute-start.14) | collective-permute-done | bytes 524320 | tf_op jit(solution)/shard_map/ppermute | solution.py:47
  135.7 2.2 %add_convert_fusion = bf16[1,256,1024]{2,1,0:T(8,128)(2,1)} fusion(bf16[1,256,1024]{2,1,0:T(8,128)(2,1)} %collective-permute-done.14, bf16[1,256,1024]{2,1,0:T(8,128)(2,1)} %note_product.5.refs_6_), kind=kLoop, calls=%fused_computation | loop fusion | flops 1048576 | bytes 1572864 | tf_op jit(solution)/shard_map/convert_element_type | solution.py:458
  (1 shorter events, 0.0 us)
Async XLA Ops:
  7.9 20.0 %collective-permute-start = (bf16[2,256,512]{2,1,0:T(8,128)(2,1)}, bf16[2,256,512]{2,1,0:T(8,128)(2,1)}, u32[]{:S(2)}, u32[]{:S(2)}) collective-permute-start(bf16[2,256,512]{2,1,0:T(8,128)(2,1)} %key_values.2.refs_5_), channel_id=1, source_target_pairs={{0,32},{32,64},{64,96},{96,0},{1,33},{33,65},{65,97},{97,1},{2,34}... | collective-permute-start | bytes 1572872 | tf_op jit(solution)/shard_map/ppermute | solution.py:30
  15.4 27.0 %collective-permute-start.1 = (bf16[2,256,512]{2,1,0:T(8,128)(2,1)}, bf16[2,256,512]{2,1,0:T(8,128)(2,1)}, u32[]{:S(2)}, u32[]{:S(2)}) collective-permute-start(bf16[2,256,512]{2,1,0:T(8,128)(2,1)} %get-tuple-element.32), channel_id=1, source_target_pairs={{0,32},{32,64},{64,96},{96,0},{1,33},{33,65},{65,97},{97,1},{2,34}... | collective-permute-start | bytes 1572872 | tf_op jit(solution)/shard_map/ppermute | solution.py:30
  16.9 43.6 %collective-permute-start.6 = (bf16[512,1024]{1,0:T(8,128)(2,1)}, bf16[512,1024]{1,0:T(8,128)(2,1)}, u32[]{:S(2)}, u32[]{:S(2)}) collective-permute-start(bf16[512,1024]{1,0:T(8,128)(2,1)} %get-tuple-element.30.refs_2_), channel_id=1, source_target_pairs={{0,17},{1,16},{2,19},{3,18},{4,21},{5,20},{6,23},{7,22},{8,25},{9,... | collective-permute-start | bytes 3145736 | tf_op jit(solution)/shard_map/ppermute | solution.py:53
  27.9 18.2 %collective-permute-start.3 = (bf16[2,256,512]{2,1,0:T(8,128)(2,1)}, bf16[2,256,512]{2,1,0:T(8,128)(2,1)}, u32[]{:S(2)}, u32[]{:S(2)}) collective-permute-start(bf16[2,256,512]{2,1,0:T(8,128)(2,1)} %collective-permute-done.refs_3_.refs_4_), channel_id=1, source_target_pairs={{2,4},{6,8},{10,12},{14,16},{18,20},{22,24},{26,28},{4,2},{8,6},{1... | collective-permute-start | bytes 1572872 | tf_op jit(solution)/shard_map/ppermute | solution.py:43
  33.1 13.0 %collective-permute-start.2 = (bf16[2,256,512]{2,1,0:T(8,128)(2,1)}, bf16[2,256,512]{2,1,0:T(8,128)(2,1)}, u32[]{:S(2)}, u32[]{:S(2)}) collective-permute-start(bf16[2,256,512]{2,1,0:T(8,128)(2,1)} %collective-permute-done.refs_3_.refs_4_), channel_id=1, source_target_pairs={{0,2},{2,0},{4,6},{6,4},{8,10},{10,8},{12,14},{14,12},{16,18},{18,... | collective-permute-start | bytes 1572872 | tf_op jit(solution)/shard_map/ppermute | solution.py:37
  42.3 18.0 %collective-permute-start.5 = (bf16[2,256,512]{2,1,0:T(8,128)(2,1)}, bf16[2,256,512]{2,1,0:T(8,128)(2,1)}, u32[]{:S(2)}, u32[]{:S(2)}) collective-permute-start(bf16[2,256,512]{2,1,0:T(8,128)(2,1)} %collective-permute-done.1.refs_4_), channel_id=1, source_target_pairs={{2,4},{6,8},{10,12},{14,16},{18,20},{22,24},{26,28},{4,2},{8,6},{1... | collective-permute-start | bytes 1572872 | tf_op jit(solution)/shard_map/ppermute | solution.py:43
  45.8 14.6 %collective-permute-start.4 = (bf16[2,256,512]{2,1,0:T(8,128)(2,1)}, bf16[2,256,512]{2,1,0:T(8,128)(2,1)}, u32[]{:S(2)}, u32[]{:S(2)}) collective-permute-start(bf16[2,256,512]{2,1,0:T(8,128)(2,1)} %collective-permute-done.1.refs_4_), channel_id=1, source_target_pairs={{0,2},{2,0},{4,6},{6,4},{8,10},{10,8},{12,14},{14,12},{16,18},{18,... | collective-permute-start | bytes 1572872 | tf_op jit(solution)/shard_map/ppermute | solution.py:37
  60.4 34.6 %collective-permute-start.11 = (bf16[1024,512]{1,0:T(8,128)(2,1)}, bf16[1024,512]{1,0:T(8,128)(2,1)}, u32[]{:S(2)}, u32[]{:S(2)}) collective-permute-start(bf16[1024,512]{1,0:T(8,128)(2,1)} %get-tuple-element.41.refs_7_.refs_1_), channel_id=1, source_target_pairs={{0,1},{1,0},{2,3},{3,2},{4,5},{5,4},{6,7},{7,6},{8,9},{9,8},{10,11... | collective-permute-start | bytes 3145736 | tf_op jit(solution)/shard_map/ppermute | solution.py:47
  60.6 19.1 %collective-permute-start.7 = (bf16[2,256,512]{2,1,0:T(8,128)(2,1)}, bf16[2,256,512]{2,1,0:T(8,128)(2,1)}, u32[]{:S(2)}, u32[]{:S(2)}) collective-permute-start(bf16[2,256,512]{2,1,0:T(8,128)(2,1)} %get-tuple-element.43), channel_id=1, source_target_pairs={{0,2},{2,0},{4,6},{6,4},{8,10},{10,8},{12,14},{14,12},{16,18},{18,... | collective-permute-start | bytes 1572872 | tf_op jit(solution)/shard_map/ppermute | solution.py:37
  61.0 18.7 %collective-permute-start.8 = (bf16[2,256,512]{2,1,0:T(8,128)(2,1)}, bf16[2,256,512]{2,1,0:T(8,128)(2,1)}, u32[]{:S(2)}, u32[]{:S(2)}) collective-permute-start(bf16[2,256,512]{2,1,0:T(8,128)(2,1)} %get-tuple-element.44), channel_id=1, source_target_pairs={{2,4},{6,8},{10,12},{14,16},{18,20},{22,24},{26,28},{4,2},{8,6},{1... | collective-permute-start | bytes 1572872 | tf_op jit(solution)/shard_map/ppermute | solution.py:43
  79.7 9.3 %collective-permute-start.9 = (bf16[2,256,512]{2,1,0:T(8,128)(2,1)}, bf16[2,256,512]{2,1,0:T(8,128)(2,1)S(1)}, u32[]{:S(2)}, u32[]{:S(2)}) collective-permute-start(bf16[2,256,512]{2,1,0:T(8,128)(2,1)} %get-tuple-element.47), channel_id=1, source_target_pairs={{0,2},{2,0},{4,6},{6,4},{8,10},{10,8},{12,14},{14,12},{16,18},{18,... | collective-permute-start | bytes 1572872 | tf_op jit(solution)/shard_map/ppermute | solution.py:37
  79.8 12.9 %collective-permute-start.10 = (bf16[2,256,512]{2,1,0:T(8,128)(2,1)}, bf16[2,256,512]{2,1,0:T(8,128)(2,1)S(1)}, u32[]{:S(2)}, u32[]{:S(2)}) collective-permute-start(bf16[2,256,512]{2,1,0:T(8,128)(2,1)} %get-tuple-element.48), channel_id=1, source_target_pairs={{2,4},{6,8},{10,12},{14,16},{18,20},{22,24},{26,28},{4,2},{8,6},{1... | collective-permute-start | bytes 1572872 | tf_op jit(solution)/shard_map/ppermute | solution.py:43
  83.2 41.8 %collective-permute-start.15 = (bf16[1024,512]{1,0:T(8,128)(2,1)}, bf16[1024,512]{1,0:T(8,128)(2,1)}, u32[]{:S(2)}, u32[]{:S(2)}) collective-permute-start(bf16[1024,512]{1,0:T(8,128)(2,1)} %get-tuple-element.53.refs_2_), channel_id=1, source_target_pairs={{0,1},{1,0},{2,3},{3,2},{4,5},{5,4},{6,7},{7,6},{8,9},{9,8},{10,11... | collective-permute-start | bytes 3145736 | tf_op jit(solution)/shard_map/ppermute | solution.py:47
  86.4 38.6 %collective-permute-start.16 = (bf16[512,1024]{1,0:T(8,128)(2,1)}, bf16[512,1024]{1,0:T(8,128)(2,1)}, u32[]{:S(2)}, u32[]{:S(2)}) collective-permute-start(bf16[512,1024]{1,0:T(8,128)(2,1)} %collective-permute-done.6.refs_4_), channel_id=1, source_target_pairs={{0,2},{2,0},{4,6},{6,4},{8,10},{10,8},{12,14},{14,12},{16,18},{18,... | collective-permute-start | bytes 3145736 | tf_op jit(solution)/shard_map/ppermute | solution.py:37
  88.9 16.2 %collective-permute-start.13 = (bf16[2,256,512]{2,1,0:T(8,128)(2,1)}, bf16[2,256,512]{2,1,0:T(8,128)(2,1)}, u32[]{:S(2)}, u32[]{:S(2)}) collective-permute-start(bf16[2,256,512]{2,1,0:T(8,128)(2,1)} %add_convert_fusion.1), channel_id=1, source_target_pairs={{0,96},{32,0},{64,32},{96,64},{1,97},{33,1},{65,33},{97,65},{2,98}... | collective-permute-start | bytes 1572872 | tf_op jit(solution)/shard_map/ppermute | solution.py:30
  94.9 21.1 %collective-permute-start.12 = (bf16[2,256,512]{2,1,0:T(8,128)(2,1)}, bf16[2,256,512]{2,1,0:T(8,128)(2,1)}, u32[]{:S(2)}, u32[]{:S(2)}) collective-permute-start(bf16[2,256,512]{2,1,0:T(8,128)(2,1)} %add_convert_fusion.2.refs_4_), channel_id=1, source_target_pairs={{0,96},{32,0},{64,32},{96,64},{1,97},{33,1},{65,33},{97,65},{2,98}... | collective-permute-start | bytes 1572872 | tf_op jit(solution)/shard_map/ppermute | solution.py:30
  120.3 15.4 %collective-permute-start.14 = (bf16[1,256,1024]{2,1,0:T(8,128)(2,1)}, bf16[1,256,1024]{2,1,0:T(8,128)(2,1)}, u32[]{:S(2)}, u32[]{:S(2)}) collective-permute-start(bf16[1,256,1024]{2,1,0:T(8,128)(2,1)} %note_product.4.refs_11_), channel_id=1, source_target_pairs={{0,1},{1,0},{2,3},{3,2},{4,5},{5,4},{6,7},{7,6},{8,9},{9,8},{10,11... | collective-permute-start | bytes 1572872 | tf_op jit(solution)/shard_map/ppermute | solution.py:47

commit v7 on v6

--- a/solution.py
+++ b/solution.py
@@ -80,61 +80,143 @@
     )(*args, *after)
 
 
-def key_values(scalars, notes, w_key, w_value, w_query, h0, hc, give, after):
+def start_all(copies):
+    for copy in copies:
+        copy.start()
+    return copies
+
+
+def key_value_copies(wk_ref, wv_ref, wk_scr, wv_scr, sems, h0, hc):
+    part = slice(h0 * HD, (h0 + hc) * HD)
+    return start_all(
+        [
+            pltpu.make_async_copy(wk_ref.at[:, part], wk_scr, sems.at[0]),
+            pltpu.make_async_copy(wv_ref.at[:, part], wv_scr, sems.at[1]),
+        ]
+    )
+
+
+def key_values(notes, w_key, w_value, h0, hc):
     rows = notes.shape[0]
-    cols = w_query.shape[1]
-    wide = 2 * HD
-    pieces = hc * HD // wide
-    quarter = D // 4
-
-    def body(s_ref, notes_ref, wk_ref, wv_ref, wq_ref, *refs):
-        if give:
-            out_ref, give_ref, n_scr, wk_scr, wv_scr, out_scr, sems, out_sems, wq_scr, give_sems = refs
-        else:
-            out_ref, n_scr, wk_scr, wv_scr, out_scr, sems, out_sems = refs
-        notes_in = pltpu.make_async_copy(notes_ref, n_scr, out_sems.at[1])
-        notes_in.start()
-        copies = []
-        for p in range(pieces):
-            part = slice(h0 * HD + p * wide, h0 * HD + (p + 1) * wide)
-            to = slice(p * wide, (p + 1) * wide)
-            for i, (src, dst) in enumerate(((wk_ref, wk_scr), (wv_ref, wv_scr))):
-                copy = pltpu.make_async_copy(src.at[:, part], dst.at[:, to], sems.at[p, i])
-                copy.start()
-                copies.append(copy)
-        if give:
-            offset = pl.multiple_of((1 - s_ref[0]) * (2 * quarter) + s_ref[1] * quarter, quarter)
-            take = pltpu.make_async_copy(
-                wq_ref.at[pl.ds(offset, quarter), :], wq_scr, give_sems.at[0]
-            )
-            take.start()
+
+    def body(notes_ref, wk_ref, wv_ref, out_ref, n_scr, wk_scr, wv_scr, out_scr, sems):
+        (notes_in,) = start_all([pltpu.make_async_copy(notes_ref, n_scr, sems.at[2])])
+        weights_in = key_value_copies(wk_ref, wv_ref, wk_scr, wv_scr, sems, h0, hc)
         notes_in.wait()
-        left = n_scr[...]
-        for p in range(pieces):
-            to = slice(p * wide, (p + 1) * wide)
-            for i, scr in enumerate((wk_scr, wv_scr)):
-                copies[2 * p + i].wait()
-                out_scr[i, :, to] = dot(left, scr[:, to], NN).astype(BF16)
-        sent = [pltpu.make_async_copy(out_scr, out_ref, out_sems.at[0])]
-        if give:
-            take.wait()
-            sent.append(pltpu.make_async_copy(wq_scr, give_ref, give_sems.at[1]))
-        for copy in sent:
-            copy.start()
-        for copy in sent:
+        for i, scr in enumerate((wk_scr, wv_scr)):
+            weights_in[i].wait()
+            out_scr[i] = dot(n_scr[...], scr[...], NN).astype(BF16)
+        for copy in start_all([pltpu.make_async_copy(out_scr, out_ref, sems.at[3])]):
             copy.wait()
 
     far = pl.BlockSpec(memory_space=pl.ANY)
-    out = jax.ShapeDtypeStruct((2, rows, hc * HD), BF16)
-    given = jax.ShapeDtypeStruct((quarter, cols), BF16)
     return call(
         body,
         (),
-        [far] * 4,
-        [far, far] if give else far,
-        [out, given] if give else out,
-        (scalars, notes, w_key, w_value, w_query),
+        [far] * 3,
+        far,
+        jax.ShapeDtypeStruct((2, rows, hc * HD), BF16),
+        (notes, w_key, w_value),
         "key_values",
+        scratch=[
+            pltpu.VMEM((rows, D), BF16),
+            pltpu.VMEM((D, hc * HD), BF16),
+            pltpu.VMEM((D, hc * HD), BF16),
+            pltpu.VMEM((2, rows, hc * HD), BF16),
+            pltpu.SemaphoreType.DMA((4,)),
+        ],
+    )
+
+
+class Product:
+    step = 256
+    parts = 2
+
+    def __init__(self, rows_in, weight, dims):
+        self.dims = dims
+        self.steps = rows_in.shape[0] // self.step
+        self.size = D // 2 // self.parts
+        self.out = jax.ShapeDtypeStruct((rows_in.shape[0], D // 2), BF16)
+        self.scratch = [
+            pltpu.VMEM(rows_in.shape, BF16),
+            pltpu.VMEM(weight.shape, BF16),
+            pltpu.VMEM(self.out.shape, BF16),
+            pltpu.SemaphoreType.DMA((self.parts,)),
+            pltpu.SemaphoreType.DMA((self.steps,)),
+            pltpu.SemaphoreType.DMA((self.steps,)),
+        ]
+
+    def rows(self, m):
+        return slice(m * self.step, (m + 1) * self.step)
+
+    def part(self, p):
+        cols = slice(p * self.size, (p + 1) * self.size)
+        return (slice(None), cols) if self.dims is NN else (cols, slice(None))
+
+    def start(self, a_ref, w_ref, a_scr, w_scr, o_scr, w_sems, row_sems, out_sems):
+        rows_in = [
+            pltpu.make_async_copy(a_ref.at[self.rows(m)], a_scr.at[self.rows(m)], row_sems.at[m])
+            for m in range(self.steps)
+        ]
+        weight_in = [
+            pltpu.make_async_copy(w_ref.at[self.part(p)], w_scr.at[self.part(p)], w_sems.at[p])
+            for p in range(self.parts)
+        ]
+        start_all(rows_in[:1] + weight_in + rows_in[1:])
+        return rows_in, weight_in
+
+    def finish(self, copies, out_ref, a_scr, w_scr, o_scr, w_sems, row_sems, out_sems):
+        rows_in, weight_in = copies
+        sent = []
+        for m in range(self.steps):
+            at = self.rows(m)
+            rows_in[m].wait()
+            for p in range(self.parts):
+                if m == 0:
+                    weight_in[p].wait()
+                cols = slice(p * self.size, (p + 1) * self.size)
+                term = dot(a_scr[at, :], w_scr[self.part(p)], self.dims)
+                o_scr[at, cols] = term.astype(BF16)
+            copy = pltpu.make_async_copy(o_scr.at[at], out_ref.at[at], out_sems.at[m])
+            sent += start_all([copy])
+        return sent
+
+
+def key_values_and_queries(scalars, notes, w_key, w_value, frames, w_query, h0, hc, after):
+    rows = notes.shape[0]
+    quarter = D // 4
+    product = Product(frames, w_query, NN)
+
+    def body(s_ref, notes_ref, wk_ref, wv_ref, f_ref, wq_ref, out_ref, q_ref, give_ref,
+             n_scr, wk_scr, wv_scr, out_scr, sems, *scrs):
+        (notes_in,) = start_all([pltpu.make_async_copy(notes_ref, n_scr, sems.at[2])])
+        weights_in = key_value_copies(wk_ref, wv_ref, wk_scr, wv_scr, sems, h0, hc)
+        copies = product.start(f_ref, wq_ref, *scrs)
+        notes_in.wait()
+        for i, scr in enumerate((wk_scr, wv_scr)):
+            weights_in[i].wait()
+            out_scr[i] = dot(n_scr[...], scr[...], NN).astype(BF16)
+        sent = start_all([pltpu.make_async_copy(out_scr, out_ref, sems.at[3])])
+        sent += product.finish(copies, q_ref, *scrs)
+        offset = pl.multiple_of((1 - s_ref[0]) * (2 * quarter) + s_ref[1] * quarter, quarter)
+        give = pltpu.make_async_copy(scrs[1].at[pl.ds(offset, quarter), :], give_ref, sems.at[4])
+        sent += start_all([give])
+        for copy in sent:
+            copy.wait()
+
+    far = pl.BlockSpec(memory_space=pl.ANY)
+    return call(
+        body,
+        (),
+        [far] * 5,
+        [far] * 3,
+        [
+            jax.ShapeDtypeStruct((2, rows, hc * HD), BF16),
+            product.out,
+            jax.ShapeDtypeStruct((quarter, w_query.shape[1]), BF16),
+        ],
+        (scalars, notes, w_key, w_value, frames, w_query),
+        "key_values_and_queries",
         after,
         scalars=1,
         scratch=[
@@ -142,63 +224,24 @@
             pltpu.VMEM((D, hc * HD), BF16),
             pltpu.VMEM((D, hc * HD), BF16),
             pltpu.VMEM((2, rows, hc * HD), BF16),
-            pltpu.SemaphoreType.DMA((pieces, 2)),
-            pltpu.SemaphoreType.DMA((2,)),
-        ]
-        + ([pltpu.VMEM((quarter, cols), BF16), pltpu.SemaphoreType.DMA((2,))] if give else []),
-    )
-
-
-def project(rows_in, weight, dims, name, after):
-    rows = rows_in.shape[0]
-    width = D // 2
-    step = 256
-    steps = rows // step
-    parts = 4
-
-    def body(a_ref, w_ref, out_ref, a_scr, w_scr, o_scr, w_sems, row_sems, out_sems):
-        size = w_ref.shape[0] // parts
-        weight_copies = []
-        row_copies = []
-        for p in range(parts):
-            at = slice(p * size, (p + 1) * size)
-            weight_copies.append(pltpu.make_async_copy(w_ref.at[at], w_scr.at[at], w_sems.at[p]))
-        for m in range(steps):
-            at = slice(m * step, (m + 1) * step)
-            row_copies.append(pltpu.make_async_copy(a_ref.at[at], a_scr.at[at], row_sems.at[m]))
-        for copy in row_copies[:1] + weight_copies + row_copies[1:]:
-            copy.start()
-        for copy in weight_copies:
-            copy.wait()
-        sent = []
-        for m in range(steps):
-            at = slice(m * step, (m + 1) * step)
-            row_copies[m].wait()
-            o_scr[at, :] = dot(a_scr[at, :], w_scr[...], dims).astype(BF16)
-            copy = pltpu.make_async_copy(o_scr.at[at], out_ref.at[at], out_sems.at[m])
-            copy.start()
-            sent.append(copy)
-        for copy in sent:
+            pltpu.SemaphoreType.DMA((5,)),
+            *product.scratch,
+        ],
+    )
+
+
+def context_gradient(grad_mixed, w_out, after):
+    product = Product(grad_mixed, w_out, NT)
+
+    def body(a_ref, w_ref, out_ref, *scrs):
+        copies = product.start(a_ref, w_ref, *scrs)
+        for copy in product.finish(copies, out_ref, *scrs):
             copy.wait()
 
     far = pl.BlockSpec(memory_space=pl.ANY)
     return call(
-        body,
-        (),
-        [far] * 2,
-        far,
-        jax.ShapeDtypeStruct((rows, width), BF16),
-        (rows_in, weight),
-        name,
-        after,
-        scratch=[
-            pltpu.VMEM(rows_in.shape, BF16),
-            pltpu.VMEM(weight.shape, BF16),
-            pltpu.VMEM((rows, width), BF16),
-            pltpu.SemaphoreType.DMA((parts,)),
-            pltpu.SemaphoreType.DMA((steps,)),
-            pltpu.SemaphoreType.DMA((steps,)),
-        ],
+        body, (), [far] * 2, far, product.out, (grad_mixed, w_out), "grad_ctx", after,
+        scratch=product.scratch,
     )
 
 
@@ -407,15 +450,15 @@
     scalars = jnp.stack([group, core, shard]).astype(jnp.int32)
     band = band_blocks[0]
 
-    arrays = (scalars, notes[0], w_key, w_value, w_query)
-    made0 = key_values(*arrays, *CHUNKS[0], False, ())
-    made1, given = key_values(*arrays, *CHUNKS[1], True, (made0,))
+    made0 = key_values(notes[0], w_key, w_value, *CHUNKS[0])
+    made1, queries, given = key_values_and_queries(
+        scalars, notes[0], w_key, w_value, frames[0], w_query, *CHUNKS[1], (made0,)
+    )
     moved = [section_shift(made0, 1), section_shift(made1, 1)]
     w_mine = across(given)
-    queries = project(frames[0], w_query, NN, "queries", (given,))
     moved[0], queries = lax.optimization_barrier((moved[0], queries))
     near0, far0 = near_swap(moved[0]), far_swap(moved[0])
-    grad_ctx = project(grad_mixed[0], w_out, NT, "grad_ctx", (queries, moved[0]))
+    grad_ctx = context_gradient(grad_mixed[0], w_out, (queries, moved[0]))
     moved[1], grad_ctx = lax.optimization_barrier((moved[1], grad_ctx))
 
     def attend(step, near, far, after):

time: 138 us -> 131 us (0.949)
  Pallas kernels: 88.2 us -> 80.9 us
    pallas_call x11 -> x10, Pallas kernels: 88.2 us -> 80.9 us  [call(): pl.pallas_call(reads, grid_spec=pltpu.PrefetchScalarGridSpec(num_scalar_p...]
  transfers between devices with their start and end apart: 17 -> 17, of which waited for: 4 -> 4; matrix products, arithmetic and copies ran while one was open for 3% -> 4% of each run, Pallas kernels for 59% -> 59%
where the time goes in v7:
time: 131 us
  Pallas kernels  80.9 us (62%)
  starting transfers between devices  26.8 us (20%)
  waiting for transfers between devices  14.4 us (11%)
  other arithmetic  7.61 us (6%)
    pallas_call x10, Pallas kernels, call(): pl.pallas_call(reads, grid_spec=pltpu.PrefetchScalarGridSpec(num_scalar_p...  80.9 us
    ppermute x4, starting transfers between devices, far_swap(): return lax.ppermute(block, 'seq', pairs + [(j, i) for i, j in pairs])  16.3 us
    ppermute x4, waiting for transfers between devices, section_shift(): lax.ppermute(block, 'section', [(i, (i + distance) % count) for i in rang...  7.78 us
    convert_element_type x2, other arithmetic, note_sum_of(): return (own + near.astype(F32) + far.astype(F32)).astype(BF16)  4.75 us
    ppermute x4, starting transfers between devices, section_shift(): lax.ppermute(block, 'section', [(i, (i + distance) % count) for i in rang...  3.95 us
    ppermute x3, starting transfers between devices, head_swap(): return lax.ppermute(block, 'head', [(0, 1), (1, 0)])  3.83 us
    ppermute x3, waiting for transfers between devices, head_swap(): return lax.ppermute(block, 'head', [(0, 1), (1, 0)])  3.42 us
    ppermute x4, waiting for transfers between devices, far_swap(): return lax.ppermute(block, 'seq', pairs + [(j, i) for i, j in pairs])  3.24 us
  transfers between devices with their start and end apart: 17, of which 4 were waited for; matrix products, arithmetic and copies ran while one was open for 4% of the time, Pallas kernels for 59%

profile of v7, /device:TPU:38, one launch (start us, length us, event | category | flops | bytes accessed | tf_op | source)
XLA Modules:
  0.0 130.6 jit_solution(7420220642760496928)
XLA Ops:
  0.6 4.2 %key_values.1.refs_6_ = bf16[2,256,512]{2,1,0:T(8,128)(2,1)} custom-call(bf16[256,2048]{1,0:T(8,128)(2,1)} %bitcast.10, bf16[2048,1024]{1,0:T(8,128)(2,1)} %refs_5_.7, bf16[2048,1024]{1,0:T(8,128)(2,1)} %refs_9_.5), custom_call_target="tpu_custom_call" | custom-call | tf_op jit(solution)/shard_map/key_values/pallas_call | solution.py:67
  4.8 0.5 collective-permute-start
  5.3 0.7 pad_add_fusion.refs_0_
  6.0 11.5 %key_values_and_queries.1 = (bf16[2,256,512]{2,1,0:T(8,128)(2,1)}, bf16[1024,1024]{1,0:T(8,128)(2,1)}, bf16[512,1024]{1,0:T(8,128)(2,1)}) custom-call(s32[3]{0:T(128)} %pad_add_fusion.refs_0_, bf16[256,2048]{1,0:T(8,128)(2,1)} %bitcast.11, bf16[2048,1024]{1,0:T(8,128)(2,1)} %refs_5_.7, bf16[2048,1024]{1,0:T(8,128)(2,1)} %refs_9_.5, ...), custom_call_target="tpu_custom_call" | custom-call | tf_op jit(solution)/shard_map/key_values_and_queries/pallas_call | solution.py:67
  17.6 1.6 %collective-permute-start.1 = (bf16[2,256,512]{2,1,0:T(8,128)(2,1)}, bf16[2,256,512]{2,1,0:T(8,128)(2,1)}, u32[]{:S(2)}, u32[]{:S(2)}) collective-permute-start(bf16[2,256,512]{2,1,0:T(8,128)(2,1)} %get-tuple-element.33), channel_id=1, source_target_pairs={{0,32},{32,64},{64,96},{96,0},{1,33},{33,65},{65,97},{97,1},{2,34}... | collective-permute-start | bytes 1572872 | tf_op jit(solution)/shard_map/ppermute | solution.py:30
  19.1 1.9 %collective-permute-start.6 = (bf16[512,1024]{1,0:T(8,128)(2,1)}, bf16[512,1024]{1,0:T(8,128)(2,1)}, u32[]{:S(2)}, u32[]{:S(2)}) collective-permute-start(bf16[512,1024]{1,0:T(8,128)(2,1)} %get-tuple-element.41), channel_id=1, source_target_pairs={{0,17},{1,16},{2,19},{3,18},{4,21},{5,20},{6,23},{7,22},{8,25},{9,... | collective-permute-start | bytes 3145736 | tf_op jit(solution)/shard_map/ppermute | solution.py:53
  21.0 0.0 collective-permute-done.refs_3_.refs_4_
  21.0 5.2 %collective-permute-start.3 = (bf16[2,256,512]{2,1,0:T(8,128)(2,1)}, bf16[2,256,512]{2,1,0:T(8,128)(2,1)}, u32[]{:S(2)}, u32[]{:S(2)}) collective-permute-start(bf16[2,256,512]{2,1,0:T(8,128)(2,1)} %collective-permute-done.refs_3_.refs_4_), channel_id=1, source_target_pairs={{2,4},{6,8},{10,12},{14,16},{18,20},{22,24},{26,28},{4,2},{8,6},{1... | collective-permute-start | bytes 1572872 | tf_op jit(solution)/shard_map/ppermute | solution.py:43
  26.2 0.1 collective-permute-start.2
  26.3 8.7 %grad_ctx.1.refs_3_ = bf16[1024,1024]{1,0:T(8,128)(2,1)} custom-call(bf16[1024,2048]{1,0:T(8,128)(2,1)} %bitcast.8, bf16[1024,2048]{1,0:T(8,128)(2,1)} %refs_1_.3, bf16[1024,1024]{1,0:T(8,128)(2,1)} %get-tuple-element.32.refs_2_, bf16[2,256,512]{2,1,0:T(8,128)(2,1)} %collective-permute-done.refs_3_.refs_4_), custom_call_target="tpu_custom_call" | custom-call | tf_op jit(solution)/shard_map/grad_ctx/pallas_call | solution.py:67
  35.0 0.0 collective-permute-done.1.refs_4_
  35.0 3.4 %collective-permute-start.5 = (bf16[2,256,512]{2,1,0:T(8,128)(2,1)}, bf16[2,256,512]{2,1,0:T(8,128)(2,1)}, u32[]{:S(2)}, u32[]{:S(2)}) collective-permute-start(bf16[2,256,512]{2,1,0:T(8,128)(2,1)} %collective-permute-done.1.refs_4_), channel_id=1, source_target_pairs={{2,4},{6,8},{10,12},{14,16},{18,20},{22,24},{26,28},{4,2},{8,6},{1... | collective-permute-start | bytes 1572872 | tf_op jit(solution)/shard_map/ppermute | solution.py:43
  38.5 0.3 collective-permute-start.4
  38.7 0.0 collective-permute-done.3.refs_6_
  38.7 0.0 collective-permute-done.2.refs_5_
  38.8 14.3 %attention.2 = (bf16[1024,512]{1,0:T(8,128)(2,1)}, f32[2,256,512]{2,1,0:T(8,128)}, bf16[2,256,512]{2,1,0:T(8,128)(2,1)}, bf16[2,256,512]{2,1,0:T(8,128)(2,1)}) custom-call(s32[3]{0:T(128)} %pad_add_fusion.refs_0_, s32[2,8]{1,0:T(2,128)} %bitcast.13, bf16[1024,1024]{1,0:T(8,128)(2,1)} %get-tuple-element.32.refs_2_, bf16[1024,1024]{1,0:T(8,128)(2,1)} %grad_ctx.1.refs_3_, ...), custom_call_target="tpu_custom_call" | custom-call | tf_op jit(solution)/shard_map/attention/pallas_call | solution.py:67
  53.0 0.0 collective-permute-done.5.refs_6_
  53.0 0.0 collective-permute-done.4.refs_5_
  53.0 0.2 collective-permute-start.11
  53.3 0.0 collective-permute-done.6.refs_4_
  53.3 0.4 collective-permute-start.7
  53.7 4.3 %collective-permute-start.8 = (bf16[2,256,512]{2,1,0:T(8,128)(2,1)}, bf16[2,256,512]{2,1,0:T(8,128)(2,1)}, u32[]{:S(2)}, u32[]{:S(2)}) collective-permute-start(bf16[2,256,512]{2,1,0:T(8,128)(2,1)} %get-tuple-element.46), channel_id=1, source_target_pairs={{2,4},{6,8},{10,12},{14,16},{18,20},{22,24},{26,28},{4,2},{8,6},{1... | collective-permute-start | bytes 1572872 | tf_op jit(solution)/shard_map/ppermute | solution.py:43
  58.0 14.4 %attention.3 = (bf16[1024,512]{1,0:T(8,128)(2,1)}, f32[2,256,512]{2,1,0:T(8,128)}, bf16[2,256,512]{2,1,0:T(8,128)(2,1)}, bf16[2,256,512]{2,1,0:T(8,128)(2,1)}) custom-call(s32[3]{0:T(128)} %pad_add_fusion.refs_0_, s32[2,8]{1,0:T(2,128)} %bitcast.14, bf16[1024,1024]{1,0:T(8,128)(2,1)} %get-tuple-element.32.refs_2_, bf16[1024,1024]{1,0:T(8,128)(2,1)} %grad_ctx.1.refs_3_, ...), custom_call_target="tpu_custom_call" | custom-call | flops 12079595520 | tf_op jit(solution)/shard_map/attention/pallas_call | solution.py:67
  72.4 0.0 collective-permute-done.7
  72.4 0.0 collective-permute-done.8
  72.4 0.1 collective-permute-start.9
  72.5 3.4 %collective-permute-start.10 = (bf16[2,256,512]{2,1,0:T(8,128)(2,1)}, bf16[2,256,512]{2,1,0:T(8,128)(2,1)S(1)}, u32[]{:S(2)}, u32[]{:S(2)}) collective-permute-start(bf16[2,256,512]{2,1,0:T(8,128)(2,1)} %get-tuple-element.50), channel_id=1, source_target_pairs={{2,4},{6,8},{10,12},{14,16},{18,20},{22,24},{26,28},{4,2},{8,6},{1... | collective-permute-start | bytes 1572872 | tf_op jit(solution)/shard_map/ppermute | solution.py:43
  75.9 3.2 %collective-permute-start.15 = (bf16[1024,512]{1,0:T(8,128)(2,1)}, bf16[1024,512]{1,0:T(8,128)(2,1)}, u32[]{:S(2)}, u32[]{:S(2)}) collective-permute-start(bf16[1024,512]{1,0:T(8,128)(2,1)} %get-tuple-element.55.refs_2_), channel_id=1, source_target_pairs={{0,1},{1,0},{2,3},{3,2},{4,5},{5,4},{6,7},{7,6},{8,9},{9,8},{10,11... | collective-permute-start | bytes 3145736 | tf_op jit(solution)/shard_map/ppermute | solution.py:47
  79.1 0.0 collective-permute-start.16
  79.1 2.5 %add_convert_fusion.1 = bf16[2,256,512]{2,1,0:T(8,128)(2,1)} fusion(bf16[2,256,512]{2,1,0:T(8,128)(2,1)} %collective-permute-done.8, f32[2,256,512]{2,1,0:T(8,128)} %get-tuple-element.52, bf16[2,256,512]{2,1,0:T(8,128)(2,1)} %collective-permute-done.7), kind=kLoop, calls=%fused_computation.1 | loop fusion | flops 1310720 | bytes 2621440 | tf_op jit(solution)/shard_map/convert_element_type | solution.py:470
  81.6 0.0 collective-permute-done.9
  81.6 0.6 collective-permute-start.13
  82.2 3.2 %collective-permute-done.10 = bf16[2,256,512]{2,1,0:T(8,128)(2,1)S(1)} collective-permute-done((bf16[2,256,512]{2,1,0:T(8,128)(2,1)}, bf16[2,256,512]{2,1,0:T(8,128)(2,1)S(1)}, u32[]{:S(2)}, u32[]{:S(2)}) %collective-permute-start.10) | collective-permute-done | bytes 524320 | tf_op jit(solution)/shard_map/ppermute | solution.py:43
  85.4 2.2 %add_convert_fusion.2.refs_4_ = bf16[2,256,512]{2,1,0:T(8,128)(2,1)} fusion(bf16[2,256,512]{2,1,0:T(8,128)(2,1)S(1)} %collective-permute-done.10, f32[2,256,512]{2,1,0:T(8,128)} %get-tuple-element.44, bf16[2,256,512]{2,1,0:T(8,128)(2,1)S(1)} %collective-permute-done.9), kind=kLoop, calls=%fused_computation.2 | loop fusion | flops 1310720 | bytes 2621440 | tf_op jit(solution)/shard_map/convert_element_type | solution.py:470
  87.6 0.0 collective-permute-done.11.refs_1_
  87.6 1.3 collective-permute-start.12
  88.9 6.7 %frame_own.1.refs_10_.refs_3_ = bf16[1024,1024]{1,0:T(8,128)(2,1)} custom-call(s32[3]{0:T(128)} %pad_add_fusion.refs_0_, bf16[1024,512]{1,0:T(8,128)(2,1)} %get-tuple-element.43.refs_7_.refs_1_, bf16[1024,512]{1,0:T(8,128)(2,1)} %get-tuple-element.55.refs_2_, bf16[2048,1024]{1,0:T(8,128)(2,1)} %refs_3_.6, bf16[2,256,512]{2,1,0:T(8,128)(2,1)} %add_convert_fusion.2.refs_4_), custom_call_target="tpu_custom_call" | custom-call | tf_op jit(solution)/shard_map/frame_own/pallas_call | solution.py:67
  95.6 2.2 %collective-permute-done.13.refs_1_ = bf16[2,256,512]{2,1,0:T(8,128)(2,1)} collective-permute-done((bf16[2,256,512]{2,1,0:T(8,128)(2,1)}, bf16[2,256,512]{2,1,0:T(8,128)(2,1)}, u32[]{:S(2)}, u32[]{:S(2)}) %collective-permute-start.13) | collective-permute-done | bytes 524320 | tf_op jit(solution)/shard_map/ppermute | solution.py:30
  97.9 5.3 %note_product.3.refs_10_ = f32[2,256,1024]{2,1,0:T(8,128)} custom-call(s32[3]{0:T(128)} %pad_add_fusion.refs_0_, bf16[2,256,512]{2,1,0:T(8,128)(2,1)} %collective-permute-done.13.refs_1_, bf16[2048,1024]{1,0:T(8,128)(2,1)} %refs_5_.7, bf16[2048,1024]{1,0:T(8,128)(2,1)} %refs_5_.7, bf16[2048,1024]{1,0:T(8,128)(2,1)} %refs_5_.7, bf16[2048,1024]{1,0:T(8,128)(2,1)} %refs_5_.7, ...), custom_call_target="tpu_custom_call" | custom-call | tf_op jit(solution)/shard_map/note_product/pallas_call | solution.py:67
  103.2 5.5 %collective-permute-done.12.refs_1_ = bf16[2,256,512]{2,1,0:T(8,128)(2,1)} collective-permute-done((bf16[2,256,512]{2,1,0:T(8,128)(2,1)}, bf16[2,256,512]{2,1,0:T(8,128)(2,1)}, u32[]{:S(2)}, u32[]{:S(2)}) %collective-permute-start.12) | collective-permute-done | bytes 524320 | tf_op jit(solution)/shard_map/ppermute | solution.py:30
  108.7 4.3 %note_product.4.refs_11_ = bf16[1,256,1024]{2,1,0:T(8,128)(2,1)} custom-call(s32[3]{0:T(128)} %pad_add_fusion.refs_0_, bf16[2,256,512]{2,1,0:T(8,128)(2,1)} %collective-permute-done.12.refs_1_, bf16[2048,1024]{1,0:T(8,128)(2,1)} %refs_5_.7, bf16[2048,1024]{1,0:T(8,128)(2,1)} %refs_5_.7, bf16[2048,1024]{1,0:T(8,128)(2,1)} %refs_5_.7, ...), custom_call_target="tpu_custom_call" | custom-call | tf_op jit(solution)/shard_map/note_product/pallas_call | solution.py:67
  113.0 0.4 collective-permute-start.14
  113.4 4.3 %note_product.5.refs_6_ = bf16[1,256,1024]{2,1,0:T(8,128)(2,1)} custom-call(s32[3]{0:T(128)} %pad_add_fusion.refs_0_, bf16[2,256,512]{2,1,0:T(8,128)(2,1)} %collective-permute-done.12.refs_1_, bf16[2048,1024]{1,0:T(8,128)(2,1)} %refs_5_.7, bf16[2048,1024]{1,0:T(8,128)(2,1)} %refs_5_.7, bf16[2048,1024]{1,0:T(8,128)(2,1)} %refs_5_.7, ...), custom_call_target="tpu_custom_call" | custom-call | tf_op jit(solution)/shard_map/note_product/pallas_call | solution.py:67
  117.7 0.0 collective-permute-done.15.refs_2_
  117.7 0.0 collective-permute-done.16.refs_5_
  117.7 7.3 %frame_sum.1 = bf16[1024,1024]{1,0:T(8,128)(2,1)} custom-call(s32[3]{0:T(128)} %pad_add_fusion.refs_0_, bf16[1024,512]{1,0:T(8,128)(2,1)} %collective-permute-done.11.refs_1_, bf16[1024,512]{1,0:T(8,128)(2,1)} %collective-permute-done.15.refs_2_, bf16[1024,1024]{1,0:T(8,128)(2,1)} %frame_own.1.refs_10_.refs_3_, ...), custom_call_target="tpu_custom_call" | custom-call | tf_op jit(solution)/shard_map/frame_sum/pallas_call | solution.py:67
  125.0 3.4 %collective-permute-done.14 = bf16[1,256,1024]{2,1,0:T(8,128)(2,1)} collective-permute-done((bf16[1,256,1024]{2,1,0:T(8,128)(2,1)}, bf16[1,256,1024]{2,1,0:T(8,128)(2,1)}, u32[]{:S(2)}, u32[]{:S(2)}) %collective-permute-start.14) | collective-permute-done | bytes 524320 | tf_op jit(solution)/shard_map/ppermute | solution.py:47
  128.4 2.2 %add_convert_fusion = bf16[1,256,1024]{2,1,0:T(8,128)(2,1)} fusion(bf16[1,256,1024]{2,1,0:T(8,128)(2,1)} %collective-permute-done.14, bf16[1,256,1024]{2,1,0:T(8,128)(2,1)} %note_product.5.refs_6_), kind=kLoop, calls=%fused_computation | loop fusion | flops 1048576 | bytes 1572864 | tf_op jit(solution)/shard_map/convert_element_type | solution.py:501
Async XLA Ops:
  4.8 16.2 %collective-permute-start = (bf16[2,256,512]{2,1,0:T(8,128)(2,1)}, bf16[2,256,512]{2,1,0:T(8,128)(2,1)}, u32[]{:S(2)}, u32[]{:S(2)}) collective-permute-start(bf16[2,256,512]{2,1,0:T(8,128)(2,1)} %key_values.1.refs_6_), channel_id=1, source_target_pairs={{0,32},{32,64},{64,96},{96,0},{1,33},{33,65},{65,97},{97,1},{2,34}... | collective-permute-start | bytes 1572872 | tf_op jit(solution)/shard_map/ppermute | solution.py:30
  17.6 17.5 %collective-permute-start.1 = (bf16[2,256,512]{2,1,0:T(8,128)(2,1)}, bf16[2,256,512]{2,1,0:T(8,128)(2,1)}, u32[]{:S(2)}, u32[]{:S(2)}) collective-permute-start(bf16[2,256,512]{2,1,0:T(8,128)(2,1)} %get-tuple-element.33), channel_id=1, source_target_pairs={{0,32},{32,64},{64,96},{96,0},{1,33},{33,65},{65,97},{97,1},{2,34}... | collective-permute-start | bytes 1572872 | tf_op jit(solution)/shard_map/ppermute | solution.py:30
  19.1 34.1 %collective-permute-start.6 = (bf16[512,1024]{1,0:T(8,128)(2,1)}, bf16[512,1024]{1,0:T(8,128)(2,1)}, u32[]{:S(2)}, u32[]{:S(2)}) collective-permute-start(bf16[512,1024]{1,0:T(8,128)(2,1)} %get-tuple-element.41), channel_id=1, source_target_pairs={{0,17},{1,16},{2,19},{3,18},{4,21},{5,20},{6,23},{7,22},{8,25},{9,... | collective-permute-start | bytes 3145736 | tf_op jit(solution)/shard_map/ppermute | solution.py:53
  21.0 17.7 %collective-permute-start.3 = (bf16[2,256,512]{2,1,0:T(8,128)(2,1)}, bf16[2,256,512]{2,1,0:T(8,128)(2,1)}, u32[]{:S(2)}, u32[]{:S(2)}) collective-permute-start(bf16[2,256,512]{2,1,0:T(8,128)(2,1)} %collective-permute-done.refs_3_.refs_4_), channel_id=1, source_target_pairs={{2,4},{6,8},{10,12},{14,16},{18,20},{22,24},{26,28},{4,2},{8,6},{1... | collective-permute-start | bytes 1572872 | tf_op jit(solution)/shard_map/ppermute | solution.py:43
  26.2 12.5 %collective-permute-start.2 = (bf16[2,256,512]{2,1,0:T(8,128)(2,1)}, bf16[2,256,512]{2,1,0:T(8,128)(2,1)}, u32[]{:S(2)}, u32[]{:S(2)}) collective-permute-start(bf16[2,256,512]{2,1,0:T(8,128)(2,1)} %collective-permute-done.refs_3_.refs_4_), channel_id=1, source_target_pairs={{0,2},{2,0},{4,6},{6,4},{8,10},{10,8},{12,14},{14,12},{16,18},{18,... | collective-permute-start | bytes 1572872 | tf_op jit(solution)/shard_map/ppermute | solution.py:37
  35.0 18.0 %collective-permute-start.5 = (bf16[2,256,512]{2,1,0:T(8,128)(2,1)}, bf16[2,256,512]{2,1,0:T(8,128)(2,1)}, u32[]{:S(2)}, u32[]{:S(2)}) collective-permute-start(bf16[2,256,512]{2,1,0:T(8,128)(2,1)} %collective-permute-done.1.refs_4_), channel_id=1, source_target_pairs={{2,4},{6,8},{10,12},{14,16},{18,20},{22,24},{26,28},{4,2},{8,6},{1... | collective-permute-start | bytes 1572872 | tf_op jit(solution)/shard_map/ppermute | solution.py:43
  38.5 14.6 %collective-permute-start.4 = (bf16[2,256,512]{2,1,0:T(8,128)(2,1)}, bf16[2,256,512]{2,1,0:T(8,128)(2,1)}, u32[]{:S(2)}, u32[]{:S(2)}) collective-permute-start(bf16[2,256,512]{2,1,0:T(8,128)(2,1)} %collective-permute-done.1.refs_4_), channel_id=1, source_target_pairs={{0,2},{2,0},{4,6},{6,4},{8,10},{10,8},{12,14},{14,12},{16,18},{18,... | collective-permute-start | bytes 1572872 | tf_op jit(solution)/shard_map/ppermute | solution.py:37
  53.0 34.6 %collective-permute-start.11 = (bf16[1024,512]{1,0:T(8,128)(2,1)}, bf16[1024,512]{1,0:T(8,128)(2,1)}, u32[]{:S(2)}, u32[]{:S(2)}) collective-permute-start(bf16[1024,512]{1,0:T(8,128)(2,1)} %get-tuple-element.43.refs_7_.refs_1_), channel_id=1, source_target_pairs={{0,1},{1,0},{2,3},{3,2},{4,5},{5,4},{6,7},{7,6},{8,9},{9,8},{10,11... | collective-permute-start | bytes 3145736 | tf_op jit(solution)/shard_map/ppermute | solution.py:47
  53.3 19.1 %collective-permute-start.7 = (bf16[2,256,512]{2,1,0:T(8,128)(2,1)}, bf16[2,256,512]{2,1,0:T(8,128)(2,1)}, u32[]{:S(2)}, u32[]{:S(2)}) collective-permute-start(bf16[2,256,512]{2,1,0:T(8,128)(2,1)} %get-tuple-element.45), channel_id=1, source_target_pairs={{0,2},{2,0},{4,6},{6,4},{8,10},{10,8},{12,14},{14,12},{16,18},{18,... | collective-permute-start | bytes 1572872 | tf_op jit(solution)/shard_map/ppermute | solution.py:37
  53.7 18.7 %collective-permute-start.8 = (bf16[2,256,512]{2,1,0:T(8,128)(2,1)}, bf16[2,256,512]{2,1,0:T(8,128)(2,1)}, u32[]{:S(2)}, u32[]{:S(2)}) collective-permute-start(bf16[2,256,512]{2,1,0:T(8,128)(2,1)} %get-tuple-element.46), channel_id=1, source_target_pairs={{2,4},{6,8},{10,12},{14,16},{18,20},{22,24},{26,28},{4,2},{8,6},{1... | collective-permute-start | bytes 1572872 | tf_op jit(solution)/shard_map/ppermute | solution.py:43
  72.4 9.2 %collective-permute-start.9 = (bf16[2,256,512]{2,1,0:T(8,128)(2,1)}, bf16[2,256,512]{2,1,0:T(8,128)(2,1)S(1)}, u32[]{:S(2)}, u32[]{:S(2)}) collective-permute-start(bf16[2,256,512]{2,1,0:T(8,128)(2,1)} %get-tuple-element.49), channel_id=1, source_target_pairs={{0,2},{2,0},{4,6},{6,4},{8,10},{10,8},{12,14},{14,12},{16,18},{18,... | collective-permute-start | bytes 1572872 | tf_op jit(solution)/shard_map/ppermute | solution.py:37
  72.5 12.9 %collective-permute-start.10 = (bf16[2,256,512]{2,1,0:T(8,128)(2,1)}, bf16[2,256,512]{2,1,0:T(8,128)(2,1)S(1)}, u32[]{:S(2)}, u32[]{:S(2)}) collective-permute-start(bf16[2,256,512]{2,1,0:T(8,128)(2,1)} %get-tuple-element.50), channel_id=1, source_target_pairs={{2,4},{6,8},{10,12},{14,16},{18,20},{22,24},{26,28},{4,2},{8,6},{1... | collective-permute-start | bytes 1572872 | tf_op jit(solution)/shard_map/ppermute | solution.py:43
  75.9 41.8 %collective-permute-start.15 = (bf16[1024,512]{1,0:T(8,128)(2,1)}, bf16[1024,512]{1,0:T(8,128)(2,1)}, u32[]{:S(2)}, u32[]{:S(2)}) collective-permute-start(bf16[1024,512]{1,0:T(8,128)(2,1)} %get-tuple-element.55.refs_2_), channel_id=1, source_target_pairs={{0,1},{1,0},{2,3},{3,2},{4,5},{5,4},{6,7},{7,6},{8,9},{9,8},{10,11... | collective-permute-start | bytes 3145736 | tf_op jit(solution)/shard_map/ppermute | solution.py:47
  79.1 38.6 %collective-permute-start.16 = (bf16[512,1024]{1,0:T(8,128)(2,1)}, bf16[512,1024]{1,0:T(8,128)(2,1)}, u32[]{:S(2)}, u32[]{:S(2)}) collective-permute-start(bf16[512,1024]{1,0:T(8,128)(2,1)} %collective-permute-done.6.refs_4_), channel_id=1, source_target_pairs={{0,2},{2,0},{4,6},{6,4},{8,10},{10,8},{12,14},{14,12},{16,18},{18,... | collective-permute-start | bytes 3145736 | tf_op jit(solution)/shard_map/ppermute | solution.py:37
  81.6 16.2 %collective-permute-start.13 = (bf16[2,256,512]{2,1,0:T(8,128)(2,1)}, bf16[2,256,512]{2,1,0:T(8,128)(2,1)}, u32[]{:S(2)}, u32[]{:S(2)}) collective-permute-start(bf16[2,256,512]{2,1,0:T(8,128)(2,1)} %add_convert_fusion.1), channel_id=1, source_target_pairs={{0,96},{32,0},{64,32},{96,64},{1,97},{33,1},{65,33},{97,65},{2,98}... | collective-permute-start | bytes 1572872 | tf_op jit(solution)/shard_map/ppermute | solution.py:30
  87.6 21.1 %collective-permute-start.12 = (bf16[2,256,512]{2,1,0:T(8,128)(2,1)}, bf16[2,256,512]{2,1,0:T(8,128)(2,1)}, u32[]{:S(2)}, u32[]{:S(2)}) collective-permute-start(bf16[2,256,512]{2,1,0:T(8,128)(2,1)} %add_convert_fusion.2.refs_4_), channel_id=1, source_target_pairs={{0,96},{32,0},{64,32},{96,64},{1,97},{33,1},{65,33},{97,65},{2,98}... | collective-permute-start | bytes 1572872 | tf_op jit(solution)/shard_map/ppermute | solution.py:30
  113.0 15.4 %collective-permute-start.14 = (bf16[1,256,1024]{2,1,0:T(8,128)(2,1)}, bf16[1,256,1024]{2,1,0:T(8,128)(2,1)}, u32[]{:S(2)}, u32[]{:S(2)}) collective-permute-start(bf16[1,256,1024]{2,1,0:T(8,128)(2,1)} %note_product.4.refs_11_), channel_id=1, source_target_pairs={{0,1},{1,0},{2,3},{3,2},{4,5},{5,4},{6,7},{7,6},{8,9},{9,8},{10,11... | collective-permute-start | bytes 1572872 | tf_op jit(solution)/shard_map/ppermute | solution.py:47

commit v8 on v7

--- a/solution.py
+++ b/solution.py
@@ -308,6 +308,7 @@
         name,
         after,
         scalars=1,
+        flops=8 * rows * half * cols if own is None else 0,
         scratch=[
             pltpu.VMEM((half, cols), BF16),
             pltpu.VMEM((rows, half), BF16),
@@ -473,16 +474,17 @@
     dq0, own0, rim_near0, rim_far0 = attend(0, near0, far0, ())
     dq0_other = head_swap(dq0)
     w_mine, dq0 = lax.optimization_barrier((w_mine, dq0))
-    w_theirs = near_swap(w_mine)
     rim_near0, rim_far0, near1, far1 = lax.optimization_barrier((rim_near0, rim_far0, near1, far1))
     in_near0, in_far0 = near_swap(rim_near0), far_swap(rim_far0)
     dq1, own1, rim_near1, rim_far1 = attend(1, near1, far1, (dq0,))
-    dq1_other = head_swap(dq1)
     in_near0, in_far0, rim_near1, rim_far1 = lax.optimization_barrier(
         (in_near0, in_far0, rim_near1, rim_far1)
     )
     in_near1, in_far1 = near_swap(rim_near1), far_swap(rim_far1)
-    notes0 = section_shift(note_sum_of(own0, in_near0, in_far0), -1)
+    owned0 = note_sum_of(own0, in_near0, in_far0)
+    notes0 = section_shift(owned0, -1)
+    dq1, owned0 = lax.optimization_barrier((dq1, owned0))
+    dq1_other = head_swap(dq1)
     owned1 = note_sum_of(own1, in_near1, in_far1)
     owned1, dq0_other = lax.optimization_barrier((owned1, dq0_other))
     notes1 = section_shift(owned1, -1)
@@ -490,6 +492,8 @@
     own_part = frame_part(scalars, [dq0, dq1], [w_query], None, "frame_own", (owned1,))
     before = note_product(scalars, [notes0], CHUNKS[:1], w_key, w_value, (own_part,))
     last = (scalars, [notes1], CHUNKS[1:], w_key, w_value)
+    w_mine, before = lax.optimization_barrier((w_mine, before))
+    w_theirs = near_swap(w_mine)
     give_notes = note_product(*last, (), before, (0,))
     notes_other = head_swap(give_notes)
     keep_notes = note_product(*last, (give_notes,), before, (1,))

time: 131 us -> 132 us (level)
  the two profiles are of different devices: /device:TPU:38 before, /device:TPU:1 now
where the time goes in v8:
time: 132 us; the launch traced here: 131 us
  Pallas kernels  80.9 us (61%)
  starting transfers between devices  30.6 us (23%)
  waiting for transfers between devices  11.1 us (8%)
  other arithmetic  7.61 us (6%)
    pallas_call x10, Pallas kernels, call(): pl.pallas_call(reads, grid_spec=pltpu.PrefetchScalarGridSpec(num_scalar_p...  80.9 us
    ppermute x4, starting transfers between devices, far_swap(): return lax.ppermute(block, 'seq', pairs + [(j, i) for i, j in pairs])  14.5 us
    ppermute x3, waiting for transfers between devices, head_swap(): return lax.ppermute(block, 'head', [(0, 1), (1, 0)])  8.85 us
    ppermute x4, starting transfers between devices, section_shift(): lax.ppermute(block, 'section', [(i, (i + distance) % count) for i in rang...  5.09 us
    convert_element_type x2, other arithmetic, note_sum_of(): return (own + near.astype(F32) + far.astype(F32)).astype(BF16)  4.75 us
    ppermute x1, starting transfers between devices, across(): return lax.ppermute(block, ('seq', 'head'), route)  3.76 us
    ppermute x5, starting transfers between devices, near_swap(): return lax.ppermute(block, 'seq', [(i, i ^ 1) for i in range(count)])  3.72 us
    ppermute x3, starting transfers between devices, head_swap(): return lax.ppermute(block, 'head', [(0, 1), (1, 0)])  3.45 us
  transfers between devices with their start and end apart: 17, of which 3 were waited for; matrix products, arithmetic and copies ran while one was open for 4% of the time, Pallas kernels for 59%

profile of v8, /device:TPU:1, one launch (start us, length us, event | category | flops | bytes accessed | tf_op | source)
XLA Modules:
  0.0 131.0 jit_solution(14449861936815846930)
XLA Ops:
  0.6 4.2 %key_values.1.refs_6_ = bf16[2,256,512]{2,1,0:T(8,128)(2,1)} custom-call(bf16[256,2048]{1,0:T(8,128)(2,1)} %bitcast.10, bf16[2048,1024]{1,0:T(8,128)(2,1)} %refs_5_.7, bf16[2048,1024]{1,0:T(8,128)(2,1)} %refs_9_.5), custom_call_target="tpu_custom_call" | custom-call | tf_op jit(solution)/shard_map/key_values/pallas_call | solution.py:67
  4.8 2.1 %collective-permute-start = (bf16[2,256,512]{2,1,0:T(8,128)(2,1)}, bf16[2,256,512]{2,1,0:T(8,128)(2,1)}, u32[]{:S(2)}, u32[]{:S(2)}) collective-permute-start(bf16[2,256,512]{2,1,0:T(8,128)(2,1)} %key_values.1.refs_6_), channel_id=1, source_target_pairs={{0,32},{32,64},{64,96},{96,0},{1,33},{33,65},{65,97},{97,1},{2,34}... | collective-permute-start | bytes 1572872 | tf_op jit(solution)/shard_map/ppermute | solution.py:30
  6.9 0.7 pad_add_fusion.refs_0_
  7.6 11.5 %key_values_and_queries.1 = (bf16[2,256,512]{2,1,0:T(8,128)(2,1)}, bf16[1024,1024]{1,0:T(8,128)(2,1)}, bf16[512,1024]{1,0:T(8,128)(2,1)}) custom-call(s32[3]{0:T(128)} %pad_add_fusion.refs_0_, bf16[256,2048]{1,0:T(8,128)(2,1)} %bitcast.11, bf16[2048,1024]{1,0:T(8,128)(2,1)} %refs_5_.7, bf16[2048,1024]{1,0:T(8,128)(2,1)} %refs_9_.5, ...), custom_call_target="tpu_custom_call" | custom-call | tf_op jit(solution)/shard_map/key_values_and_queries/pallas_call | solution.py:67
  19.1 1.3 collective-permute-start.1
  20.4 3.8 %collective-permute-start.6 = (bf16[512,1024]{1,0:T(8,128)(2,1)}, bf16[512,1024]{1,0:T(8,128)(2,1)}, u32[]{:S(2)}, u32[]{:S(2)}) collective-permute-start(bf16[512,1024]{1,0:T(8,128)(2,1)} %get-tuple-element.44), channel_id=1, source_target_pairs={{0,17},{1,16},{2,19},{3,18},{4,21},{5,20},{6,23},{7,22},{8,25},{9,... | collective-permute-start | bytes 3145736 | tf_op jit(solution)/shard_map/ppermute | solution.py:53
  24.2 0.0 collective-permute-done.refs_3_.refs_4_
  24.2 4.6 %collective-permute-start.3 = (bf16[2,256,512]{2,1,0:T(8,128)(2,1)}, bf16[2,256,512]{2,1,0:T(8,128)(2,1)}, u32[]{:S(2)}, u32[]{:S(2)}) collective-permute-start(bf16[2,256,512]{2,1,0:T(8,128)(2,1)} %collective-permute-done.refs_3_.refs_4_), channel_id=1, source_target_pairs={{2,4},{6,8},{10,12},{14,16},{18,20},{22,24},{26,28},{4,2},{8,6},{1... | collective-permute-start | bytes 1572872 | tf_op jit(solution)/shard_map/ppermute | solution.py:43
  28.8 0.1 collective-permute-start.2
  28.9 8.7 %grad_ctx.1.refs_3_ = bf16[1024,1024]{1,0:T(8,128)(2,1)} custom-call(bf16[1024,2048]{1,0:T(8,128)(2,1)} %bitcast.8, bf16[1024,2048]{1,0:T(8,128)(2,1)} %refs_1_.3, bf16[1024,1024]{1,0:T(8,128)(2,1)} %get-tuple-element.35.refs_2_, bf16[2,256,512]{2,1,0:T(8,128)(2,1)} %collective-permute-done.refs_3_.refs_4_), custom_call_target="tpu_custom_call" | custom-call | tf_op jit(solution)/shard_map/grad_ctx/pallas_call | solution.py:67
  37.6 0.0 collective-permute-done.1.refs_4_
  37.6 3.6 %collective-permute-start.5 = (bf16[2,256,512]{2,1,0:T(8,128)(2,1)}, bf16[2,256,512]{2,1,0:T(8,128)(2,1)}, u32[]{:S(2)}, u32[]{:S(2)}) collective-permute-start(bf16[2,256,512]{2,1,0:T(8,128)(2,1)} %collective-permute-done.1.refs_4_), channel_id=1, source_target_pairs={{2,4},{6,8},{10,12},{14,16},{18,20},{22,24},{26,28},{4,2},{8,6},{1... | collective-permute-start | bytes 1572872 | tf_op jit(solution)/shard_map/ppermute | solution.py:43
  41.2 0.3 collective-permute-start.4
  41.4 0.0 collective-permute-done.3.refs_6_
  41.4 0.0 collective-permute-done.2.refs_5_
  41.5 14.3 %attention.2 = (bf16[1024,512]{1,0:T(8,128)(2,1)}, f32[2,256,512]{2,1,0:T(8,128)}, bf16[2,256,512]{2,1,0:T(8,128)(2,1)}, bf16[2,256,512]{2,1,0:T(8,128)(2,1)}) custom-call(s32[3]{0:T(128)} %pad_add_fusion.refs_0_, s32[2,8]{1,0:T(2,128)} %bitcast.13, bf16[1024,1024]{1,0:T(8,128)(2,1)} %get-tuple-element.35.refs_2_, bf16[1024,1024]{1,0:T(8,128)(2,1)} %grad_ctx.1.refs_3_, ...), custom_call_target="tpu_custom_call" | custom-call | tf_op jit(solution)/shard_map/attention/pallas_call | solution.py:67
  55.7 0.0 collective-permute-done.5.refs_6_
  55.7 0.0 collective-permute-done.4.refs_5_
  55.7 0.7 collective-permute-start.11
  56.4 0.0 collective-permute-done.6.refs_4_
  56.4 0.8 collective-permute-start.7
  57.2 3.1 %collective-permute-start.8 = (bf16[2,256,512]{2,1,0:T(8,128)(2,1)}, bf16[2,256,512]{2,1,0:T(8,128)(2,1)}, u32[]{:S(2)}, u32[]{:S(2)}) collective-permute-start(bf16[2,256,512]{2,1,0:T(8,128)(2,1)} %get-tuple-element.49), channel_id=1, source_target_pairs={{2,4},{6,8},{10,12},{14,16},{18,20},{22,24},{26,28},{4,2},{8,6},{1... | collective-permute-start | bytes 1572872 | tf_op jit(solution)/shard_map/ppermute | solution.py:43
  60.3 14.4 %attention.3 = (bf16[1024,512]{1,0:T(8,128)(2,1)}, f32[2,256,512]{2,1,0:T(8,128)}, bf16[2,256,512]{2,1,0:T(8,128)(2,1)}, bf16[2,256,512]{2,1,0:T(8,128)(2,1)}) custom-call(s32[3]{0:T(128)} %pad_add_fusion.refs_0_, s32[2,8]{1,0:T(2,128)} %bitcast.14, bf16[1024,1024]{1,0:T(8,128)(2,1)} %get-tuple-element.35.refs_2_, bf16[1024,1024]{1,0:T(8,128)(2,1)} %grad_ctx.1.refs_3_, ...), custom_call_target="tpu_custom_call" | custom-call | flops 12079595520 | tf_op jit(solution)/shard_map/attention/pallas_call | solution.py:67
  74.6 0.0 collective-permute-done.7
  74.6 0.0 collective-permute-done.8
  74.6 0.1 collective-permute-start.9
  74.7 3.3 %collective-permute-start.10 = (bf16[2,256,512]{2,1,0:T(8,128)(2,1)}, bf16[2,256,512]{2,1,0:T(8,128)(2,1)S(1)}, u32[]{:S(2)}, u32[]{:S(2)}) collective-permute-start(bf16[2,256,512]{2,1,0:T(8,128)(2,1)} %get-tuple-element.53), channel_id=1, source_target_pairs={{2,4},{6,8},{10,12},{14,16},{18,20},{22,24},{26,28},{4,2},{8,6},{1... | collective-permute-start | bytes 1572872 | tf_op jit(solution)/shard_map/ppermute | solution.py:43
  78.0 2.5 %add_convert_fusion.1 = bf16[2,256,512]{2,1,0:T(8,128)(2,1)} fusion(bf16[2,256,512]{2,1,0:T(8,128)(2,1)} %collective-permute-done.8, f32[2,256,512]{2,1,0:T(8,128)} %get-tuple-element.56, bf16[2,256,512]{2,1,0:T(8,128)(2,1)} %collective-permute-done.7), kind=kLoop, calls=%fused_computation.1 | loop fusion | flops 1310720 | bytes 2621440 | tf_op jit(solution)/shard_map/convert_element_type | solution.py:471
  80.5 0.3 collective-permute-start.13
  80.8 2.8 %collective-permute-start.15 = (bf16[1024,512]{1,0:T(8,128)(2,1)}, bf16[1024,512]{1,0:T(8,128)(2,1)}, u32[]{:S(2)}, u32[]{:S(2)}) collective-permute-start(bf16[1024,512]{1,0:T(8,128)(2,1)} %get-tuple-element.60.refs_2_), channel_id=1, source_target_pairs={{0,1},{1,0},{2,3},{3,2},{4,5},{5,4},{6,7},{7,6},{8,9},{9,8},{10,11... | collective-permute-start | bytes 3145736 | tf_op jit(solution)/shard_map/ppermute | solution.py:47
  83.6 0.0 collective-permute-done.9
  83.6 2.2 %collective-permute-done.10 = bf16[2,256,512]{2,1,0:T(8,128)(2,1)S(1)} collective-permute-done((bf16[2,256,512]{2,1,0:T(8,128)(2,1)}, bf16[2,256,512]{2,1,0:T(8,128)(2,1)S(1)}, u32[]{:S(2)}, u32[]{:S(2)}) %collective-permute-start.10) | collective-permute-done | bytes 524320 | tf_op jit(solution)/shard_map/ppermute | solution.py:43
  85.8 2.2 %add_convert_fusion.2.refs_4_ = bf16[2,256,512]{2,1,0:T(8,128)(2,1)} fusion(bf16[2,256,512]{2,1,0:T(8,128)(2,1)S(1)} %collective-permute-done.10, f32[2,256,512]{2,1,0:T(8,128)} %get-tuple-element.47, bf16[2,256,512]{2,1,0:T(8,128)(2,1)S(1)} %collective-permute-done.9), kind=kLoop, calls=%fused_computation.2 | loop fusion | flops 1310720 | bytes 2621440 | tf_op jit(solution)/shard_map/convert_element_type | solution.py:471
  88.1 5.1 %collective-permute-done.11.refs_1_ = bf16[1024,512]{1,0:T(8,128)(2,1)} collective-permute-done((bf16[1024,512]{1,0:T(8,128)(2,1)}, bf16[1024,512]{1,0:T(8,128)(2,1)}, u32[]{:S(2)}, u32[]{:S(2)}) %collective-permute-start.11) | collective-permute-done | bytes 1048608 | tf_op jit(solution)/shard_map/ppermute | solution.py:47
  93.1 1.4 %collective-permute-start.12 = (bf16[2,256,512]{2,1,0:T(8,128)(2,1)}, bf16[2,256,512]{2,1,0:T(8,128)(2,1)}, u32[]{:S(2)}, u32[]{:S(2)}) collective-permute-start(bf16[2,256,512]{2,1,0:T(8,128)(2,1)} %add_convert_fusion.2.refs_4_), channel_id=1, source_target_pairs={{0,96},{32,0},{64,32},{96,64},{1,97},{33,1},{65,33},{97,65},{2,98}... | collective-permute-start | bytes 1572872 | tf_op jit(solution)/shard_map/ppermute | solution.py:30
  94.6 6.7 %frame_own.1.refs_10_.refs_3_ = bf16[1024,1024]{1,0:T(8,128)(2,1)} custom-call(s32[3]{0:T(128)} %pad_add_fusion.refs_0_, bf16[1024,512]{1,0:T(8,128)(2,1)} %get-tuple-element.46.refs_7_.refs_1_, bf16[1024,512]{1,0:T(8,128)(2,1)} %get-tuple-element.60.refs_2_, bf16[2048,1024]{1,0:T(8,128)(2,1)} %refs_3_.6, bf16[2,256,512]{2,1,0:T(8,128)(2,1)} %add_convert_fusion.2.refs_4_), custom_call_target="tpu_custom_call" | custom-call | flops 8589934592 | tf_op jit(solution)/shard_map/frame_own/pallas_call | solution.py:67
  101.3 0.0 collective-permute-done.13.refs_1_
  101.3 5.3 %note_product.3.refs_10_ = f32[2,256,1024]{2,1,0:T(8,128)} custom-call(s32[3]{0:T(128)} %pad_add_fusion.refs_0_, bf16[2,256,512]{2,1,0:T(8,128)(2,1)} %collective-permute-done.13.refs_1_, bf16[2048,1024]{1,0:T(8,128)(2,1)} %refs_5_.7, bf16[2048,1024]{1,0:T(8,128)(2,1)} %refs_5_.7, bf16[2048,1024]{1,0:T(8,128)(2,1)} %refs_5_.7, bf16[2048,1024]{1,0:T(8,128)(2,1)} %refs_5_.7, ...), custom_call_target="tpu_custom_call" | custom-call | tf_op jit(solution)/shard_map/note_product/pallas_call | solution.py:67
  106.6 2.5 %collective-permute-start.16 = (bf16[512,1024]{1,0:T(8,128)(2,1)}, bf16[512,1024]{1,0:T(8,128)(2,1)}, u32[]{:S(2)}, u32[]{:S(2)}) collective-permute-start(bf16[512,1024]{1,0:T(8,128)(2,1)} %collective-permute-done.6.refs_4_), channel_id=1, source_target_pairs={{0,2},{2,0},{4,6},{6,4},{8,10},{10,8},{12,14},{14,12},{16,18},{18,... | collective-permute-start | bytes 3145736 | tf_op jit(solution)/shard_map/ppermute | solution.py:37
  109.2 0.0 collective-permute-done.12.refs_1_
  109.2 4.3 %note_product.4.refs_11_ = bf16[1,256,1024]{2,1,0:T(8,128)(2,1)} custom-call(s32[3]{0:T(128)} %pad_add_fusion.refs_0_, bf16[2,256,512]{2,1,0:T(8,128)(2,1)} %collective-permute-done.12.refs_1_, bf16[2048,1024]{1,0:T(8,128)(2,1)} %refs_5_.7, bf16[2048,1024]{1,0:T(8,128)(2,1)} %refs_5_.7, bf16[2048,1024]{1,0:T(8,128)(2,1)} %refs_5_.7, ...), custom_call_target="tpu_custom_call" | custom-call | tf_op jit(solution)/shard_map/note_product/pallas_call | solution.py:67
  113.5 0.0 collective-permute-start.14
  113.5 4.3 %note_product.5.refs_6_ = bf16[1,256,1024]{2,1,0:T(8,128)(2,1)} custom-call(s32[3]{0:T(128)} %pad_add_fusion.refs_0_, bf16[2,256,512]{2,1,0:T(8,128)(2,1)} %collective-permute-done.12.refs_1_, bf16[2048,1024]{1,0:T(8,128)(2,1)} %refs_5_.7, bf16[2048,1024]{1,0:T(8,128)(2,1)} %refs_5_.7, bf16[2048,1024]{1,0:T(8,128)(2,1)} %refs_5_.7, ...), custom_call_target="tpu_custom_call" | custom-call | tf_op jit(solution)/shard_map/note_product/pallas_call | solution.py:67
  117.8 0.0 collective-permute-done.15.refs_2_
  117.8 0.0 collective-permute-done.16.refs_5_
  117.8 7.3 %frame_sum.1 = bf16[1024,1024]{1,0:T(8,128)(2,1)} custom-call(s32[3]{0:T(128)} %pad_add_fusion.refs_0_, bf16[1024,512]{1,0:T(8,128)(2,1)} %collective-permute-done.11.refs_1_, bf16[1024,512]{1,0:T(8,128)(2,1)} %collective-permute-done.15.refs_2_, bf16[1024,1024]{1,0:T(8,128)(2,1)} %frame_own.1.refs_10_.refs_3_, ...), custom_call_target="tpu_custom_call" | custom-call | tf_op jit(solution)/shard_map/frame_sum/pallas_call | solution.py:67
  125.1 3.8 %collective-permute-done.14 = bf16[1,256,1024]{2,1,0:T(8,128)(2,1)} collective-permute-done((bf16[1,256,1024]{2,1,0:T(8,128)(2,1)}, bf16[1,256,1024]{2,1,0:T(8,128)(2,1)}, u32[]{:S(2)}, u32[]{:S(2)}) %collective-permute-start.14) | collective-permute-done | bytes 524320 | tf_op jit(solution)/shard_map/ppermute | solution.py:47
  128.8 2.2 %add_convert_fusion = bf16[1,256,1024]{2,1,0:T(8,128)(2,1)} fusion(bf16[1,256,1024]{2,1,0:T(8,128)(2,1)} %collective-permute-done.14, bf16[1,256,1024]{2,1,0:T(8,128)(2,1)} %note_product.5.refs_6_), kind=kLoop, calls=%fused_computation | loop fusion | flops 1048576 | bytes 1572864 | tf_op jit(solution)/shard_map/convert_element_type | solution.py:505
Async XLA Ops:
  4.8 19.4 %collective-permute-start = (bf16[2,256,512]{2,1,0:T(8,128)(2,1)}, bf16[2,256,512]{2,1,0:T(8,128)(2,1)}, u32[]{:S(2)}, u32[]{:S(2)}) collective-permute-start(bf16[2,256,512]{2,1,0:T(8,128)(2,1)} %key_values.1.refs_6_), channel_id=1, source_target_pairs={{0,32},{32,64},{64,96},{96,0},{1,33},{33,65},{65,97},{97,1},{2,34}... | collective-permute-start | bytes 1572872 | tf_op jit(solution)/shard_map/ppermute | solution.py:30
  19.1 18.4 %collective-permute-start.1 = (bf16[2,256,512]{2,1,0:T(8,128)(2,1)}, bf16[2,256,512]{2,1,0:T(8,128)(2,1)}, u32[]{:S(2)}, u32[]{:S(2)}) collective-permute-start(bf16[2,256,512]{2,1,0:T(8,128)(2,1)} %get-tuple-element.36), channel_id=1, source_target_pairs={{0,32},{32,64},{64,96},{96,0},{1,33},{33,65},{65,97},{97,1},{2,34}... | collective-permute-start | bytes 1572872 | tf_op jit(solution)/shard_map/ppermute | solution.py:30
  20.4 36.0 %collective-permute-start.6 = (bf16[512,1024]{1,0:T(8,128)(2,1)}, bf16[512,1024]{1,0:T(8,128)(2,1)}, u32[]{:S(2)}, u32[]{:S(2)}) collective-permute-start(bf16[512,1024]{1,0:T(8,128)(2,1)} %get-tuple-element.44), channel_id=1, source_target_pairs={{0,17},{1,16},{2,19},{3,18},{4,21},{5,20},{6,23},{7,22},{8,25},{9,... | collective-permute-start | bytes 3145736 | tf_op jit(solution)/shard_map/ppermute | solution.py:53
  24.2 17.3 %collective-permute-start.3 = (bf16[2,256,512]{2,1,0:T(8,128)(2,1)}, bf16[2,256,512]{2,1,0:T(8,128)(2,1)}, u32[]{:S(2)}, u32[]{:S(2)}) collective-permute-start(bf16[2,256,512]{2,1,0:T(8,128)(2,1)} %collective-permute-done.refs_3_.refs_4_), channel_id=1, source_target_pairs={{2,4},{6,8},{10,12},{14,16},{18,20},{22,24},{26,28},{4,2},{8,6},{1... | collective-permute-start | bytes 1572872 | tf_op jit(solution)/shard_map/ppermute | solution.py:43
  28.8 12.7 %collective-permute-start.2 = (bf16[2,256,512]{2,1,0:T(8,128)(2,1)}, bf16[2,256,512]{2,1,0:T(8,128)(2,1)}, u32[]{:S(2)}, u32[]{:S(2)}) collective-permute-start(bf16[2,256,512]{2,1,0:T(8,128)(2,1)} %collective-permute-done.refs_3_.refs_4_), channel_id=1, source_target_pairs={{0,2},{2,0},{4,6},{6,4},{8,10},{10,8},{12,14},{14,12},{16,18},{18,... | collective-permute-start | bytes 1572872 | tf_op jit(solution)/shard_map/ppermute | solution.py:37
  37.6 18.2 %collective-permute-start.5 = (bf16[2,256,512]{2,1,0:T(8,128)(2,1)}, bf16[2,256,512]{2,1,0:T(8,128)(2,1)}, u32[]{:S(2)}, u32[]{:S(2)}) collective-permute-start(bf16[2,256,512]{2,1,0:T(8,128)(2,1)} %collective-permute-done.1.refs_4_), channel_id=1, source_target_pairs={{2,4},{6,8},{10,12},{14,16},{18,20},{22,24},{26,28},{4,2},{8,6},{1... | collective-permute-start | bytes 1572872 | tf_op jit(solution)/shard_map/ppermute | solution.py:43
  41.2 14.6 %collective-permute-start.4 = (bf16[2,256,512]{2,1,0:T(8,128)(2,1)}, bf16[2,256,512]{2,1,0:T(8,128)(2,1)}, u32[]{:S(2)}, u32[]{:S(2)}) collective-permute-start(bf16[2,256,512]{2,1,0:T(8,128)(2,1)} %collective-permute-done.1.refs_4_), channel_id=1, source_target_pairs={{0,2},{2,0},{4,6},{6,4},{8,10},{10,8},{12,14},{14,12},{16,18},{18,... | collective-permute-start | bytes 1572872 | tf_op jit(solution)/shard_map/ppermute | solution.py:37
  55.7 37.4 %collective-permute-start.11 = (bf16[1024,512]{1,0:T(8,128)(2,1)}, bf16[1024,512]{1,0:T(8,128)(2,1)}, u32[]{:S(2)}, u32[]{:S(2)}) collective-permute-start(bf16[1024,512]{1,0:T(8,128)(2,1)} %get-tuple-element.46.refs_7_.refs_1_), channel_id=1, source_target_pairs={{0,1},{1,0},{2,3},{3,2},{4,5},{5,4},{6,7},{7,6},{8,9},{9,8},{10,11... | collective-permute-start | bytes 3145736 | tf_op jit(solution)/shard_map/ppermute | solution.py:47
  56.4 18.2 %collective-permute-start.7 = (bf16[2,256,512]{2,1,0:T(8,128)(2,1)}, bf16[2,256,512]{2,1,0:T(8,128)(2,1)}, u32[]{:S(2)}, u32[]{:S(2)}) collective-permute-start(bf16[2,256,512]{2,1,0:T(8,128)(2,1)} %get-tuple-element.48), channel_id=1, source_target_pairs={{0,2},{2,0},{4,6},{6,4},{8,10},{10,8},{12,14},{14,12},{16,18},{18,... | collective-permute-start | bytes 1572872 | tf_op jit(solution)/shard_map/ppermute | solution.py:37
  57.2 17.5 %collective-permute-start.8 = (bf16[2,256,512]{2,1,0:T(8,128)(2,1)}, bf16[2,256,512]{2,1,0:T(8,128)(2,1)}, u32[]{:S(2)}, u32[]{:S(2)}) collective-permute-start(bf16[2,256,512]{2,1,0:T(8,128)(2,1)} %get-tuple-element.49), channel_id=1, source_target_pairs={{2,4},{6,8},{10,12},{14,16},{18,20},{22,24},{26,28},{4,2},{8,6},{1... | collective-permute-start | bytes 1572872 | tf_op jit(solution)/shard_map/ppermute | solution.py:43
  74.6 9.0 %collective-permute-start.9 = (bf16[2,256,512]{2,1,0:T(8,128)(2,1)}, bf16[2,256,512]{2,1,0:T(8,128)(2,1)S(1)}, u32[]{:S(2)}, u32[]{:S(2)}) collective-permute-start(bf16[2,256,512]{2,1,0:T(8,128)(2,1)} %get-tuple-element.52), channel_id=1, source_target_pairs={{0,2},{2,0},{4,6},{6,4},{8,10},{10,8},{12,14},{14,12},{16,18},{18,... | collective-permute-start | bytes 1572872 | tf_op jit(solution)/shard_map/ppermute | solution.py:37
  74.7 11.1 %collective-permute-start.10 = (bf16[2,256,512]{2,1,0:T(8,128)(2,1)}, bf16[2,256,512]{2,1,0:T(8,128)(2,1)S(1)}, u32[]{:S(2)}, u32[]{:S(2)}) collective-permute-start(bf16[2,256,512]{2,1,0:T(8,128)(2,1)} %get-tuple-element.53), channel_id=1, source_target_pairs={{2,4},{6,8},{10,12},{14,16},{18,20},{22,24},{26,28},{4,2},{8,6},{1... | collective-permute-start | bytes 1572872 | tf_op jit(solution)/shard_map/ppermute | solution.py:43
  80.5 20.8 %collective-permute-start.13 = (bf16[2,256,512]{2,1,0:T(8,128)(2,1)}, bf16[2,256,512]{2,1,0:T(8,128)(2,1)}, u32[]{:S(2)}, u32[]{:S(2)}) collective-permute-start(bf16[2,256,512]{2,1,0:T(8,128)(2,1)} %add_convert_fusion.1), channel_id=1, source_target_pairs={{0,96},{32,0},{64,32},{96,64},{1,97},{33,1},{65,33},{97,65},{2,98}... | collective-permute-start | bytes 1572872 | tf_op jit(solution)/shard_map/ppermute | solution.py:30
  80.8 37.0 %collective-permute-start.15 = (bf16[1024,512]{1,0:T(8,128)(2,1)}, bf16[1024,512]{1,0:T(8,128)(2,1)}, u32[]{:S(2)}, u32[]{:S(2)}) collective-permute-start(bf16[1024,512]{1,0:T(8,128)(2,1)} %get-tuple-element.60.refs_2_), channel_id=1, source_target_pairs={{0,1},{1,0},{2,3},{3,2},{4,5},{5,4},{6,7},{7,6},{8,9},{9,8},{10,11... | collective-permute-start | bytes 3145736 | tf_op jit(solution)/shard_map/ppermute | solution.py:47
  93.1 16.0 %collective-permute-start.12 = (bf16[2,256,512]{2,1,0:T(8,128)(2,1)}, bf16[2,256,512]{2,1,0:T(8,128)(2,1)}, u32[]{:S(2)}, u32[]{:S(2)}) collective-permute-start(bf16[2,256,512]{2,1,0:T(8,128)(2,1)} %add_convert_fusion.2.refs_4_), channel_id=1, source_target_pairs={{0,96},{32,0},{64,32},{96,64},{1,97},{33,1},{65,33},{97,65},{2,98}... | collective-permute-start | bytes 1572872 | tf_op jit(solution)/shard_map/ppermute | solution.py:30
  106.6 11.2 %collective-permute-start.16 = (bf16[512,1024]{1,0:T(8,128)(2,1)}, bf16[512,1024]{1,0:T(8,128)(2,1)}, u32[]{:S(2)}, u32[]{:S(2)}) collective-permute-start(bf16[512,1024]{1,0:T(8,128)(2,1)} %collective-permute-done.6.refs_4_), channel_id=1, source_target_pairs={{0,2},{2,0},{4,6},{6,4},{8,10},{10,8},{12,14},{14,12},{16,18},{18,... | collective-permute-start | bytes 3145736 | tf_op jit(solution)/shard_map/ppermute | solution.py:37
  113.5 15.4 %collective-permute-start.14 = (bf16[1,256,1024]{2,1,0:T(8,128)(2,1)}, bf16[1,256,1024]{2,1,0:T(8,128)(2,1)}, u32[]{:S(2)}, u32[]{:S(2)}) collective-permute-start(bf16[1,256,1024]{2,1,0:T(8,128)(2,1)} %note_product.4.refs_11_), channel_id=1, source_target_pairs={{0,1},{1,0},{2,3},{3,2},{4,5},{5,4},{6,7},{7,6},{8,9},{9,8},{10,11... | collective-permute-start | bytes 1572872 | tf_op jit(solution)/shard_map/ppermute | solution.py:47

commit v9 on v8

--- a/solution.py
+++ b/solution.py
@@ -486,15 +486,16 @@
     dq1, owned0 = lax.optimization_barrier((dq1, owned0))
     dq1_other = head_swap(dq1)
     owned1 = note_sum_of(own1, in_near1, in_far1)
-    owned1, dq0_other = lax.optimization_barrier((owned1, dq0_other))
     notes1 = section_shift(owned1, -1)
 
-    own_part = frame_part(scalars, [dq0, dq1], [w_query], None, "frame_own", (owned1,))
-    before = note_product(scalars, [notes0], CHUNKS[:1], w_key, w_value, (own_part,))
+    before = note_product(scalars, [notes0], CHUNKS[:1], w_key, w_value, (owned1,))
+    own_part = frame_part(
+        scalars, [dq0, dq1], [w_query], None, "frame_own", (before, dq0_other)
+    )
     last = (scalars, [notes1], CHUNKS[1:], w_key, w_value)
-    w_mine, before = lax.optimization_barrier((w_mine, before))
+    w_mine, own_part = lax.optimization_barrier((w_mine, own_part))
     w_theirs = near_swap(w_mine)
-    give_notes = note_product(*last, (), before, (0,))
+    give_notes = note_product(*last, (own_part,), before, (0,))
     notes_other = head_swap(give_notes)
     keep_notes = note_product(*last, (give_notes,), before, (1,))
     frame_out = frame_part(

time: 132 us -> 130 us (0.985)
  starting transfers between devices: 30.6 us -> 28.7 us
    ppermute x3, waiting for transfers between devices: 8.85 us -> 3.37 us  [head_swap(): return lax.ppermute(block, 'head', [(0, 1), (1, 0)])]
    ppermute x4, waiting for transfers between devices: 0.01 us -> 5.42 us  [section_shift(): lax.ppermute(block, 'section', [(i, (i + distance) % count) for i in rang...]
    ppermute x5, starting transfers between devices: 3.72 us -> 1.28 us  [near_swap(): return lax.ppermute(block, 'seq', [(i, i ^ 1) for i in range(count)])]
    ppermute x3, starting transfers between devices: 3.45 us -> 4.97 us  [head_swap(): return lax.ppermute(block, 'head', [(0, 1), (1, 0)])]
where the time goes in v9:
time: 130 us; the launch traced here: 129 us
  Pallas kernels  80.9 us (62%)
  starting transfers between devices  28.7 us (22%)
  waiting for transfers between devices  11.8 us (9%)
  other arithmetic  6.82 us (5%)
    pallas_call x10, Pallas kernels, call(): pl.pallas_call(reads, grid_spec=pltpu.PrefetchScalarGridSpec(num_scalar_p...  80.9 us
    ppermute x4, starting transfers between devices, far_swap(): return lax.ppermute(block, 'seq', pairs + [(j, i) for i, j in pairs])  14.5 us
    ppermute x4, waiting for transfers between devices, section_shift(): lax.ppermute(block, 'section', [(i, (i + distance) % count) for i in rang...  5.42 us
    ppermute x3, starting transfers between devices, head_swap(): return lax.ppermute(block, 'head', [(0, 1), (1, 0)])  4.97 us
    ppermute x4, starting transfers between devices, section_shift(): lax.ppermute(block, 'section', [(i, (i + distance) % count) for i in rang...  4.16 us
    convert_element_type x2, other arithmetic, note_sum_of(): return (own + near.astype(F32) + far.astype(F32)).astype(BF16)  3.96 us
    ppermute x1, starting transfers between devices, across(): return lax.ppermute(block, ('seq', 'head'), route)  3.76 us
    ppermute x3, waiting for transfers between devices, head_swap(): return lax.ppermute(block, 'head', [(0, 1), (1, 0)])  3.37 us
  transfers between devices with their start and end apart: 17, of which 3 were waited for; matrix products, arithmetic and copies ran while one was open for 4% of the time, Pallas kernels for 59%

profile of v9, /device:TPU:1, one launch (start us, length us, event | category | flops | bytes accessed | tf_op | source)
XLA Modules:
  0.0 129.0 jit_solution(3283922468373920254)
XLA Ops:
  0.6 4.2 %key_values.1.refs_6_ = bf16[2,256,512]{2,1,0:T(8,128)(2,1)} custom-call(bf16[256,2048]{1,0:T(8,128)(2,1)} %bitcast.10, bf16[2048,1024]{1,0:T(8,128)(2,1)} %refs_5_.7, bf16[2048,1024]{1,0:T(8,128)(2,1)} %refs_9_.5), custom_call_target="tpu_custom_call" | custom-call | tf_op jit(solution)/shard_map/key_values/pallas_call | solution.py:67
  4.8 2.1 %collective-permute-start = (bf16[2,256,512]{2,1,0:T(8,128)(2,1)}, bf16[2,256,512]{2,1,0:T(8,128)(2,1)}, u32[]{:S(2)}, u32[]{:S(2)}) collective-permute-start(bf16[2,256,512]{2,1,0:T(8,128)(2,1)} %key_values.1.refs_6_), channel_id=1, source_target_pairs={{0,32},{32,64},{64,96},{96,0},{1,33},{33,65},{65,97},{97,1},{2,34}... | collective-permute-start | bytes 1572872 | tf_op jit(solution)/shard_map/ppermute | solution.py:30
  6.9 0.7 pad_add_fusion.refs_0_
  7.6 11.5 %key_values_and_queries.1 = (bf16[2,256,512]{2,1,0:T(8,128)(2,1)}, bf16[1024,1024]{1,0:T(8,128)(2,1)}, bf16[512,1024]{1,0:T(8,128)(2,1)}) custom-call(s32[3]{0:T(128)} %pad_add_fusion.refs_0_, bf16[256,2048]{1,0:T(8,128)(2,1)} %bitcast.11, bf16[2048,1024]{1,0:T(8,128)(2,1)} %refs_5_.7, bf16[2048,1024]{1,0:T(8,128)(2,1)} %refs_9_.5, ...), custom_call_target="tpu_custom_call" | custom-call | tf_op jit(solution)/shard_map/key_values_and_queries/pallas_call | solution.py:67
  19.1 1.3 collective-permute-start.1
  20.4 3.8 %collective-permute-start.6 = (bf16[512,1024]{1,0:T(8,128)(2,1)}, bf16[512,1024]{1,0:T(8,128)(2,1)}, u32[]{:S(2)}, u32[]{:S(2)}) collective-permute-start(bf16[512,1024]{1,0:T(8,128)(2,1)} %get-tuple-element.42), channel_id=1, source_target_pairs={{0,17},{1,16},{2,19},{3,18},{4,21},{5,20},{6,23},{7,22},{8,25},{9,... | collective-permute-start | bytes 3145736 | tf_op jit(solution)/shard_map/ppermute | solution.py:53
  24.2 0.0 collective-permute-done.refs_3_.refs_4_
  24.2 4.6 %collective-permute-start.3 = (bf16[2,256,512]{2,1,0:T(8,128)(2,1)}, bf16[2,256,512]{2,1,0:T(8,128)(2,1)}, u32[]{:S(2)}, u32[]{:S(2)}) collective-permute-start(bf16[2,256,512]{2,1,0:T(8,128)(2,1)} %collective-permute-done.refs_3_.refs_4_), channel_id=1, source_target_pairs={{2,4},{6,8},{10,12},{14,16},{18,20},{22,24},{26,28},{4,2},{8,6},{1... | collective-permute-start | bytes 1572872 | tf_op jit(solution)/shard_map/ppermute | solution.py:43
  28.8 0.1 collective-permute-start.2
  28.9 8.7 %grad_ctx.1.refs_3_ = bf16[1024,1024]{1,0:T(8,128)(2,1)} custom-call(bf16[1024,2048]{1,0:T(8,128)(2,1)} %bitcast.8, bf16[1024,2048]{1,0:T(8,128)(2,1)} %refs_1_.3, bf16[1024,1024]{1,0:T(8,128)(2,1)} %get-tuple-element.33.refs_2_, bf16[2,256,512]{2,1,0:T(8,128)(2,1)} %collective-permute-done.refs_3_.refs_4_), custom_call_target="tpu_custom_call" | custom-call | tf_op jit(solution)/shard_map/grad_ctx/pallas_call | solution.py:67
  37.6 0.0 collective-permute-done.1.refs_4_
  37.6 3.6 %collective-permute-start.5 = (bf16[2,256,512]{2,1,0:T(8,128)(2,1)}, bf16[2,256,512]{2,1,0:T(8,128)(2,1)}, u32[]{:S(2)}, u32[]{:S(2)}) collective-permute-start(bf16[2,256,512]{2,1,0:T(8,128)(2,1)} %collective-permute-done.1.refs_4_), channel_id=1, source_target_pairs={{2,4},{6,8},{10,12},{14,16},{18,20},{22,24},{26,28},{4,2},{8,6},{1... | collective-permute-start | bytes 1572872 | tf_op jit(solution)/shard_map/ppermute | solution.py:43
  41.2 0.3 collective-permute-start.4
  41.4 0.0 collective-permute-done.3.refs_6_
  41.4 0.0 collective-permute-done.2.refs_5_
  41.5 14.3 %attention.2 = (bf16[1024,512]{1,0:T(8,128)(2,1)}, f32[2,256,512]{2,1,0:T(8,128)}, bf16[2,256,512]{2,1,0:T(8,128)(2,1)}, bf16[2,256,512]{2,1,0:T(8,128)(2,1)}) custom-call(s32[3]{0:T(128)} %pad_add_fusion.refs_0_, s32[2,8]{1,0:T(2,128)} %bitcast.13, bf16[1024,1024]{1,0:T(8,128)(2,1)} %get-tuple-element.33.refs_2_, bf16[1024,1024]{1,0:T(8,128)(2,1)} %grad_ctx.1.refs_3_, ...), custom_call_target="tpu_custom_call" | custom-call | tf_op jit(solution)/shard_map/attention/pallas_call | solution.py:67
  55.7 0.0 collective-permute-done.5.refs_6_
  55.7 0.0 collective-permute-done.4.refs_5_
  55.7 0.7 collective-permute-start.13
  56.4 0.0 collective-permute-done.6.refs_4_
  56.4 0.8 collective-permute-start.7
  57.2 3.1 %collective-permute-start.8 = (bf16[2,256,512]{2,1,0:T(8,128)(2,1)}, bf16[2,256,512]{2,1,0:T(8,128)(2,1)}, u32[]{:S(2)}, u32[]{:S(2)}) collective-permute-start(bf16[2,256,512]{2,1,0:T(8,128)(2,1)} %get-tuple-element.47), channel_id=1, source_target_pairs={{2,4},{6,8},{10,12},{14,16},{18,20},{22,24},{26,28},{4,2},{8,6},{1... | collective-permute-start | bytes 1572872 | tf_op jit(solution)/shard_map/ppermute | solution.py:43
  60.3 14.4 %attention.3 = (bf16[1024,512]{1,0:T(8,128)(2,1)}, f32[2,256,512]{2,1,0:T(8,128)}, bf16[2,256,512]{2,1,0:T(8,128)(2,1)}, bf16[2,256,512]{2,1,0:T(8,128)(2,1)}) custom-call(s32[3]{0:T(128)} %pad_add_fusion.refs_0_, s32[2,8]{1,0:T(2,128)} %bitcast.14, bf16[1024,1024]{1,0:T(8,128)(2,1)} %get-tuple-element.33.refs_2_, bf16[1024,1024]{1,0:T(8,128)(2,1)} %grad_ctx.1.refs_3_, ...), custom_call_target="tpu_custom_call" | custom-call | flops 12079595520 | tf_op jit(solution)/shard_map/attention/pallas_call | solution.py:67
  74.6 0.0 collective-permute-done.7
  74.6 0.0 collective-permute-done.8
  74.6 0.1 collective-permute-start.9
  74.7 3.3 %collective-permute-start.10 = (bf16[2,256,512]{2,1,0:T(8,128)(2,1)}, bf16[2,256,512]{2,1,0:T(8,128)(2,1)S(1)}, u32[]{:S(2)}, u32[]{:S(2)}) collective-permute-start(bf16[2,256,512]{2,1,0:T(8,128)(2,1)} %get-tuple-element.51), channel_id=1, source_target_pairs={{2,4},{6,8},{10,12},{14,16},{18,20},{22,24},{26,28},{4,2},{8,6},{1... | collective-permute-start | bytes 1572872 | tf_op jit(solution)/shard_map/ppermute | solution.py:43
  78.0 1.7 %add_convert_fusion.1 = bf16[2,256,512]{2,1,0:T(8,128)(2,1)S(1)} fusion(bf16[2,256,512]{2,1,0:T(8,128)(2,1)} %collective-permute-done.8, f32[2,256,512]{2,1,0:T(8,128)} %get-tuple-element.52, bf16[2,256,512]{2,1,0:T(8,128)(2,1)} %collective-permute-done.7), kind=kLoop, calls=%fused_computation.1 | loop fusion | flops 1310720 | bytes 2621440 | tf_op jit(solution)/shard_map/convert_element_type | solution.py:471
  79.7 0.3 collective-permute-start.12
  80.1 2.8 %collective-permute-start.15 = (bf16[1024,512]{1,0:T(8,128)(2,1)}, bf16[1024,512]{1,0:T(8,128)(2,1)}, u32[]{:S(2)}, u32[]{:S(2)}) collective-permute-start(bf16[1024,512]{1,0:T(8,128)(2,1)} %get-tuple-element.57.refs_2_), channel_id=1, source_target_pairs={{0,1},{1,0},{2,3},{3,2},{4,5},{5,4},{6,7},{7,6},{8,9},{9,8},{10,11... | collective-permute-start | bytes 3145736 | tf_op jit(solution)/shard_map/ppermute | solution.py:47
  82.9 0.0 collective-permute-done.9
  82.9 3.0 %collective-permute-done.10 = bf16[2,256,512]{2,1,0:T(8,128)(2,1)S(1)} collective-permute-done((bf16[2,256,512]{2,1,0:T(8,128)(2,1)}, bf16[2,256,512]{2,1,0:T(8,128)(2,1)S(1)}, u32[]{:S(2)}, u32[]{:S(2)}) %collective-permute-start.10) | collective-permute-done | bytes 524320 | tf_op jit(solution)/shard_map/ppermute | solution.py:43
  85.8 2.2 %add_convert_fusion.2.refs_10_ = bf16[2,256,512]{2,1,0:T(8,128)(2,1)} fusion(bf16[2,256,512]{2,1,0:T(8,128)(2,1)S(1)} %collective-permute-done.10, f32[2,256,512]{2,1,0:T(8,128)} %get-tuple-element.45, bf16[2,256,512]{2,1,0:T(8,128)(2,1)S(1)} %collective-permute-done.9), kind=kLoop, calls=%fused_computation.2 | loop fusion | flops 1310720 | bytes 2621440 | tf_op jit(solution)/shard_map/convert_element_type | solution.py:471
  88.1 0.5 collective-permute-start.11
  88.5 5.4 %collective-permute-done.12.refs_1_ = bf16[2,256,512]{2,1,0:T(8,128)(2,1)} collective-permute-done((bf16[2,256,512]{2,1,0:T(8,128)(2,1)S(1)}, bf16[2,256,512]{2,1,0:T(8,128)(2,1)}, u32[]{:S(2)}, u32[]{:S(2)}) %collective-permute-start.12) | collective-permute-done | bytes 524320 | tf_op jit(solution)/shard_map/ppermute | solution.py:30
  93.9 5.3 %note_product.3.refs_4_.refs_10_ = f32[2,256,1024]{2,1,0:T(8,128)} custom-call(s32[3]{0:T(128)} %pad_add_fusion.refs_0_, bf16[2,256,512]{2,1,0:T(8,128)(2,1)} %collective-permute-done.12.refs_1_, bf16[2048,1024]{1,0:T(8,128)(2,1)} %refs_5_.7, bf16[2048,1024]{1,0:T(8,128)(2,1)} %refs_5_.7, bf16[2048,1024]{1,0:T(8,128)(2,1)} %refs_5_.7, ...), custom_call_target="tpu_custom_call" | custom-call | tf_op jit(solution)/shard_map/note_product/pallas_call | solution.py:67
  99.2 0.0 collective-permute-done.13.refs_5_.refs_1_
  99.2 6.7 %frame_own.1.refs_11_.refs_3_ = bf16[1024,1024]{1,0:T(8,128)(2,1)} custom-call(s32[3]{0:T(128)} %pad_add_fusion.refs_0_, bf16[1024,512]{1,0:T(8,128)(2,1)} %get-tuple-element.44.refs_7_.refs_1_, bf16[1024,512]{1,0:T(8,128)(2,1)} %get-tuple-element.57.refs_2_, bf16[2048,1024]{1,0:T(8,128)(2,1)} %refs_3_.7, f32[2,256,1024]{2,1,0:T(8,128)} %note_product.3.refs_4_.refs_10_, ...), custom_call_target="tpu_custom_call" | custom-call | flops 8589934592 | tf_op jit(solution)/shard_map/frame_own/pallas_call | solution.py:67
  106.0 0.1 collective-permute-start.16
  106.0 0.0 collective-permute-done.11.refs_1_
  106.1 4.3 %note_product.4.refs_11_ = bf16[1,256,1024]{2,1,0:T(8,128)(2,1)} custom-call(s32[3]{0:T(128)} %pad_add_fusion.refs_0_, bf16[2,256,512]{2,1,0:T(8,128)(2,1)} %collective-permute-done.11.refs_1_, bf16[2048,1024]{1,0:T(8,128)(2,1)} %refs_5_.7, bf16[2048,1024]{1,0:T(8,128)(2,1)} %refs_5_.7, bf16[2048,1024]{1,0:T(8,128)(2,1)} %refs_5_.7, ...), custom_call_target="tpu_custom_call" | custom-call | tf_op jit(solution)/shard_map/note_product/pallas_call | solution.py:67
  110.4 1.5 %collective-permute-start.14 = (bf16[1,256,1024]{2,1,0:T(8,128)(2,1)}, bf16[1,256,1024]{2,1,0:T(8,128)(2,1)}, u32[]{:S(2)}, u32[]{:S(2)}) collective-permute-start(bf16[1,256,1024]{2,1,0:T(8,128)(2,1)} %note_product.4.refs_11_), channel_id=1, source_target_pairs={{0,1},{1,0},{2,3},{3,2},{4,5},{5,4},{6,7},{7,6},{8,9},{9,8},{10,11... | collective-permute-start | bytes 1572872 | tf_op jit(solution)/shard_map/ppermute | solution.py:47
  111.9 4.3 %note_product.5.refs_6_ = bf16[1,256,1024]{2,1,0:T(8,128)(2,1)} custom-call(s32[3]{0:T(128)} %pad_add_fusion.refs_0_, bf16[2,256,512]{2,1,0:T(8,128)(2,1)} %collective-permute-done.11.refs_1_, bf16[2048,1024]{1,0:T(8,128)(2,1)} %refs_5_.7, bf16[2048,1024]{1,0:T(8,128)(2,1)} %refs_5_.7, bf16[2048,1024]{1,0:T(8,128)(2,1)} %refs_5_.7, ...), custom_call_target="tpu_custom_call" | custom-call | tf_op jit(solution)/shard_map/note_product/pallas_call | solution.py:67
  116.2 0.0 collective-permute-done.15.refs_2_
  116.2 0.0 collective-permute-done.16.refs_5_
  116.2 7.3 %frame_sum.1 = bf16[1024,1024]{1,0:T(8,128)(2,1)} custom-call(s32[3]{0:T(128)} %pad_add_fusion.refs_0_, bf16[1024,512]{1,0:T(8,128)(2,1)} %collective-permute-done.13.refs_5_.refs_1_, bf16[1024,512]{1,0:T(8,128)(2,1)} %collective-permute-done.15.refs_2_, bf16[1024,1024]{1,0:T(8,128)(2,1)} %frame_own.1.refs_11_.refs_3_, ...), custom_call_target="tpu_custom_call" | custom-call | tf_op jit(solution)/shard_map/frame_sum/pallas_call | solution.py:67
  123.5 3.4 %collective-permute-done.14 = bf16[1,256,1024]{2,1,0:T(8,128)(2,1)} collective-permute-done((bf16[1,256,1024]{2,1,0:T(8,128)(2,1)}, bf16[1,256,1024]{2,1,0:T(8,128)(2,1)}, u32[]{:S(2)}, u32[]{:S(2)}) %collective-permute-start.14) | collective-permute-done | bytes 524320 | tf_op jit(solution)/shard_map/ppermute | solution.py:47
  126.8 2.2 %add_convert_fusion = bf16[1,256,1024]{2,1,0:T(8,128)(2,1)} fusion(bf16[1,256,1024]{2,1,0:T(8,128)(2,1)} %collective-permute-done.14, bf16[1,256,1024]{2,1,0:T(8,128)(2,1)} %note_product.5.refs_6_), kind=kLoop, calls=%fused_computation | loop fusion | flops 1048576 | bytes 1572864 | tf_op jit(solution)/shard_map/convert_element_type | solution.py:506
Async XLA Ops:
  4.8 19.4 %collective-permute-start = (bf16[2,256,512]{2,1,0:T(8,128)(2,1)}, bf16[2,256,512]{2,1,0:T(8,128)(2,1)}, u32[]{:S(2)}, u32[]{:S(2)}) collective-permute-start(bf16[2,256,512]{2,1,0:T(8,128)(2,1)} %key_values.1.refs_6_), channel_id=1, source_target_pairs={{0,32},{32,64},{64,96},{96,0},{1,33},{33,65},{65,97},{97,1},{2,34}... | collective-permute-start | bytes 1572872 | tf_op jit(solution)/shard_map/ppermute | solution.py:30
  19.1 18.4 %collective-permute-start.1 = (bf16[2,256,512]{2,1,0:T(8,128)(2,1)}, bf16[2,256,512]{2,1,0:T(8,128)(2,1)}, u32[]{:S(2)}, u32[]{:S(2)}) collective-permute-start(bf16[2,256,512]{2,1,0:T(8,128)(2,1)} %get-tuple-element.34), channel_id=1, source_target_pairs={{0,32},{32,64},{64,96},{96,0},{1,33},{33,65},{65,97},{97,1},{2,34}... | collective-permute-start | bytes 1572872 | tf_op jit(solution)/shard_map/ppermute | solution.py:30
  20.4 36.0 %collective-permute-start.6 = (bf16[512,1024]{1,0:T(8,128)(2,1)}, bf16[512,1024]{1,0:T(8,128)(2,1)}, u32[]{:S(2)}, u32[]{:S(2)}) collective-permute-start(bf16[512,1024]{1,0:T(8,128)(2,1)} %get-tuple-element.42), channel_id=1, source_target_pairs={{0,17},{1,16},{2,19},{3,18},{4,21},{5,20},{6,23},{7,22},{8,25},{9,... | collective-permute-start | bytes 3145736 | tf_op jit(solution)/shard_map/ppermute | solution.py:53
  24.2 17.3 %collective-permute-start.3 = (bf16[2,256,512]{2,1,0:T(8,128)(2,1)}, bf16[2,256,512]{2,1,0:T(8,128)(2,1)}, u32[]{:S(2)}, u32[]{:S(2)}) collective-permute-start(bf16[2,256,512]{2,1,0:T(8,128)(2,1)} %collective-permute-done.refs_3_.refs_4_), channel_id=1, source_target_pairs={{2,4},{6,8},{10,12},{14,16},{18,20},{22,24},{26,28},{4,2},{8,6},{1... | collective-permute-start | bytes 1572872 | tf_op jit(solution)/shard_map/ppermute | solution.py:43
  28.8 12.7 %collective-permute-start.2 = (bf16[2,256,512]{2,1,0:T(8,128)(2,1)}, bf16[2,256,512]{2,1,0:T(8,128)(2,1)}, u32[]{:S(2)}, u32[]{:S(2)}) collective-permute-start(bf16[2,256,512]{2,1,0:T(8,128)(2,1)} %collective-permute-done.refs_3_.refs_4_), channel_id=1, source_target_pairs={{0,2},{2,0},{4,6},{6,4},{8,10},{10,8},{12,14},{14,12},{16,18},{18,... | collective-permute-start | bytes 1572872 | tf_op jit(solution)/shard_map/ppermute | solution.py:37
  37.6 18.2 %collective-permute-start.5 = (bf16[2,256,512]{2,1,0:T(8,128)(2,1)}, bf16[2,256,512]{2,1,0:T(8,128)(2,1)}, u32[]{:S(2)}, u32[]{:S(2)}) collective-permute-start(bf16[2,256,512]{2,1,0:T(8,128)(2,1)} %collective-permute-done.1.refs_4_), channel_id=1, source_target_pairs={{2,4},{6,8},{10,12},{14,16},{18,20},{22,24},{26,28},{4,2},{8,6},{1... | collective-permute-start | bytes 1572872 | tf_op jit(solution)/shard_map/ppermute | solution.py:43
  41.2 14.6 %collective-permute-start.4 = (bf16[2,256,512]{2,1,0:T(8,128)(2,1)}, bf16[2,256,512]{2,1,0:T(8,128)(2,1)}, u32[]{:S(2)}, u32[]{:S(2)}) collective-permute-start(bf16[2,256,512]{2,1,0:T(8,128)(2,1)} %collective-permute-done.1.refs_4_), channel_id=1, source_target_pairs={{0,2},{2,0},{4,6},{6,4},{8,10},{10,8},{12,14},{14,12},{16,18},{18,... | collective-permute-start | bytes 1572872 | tf_op jit(solution)/shard_map/ppermute | solution.py:37
  55.7 43.5 %collective-permute-start.13 = (bf16[1024,512]{1,0:T(8,128)(2,1)}, bf16[1024,512]{1,0:T(8,128)(2,1)}, u32[]{:S(2)}, u32[]{:S(2)}) collective-permute-start(bf16[1024,512]{1,0:T(8,128)(2,1)} %get-tuple-element.44.refs_7_.refs_1_), channel_id=1, source_target_pairs={{0,1},{1,0},{2,3},{3,2},{4,5},{5,4},{6,7},{7,6},{8,9},{9,8},{10,11... | collective-permute-start | bytes 3145736 | tf_op jit(solution)/shard_map/ppermute | solution.py:47
  56.4 18.2 %collective-permute-start.7 = (bf16[2,256,512]{2,1,0:T(8,128)(2,1)}, bf16[2,256,512]{2,1,0:T(8,128)(2,1)}, u32[]{:S(2)}, u32[]{:S(2)}) collective-permute-start(bf16[2,256,512]{2,1,0:T(8,128)(2,1)} %get-tuple-element.46), channel_id=1, source_target_pairs={{0,2},{2,0},{4,6},{6,4},{8,10},{10,8},{12,14},{14,12},{16,18},{18,... | collective-permute-start | bytes 1572872 | tf_op jit(solution)/shard_map/ppermute | solution.py:37
  57.2 17.5 %collective-permute-start.8 = (bf16[2,256,512]{2,1,0:T(8,128)(2,1)}, bf16[2,256,512]{2,1,0:T(8,128)(2,1)}, u32[]{:S(2)}, u32[]{:S(2)}) collective-permute-start(bf16[2,256,512]{2,1,0:T(8,128)(2,1)} %get-tuple-element.47), channel_id=1, source_target_pairs={{2,4},{6,8},{10,12},{14,16},{18,20},{22,24},{26,28},{4,2},{8,6},{1... | collective-permute-start | bytes 1572872 | tf_op jit(solution)/shard_map/ppermute | solution.py:43
  74.6 8.2 %collective-permute-start.9 = (bf16[2,256,512]{2,1,0:T(8,128)(2,1)}, bf16[2,256,512]{2,1,0:T(8,128)(2,1)S(1)}, u32[]{:S(2)}, u32[]{:S(2)}) collective-permute-start(bf16[2,256,512]{2,1,0:T(8,128)(2,1)} %get-tuple-element.50), channel_id=1, source_target_pairs={{0,2},{2,0},{4,6},{6,4},{8,10},{10,8},{12,14},{14,12},{16,18},{18,... | collective-permute-start | bytes 1572872 | tf_op jit(solution)/shard_map/ppermute | solution.py:37
  74.7 11.1 %collective-permute-start.10 = (bf16[2,256,512]{2,1,0:T(8,128)(2,1)}, bf16[2,256,512]{2,1,0:T(8,128)(2,1)S(1)}, u32[]{:S(2)}, u32[]{:S(2)}) collective-permute-start(bf16[2,256,512]{2,1,0:T(8,128)(2,1)} %get-tuple-element.51), channel_id=1, source_target_pairs={{2,4},{6,8},{10,12},{14,16},{18,20},{22,24},{26,28},{4,2},{8,6},{1... | collective-permute-start | bytes 1572872 | tf_op jit(solution)/shard_map/ppermute | solution.py:43
  79.7 14.2 %collective-permute-start.12 = (bf16[2,256,512]{2,1,0:T(8,128)(2,1)S(1)}, bf16[2,256,512]{2,1,0:T(8,128)(2,1)}, u32[]{:S(2)}, u32[]{:S(2)}) collective-permute-start(bf16[2,256,512]{2,1,0:T(8,128)(2,1)S(1)} %add_convert_fusion.1), channel_id=1, source_target_pairs={{0,96},{32,0},{64,32},{96,64},{1,97},{33,1},{65,33},{97,65},{2,98}... | collective-permute-start | bytes 1572872 | tf_op jit(solution)/shard_map/ppermute | solution.py:30
  80.1 36.1 %collective-permute-start.15 = (bf16[1024,512]{1,0:T(8,128)(2,1)}, bf16[1024,512]{1,0:T(8,128)(2,1)}, u32[]{:S(2)}, u32[]{:S(2)}) collective-permute-start(bf16[1024,512]{1,0:T(8,128)(2,1)} %get-tuple-element.57.refs_2_), channel_id=1, source_target_pairs={{0,1},{1,0},{2,3},{3,2},{4,5},{5,4},{6,7},{7,6},{8,9},{9,8},{10,11... | collective-permute-start | bytes 3145736 | tf_op jit(solution)/shard_map/ppermute | solution.py:47
  88.1 18.0 %collective-permute-start.11 = (bf16[2,256,512]{2,1,0:T(8,128)(2,1)}, bf16[2,256,512]{2,1,0:T(8,128)(2,1)}, u32[]{:S(2)}, u32[]{:S(2)}) collective-permute-start(bf16[2,256,512]{2,1,0:T(8,128)(2,1)} %add_convert_fusion.2.refs_10_), channel_id=1, source_target_pairs={{0,96},{32,0},{64,32},{96,64},{1,97},{33,1},{65,33},{97,65},{2,98}... | collective-permute-start | bytes 1572872 | tf_op jit(solution)/shard_map/ppermute | solution.py:30
  106.0 10.3 %collective-permute-start.16 = (bf16[512,1024]{1,0:T(8,128)(2,1)}, bf16[512,1024]{1,0:T(8,128)(2,1)}, u32[]{:S(2)}, u32[]{:S(2)}) collective-permute-start(bf16[512,1024]{1,0:T(8,128)(2,1)} %collective-permute-done.6.refs_4_), channel_id=1, source_target_pairs={{0,2},{2,0},{4,6},{6,4},{8,10},{10,8},{12,14},{14,12},{16,18},{18,... | collective-permute-start | bytes 3145736 | tf_op jit(solution)/shard_map/ppermute | solution.py:37
  110.4 16.5 %collective-permute-start.14 = (bf16[1,256,1024]{2,1,0:T(8,128)(2,1)}, bf16[1,256,1024]{2,1,0:T(8,128)(2,1)}, u32[]{:S(2)}, u32[]{:S(2)}) collective-permute-start(bf16[1,256,1024]{2,1,0:T(8,128)(2,1)} %note_product.4.refs_11_), channel_id=1, source_target_pairs={{0,1},{1,0},{2,3},{3,2},{4,5},{5,4},{6,7},{7,6},{8,9},{9,8},{10,11... | collective-permute-start | bytes 1572872 | tf_op jit(solution)/shard_map/ppermute | solution.py:47

commit v10 on v9

--- a/solution.py
+++ b/solution.py
@@ -182,12 +182,12 @@
         return sent
 
 
-def key_values_and_queries(scalars, notes, w_key, w_value, frames, w_query, h0, hc, after):
+def key_values_and_queries(notes, w_key, w_value, frames, w_query, h0, hc, after):
     rows = notes.shape[0]
     quarter = D // 4
     product = Product(frames, w_query, NN)
 
-    def body(s_ref, notes_ref, wk_ref, wv_ref, f_ref, wq_ref, out_ref, q_ref, give_ref,
+    def body(notes_ref, wk_ref, wv_ref, f_ref, wq_ref, out_ref, q_ref, give_ref,
              n_scr, wk_scr, wv_scr, out_scr, sems, *scrs):
         (notes_in,) = start_all([pltpu.make_async_copy(notes_ref, n_scr, sems.at[2])])
         weights_in = key_value_copies(wk_ref, wv_ref, wk_scr, wv_scr, sems, h0, hc)
@@ -198,7 +198,9 @@
             out_scr[i] = dot(n_scr[...], scr[...], NN).astype(BF16)
         sent = start_all([pltpu.make_async_copy(out_scr, out_ref, sems.at[3])])
         sent += product.finish(copies, q_ref, *scrs)
-        offset = pl.multiple_of((1 - s_ref[0]) * (2 * quarter) + s_ref[1] * quarter, quarter)
+        group = lax.axis_index("head")
+        core = lax.rem(lax.axis_index("seq"), 2)
+        offset = pl.multiple_of((1 - group) * (2 * quarter) + core * quarter, quarter)
         give = pltpu.make_async_copy(scrs[1].at[pl.ds(offset, quarter), :], give_ref, sems.at[4])
         sent += start_all([give])
         for copy in sent:
@@ -215,10 +217,9 @@
             product.out,
             jax.ShapeDtypeStruct((quarter, w_query.shape[1]), BF16),
         ],
-        (scalars, notes, w_key, w_value, frames, w_query),
+        (notes, w_key, w_value, frames, w_query),
         "key_values_and_queries",
         after,
-        scalars=1,
         scratch=[
             pltpu.VMEM((rows, D), BF16),
             pltpu.VMEM((D, hc * HD), BF16),
@@ -323,37 +324,32 @@
 def note_product(scalars, grads, chunks, w_key, w_value, after, before=None, which=(0, 1)):
     nt = grads[0].shape[1]
     half = D // 2
-    heads = [h for h0, hc in chunks for h in range(h0, h0 + hc)]
-    hc = len(heads)
+    ((h0, hc),) = chunks
     last = before is not None
     start = which[0]
 
     def body(s_ref, *refs):
         grad_refs, refs = refs[: len(grads)], refs[len(grads) :]
-        wk = jnp.concatenate([r[...] for r in refs[:hc]], axis=1)
-        wv = jnp.concatenate([r[...] for r in refs[hc : 2 * hc]], axis=1)
-        gk = jnp.concatenate([r[0] for r in grad_refs], axis=1)
-        gv = jnp.concatenate([r[1] for r in grad_refs], axis=1)
-        total = dot(gk, wk, NT) + dot(gv, wv, NT)
+        grad_ref = grad_refs[0]
+        total = dot(grad_ref[0], refs[0][...], NT) + dot(grad_ref[1], refs[1][...], NT)
         if last:
-            total = total + refs[2 * hc][0]
+            total = total + refs[2][0]
         out_ref = refs[-1]
         out_ref[0] = total.astype(out_ref.dtype)
 
-    def weight_in(h):
-        return pl.BlockSpec(
-            (half, HD), lambda n, s: (jnp.where(n + start == 0, 1 - s[0], s[0]), h)
-        )
+    weight_in = pl.BlockSpec(
+        (half, hc * HD), lambda n, s: (jnp.where(n + start == 0, 1 - s[0], s[0]), h0 // hc)
+    )
 
     return call(
         body,
         (len(which),),
         [pl.BlockSpec(g.shape, lambda n, s: (0, 0, 0)) for g in grads]
-        + [weight_in(h) for h in heads] * 2
+        + [weight_in] * 2
         + ([pl.BlockSpec((1, nt, half), lambda n, s: (n + start, 0, 0))] if last else []),
         pl.BlockSpec((1, nt, half), lambda n, s: (n, 0, 0)),
         jax.ShapeDtypeStruct((len(which), nt, half), BF16 if last else F32),
-        (scalars, *grads) + (w_key,) * hc + (w_value,) * hc + ((before,) if last else ()),
+        (scalars, *grads, w_key, w_value) + ((before,) if last else ()),
         "note_product",
         after,
         scalars=1,
@@ -361,14 +357,14 @@
 
 
 def attention_body(
-    s_ref, band_ref, q_ref, g_ref, kvo_ref, kvn_ref, kvf_ref, dq_ref, own_ref, near_ref, far_ref,
+    band_ref, q_ref, g_ref, kvo_ref, kvn_ref, kvf_ref, dq_ref, own_ref, near_ref, far_ref,
     p_scr, ds_scr, bias_ref,
 ):
     @pl.when(pl.program_id(0) == 0)
     def _():
         row = lax.broadcasted_iota(jnp.int32, (8, BLK), 0)
-        shard = s_ref[2]
-        far = shard - 1 + 2 * s_ref[1]
+        shard = lax.axis_index("seq")
+        far = shard - 1 + 2 * lax.rem(shard, 2)
         block = jnp.where(row < 2, 2 * shard, jnp.where(row < 4, 2 * (shard ^ 1), 2 * far)) + row % 2
         for b in range(q_ref.shape[0] // BLK):
             inside = (block >= band_ref[0, b]) & (block <= band_ref[1, b])
@@ -414,27 +410,27 @@
         far_ref[i] = grad[2 * nt :].astype(BF16)
 
 
-def attention(scalars, band, queries, grad_ctx, kv_own, kv_near, kv_far, h0, hc, after):
+def attention(band, queries, grad_ctx, kv_own, kv_near, kv_far, h0, hc, after):
     frames = queries.shape[0]
     nt = kv_own.shape[1]
-    frame_in = pl.BlockSpec((frames, HD), lambda h, s, b: (0, h0 + h))
-    note_io = pl.BlockSpec((2, nt, HD), lambda h, s, b: (0, 0, h))
+    frame_in = pl.BlockSpec((frames, HD), lambda h, b: (0, h0 + h))
+    note_io = pl.BlockSpec((2, nt, HD), lambda h, b: (0, 0, h))
     notes_out = jax.ShapeDtypeStruct((2, nt, hc * HD), BF16)
     return call(
         attention_body,
         (hc,),
         [frame_in, frame_in, note_io, note_io, note_io],
-        [pl.BlockSpec((frames, HD), lambda h, s, b: (0, h)), note_io, note_io, note_io],
+        [pl.BlockSpec((frames, HD), lambda h, b: (0, h)), note_io, note_io, note_io],
         [
             jax.ShapeDtypeStruct((frames, hc * HD), BF16),
             jax.ShapeDtypeStruct((2, nt, hc * HD), F32),
             notes_out,
             notes_out,
         ],
-        (scalars, band, queries, grad_ctx, kv_own, kv_near, kv_far),
+        (band, queries, grad_ctx, kv_own, kv_near, kv_far),
         "attention",
         after,
-        scalars=2,
+        scalars=1,
         scratch=[
             pltpu.VMEM((3 * nt, frames), BF16),
             pltpu.VMEM((3 * nt, frames), BF16),
@@ -453,7 +449,7 @@
 
     made0 = key_values(notes[0], w_key, w_value, *CHUNKS[0])
     made1, queries, given = key_values_and_queries(
-        scalars, notes[0], w_key, w_value, frames[0], w_query, *CHUNKS[1], (made0,)
+        notes[0], w_key, w_value, frames[0], w_query, *CHUNKS[1], (made0,)
     )
     moved = [section_shift(made0, 1), section_shift(made1, 1)]
     w_mine = across(given)
@@ -464,7 +460,7 @@
 
     def attend(step, near, far, after):
         return attention(
-            scalars, band, queries, grad_ctx, moved[step], near, far, *CHUNKS[step], after
+            band, queries, grad_ctx, moved[step], near, far, *CHUNKS[step], after
         )
 
     def note_sum_of(own, near, far):

time: 130 us -> 129 us (level)
  waiting for transfers between devices: 11.8 us -> 8.22 us
  starting transfers between devices: 28.7 us -> 31.5 us
  Pallas kernels: 80.9 us -> 79.6 us
    ppermute x5, starting transfers between devices: 1.28 us -> 4.06 us  [near_swap(): return lax.ppermute(block, 'seq', [(i, i ^ 1) for i in range(count)])]
    ppermute x4, waiting for transfers between devices: 5.42 us -> 2.66 us  [section_shift(): lax.ppermute(block, 'section', [(i, (i + distance) % count) for i in rang...]
    ppermute x4, starting transfers between devices: 14.5 us -> 12.4 us  [far_swap(): return lax.ppermute(block, 'seq', pairs + [(j, i) for i, j in pairs])]
    ppermute x4, starting transfers between devices: 4.16 us -> 5.92 us  [section_shift(): lax.ppermute(block, 'section', [(i, (i + distance) % count) for i in rang...]
where the time goes in v10:
time: 129 us; the launch traced here: 127 us
  Pallas kernels  79.6 us (62%)
  starting transfers between devices  31.5 us (24%)
  waiting for transfers between devices  8.22 us (6%)
  other arithmetic  6.73 us (5%)
    pallas_call x10, Pallas kernels, call(): pl.pallas_call(reads, grid_spec=pltpu.PrefetchScalarGridSpec(num_scalar_p...  79.6 us
    ppermute x4, starting transfers between devices, far_swap(): return lax.ppermute(block, 'seq', pairs + [(j, i) for i, j in pairs])  12.4 us
    ppermute x4, starting transfers between devices, section_shift(): lax.ppermute(block, 'section', [(i, (i + distance) % count) for i in rang...  5.92 us
    ppermute x3, starting transfers between devices, head_swap(): return lax.ppermute(block, 'head', [(0, 1), (1, 0)])  5.35 us
    ppermute x5, starting transfers between devices, near_swap(): return lax.ppermute(block, 'seq', [(i, i ^ 1) for i in range(count)])  4.06 us
    convert_element_type x2, other arithmetic, note_sum_of(): return (own + near.astype(F32) + far.astype(F32)).astype(BF16)  3.96 us
    ppermute x1, starting transfers between devices, across(): return lax.ppermute(block, ('seq', 'head'), route)  3.76 us
    ppermute x4, waiting for transfers between devices, far_swap(): return lax.ppermute(block, 'seq', pairs + [(j, i) for i, j in pairs])  2.81 us
  transfers between devices with their start and end apart: 17, of which 3 were waited for; matrix products, arithmetic and copies ran while one was open for 4% of the time, Pallas kernels for 59%

profile of v10, /device:TPU:1, one launch (start us, length us, event | category | flops | bytes accessed | tf_op | source)
XLA Modules:
  0.0 126.9 jit_solution(3430273301731358948)
XLA Ops:
  0.6 4.2 %key_values.1.refs_5_ = bf16[2,256,512]{2,1,0:T(8,128)(2,1)} custom-call(bf16[256,2048]{1,0:T(8,128)(2,1)} %bitcast.9, bf16[2048,1024]{1,0:T(8,128)(2,1)} %refs_2_.9, bf16[2048,1024]{1,0:T(8,128)(2,1)} %refs_3_.7), custom_call_target="tpu_custom_call" | custom-call | tf_op jit(solution)/shard_map/key_values/pallas_call | solution.py:67
  4.8 2.1 %collective-permute-start = (bf16[2,256,512]{2,1,0:T(8,128)(2,1)}, bf16[2,256,512]{2,1,0:T(8,128)(2,1)}, u32[]{:S(2)}, u32[]{:S(2)}) collective-permute-start(bf16[2,256,512]{2,1,0:T(8,128)(2,1)} %key_values.1.refs_5_), channel_id=1, source_target_pairs={{0,32},{32,64},{64,96},{96,0},{1,33},{33,65},{65,97},{97,1},{2,34}... | collective-permute-start | bytes 1572872 | tf_op jit(solution)/shard_map/ppermute | solution.py:30
  6.9 10.9 %key_values_and_queries.1 = (bf16[2,256,512]{2,1,0:T(8,128)(2,1)}, bf16[1024,1024]{1,0:T(8,128)(2,1)}, bf16[512,1024]{1,0:T(8,128)(2,1)}) custom-call(bf16[256,2048]{1,0:T(8,128)(2,1)} %bitcast.10, bf16[2048,1024]{1,0:T(8,128)(2,1)} %refs_2_.9, bf16[2048,1024]{1,0:T(8,128)(2,1)} %refs_3_.7, bf16[1024,2048]{1,0:T(8,128)(2,1)} %bitcast.11, ...), custom_call_target="tpu_custom_call" | custom-call | tf_op jit(solution)/shard_map/key_values_and_queries/pallas_call | solution.py:67
  17.8 1.3 %collective-permute-start.1 = (bf16[2,256,512]{2,1,0:T(8,128)(2,1)}, bf16[2,256,512]{2,1,0:T(8,128)(2,1)}, u32[]{:S(2)}, u32[]{:S(2)}) collective-permute-start(bf16[2,256,512]{2,1,0:T(8,128)(2,1)} %get-tuple-element.34), channel_id=1, source_target_pairs={{0,32},{32,64},{64,96},{96,0},{1,33},{33,65},{65,97},{97,1},{2,34}... | collective-permute-start | bytes 1572872 | tf_op jit(solution)/shard_map/ppermute | solution.py:30
  19.1 3.8 %collective-permute-start.6 = (bf16[512,1024]{1,0:T(8,128)(2,1)}, bf16[512,1024]{1,0:T(8,128)(2,1)}, u32[]{:S(2)}, u32[]{:S(2)}) collective-permute-start(bf16[512,1024]{1,0:T(8,128)(2,1)} %get-tuple-element.42), channel_id=1, source_target_pairs={{0,17},{1,16},{2,19},{3,18},{4,21},{5,20},{6,23},{7,22},{8,25},{9,... | collective-permute-start | bytes 3145736 | tf_op jit(solution)/shard_map/ppermute | solution.py:53
  22.8 0.0 collective-permute-done.refs_3_
  22.8 1.5 %collective-permute-start.2 = (bf16[2,256,512]{2,1,0:T(8,128)(2,1)}, bf16[2,256,512]{2,1,0:T(8,128)(2,1)}, u32[]{:S(2)}, u32[]{:S(2)}) collective-permute-start(bf16[2,256,512]{2,1,0:T(8,128)(2,1)} %collective-permute-done.refs_3_), channel_id=1, source_target_pairs={{0,2},{2,0},{4,6},{6,4},{8,10},{10,8},{12,14},{14,12},{16,18},{18,... | collective-permute-start | bytes 1572872 | tf_op jit(solution)/shard_map/ppermute | solution.py:37
  24.4 3.1 %collective-permute-start.3 = (bf16[2,256,512]{2,1,0:T(8,128)(2,1)}, bf16[2,256,512]{2,1,0:T(8,128)(2,1)}, u32[]{:S(2)}, u32[]{:S(2)}) collective-permute-start(bf16[2,256,512]{2,1,0:T(8,128)(2,1)} %collective-permute-done.refs_3_), channel_id=1, source_target_pairs={{2,4},{6,8},{10,12},{14,16},{18,20},{22,24},{26,28},{4,2},{8,6},{1... | collective-permute-start | bytes 1572872 | tf_op jit(solution)/shard_map/ppermute | solution.py:43
  27.4 8.7 %grad_ctx.1.refs_2_ = bf16[1024,1024]{1,0:T(8,128)(2,1)} custom-call(bf16[1024,2048]{1,0:T(8,128)(2,1)} %bitcast.8, bf16[1024,2048]{1,0:T(8,128)(2,1)} %refs_1_.5, bf16[1024,1024]{1,0:T(8,128)(2,1)} %get-tuple-element.33.refs_2_.refs_1_, bf16[2,256,512]{2,1,0:T(8,128)(2,1)} %collective-permute-done.refs_3_), custom_call_target="tpu_custom_call" | custom-call | tf_op jit(solution)/shard_map/grad_ctx/pallas_call | solution.py:67
  36.1 0.0 collective-permute-done.1.refs_3_
  36.2 0.1 collective-permute-start.4
  36.2 3.8 %collective-permute-start.5 = (bf16[2,256,512]{2,1,0:T(8,128)(2,1)}, bf16[2,256,512]{2,1,0:T(8,128)(2,1)}, u32[]{:S(2)}, u32[]{:S(2)}) collective-permute-start(bf16[2,256,512]{2,1,0:T(8,128)(2,1)} %collective-permute-done.1.refs_3_), channel_id=1, source_target_pairs={{2,4},{6,8},{10,12},{14,16},{18,20},{22,24},{26,28},{4,2},{8,6},{1... | collective-permute-start | bytes 1572872 | tf_op jit(solution)/shard_map/ppermute | solution.py:43
  40.0 0.0 collective-permute-done.2.refs_4_
  40.0 0.0 collective-permute-done.3.refs_5_
  40.0 14.3 %attention.2 = (bf16[1024,512]{1,0:T(8,128)(2,1)}, f32[2,256,512]{2,1,0:T(8,128)}, bf16[2,256,512]{2,1,0:T(8,128)(2,1)}, bf16[2,256,512]{2,1,0:T(8,128)(2,1)}) custom-call(s32[2,8]{1,0:T(2,128)} %bitcast.13, bf16[1024,1024]{1,0:T(8,128)(2,1)} %get-tuple-element.33.refs_2_.refs_1_, bf16[1024,1024]{1,0:T(8,128)(2,1)} %grad_ctx.1.refs_2_, ...), custom_call_target="tpu_custom_call" | custom-call | tf_op jit(solution)/shard_map/attention/pallas_call | solution.py:67
  54.3 0.0 collective-permute-done.4.refs_4_
  54.3 0.0 collective-permute-done.5.refs_5_
  54.3 0.9 collective-permute-start.13
  55.2 0.0 collective-permute-done.6.refs_4_
  55.2 0.0 collective-permute-start.7
  55.2 3.4 %collective-permute-start.8 = (bf16[2,256,512]{2,1,0:T(8,128)(2,1)}, bf16[2,256,512]{2,1,0:T(8,128)(2,1)}, u32[]{:S(2)}, u32[]{:S(2)}) collective-permute-start(bf16[2,256,512]{2,1,0:T(8,128)(2,1)} %get-tuple-element.47), channel_id=1, source_target_pairs={{2,4},{6,8},{10,12},{14,16},{18,20},{22,24},{26,28},{4,2},{8,6},{1... | collective-permute-start | bytes 1572872 | tf_op jit(solution)/shard_map/ppermute | solution.py:43
  58.6 14.4 %attention.3 = (bf16[1024,512]{1,0:T(8,128)(2,1)}, f32[2,256,512]{2,1,0:T(8,128)}, bf16[2,256,512]{2,1,0:T(8,128)(2,1)}, bf16[2,256,512]{2,1,0:T(8,128)(2,1)}) custom-call(s32[2,8]{1,0:T(2,128)} %bitcast.14, bf16[1024,1024]{1,0:T(8,128)(2,1)} %get-tuple-element.33.refs_2_.refs_1_, bf16[1024,1024]{1,0:T(8,128)(2,1)} %grad_ctx.1.refs_2_, ...), custom_call_target="tpu_custom_call" | custom-call | flops 12079595520 | tf_op jit(solution)/shard_map/attention/pallas_call | solution.py:67
  72.9 0.0 collective-permute-done.7
  72.9 0.0 collective-permute-done.8
  73.0 2.2 %collective-permute-start.10 = (bf16[2,256,512]{2,1,0:T(8,128)(2,1)}, bf16[2,256,512]{2,1,0:T(8,128)(2,1)S(1)}, u32[]{:S(2)}, u32[]{:S(2)}) collective-permute-start(bf16[2,256,512]{2,1,0:T(8,128)(2,1)} %get-tuple-element.51), channel_id=1, source_target_pairs={{2,4},{6,8},{10,12},{14,16},{18,20},{22,24},{26,28},{4,2},{8,6},{1... | collective-permute-start | bytes 1572872 | tf_op jit(solution)/shard_map/ppermute | solution.py:43
  75.2 0.1 collective-permute-start.9
  75.3 1.7 %add_convert_fusion.1 = bf16[2,256,512]{2,1,0:T(8,128)(2,1)S(1)} fusion(bf16[2,256,512]{2,1,0:T(8,128)(2,1)} %collective-permute-done.8, f32[2,256,512]{2,1,0:T(8,128)} %get-tuple-element.52, bf16[2,256,512]{2,1,0:T(8,128)(2,1)} %collective-permute-done.7), kind=kLoop, calls=%fused_computation.1 | loop fusion | flops 1310720 | bytes 2621440 | tf_op jit(solution)/shard_map/convert_element_type | solution.py:467
  77.0 1.3 %collective-permute-start.12 = (bf16[2,256,512]{2,1,0:T(8,128)(2,1)S(1)}, bf16[2,256,512]{2,1,0:T(8,128)(2,1)}, u32[]{:S(2)}, u32[]{:S(2)}) collective-permute-start(bf16[2,256,512]{2,1,0:T(8,128)(2,1)S(1)} %add_convert_fusion.1), channel_id=1, source_target_pairs={{0,96},{32,0},{64,32},{96,64},{1,97},{33,1},{65,33},{97,65},{2,98}... | collective-permute-start | bytes 1572872 | tf_op jit(solution)/shard_map/ppermute | solution.py:30
  78.3 0.6 pad_add_fusion.refs_0_
  78.9 2.4 %collective-permute-start.15 = (bf16[1024,512]{1,0:T(8,128)(2,1)}, bf16[1024,512]{1,0:T(8,128)(2,1)}, u32[]{:S(2)}, u32[]{:S(2)}) collective-permute-start(bf16[1024,512]{1,0:T(8,128)(2,1)} %get-tuple-element.57.refs_2_), channel_id=1, source_target_pairs={{0,1},{1,0},{2,3},{3,2},{4,5},{5,4},{6,7},{7,6},{8,9},{9,8},{10,11... | collective-permute-start | bytes 3145736 | tf_op jit(solution)/shard_map/ppermute | solution.py:47
  81.3 2.8 %collective-permute-done.10 = bf16[2,256,512]{2,1,0:T(8,128)(2,1)S(1)} collective-permute-done((bf16[2,256,512]{2,1,0:T(8,128)(2,1)}, bf16[2,256,512]{2,1,0:T(8,128)(2,1)S(1)}, u32[]{:S(2)}, u32[]{:S(2)}) %collective-permute-start.10) | collective-permute-done | bytes 524320 | tf_op jit(solution)/shard_map/ppermute | solution.py:43
  84.1 0.0 collective-permute-done.9
  84.1 2.2 %add_convert_fusion.2.refs_4_ = bf16[2,256,512]{2,1,0:T(8,128)(2,1)} fusion(bf16[2,256,512]{2,1,0:T(8,128)(2,1)S(1)} %collective-permute-done.10, f32[2,256,512]{2,1,0:T(8,128)} %get-tuple-element.45, bf16[2,256,512]{2,1,0:T(8,128)(2,1)S(1)} %collective-permute-done.9), kind=kLoop, calls=%fused_computation.2 | loop fusion | flops 1310720 | bytes 2621440 | tf_op jit(solution)/shard_map/convert_element_type | solution.py:467
  86.3 1.2 collective-permute-start.11
  87.5 2.7 %collective-permute-done.12.refs_1_ = bf16[2,256,512]{2,1,0:T(8,128)(2,1)} collective-permute-done((bf16[2,256,512]{2,1,0:T(8,128)(2,1)S(1)}, bf16[2,256,512]{2,1,0:T(8,128)(2,1)}, u32[]{:S(2)}, u32[]{:S(2)}) %collective-permute-start.12) | collective-permute-done | bytes 524320 | tf_op jit(solution)/shard_map/ppermute | solution.py:30
  90.2 4.9 %note_product.3.refs_4_ = f32[2,256,1024]{2,1,0:T(8,128)} custom-call(s32[3]{0:T(128)} %pad_add_fusion.refs_0_, bf16[2,256,512]{2,1,0:T(8,128)(2,1)} %collective-permute-done.12.refs_1_, bf16[2048,1024]{1,0:T(8,128)(2,1)} %refs_2_.9, bf16[2048,1024]{1,0:T(8,128)(2,1)} %refs_3_.7, bf16[2,256,512]{2,1,0:T(8,128)(2,1)} %add_convert_fusion.2.refs_4_), custom_call_target="tpu_custom_call" | custom-call | tf_op jit(solution)/shard_map/note_product/pallas_call | solution.py:67
  95.0 0.0 collective-permute-done.13.refs_5_.refs_1_
  95.0 6.7 %frame_own.1.refs_5_.refs_3_ = bf16[1024,1024]{1,0:T(8,128)(2,1)} custom-call(s32[3]{0:T(128)} %pad_add_fusion.refs_0_, bf16[1024,512]{1,0:T(8,128)(2,1)} %get-tuple-element.44.refs_6_.refs_1_, bf16[1024,512]{1,0:T(8,128)(2,1)} %get-tuple-element.57.refs_2_, bf16[2048,1024]{1,0:T(8,128)(2,1)} %refs_3_.5, f32[2,256,1024]{2,1,0:T(8,128)} %note_product.3.refs_4_, ...), custom_call_target="tpu_custom_call" | custom-call | flops 8589934592 | tf_op jit(solution)/shard_map/frame_own/pallas_call | solution.py:67
  101.7 2.4 %collective-permute-start.16 = (bf16[512,1024]{1,0:T(8,128)(2,1)}, bf16[512,1024]{1,0:T(8,128)(2,1)}, u32[]{:S(2)}, u32[]{:S(2)}) collective-permute-start(bf16[512,1024]{1,0:T(8,128)(2,1)} %collective-permute-done.6.refs_4_), channel_id=1, source_target_pairs={{0,2},{2,0},{4,6},{6,4},{8,10},{10,8},{12,14},{14,12},{16,18},{18,... | collective-permute-start | bytes 3145736 | tf_op jit(solution)/shard_map/ppermute | solution.py:37
  104.1 0.0 collective-permute-done.11.refs_1_
  104.1 4.2 %note_product.4.refs_5_ = bf16[1,256,1024]{2,1,0:T(8,128)(2,1)} custom-call(s32[3]{0:T(128)} %pad_add_fusion.refs_0_, bf16[2,256,512]{2,1,0:T(8,128)(2,1)} %collective-permute-done.11.refs_1_, bf16[2048,1024]{1,0:T(8,128)(2,1)} %refs_2_.9, bf16[2048,1024]{1,0:T(8,128)(2,1)} %refs_3_.7, f32[2,256,1024]{2,1,0:T(8,128)} %note_product.3.refs_4_, ...), custom_call_target="tpu_custom_call" | custom-call | tf_op jit(solution)/shard_map/note_product/pallas_call | solution.py:67
  108.4 2.1 %collective-permute-start.14 = (bf16[1,256,1024]{2,1,0:T(8,128)(2,1)}, bf16[1,256,1024]{2,1,0:T(8,128)(2,1)}, u32[]{:S(2)}, u32[]{:S(2)}) collective-permute-start(bf16[1,256,1024]{2,1,0:T(8,128)(2,1)} %note_product.4.refs_5_), channel_id=1, source_target_pairs={{0,1},{1,0},{2,3},{3,2},{4,5},{5,4},{6,7},{7,6},{8,9},{9,8},{10,11... | collective-permute-start | bytes 1572872 | tf_op jit(solution)/shard_map/ppermute | solution.py:47
  110.5 4.2 %note_product.5.refs_6_ = bf16[1,256,1024]{2,1,0:T(8,128)(2,1)} custom-call(s32[3]{0:T(128)} %pad_add_fusion.refs_0_, bf16[2,256,512]{2,1,0:T(8,128)(2,1)} %collective-permute-done.11.refs_1_, bf16[2048,1024]{1,0:T(8,128)(2,1)} %refs_2_.9, bf16[2048,1024]{1,0:T(8,128)(2,1)} %refs_3_.7, f32[2,256,1024]{2,1,0:T(8,128)} %note_product.3.refs_4_, ...), custom_call_target="tpu_custom_call" | custom-call | tf_op jit(solution)/shard_map/note_product/pallas_call | solution.py:67
  114.7 0.0 collective-permute-done.15.refs_2_
  114.7 0.0 collective-permute-done.16.refs_5_
  114.7 7.3 %frame_sum.1 = bf16[1024,1024]{1,0:T(8,128)(2,1)} custom-call(s32[3]{0:T(128)} %pad_add_fusion.refs_0_, bf16[1024,512]{1,0:T(8,128)(2,1)} %collective-permute-done.13.refs_5_.refs_1_, bf16[1024,512]{1,0:T(8,128)(2,1)} %collective-permute-done.15.refs_2_, bf16[1024,1024]{1,0:T(8,128)(2,1)} %frame_own.1.refs_5_.refs_3_, ...), custom_call_target="tpu_custom_call" | custom-call | tf_op jit(solution)/shard_map/frame_sum/pallas_call | solution.py:67
  122.0 2.7 %collective-permute-done.14 = bf16[1,256,1024]{2,1,0:T(8,128)(2,1)} collective-permute-done((bf16[1,256,1024]{2,1,0:T(8,128)(2,1)}, bf16[1,256,1024]{2,1,0:T(8,128)(2,1)}, u32[]{:S(2)}, u32[]{:S(2)}) %collective-permute-start.14) | collective-permute-done | bytes 524320 | tf_op jit(solution)/shard_map/ppermute | solution.py:47
  124.7 2.2 %add_convert_fusion = bf16[1,256,1024]{2,1,0:T(8,128)(2,1)} fusion(bf16[1,256,1024]{2,1,0:T(8,128)(2,1)} %collective-permute-done.14, bf16[1,256,1024]{2,1,0:T(8,128)(2,1)} %note_product.5.refs_6_), kind=kLoop, calls=%fused_computation | loop fusion | flops 1048576 | bytes 1572864 | tf_op jit(solution)/shard_map/convert_element_type | solution.py:502
Async XLA Ops:
  4.8 18.0 %collective-permute-start = (bf16[2,256,512]{2,1,0:T(8,128)(2,1)}, bf16[2,256,512]{2,1,0:T(8,128)(2,1)}, u32[]{:S(2)}, u32[]{:S(2)}) collective-permute-start(bf16[2,256,512]{2,1,0:T(8,128)(2,1)} %key_values.1.refs_5_), channel_id=1, source_target_pairs={{0,32},{32,64},{64,96},{96,0},{1,33},{33,65},{65,97},{97,1},{2,34}... | collective-permute-start | bytes 1572872 | tf_op jit(solution)/shard_map/ppermute | solution.py:30
  17.8 18.3 %collective-permute-start.1 = (bf16[2,256,512]{2,1,0:T(8,128)(2,1)}, bf16[2,256,512]{2,1,0:T(8,128)(2,1)}, u32[]{:S(2)}, u32[]{:S(2)}) collective-permute-start(bf16[2,256,512]{2,1,0:T(8,128)(2,1)} %get-tuple-element.34), channel_id=1, source_target_pairs={{0,32},{32,64},{64,96},{96,0},{1,33},{33,65},{65,97},{97,1},{2,34}... | collective-permute-start | bytes 1572872 | tf_op jit(solution)/shard_map/ppermute | solution.py:30
  19.1 36.1 %collective-permute-start.6 = (bf16[512,1024]{1,0:T(8,128)(2,1)}, bf16[512,1024]{1,0:T(8,128)(2,1)}, u32[]{:S(2)}, u32[]{:S(2)}) collective-permute-start(bf16[512,1024]{1,0:T(8,128)(2,1)} %get-tuple-element.42), channel_id=1, source_target_pairs={{0,17},{1,16},{2,19},{3,18},{4,21},{5,20},{6,23},{7,22},{8,25},{9,... | collective-permute-start | bytes 3145736 | tf_op jit(solution)/shard_map/ppermute | solution.py:53
  22.8 17.2 %collective-permute-start.2 = (bf16[2,256,512]{2,1,0:T(8,128)(2,1)}, bf16[2,256,512]{2,1,0:T(8,128)(2,1)}, u32[]{:S(2)}, u32[]{:S(2)}) collective-permute-start(bf16[2,256,512]{2,1,0:T(8,128)(2,1)} %collective-permute-done.refs_3_), channel_id=1, source_target_pairs={{0,2},{2,0},{4,6},{6,4},{8,10},{10,8},{12,14},{14,12},{16,18},{18,... | collective-permute-start | bytes 1572872 | tf_op jit(solution)/shard_map/ppermute | solution.py:37
  24.4 15.7 %collective-permute-start.3 = (bf16[2,256,512]{2,1,0:T(8,128)(2,1)}, bf16[2,256,512]{2,1,0:T(8,128)(2,1)}, u32[]{:S(2)}, u32[]{:S(2)}) collective-permute-start(bf16[2,256,512]{2,1,0:T(8,128)(2,1)} %collective-permute-done.refs_3_), channel_id=1, source_target_pairs={{2,4},{6,8},{10,12},{14,16},{18,20},{22,24},{26,28},{4,2},{8,6},{1... | collective-permute-start | bytes 1572872 | tf_op jit(solution)/shard_map/ppermute | solution.py:43
  36.2 18.1 %collective-permute-start.4 = (bf16[2,256,512]{2,1,0:T(8,128)(2,1)}, bf16[2,256,512]{2,1,0:T(8,128)(2,1)}, u32[]{:S(2)}, u32[]{:S(2)}) collective-permute-start(bf16[2,256,512]{2,1,0:T(8,128)(2,1)} %collective-permute-done.1.refs_3_), channel_id=1, source_target_pairs={{0,2},{2,0},{4,6},{6,4},{8,10},{10,8},{12,14},{14,12},{16,18},{18,... | collective-permute-start | bytes 1572872 | tf_op jit(solution)/shard_map/ppermute | solution.py:37
  36.2 18.0 %collective-permute-start.5 = (bf16[2,256,512]{2,1,0:T(8,128)(2,1)}, bf16[2,256,512]{2,1,0:T(8,128)(2,1)}, u32[]{:S(2)}, u32[]{:S(2)}) collective-permute-start(bf16[2,256,512]{2,1,0:T(8,128)(2,1)} %collective-permute-done.1.refs_3_), channel_id=1, source_target_pairs={{2,4},{6,8},{10,12},{14,16},{18,20},{22,24},{26,28},{4,2},{8,6},{1... | collective-permute-start | bytes 1572872 | tf_op jit(solution)/shard_map/ppermute | solution.py:43
  54.3 40.7 %collective-permute-start.13 = (bf16[1024,512]{1,0:T(8,128)(2,1)}, bf16[1024,512]{1,0:T(8,128)(2,1)}, u32[]{:S(2)}, u32[]{:S(2)}) collective-permute-start(bf16[1024,512]{1,0:T(8,128)(2,1)} %get-tuple-element.44.refs_6_.refs_1_), channel_id=1, source_target_pairs={{0,1},{1,0},{2,3},{3,2},{4,5},{5,4},{6,7},{7,6},{8,9},{9,8},{10,11... | collective-permute-start | bytes 3145736 | tf_op jit(solution)/shard_map/ppermute | solution.py:47
  55.2 17.7 %collective-permute-start.7 = (bf16[2,256,512]{2,1,0:T(8,128)(2,1)}, bf16[2,256,512]{2,1,0:T(8,128)(2,1)}, u32[]{:S(2)}, u32[]{:S(2)}) collective-permute-start(bf16[2,256,512]{2,1,0:T(8,128)(2,1)} %get-tuple-element.46), channel_id=1, source_target_pairs={{0,2},{2,0},{4,6},{6,4},{8,10},{10,8},{12,14},{14,12},{16,18},{18,... | collective-permute-start | bytes 1572872 | tf_op jit(solution)/shard_map/ppermute | solution.py:37
  55.2 17.7 %collective-permute-start.8 = (bf16[2,256,512]{2,1,0:T(8,128)(2,1)}, bf16[2,256,512]{2,1,0:T(8,128)(2,1)}, u32[]{:S(2)}, u32[]{:S(2)}) collective-permute-start(bf16[2,256,512]{2,1,0:T(8,128)(2,1)} %get-tuple-element.47), channel_id=1, source_target_pairs={{2,4},{6,8},{10,12},{14,16},{18,20},{22,24},{26,28},{4,2},{8,6},{1... | collective-permute-start | bytes 1572872 | tf_op jit(solution)/shard_map/ppermute | solution.py:43
  73.0 11.1 %collective-permute-start.10 = (bf16[2,256,512]{2,1,0:T(8,128)(2,1)}, bf16[2,256,512]{2,1,0:T(8,128)(2,1)S(1)}, u32[]{:S(2)}, u32[]{:S(2)}) collective-permute-start(bf16[2,256,512]{2,1,0:T(8,128)(2,1)} %get-tuple-element.51), channel_id=1, source_target_pairs={{2,4},{6,8},{10,12},{14,16},{18,20},{22,24},{26,28},{4,2},{8,6},{1... | collective-permute-start | bytes 1572872 | tf_op jit(solution)/shard_map/ppermute | solution.py:43
  75.2 8.9 %collective-permute-start.9 = (bf16[2,256,512]{2,1,0:T(8,128)(2,1)}, bf16[2,256,512]{2,1,0:T(8,128)(2,1)S(1)}, u32[]{:S(2)}, u32[]{:S(2)}) collective-permute-start(bf16[2,256,512]{2,1,0:T(8,128)(2,1)} %get-tuple-element.50), channel_id=1, source_target_pairs={{0,2},{2,0},{4,6},{6,4},{8,10},{10,8},{12,14},{14,12},{16,18},{18,... | collective-permute-start | bytes 1572872 | tf_op jit(solution)/shard_map/ppermute | solution.py:37
  77.0 13.2 %collective-permute-start.12 = (bf16[2,256,512]{2,1,0:T(8,128)(2,1)S(1)}, bf16[2,256,512]{2,1,0:T(8,128)(2,1)}, u32[]{:S(2)}, u32[]{:S(2)}) collective-permute-start(bf16[2,256,512]{2,1,0:T(8,128)(2,1)S(1)} %add_convert_fusion.1), channel_id=1, source_target_pairs={{0,96},{32,0},{64,32},{96,64},{1,97},{33,1},{65,33},{97,65},{2,98}... | collective-permute-start | bytes 1572872 | tf_op jit(solution)/shard_map/ppermute | solution.py:30
  78.9 35.8 %collective-permute-start.15 = (bf16[1024,512]{1,0:T(8,128)(2,1)}, bf16[1024,512]{1,0:T(8,128)(2,1)}, u32[]{:S(2)}, u32[]{:S(2)}) collective-permute-start(bf16[1024,512]{1,0:T(8,128)(2,1)} %get-tuple-element.57.refs_2_), channel_id=1, source_target_pairs={{0,1},{1,0},{2,3},{3,2},{4,5},{5,4},{6,7},{7,6},{8,9},{9,8},{10,11... | collective-permute-start | bytes 3145736 | tf_op jit(solution)/shard_map/ppermute | solution.py:47
  86.3 17.8 %collective-permute-start.11 = (bf16[2,256,512]{2,1,0:T(8,128)(2,1)}, bf16[2,256,512]{2,1,0:T(8,128)(2,1)}, u32[]{:S(2)}, u32[]{:S(2)}) collective-permute-start(bf16[2,256,512]{2,1,0:T(8,128)(2,1)} %add_convert_fusion.2.refs_4_), channel_id=1, source_target_pairs={{0,96},{32,0},{64,32},{96,64},{1,97},{33,1},{65,33},{97,65},{2,98}... | collective-permute-start | bytes 1572872 | tf_op jit(solution)/shard_map/ppermute | solution.py:30
  101.7 12.9 %collective-permute-start.16 = (bf16[512,1024]{1,0:T(8,128)(2,1)}, bf16[512,1024]{1,0:T(8,128)(2,1)}, u32[]{:S(2)}, u32[]{:S(2)}) collective-permute-start(bf16[512,1024]{1,0:T(8,128)(2,1)} %collective-permute-done.6.refs_4_), channel_id=1, source_target_pairs={{0,2},{2,0},{4,6},{6,4},{8,10},{10,8},{12,14},{14,12},{16,18},{18,... | collective-permute-start | bytes 3145736 | tf_op jit(solution)/shard_map/ppermute | solution.py:37
  108.4 16.3 %collective-permute-start.14 = (bf16[1,256,1024]{2,1,0:T(8,128)(2,1)}, bf16[1,256,1024]{2,1,0:T(8,128)(2,1)}, u32[]{:S(2)}, u32[]{:S(2)}) collective-permute-start(bf16[1,256,1024]{2,1,0:T(8,128)(2,1)} %note_product.4.refs_5_), channel_id=1, source_target_pairs={{0,1},{1,0},{2,3},{3,2},{4,5},{5,4},{6,7},{7,6},{8,9},{9,8},{10,11... | collective-permute-start | bytes 1572872 | tf_op jit(solution)/shard_map/ppermute | solution.py:47

commit v11 on v10

--- a/solution.py
+++ b/solution.py
@@ -246,7 +246,7 @@
     )
 
 
-def frame_part(scalars, grads, weights, own, name, after):
+def frame_part(grads, weights, own, name, after):
     rows = grads[0].shape[0]
     half = D // 2
     cols = sum(g.shape[1] for g in grads)
@@ -256,7 +256,9 @@
     terms = list(grads) + ([] if own is None else [own])
     count = len(terms)
 
-    def body(s_ref, *refs):
+    def body(*refs):
+        group = lax.axis_index("head")
+        odd = lax.rem(lax.axis_index("seq"), 2)
         term_refs, refs = refs[:count], refs[count:]
         weight_refs, refs = refs[: len(weights)], refs[len(weights) :]
         out_ref, w_scr, o_scr, *refs = refs
@@ -264,10 +266,10 @@
         weight_copies = []
         for p in range(2):
             if own is None:
-                at = pl.ds(pl.multiple_of(s_ref[0] * half + p * quarter, quarter), quarter)
+                at = pl.ds(pl.multiple_of(group * half + p * quarter, quarter), quarter)
                 src, dst = weight_refs[0].at[at], w_scr.at[p * quarter : (p + 1) * quarter]
             else:
-                core = s_ref[1] if p == 0 else 1 - s_ref[1]
+                core = odd if p == 0 else 1 - odd
                 to = pl.ds(pl.multiple_of(core * quarter, quarter), quarter)
                 src, dst = weight_refs[p], w_scr.at[to]
             weight_copies.append(pltpu.make_async_copy(src, dst, w_sems.at[p]))
@@ -305,10 +307,9 @@
         [far] * (count + len(weights)),
         far,
         jax.ShapeDtypeStruct((rows, half), BF16),
-        (scalars, *terms, *weights),
+        (*terms, *weights),
         name,
         after,
-        scalars=1,
         flops=8 * rows * half * cols if own is None else 0,
         scratch=[
             pltpu.VMEM((half, cols), BF16),
@@ -321,14 +322,14 @@
     )
 
 
-def note_product(scalars, grads, chunks, w_key, w_value, after, before=None, which=(0, 1)):
+def note_product(grads, chunks, w_key, w_value, after, before=None, which=(0, 1)):
     nt = grads[0].shape[1]
     half = D // 2
     ((h0, hc),) = chunks
     last = before is not None
     start = which[0]
 
-    def body(s_ref, *refs):
+    def body(*refs):
         grad_refs, refs = refs[: len(grads)], refs[len(grads) :]
         grad_ref = grad_refs[0]
         total = dot(grad_ref[0], refs[0][...], NT) + dot(grad_ref[1], refs[1][...], NT)
@@ -337,22 +338,23 @@
         out_ref = refs[-1]
         out_ref[0] = total.astype(out_ref.dtype)
 
-    weight_in = pl.BlockSpec(
-        (half, hc * HD), lambda n, s: (jnp.where(n + start == 0, 1 - s[0], s[0]), h0 // hc)
-    )
+    def rows_of(n):
+        group = lax.axis_index("head")
+        return jnp.where(n + start == 0, 1 - group, group), h0 // hc
+
+    weight_in = pl.BlockSpec((half, hc * HD), rows_of)
 
     return call(
         body,
         (len(which),),
-        [pl.BlockSpec(g.shape, lambda n, s: (0, 0, 0)) for g in grads]
+        [pl.BlockSpec(g.shape, lambda n: (0, 0, 0)) for g in grads]
         + [weight_in] * 2
-        + ([pl.BlockSpec((1, nt, half), lambda n, s: (n + start, 0, 0))] if last else []),
-        pl.BlockSpec((1, nt, half), lambda n, s: (n, 0, 0)),
+        + ([pl.BlockSpec((1, nt, half), lambda n: (n + start, 0, 0))] if last else []),
+        pl.BlockSpec((1, nt, half), lambda n: (n, 0, 0)),
         jax.ShapeDtypeStruct((len(which), nt, half), BF16 if last else F32),
-        (scalars, *grads, w_key, w_value) + ((before,) if last else ()),
+        (*grads, w_key, w_value) + ((before,) if last else ()),
         "note_product",
         after,
-        scalars=1,
     )
 
 
@@ -441,10 +443,6 @@
 
 
 def per_device(notes, frames, w_query, w_key, w_value, w_out, band_blocks, grad_mixed):
-    shard = lax.axis_index("seq")
-    group = lax.axis_index("head")
-    core = shard % 2
-    scalars = jnp.stack([group, core, shard]).astype(jnp.int32)
     band = band_blocks[0]
 
     made0 = key_values(notes[0], w_key, w_value, *CHUNKS[0])
@@ -484,18 +482,18 @@
     owned1 = note_sum_of(own1, in_near1, in_far1)
     notes1 = section_shift(owned1, -1)
 
-    before = note_product(scalars, [notes0], CHUNKS[:1], w_key, w_value, (owned1,))
+    before = note_product([notes0], CHUNKS[:1], w_key, w_value, (owned1,))
     own_part = frame_part(
-        scalars, [dq0, dq1], [w_query], None, "frame_own", (before, dq0_other)
-    )
-    last = (scalars, [notes1], CHUNKS[1:], w_key, w_value)
+        [dq0, dq1], [w_query], None, "frame_own", (before, dq0_other)
+    )
     w_mine, own_part = lax.optimization_barrier((w_mine, own_part))
     w_theirs = near_swap(w_mine)
+    last = ([notes1], CHUNKS[1:], w_key, w_value)
     give_notes = note_product(*last, (own_part,), before, (0,))
     notes_other = head_swap(give_notes)
     keep_notes = note_product(*last, (give_notes,), before, (1,))
     frame_out = frame_part(
-        scalars, [dq0_other, dq1_other], [w_mine, w_theirs], own_part, "frame_sum", (keep_notes,)
+        [dq0_other, dq1_other], [w_mine, w_theirs], own_part, "frame_sum", (keep_notes,)
     )
     notes_other, frame_out = lax.optimization_barrier((notes_other, frame_out))
     note_out = keep_notes[0].astype(F32) + notes_other[0].astype(F32)

time: 129 us -> 128 us (level); the launches traced: 127 us -> 128 us
  waiting for transfers between devices: 8.22 us -> 14.9 us
  Pallas kernels: 79.6 us -> 76.6 us
  starting transfers between devices: 31.5 us -> 29.3 us
    ppermute x3, waiting for transfers between devices: 2.73 us -> 7.17 us  [head_swap(): return lax.ppermute(block, 'head', [(0, 1), (1, 0)])]
    pallas_call x10, Pallas kernels: 79.6 us -> 76.6 us  [call(): pl.pallas_call(reads, grid_spec=pltpu.PrefetchScalarGridSpec(num_scalar_p...]
    ppermute x5, starting transfers between devices: 4.06 us -> 1.28 us  [near_swap(): return lax.ppermute(block, 'seq', [(i, i ^ 1) for i in range(count)])]
    ppermute x4, waiting for transfers between devices: 2.66 us -> 4.68 us  [section_shift(): lax.ppermute(block, 'section', [(i, (i + distance) % count) for i in rang...]
    ppermute x4, starting transfers between devices: 12.4 us -> 14.3 us  [far_swap(): return lax.ppermute(block, 'seq', pairs + [(j, i) for i, j in pairs])]
  transfers between devices with their start and end apart: 17 -> 17, of which waited for: 3 -> 4; matrix products, arithmetic and copies ran while one was open for 4% -> 3% of each run, Pallas kernels for 59% -> 57%
where the time goes in v11:
time: 128 us
  Pallas kernels  76.6 us (60%)
  starting transfers between devices  29.3 us (23%)
  waiting for transfers between devices  14.9 us (12%)
  other arithmetic  6.15 us (5%)
    pallas_call x10, Pallas kernels, call(): pl.pallas_call(reads, grid_spec=pltpu.PrefetchScalarGridSpec(num_scalar_p...  76.6 us
    ppermute x4, starting transfers between devices, far_swap(): return lax.ppermute(block, 'seq', pairs + [(j, i) for i, j in pairs])  14.3 us
    ppermute x3, waiting for transfers between devices, head_swap(): return lax.ppermute(block, 'head', [(0, 1), (1, 0)])  7.17 us
    ppermute x4, starting transfers between devices, section_shift(): lax.ppermute(block, 'section', [(i, (i + distance) % count) for i in rang...  5.86 us
    ppermute x4, waiting for transfers between devices, section_shift(): lax.ppermute(block, 'section', [(i, (i + distance) % count) for i in rang...  4.68 us
    ppermute x3, starting transfers between devices, head_swap(): return lax.ppermute(block, 'head', [(0, 1), (1, 0)])  4.07 us
    convert_element_type x2, other arithmetic, note_sum_of(): return (own + near.astype(F32) + far.astype(F32)).astype(BF16)  3.96 us
    ppermute x1, starting transfers between devices, across(): return lax.ppermute(block, ('seq', 'head'), route)  3.76 us
  transfers between devices with their start and end apart: 17, of which 4 were waited for; matrix products, arithmetic and copies ran while one was open for 3% of the time, Pallas kernels for 57%

profile of v11, /device:TPU:1, one launch (start us, length us, event | category | flops | bytes accessed | tf_op | source)
XLA Modules:
  0.0 127.7 jit_solution(13285652983797964307)
XLA Ops:
  0.6 4.2 %key_values.1.refs_5_ = bf16[2,256,512]{2,1,0:T(8,128)(2,1)} custom-call(bf16[256,2048]{1,0:T(8,128)(2,1)} %bitcast.6, bf16[2048,1024]{1,0:T(8,128)(2,1)} %refs_1_.11, bf16[2048,1024]{1,0:T(8,128)(2,1)} %refs_2_.11), custom_call_target="tpu_custom_call" | custom-call | tf_op jit(solution)/shard_map/key_values/pallas_call | solution.py:67
  4.8 2.1 %collective-permute-start = (bf16[2,256,512]{2,1,0:T(8,128)(2,1)}, bf16[2,256,512]{2,1,0:T(8,128)(2,1)}, u32[]{:S(2)}, u32[]{:S(2)}) collective-permute-start(bf16[2,256,512]{2,1,0:T(8,128)(2,1)} %key_values.1.refs_5_), channel_id=1, source_target_pairs={{0,32},{32,64},{64,96},{96,0},{1,33},{33,65},{65,97},{97,1},{2,34}... | collective-permute-start | bytes 1572872 | tf_op jit(solution)/shard_map/ppermute | solution.py:30
  6.9 10.9 %key_values_and_queries.1 = (bf16[2,256,512]{2,1,0:T(8,128)(2,1)}, bf16[1024,1024]{1,0:T(8,128)(2,1)}, bf16[512,1024]{1,0:T(8,128)(2,1)}) custom-call(bf16[256,2048]{1,0:T(8,128)(2,1)} %bitcast.7, bf16[2048,1024]{1,0:T(8,128)(2,1)} %refs_1_.11, bf16[2048,1024]{1,0:T(8,128)(2,1)} %refs_2_.11, bf16[1024,2048]{1,0:T(8,128)(2,1)} %bitcast.8, ...), custom_call_target="tpu_custom_call" | custom-call | tf_op jit(solution)/shard_map/key_values_and_queries/pallas_call | solution.py:67
  17.8 1.3 %collective-permute-start.1 = (bf16[2,256,512]{2,1,0:T(8,128)(2,1)}, bf16[2,256,512]{2,1,0:T(8,128)(2,1)}, u32[]{:S(2)}, u32[]{:S(2)}) collective-permute-start(bf16[2,256,512]{2,1,0:T(8,128)(2,1)} %get-tuple-element.34), channel_id=1, source_target_pairs={{0,32},{32,64},{64,96},{96,0},{1,33},{33,65},{65,97},{97,1},{2,34}... | collective-permute-start | bytes 1572872 | tf_op jit(solution)/shard_map/ppermute | solution.py:30
  19.1 3.8 %collective-permute-start.6 = (bf16[512,1024]{1,0:T(8,128)(2,1)}, bf16[512,1024]{1,0:T(8,128)(2,1)}, u32[]{:S(2)}, u32[]{:S(2)}) collective-permute-start(bf16[512,1024]{1,0:T(8,128)(2,1)} %get-tuple-element.42), channel_id=1, source_target_pairs={{0,17},{1,16},{2,19},{3,18},{4,21},{5,20},{6,23},{7,22},{8,25},{9,... | collective-permute-start | bytes 3145736 | tf_op jit(solution)/shard_map/ppermute | solution.py:53
  22.8 0.0 collective-permute-done.refs_3_
  22.8 4.6 %collective-permute-start.3 = (bf16[2,256,512]{2,1,0:T(8,128)(2,1)}, bf16[2,256,512]{2,1,0:T(8,128)(2,1)}, u32[]{:S(2)}, u32[]{:S(2)}) collective-permute-start(bf16[2,256,512]{2,1,0:T(8,128)(2,1)} %collective-permute-done.refs_3_), channel_id=1, source_target_pairs={{2,4},{6,8},{10,12},{14,16},{18,20},{22,24},{26,28},{4,2},{8,6},{1... | collective-permute-start | bytes 1572872 | tf_op jit(solution)/shard_map/ppermute | solution.py:43
  27.4 0.1 collective-permute-start.2
  27.5 8.7 %grad_ctx.1.refs_2_ = bf16[1024,1024]{1,0:T(8,128)(2,1)} custom-call(bf16[1024,2048]{1,0:T(8,128)(2,1)} %bitcast.5, bf16[1024,2048]{1,0:T(8,128)(2,1)} %refs_1_.8, bf16[1024,1024]{1,0:T(8,128)(2,1)} %get-tuple-element.33.refs_2_.refs_1_, bf16[2,256,512]{2,1,0:T(8,128)(2,1)} %collective-permute-done.refs_3_), custom_call_target="tpu_custom_call" | custom-call | tf_op jit(solution)/shard_map/grad_ctx/pallas_call | solution.py:67
  36.2 0.0 collective-permute-done.1.refs_3_
  36.2 3.6 %collective-permute-start.5 = (bf16[2,256,512]{2,1,0:T(8,128)(2,1)}, bf16[2,256,512]{2,1,0:T(8,128)(2,1)}, u32[]{:S(2)}, u32[]{:S(2)}) collective-permute-start(bf16[2,256,512]{2,1,0:T(8,128)(2,1)} %collective-permute-done.1.refs_3_), channel_id=1, source_target_pairs={{2,4},{6,8},{10,12},{14,16},{18,20},{22,24},{26,28},{4,2},{8,6},{1... | collective-permute-start | bytes 1572872 | tf_op jit(solution)/shard_map/ppermute | solution.py:43
  39.8 0.3 collective-permute-start.4
  40.1 0.0 collective-permute-done.3.refs_5_
  40.1 0.0 collective-permute-done.2.refs_4_
  40.1 14.3 %attention.2 = (bf16[1024,512]{1,0:T(8,128)(2,1)}, f32[2,256,512]{2,1,0:T(8,128)}, bf16[2,256,512]{2,1,0:T(8,128)(2,1)}, bf16[2,256,512]{2,1,0:T(8,128)(2,1)}) custom-call(s32[2,8]{1,0:T(2,128)} %bitcast.10, bf16[1024,1024]{1,0:T(8,128)(2,1)} %get-tuple-element.33.refs_2_.refs_1_, bf16[1024,1024]{1,0:T(8,128)(2,1)} %grad_ctx.1.refs_2_, ...), custom_call_target="tpu_custom_call" | custom-call | tf_op jit(solution)/shard_map/attention/pallas_call | solution.py:67
  54.4 0.0 collective-permute-done.5.refs_5_
  54.4 0.0 collective-permute-done.4.refs_4_
  54.4 0.9 collective-permute-start.13
  55.3 0.0 collective-permute-done.6.refs_3_
  55.3 0.8 collective-permute-start.7
  56.1 2.9 %collective-permute-start.8 = (bf16[2,256,512]{2,1,0:T(8,128)(2,1)}, bf16[2,256,512]{2,1,0:T(8,128)(2,1)}, u32[]{:S(2)}, u32[]{:S(2)}) collective-permute-start(bf16[2,256,512]{2,1,0:T(8,128)(2,1)} %get-tuple-element.47), channel_id=1, source_target_pairs={{2,4},{6,8},{10,12},{14,16},{18,20},{22,24},{26,28},{4,2},{8,6},{1... | collective-permute-start | bytes 1572872 | tf_op jit(solution)/shard_map/ppermute | solution.py:43
  58.9 14.4 %attention.3 = (bf16[1024,512]{1,0:T(8,128)(2,1)}, f32[2,256,512]{2,1,0:T(8,128)}, bf16[2,256,512]{2,1,0:T(8,128)(2,1)}, bf16[2,256,512]{2,1,0:T(8,128)(2,1)}) custom-call(s32[2,8]{1,0:T(2,128)} %bitcast.11, bf16[1024,1024]{1,0:T(8,128)(2,1)} %get-tuple-element.33.refs_2_.refs_1_, bf16[1024,1024]{1,0:T(8,128)(2,1)} %grad_ctx.1.refs_2_, ...), custom_call_target="tpu_custom_call" | custom-call | flops 12079595520 | tf_op jit(solution)/shard_map/attention/pallas_call | solution.py:67
  73.3 0.0 collective-permute-done.7
  73.3 0.0 collective-permute-done.8
  73.3 0.1 collective-permute-start.9
  73.4 3.3 %collective-permute-start.10 = (bf16[2,256,512]{2,1,0:T(8,128)(2,1)}, bf16[2,256,512]{2,1,0:T(8,128)(2,1)S(1)}, u32[]{:S(2)}, u32[]{:S(2)}) collective-permute-start(bf16[2,256,512]{2,1,0:T(8,128)(2,1)} %get-tuple-element.51), channel_id=1, source_target_pairs={{2,4},{6,8},{10,12},{14,16},{18,20},{22,24},{26,28},{4,2},{8,6},{1... | collective-permute-start | bytes 1572872 | tf_op jit(solution)/shard_map/ppermute | solution.py:43
  76.7 1.7 %add_convert_fusion.1 = bf16[2,256,512]{2,1,0:T(8,128)(2,1)S(1)} fusion(bf16[2,256,512]{2,1,0:T(8,128)(2,1)} %collective-permute-done.8, f32[2,256,512]{2,1,0:T(8,128)} %get-tuple-element.52, bf16[2,256,512]{2,1,0:T(8,128)(2,1)} %collective-permute-done.7), kind=kLoop, calls=%fused_computation.1 | loop fusion | flops 1310720 | bytes 2621440 | tf_op jit(solution)/shard_map/convert_element_type | solution.py:465
  78.4 1.3 collective-permute-start.12
  79.7 1.8 %collective-permute-start.15 = (bf16[1024,512]{1,0:T(8,128)(2,1)}, bf16[1024,512]{1,0:T(8,128)(2,1)}, u32[]{:S(2)}, u32[]{:S(2)}) collective-permute-start(bf16[1024,512]{1,0:T(8,128)(2,1)} %get-tuple-element.57.refs_1_), channel_id=1, source_target_pairs={{0,1},{1,0},{2,3},{3,2},{4,5},{5,4},{6,7},{7,6},{8,9},{9,8},{10,11... | collective-permute-start | bytes 3145736 | tf_op jit(solution)/shard_map/ppermute | solution.py:47
  81.5 0.0 collective-permute-done.9
  81.5 3.0 %collective-permute-done.10 = bf16[2,256,512]{2,1,0:T(8,128)(2,1)S(1)} collective-permute-done((bf16[2,256,512]{2,1,0:T(8,128)(2,1)}, bf16[2,256,512]{2,1,0:T(8,128)(2,1)S(1)}, u32[]{:S(2)}, u32[]{:S(2)}) %collective-permute-start.10) | collective-permute-done | bytes 524320 | tf_op jit(solution)/shard_map/ppermute | solution.py:43
  84.5 2.2 %add_convert_fusion.2.refs_3_ = bf16[2,256,512]{2,1,0:T(8,128)(2,1)} fusion(bf16[2,256,512]{2,1,0:T(8,128)(2,1)S(1)} %collective-permute-done.10, f32[2,256,512]{2,1,0:T(8,128)} %get-tuple-element.45, bf16[2,256,512]{2,1,0:T(8,128)(2,1)S(1)} %collective-permute-done.9), kind=kLoop, calls=%fused_computation.2 | loop fusion | flops 1310720 | bytes 2621440 | tf_op jit(solution)/shard_map/convert_element_type | solution.py:465
  86.7 1.2 collective-permute-start.11
  87.9 4.7 %collective-permute-done.12.refs_0_ = bf16[2,256,512]{2,1,0:T(8,128)(2,1)} collective-permute-done((bf16[2,256,512]{2,1,0:T(8,128)(2,1)S(1)}, bf16[2,256,512]{2,1,0:T(8,128)(2,1)}, u32[]{:S(2)}, u32[]{:S(2)}) %collective-permute-start.12) | collective-permute-done | bytes 524320 | tf_op jit(solution)/shard_map/ppermute | solution.py:30
  92.6 4.3 %note_product.3.refs_3_ = f32[2,256,1024]{2,1,0:T(8,128)} custom-call(bf16[2,256,512]{2,1,0:T(8,128)(2,1)} %collective-permute-done.12.refs_0_, bf16[2048,1024]{1,0:T(8,128)(2,1)} %refs_1_.11, bf16[2048,1024]{1,0:T(8,128)(2,1)} %refs_2_.11, bf16[2,256,512]{2,1,0:T(8,128)(2,1)} %add_convert_fusion.2.refs_3_), custom_call_target="tpu_custom_call" | custom-call | tf_op jit(solution)/shard_map/note_product/pallas_call | solution.py:67
  96.9 0.0 collective-permute-done.13.refs_4_.refs_0_
  96.9 6.0 %frame_own.1.refs_4_.refs_2_ = bf16[1024,1024]{1,0:T(8,128)(2,1)} custom-call(bf16[1024,512]{1,0:T(8,128)(2,1)} %get-tuple-element.44.refs_6_.refs_0_, bf16[1024,512]{1,0:T(8,128)(2,1)} %get-tuple-element.57.refs_1_, bf16[2048,1024]{1,0:T(8,128)(2,1)} %refs_2_.9, f32[2,256,1024]{2,1,0:T(8,128)} %note_product.3.refs_3_, ...), custom_call_target="tpu_custom_call" | custom-call | flops 8589934592 | tf_op jit(solution)/shard_map/frame_own/pallas_call | solution.py:67
  103.0 0.1 collective-permute-start.16
  103.1 0.0 collective-permute-done.11.refs_0_
  103.1 3.6 %note_product.4.refs_4_ = bf16[1,256,1024]{2,1,0:T(8,128)(2,1)} custom-call(bf16[2,256,512]{2,1,0:T(8,128)(2,1)} %collective-permute-done.11.refs_0_, bf16[2048,1024]{1,0:T(8,128)(2,1)} %refs_1_.11, bf16[2048,1024]{1,0:T(8,128)(2,1)} %refs_2_.11, f32[2,256,1024]{2,1,0:T(8,128)} %note_product.3.refs_3_, bf16[1024,1024]{1,0:T(8,128)(2,1)} %frame_own.1.refs_4_.refs_2_), custom_call_target="tpu_custom_call" | custom-call | tf_op jit(solution)/shard_map/note_product/pallas_call | solution.py:67
  106.7 1.4 %collective-permute-start.14 = (bf16[1,256,1024]{2,1,0:T(8,128)(2,1)}, bf16[1,256,1024]{2,1,0:T(8,128)(2,1)}, u32[]{:S(2)}, u32[]{:S(2)}) collective-permute-start(bf16[1,256,1024]{2,1,0:T(8,128)(2,1)} %note_product.4.refs_4_), channel_id=1, source_target_pairs={{0,1},{1,0},{2,3},{3,2},{4,5},{5,4},{6,7},{7,6},{8,9},{9,8},{10,11... | collective-permute-start | bytes 1572872 | tf_op jit(solution)/shard_map/ppermute | solution.py:47
  108.0 3.6 %note_product.5.refs_5_ = bf16[1,256,1024]{2,1,0:T(8,128)(2,1)} custom-call(bf16[2,256,512]{2,1,0:T(8,128)(2,1)} %collective-permute-done.11.refs_0_, bf16[2048,1024]{1,0:T(8,128)(2,1)} %refs_1_.11, bf16[2048,1024]{1,0:T(8,128)(2,1)} %refs_2_.11, f32[2,256,1024]{2,1,0:T(8,128)} %note_product.3.refs_3_, bf16[1,256,1024]{2,1,0:T(8,128)(2,1)} %note_product.4.refs_4_), custom_call_target="tpu_custom_call" | custom-call | tf_op jit(solution)/shard_map/note_product/pallas_call | solution.py:67
  111.6 2.7 %collective-permute-done.15.refs_1_ = bf16[1024,512]{1,0:T(8,128)(2,1)} collective-permute-done((bf16[1024,512]{1,0:T(8,128)(2,1)}, bf16[1024,512]{1,0:T(8,128)(2,1)}, u32[]{:S(2)}, u32[]{:S(2)}) %collective-permute-start.15) | collective-permute-done | bytes 1048608 | tf_op jit(solution)/shard_map/ppermute | solution.py:47
  114.3 0.0 collective-permute-done.16.refs_4_
  114.3 6.8 %frame_sum.1 = bf16[1024,1024]{1,0:T(8,128)(2,1)} custom-call(bf16[1024,512]{1,0:T(8,128)(2,1)} %collective-permute-done.13.refs_4_.refs_0_, bf16[1024,512]{1,0:T(8,128)(2,1)} %collective-permute-done.15.refs_1_, bf16[1024,1024]{1,0:T(8,128)(2,1)} %frame_own.1.refs_4_.refs_2_, bf16[512,1024]{1,0:T(8,128)(2,1)} %collective-permute-done.6.refs_3_, ...), custom_call_target="tpu_custom_call" | custom-call | tf_op jit(solution)/shard_map/frame_sum/pallas_call | solution.py:67
  121.0 4.5 %collective-permute-done.14 = bf16[1,256,1024]{2,1,0:T(8,128)(2,1)} collective-permute-done((bf16[1,256,1024]{2,1,0:T(8,128)(2,1)}, bf16[1,256,1024]{2,1,0:T(8,128)(2,1)}, u32[]{:S(2)}, u32[]{:S(2)}) %collective-permute-start.14) | collective-permute-done | bytes 524320 | tf_op jit(solution)/shard_map/ppermute | solution.py:47
  125.5 2.2 %add_convert_fusion = bf16[1,256,1024]{2,1,0:T(8,128)(2,1)} fusion(bf16[1,256,1024]{2,1,0:T(8,128)(2,1)} %collective-permute-done.14, bf16[1,256,1024]{2,1,0:T(8,128)(2,1)} %note_product.5.refs_5_), kind=kLoop, calls=%fused_computation | loop fusion | flops 1048576 | bytes 1572864 | tf_op jit(solution)/shard_map/convert_element_type | solution.py:500
Async XLA Ops:
  4.8 18.0 %collective-permute-start = (bf16[2,256,512]{2,1,0:T(8,128)(2,1)}, bf16[2,256,512]{2,1,0:T(8,128)(2,1)}, u32[]{:S(2)}, u32[]{:S(2)}) collective-permute-start(bf16[2,256,512]{2,1,0:T(8,128)(2,1)} %key_values.1.refs_5_), channel_id=1, source_target_pairs={{0,32},{32,64},{64,96},{96,0},{1,33},{33,65},{65,97},{97,1},{2,34}... | collective-permute-start | bytes 1572872 | tf_op jit(solution)/shard_map/ppermute | solution.py:30
  17.8 18.4 %collective-permute-start.1 = (bf16[2,256,512]{2,1,0:T(8,128)(2,1)}, bf16[2,256,512]{2,1,0:T(8,128)(2,1)}, u32[]{:S(2)}, u32[]{:S(2)}) collective-permute-start(bf16[2,256,512]{2,1,0:T(8,128)(2,1)} %get-tuple-element.34), channel_id=1, source_target_pairs={{0,32},{32,64},{64,96},{96,0},{1,33},{33,65},{65,97},{97,1},{2,34}... | collective-permute-start | bytes 1572872 | tf_op jit(solution)/shard_map/ppermute | solution.py:30
  19.1 36.2 %collective-permute-start.6 = (bf16[512,1024]{1,0:T(8,128)(2,1)}, bf16[512,1024]{1,0:T(8,128)(2,1)}, u32[]{:S(2)}, u32[]{:S(2)}) collective-permute-start(bf16[512,1024]{1,0:T(8,128)(2,1)} %get-tuple-element.42), channel_id=1, source_target_pairs={{0,17},{1,16},{2,19},{3,18},{4,21},{5,20},{6,23},{7,22},{8,25},{9,... | collective-permute-start | bytes 3145736 | tf_op jit(solution)/shard_map/ppermute | solution.py:53
  22.8 17.3 %collective-permute-start.3 = (bf16[2,256,512]{2,1,0:T(8,128)(2,1)}, bf16[2,256,512]{2,1,0:T(8,128)(2,1)}, u32[]{:S(2)}, u32[]{:S(2)}) collective-permute-start(bf16[2,256,512]{2,1,0:T(8,128)(2,1)} %collective-permute-done.refs_3_), channel_id=1, source_target_pairs={{2,4},{6,8},{10,12},{14,16},{18,20},{22,24},{26,28},{4,2},{8,6},{1... | collective-permute-start | bytes 1572872 | tf_op jit(solution)/shard_map/ppermute | solution.py:43
  27.4 12.7 %collective-permute-start.2 = (bf16[2,256,512]{2,1,0:T(8,128)(2,1)}, bf16[2,256,512]{2,1,0:T(8,128)(2,1)}, u32[]{:S(2)}, u32[]{:S(2)}) collective-permute-start(bf16[2,256,512]{2,1,0:T(8,128)(2,1)} %collective-permute-done.refs_3_), channel_id=1, source_target_pairs={{0,2},{2,0},{4,6},{6,4},{8,10},{10,8},{12,14},{14,12},{16,18},{18,... | collective-permute-start | bytes 1572872 | tf_op jit(solution)/shard_map/ppermute | solution.py:37
  36.2 18.2 %collective-permute-start.5 = (bf16[2,256,512]{2,1,0:T(8,128)(2,1)}, bf16[2,256,512]{2,1,0:T(8,128)(2,1)}, u32[]{:S(2)}, u32[]{:S(2)}) collective-permute-start(bf16[2,256,512]{2,1,0:T(8,128)(2,1)} %collective-permute-done.1.refs_3_), channel_id=1, source_target_pairs={{2,4},{6,8},{10,12},{14,16},{18,20},{22,24},{26,28},{4,2},{8,6},{1... | collective-permute-start | bytes 1572872 | tf_op jit(solution)/shard_map/ppermute | solution.py:43
  39.8 14.6 %collective-permute-start.4 = (bf16[2,256,512]{2,1,0:T(8,128)(2,1)}, bf16[2,256,512]{2,1,0:T(8,128)(2,1)}, u32[]{:S(2)}, u32[]{:S(2)}) collective-permute-start(bf16[2,256,512]{2,1,0:T(8,128)(2,1)} %collective-permute-done.1.refs_3_), channel_id=1, source_target_pairs={{0,2},{2,0},{4,6},{6,4},{8,10},{10,8},{12,14},{14,12},{16,18},{18,... | collective-permute-start | bytes 1572872 | tf_op jit(solution)/shard_map/ppermute | solution.py:37
  54.4 42.5 %collective-permute-start.13 = (bf16[1024,512]{1,0:T(8,128)(2,1)}, bf16[1024,512]{1,0:T(8,128)(2,1)}, u32[]{:S(2)}, u32[]{:S(2)}) collective-permute-start(bf16[1024,512]{1,0:T(8,128)(2,1)} %get-tuple-element.44.refs_6_.refs_0_), channel_id=1, source_target_pairs={{0,1},{1,0},{2,3},{3,2},{4,5},{5,4},{6,7},{7,6},{8,9},{9,8},{10,11... | collective-permute-start | bytes 3145736 | tf_op jit(solution)/shard_map/ppermute | solution.py:47
  55.3 18.0 %collective-permute-start.7 = (bf16[2,256,512]{2,1,0:T(8,128)(2,1)}, bf16[2,256,512]{2,1,0:T(8,128)(2,1)}, u32[]{:S(2)}, u32[]{:S(2)}) collective-permute-start(bf16[2,256,512]{2,1,0:T(8,128)(2,1)} %get-tuple-element.46), channel_id=1, source_target_pairs={{0,2},{2,0},{4,6},{6,4},{8,10},{10,8},{12,14},{14,12},{16,18},{18,... | collective-permute-start | bytes 1572872 | tf_op jit(solution)/shard_map/ppermute | solution.py:37
  56.1 17.2 %collective-permute-start.8 = (bf16[2,256,512]{2,1,0:T(8,128)(2,1)}, bf16[2,256,512]{2,1,0:T(8,128)(2,1)}, u32[]{:S(2)}, u32[]{:S(2)}) collective-permute-start(bf16[2,256,512]{2,1,0:T(8,128)(2,1)} %get-tuple-element.47), channel_id=1, source_target_pairs={{2,4},{6,8},{10,12},{14,16},{18,20},{22,24},{26,28},{4,2},{8,6},{1... | collective-permute-start | bytes 1572872 | tf_op jit(solution)/shard_map/ppermute | solution.py:43
  73.3 8.2 %collective-permute-start.9 = (bf16[2,256,512]{2,1,0:T(8,128)(2,1)}, bf16[2,256,512]{2,1,0:T(8,128)(2,1)S(1)}, u32[]{:S(2)}, u32[]{:S(2)}) collective-permute-start(bf16[2,256,512]{2,1,0:T(8,128)(2,1)} %get-tuple-element.50), channel_id=1, source_target_pairs={{0,2},{2,0},{4,6},{6,4},{8,10},{10,8},{12,14},{14,12},{16,18},{18,... | collective-permute-start | bytes 1572872 | tf_op jit(solution)/shard_map/ppermute | solution.py:37
  73.4 11.1 %collective-permute-start.10 = (bf16[2,256,512]{2,1,0:T(8,128)(2,1)}, bf16[2,256,512]{2,1,0:T(8,128)(2,1)S(1)}, u32[]{:S(2)}, u32[]{:S(2)}) collective-permute-start(bf16[2,256,512]{2,1,0:T(8,128)(2,1)} %get-tuple-element.51), channel_id=1, source_target_pairs={{2,4},{6,8},{10,12},{14,16},{18,20},{22,24},{26,28},{4,2},{8,6},{1... | collective-permute-start | bytes 1572872 | tf_op jit(solution)/shard_map/ppermute | solution.py:43
  78.4 14.2 %collective-permute-start.12 = (bf16[2,256,512]{2,1,0:T(8,128)(2,1)S(1)}, bf16[2,256,512]{2,1,0:T(8,128)(2,1)}, u32[]{:S(2)}, u32[]{:S(2)}) collective-permute-start(bf16[2,256,512]{2,1,0:T(8,128)(2,1)S(1)} %add_convert_fusion.1), channel_id=1, source_target_pairs={{0,96},{32,0},{64,32},{96,64},{1,97},{33,1},{65,33},{97,65},{2,98}... | collective-permute-start | bytes 1572872 | tf_op jit(solution)/shard_map/ppermute | solution.py:30
  79.7 34.6 %collective-permute-start.15 = (bf16[1024,512]{1,0:T(8,128)(2,1)}, bf16[1024,512]{1,0:T(8,128)(2,1)}, u32[]{:S(2)}, u32[]{:S(2)}) collective-permute-start(bf16[1024,512]{1,0:T(8,128)(2,1)} %get-tuple-element.57.refs_1_), channel_id=1, source_target_pairs={{0,1},{1,0},{2,3},{3,2},{4,5},{5,4},{6,7},{7,6},{8,9},{9,8},{10,11... | collective-permute-start | bytes 3145736 | tf_op jit(solution)/shard_map/ppermute | solution.py:47
  86.7 16.3 %collective-permute-start.11 = (bf16[2,256,512]{2,1,0:T(8,128)(2,1)}, bf16[2,256,512]{2,1,0:T(8,128)(2,1)}, u32[]{:S(2)}, u32[]{:S(2)}) collective-permute-start(bf16[2,256,512]{2,1,0:T(8,128)(2,1)} %add_convert_fusion.2.refs_3_), channel_id=1, source_target_pairs={{0,96},{32,0},{64,32},{96,64},{1,97},{33,1},{65,33},{97,65},{2,98}... | collective-permute-start | bytes 1572872 | tf_op jit(solution)/shard_map/ppermute | solution.py:30
  103.0 11.3 %collective-permute-start.16 = (bf16[512,1024]{1,0:T(8,128)(2,1)}, bf16[512,1024]{1,0:T(8,128)(2,1)}, u32[]{:S(2)}, u32[]{:S(2)}) collective-permute-start(bf16[512,1024]{1,0:T(8,128)(2,1)} %collective-permute-done.6.refs_3_), channel_id=1, source_target_pairs={{0,2},{2,0},{4,6},{6,4},{8,10},{10,8},{12,14},{14,12},{16,18},{18,... | collective-permute-start | bytes 3145736 | tf_op jit(solution)/shard_map/ppermute | solution.py:37
  106.7 18.9 %collective-permute-start.14 = (bf16[1,256,1024]{2,1,0:T(8,128)(2,1)}, bf16[1,256,1024]{2,1,0:T(8,128)(2,1)}, u32[]{:S(2)}, u32[]{:S(2)}) collective-permute-start(bf16[1,256,1024]{2,1,0:T(8,128)(2,1)} %note_product.4.refs_4_), channel_id=1, source_target_pairs={{0,1},{1,0},{2,3},{3,2},{4,5},{5,4},{6,7},{7,6},{8,9},{9,8},{10,11... | collective-permute-start | bytes 1572872 | tf_op jit(solution)/shard_map/ppermute | solution.py:47

commit v12 on v11

--- a/solution.py
+++ b/solution.py
@@ -102,11 +102,15 @@
     def body(notes_ref, wk_ref, wv_ref, out_ref, n_scr, wk_scr, wv_scr, out_scr, sems):
         (notes_in,) = start_all([pltpu.make_async_copy(notes_ref, n_scr, sems.at[2])])
         weights_in = key_value_copies(wk_ref, wv_ref, wk_scr, wv_scr, sems, h0, hc)
+        sent = []
         notes_in.wait()
         for i, scr in enumerate((wk_scr, wv_scr)):
             weights_in[i].wait()
             out_scr[i] = dot(n_scr[...], scr[...], NN).astype(BF16)
-        for copy in start_all([pltpu.make_async_copy(out_scr, out_ref, sems.at[3])]):
+            sent += start_all(
+                [pltpu.make_async_copy(out_scr.at[i], out_ref.at[i], sems.at[3 + i])]
+            )
+        for copy in sent:
             copy.wait()
 
     far = pl.BlockSpec(memory_space=pl.ANY)
@@ -123,7 +127,7 @@
             pltpu.VMEM((D, hc * HD), BF16),
             pltpu.VMEM((D, hc * HD), BF16),
             pltpu.VMEM((2, rows, hc * HD), BF16),
-            pltpu.SemaphoreType.DMA((4,)),
+            pltpu.SemaphoreType.DMA((5,)),
         ],
     )
 

time: 128 us -> 128 us (level)
  no operation moved by 1% of the time
where the time goes in v12:
time: 128 us
  Pallas kernels  76.5 us (60%)
  starting transfers between devices  29.3 us (23%)
  waiting for transfers between devices  14.8 us (12%)
  other arithmetic  6.15 us (5%)
    pallas_call x10, Pallas kernels, call(): pl.pallas_call(reads, grid_spec=pltpu.PrefetchScalarGridSpec(num_scalar_p...  76.5 us
    ppermute x4, starting transfers between devices, far_swap(): return lax.ppermute(block, 'seq', pairs + [(j, i) for i, j in pairs])  14.3 us
    ppermute x3, waiting for transfers between devices, head_swap(): return lax.ppermute(block, 'head', [(0, 1), (1, 0)])  7.15 us
    ppermute x4, starting transfers between devices, section_shift(): lax.ppermute(block, 'section', [(i, (i + distance) % count) for i in rang...  5.87 us
    ppermute x4, waiting for transfers between devices, section_shift(): lax.ppermute(block, 'section', [(i, (i + distance) % count) for i in rang...  4.66 us
    ppermute x3, starting transfers between devices, head_swap(): return lax.ppermute(block, 'head', [(0, 1), (1, 0)])  4.09 us
    convert_element_type x2, other arithmetic, note_sum_of(): return (own + near.astype(F32) + far.astype(F32)).astype(BF16)  3.96 us
    ppermute x1, starting transfers between devices, across(): return lax.ppermute(block, ('seq', 'head'), route)  3.76 us
  transfers between devices with their start and end apart: 17, of which 4 were waited for; matrix products, arithmetic and copies ran while one was open for 3% of the time, Pallas kernels for 57%

profile of v12, /device:TPU:1, one launch (start us, length us, event | category | flops | bytes accessed | tf_op | source)
XLA Modules:
  0.0 127.6 jit_solution(6251265599307476801)
XLA Ops:
  0.6 4.1 %key_values.1.refs_5_ = bf16[2,256,512]{2,1,0:T(8,128)(2,1)} custom-call(bf16[256,2048]{1,0:T(8,128)(2,1)} %bitcast.6, bf16[2048,1024]{1,0:T(8,128)(2,1)} %refs_1_.11, bf16[2048,1024]{1,0:T(8,128)(2,1)} %refs_2_.11), custom_call_target="tpu_custom_call" | custom-call | tf_op jit(solution)/shard_map/key_values/pallas_call | solution.py:67
  4.7 2.1 %collective-permute-start = (bf16[2,256,512]{2,1,0:T(8,128)(2,1)}, bf16[2,256,512]{2,1,0:T(8,128)(2,1)}, u32[]{:S(2)}, u32[]{:S(2)}) collective-permute-start(bf16[2,256,512]{2,1,0:T(8,128)(2,1)} %key_values.1.refs_5_), channel_id=1, source_target_pairs={{0,32},{32,64},{64,96},{96,0},{1,33},{33,65},{65,97},{97,1},{2,34}... | collective-permute-start | bytes 1572872 | tf_op jit(solution)/shard_map/ppermute | solution.py:30
  6.8 10.9 %key_values_and_queries.1 = (bf16[2,256,512]{2,1,0:T(8,128)(2,1)}, bf16[1024,1024]{1,0:T(8,128)(2,1)}, bf16[512,1024]{1,0:T(8,128)(2,1)}) custom-call(bf16[256,2048]{1,0:T(8,128)(2,1)} %bitcast.7, bf16[2048,1024]{1,0:T(8,128)(2,1)} %refs_1_.11, bf16[2048,1024]{1,0:T(8,128)(2,1)} %refs_2_.11, bf16[1024,2048]{1,0:T(8,128)(2,1)} %bitcast.8, ...), custom_call_target="tpu_custom_call" | custom-call | tf_op jit(solution)/shard_map/key_values_and_queries/pallas_call | solution.py:67
  17.7 1.3 %collective-permute-start.1 = (bf16[2,256,512]{2,1,0:T(8,128)(2,1)}, bf16[2,256,512]{2,1,0:T(8,128)(2,1)}, u32[]{:S(2)}, u32[]{:S(2)}) collective-permute-start(bf16[2,256,512]{2,1,0:T(8,128)(2,1)} %get-tuple-element.34), channel_id=1, source_target_pairs={{0,32},{32,64},{64,96},{96,0},{1,33},{33,65},{65,97},{97,1},{2,34}... | collective-permute-start | bytes 1572872 | tf_op jit(solution)/shard_map/ppermute | solution.py:30
  19.0 3.8 %collective-permute-start.6 = (bf16[512,1024]{1,0:T(8,128)(2,1)}, bf16[512,1024]{1,0:T(8,128)(2,1)}, u32[]{:S(2)}, u32[]{:S(2)}) collective-permute-start(bf16[512,1024]{1,0:T(8,128)(2,1)} %get-tuple-element.42), channel_id=1, source_target_pairs={{0,17},{1,16},{2,19},{3,18},{4,21},{5,20},{6,23},{7,22},{8,25},{9,... | collective-permute-start | bytes 3145736 | tf_op jit(solution)/shard_map/ppermute | solution.py:53
  22.8 0.0 collective-permute-done.refs_3_
  22.8 4.6 %collective-permute-start.3 = (bf16[2,256,512]{2,1,0:T(8,128)(2,1)}, bf16[2,256,512]{2,1,0:T(8,128)(2,1)}, u32[]{:S(2)}, u32[]{:S(2)}) collective-permute-start(bf16[2,256,512]{2,1,0:T(8,128)(2,1)} %collective-permute-done.refs_3_), channel_id=1, source_target_pairs={{2,4},{6,8},{10,12},{14,16},{18,20},{22,24},{26,28},{4,2},{8,6},{1... | collective-permute-start | bytes 1572872 | tf_op jit(solution)/shard_map/ppermute | solution.py:43
  27.4 0.1 collective-permute-start.2
  27.5 8.7 %grad_ctx.1.refs_2_ = bf16[1024,1024]{1,0:T(8,128)(2,1)} custom-call(bf16[1024,2048]{1,0:T(8,128)(2,1)} %bitcast.5, bf16[1024,2048]{1,0:T(8,128)(2,1)} %refs_1_.8, bf16[1024,1024]{1,0:T(8,128)(2,1)} %get-tuple-element.33.refs_2_.refs_1_, bf16[2,256,512]{2,1,0:T(8,128)(2,1)} %collective-permute-done.refs_3_), custom_call_target="tpu_custom_call" | custom-call | tf_op jit(solution)/shard_map/grad_ctx/pallas_call | solution.py:67
  36.2 0.0 collective-permute-done.1.refs_3_
  36.2 3.6 %collective-permute-start.5 = (bf16[2,256,512]{2,1,0:T(8,128)(2,1)}, bf16[2,256,512]{2,1,0:T(8,128)(2,1)}, u32[]{:S(2)}, u32[]{:S(2)}) collective-permute-start(bf16[2,256,512]{2,1,0:T(8,128)(2,1)} %collective-permute-done.1.refs_3_), channel_id=1, source_target_pairs={{2,4},{6,8},{10,12},{14,16},{18,20},{22,24},{26,28},{4,2},{8,6},{1... | collective-permute-start | bytes 1572872 | tf_op jit(solution)/shard_map/ppermute | solution.py:43
  39.7 0.3 collective-permute-start.4
  40.0 0.0 collective-permute-done.3.refs_5_
  40.0 0.0 collective-permute-done.2.refs_4_
  40.0 14.3 %attention.2 = (bf16[1024,512]{1,0:T(8,128)(2,1)}, f32[2,256,512]{2,1,0:T(8,128)}, bf16[2,256,512]{2,1,0:T(8,128)(2,1)}, bf16[2,256,512]{2,1,0:T(8,128)(2,1)}) custom-call(s32[2,8]{1,0:T(2,128)} %bitcast.10, bf16[1024,1024]{1,0:T(8,128)(2,1)} %get-tuple-element.33.refs_2_.refs_1_, bf16[1024,1024]{1,0:T(8,128)(2,1)} %grad_ctx.1.refs_2_, ...), custom_call_target="tpu_custom_call" | custom-call | tf_op jit(solution)/shard_map/attention/pallas_call | solution.py:67
  54.3 0.0 collective-permute-done.5.refs_5_
  54.3 0.0 collective-permute-done.4.refs_4_
  54.3 0.9 collective-permute-start.13
  55.2 0.0 collective-permute-done.6.refs_3_
  55.2 0.8 collective-permute-start.7
  56.0 2.9 %collective-permute-start.8 = (bf16[2,256,512]{2,1,0:T(8,128)(2,1)}, bf16[2,256,512]{2,1,0:T(8,128)(2,1)}, u32[]{:S(2)}, u32[]{:S(2)}) collective-permute-start(bf16[2,256,512]{2,1,0:T(8,128)(2,1)} %get-tuple-element.47), channel_id=1, source_target_pairs={{2,4},{6,8},{10,12},{14,16},{18,20},{22,24},{26,28},{4,2},{8,6},{1... | collective-permute-start | bytes 1572872 | tf_op jit(solution)/shard_map/ppermute | solution.py:43
  58.8 14.4 %attention.3 = (bf16[1024,512]{1,0:T(8,128)(2,1)}, f32[2,256,512]{2,1,0:T(8,128)}, bf16[2,256,512]{2,1,0:T(8,128)(2,1)}, bf16[2,256,512]{2,1,0:T(8,128)(2,1)}) custom-call(s32[2,8]{1,0:T(2,128)} %bitcast.11, bf16[1024,1024]{1,0:T(8,128)(2,1)} %get-tuple-element.33.refs_2_.refs_1_, bf16[1024,1024]{1,0:T(8,128)(2,1)} %grad_ctx.1.refs_2_, ...), custom_call_target="tpu_custom_call" | custom-call | flops 12079595520 | tf_op jit(solution)/shard_map/attention/pallas_call | solution.py:67
  73.2 0.0 collective-permute-done.7
  73.2 0.0 collective-permute-done.8
  73.2 0.1 collective-permute-start.9
  73.3 3.3 %collective-permute-start.10 = (bf16[2,256,512]{2,1,0:T(8,128)(2,1)}, bf16[2,256,512]{2,1,0:T(8,128)(2,1)S(1)}, u32[]{:S(2)}, u32[]{:S(2)}) collective-permute-start(bf16[2,256,512]{2,1,0:T(8,128)(2,1)} %get-tuple-element.51), channel_id=1, source_target_pairs={{2,4},{6,8},{10,12},{14,16},{18,20},{22,24},{26,28},{4,2},{8,6},{1... | collective-permute-start | bytes 1572872 | tf_op jit(solution)/shard_map/ppermute | solution.py:43
  76.6 1.7 %add_convert_fusion.1 = bf16[2,256,512]{2,1,0:T(8,128)(2,1)S(1)} fusion(bf16[2,256,512]{2,1,0:T(8,128)(2,1)} %collective-permute-done.8, f32[2,256,512]{2,1,0:T(8,128)} %get-tuple-element.52, bf16[2,256,512]{2,1,0:T(8,128)(2,1)} %collective-permute-done.7), kind=kLoop, calls=%fused_computation.1 | loop fusion | flops 1310720 | bytes 2621440 | tf_op jit(solution)/shard_map/convert_element_type | solution.py:469
  78.3 1.3 %collective-permute-start.12 = (bf16[2,256,512]{2,1,0:T(8,128)(2,1)S(1)}, bf16[2,256,512]{2,1,0:T(8,128)(2,1)}, u32[]{:S(2)}, u32[]{:S(2)}) collective-permute-start(bf16[2,256,512]{2,1,0:T(8,128)(2,1)S(1)} %add_convert_fusion.1), channel_id=1, source_target_pairs={{0,96},{32,0},{64,32},{96,64},{1,97},{33,1},{65,33},{97,65},{2,98}... | collective-permute-start | bytes 1572872 | tf_op jit(solution)/shard_map/ppermute | solution.py:30
  79.6 1.8 %collective-permute-start.15 = (bf16[1024,512]{1,0:T(8,128)(2,1)}, bf16[1024,512]{1,0:T(8,128)(2,1)}, u32[]{:S(2)}, u32[]{:S(2)}) collective-permute-start(bf16[1024,512]{1,0:T(8,128)(2,1)} %get-tuple-element.57.refs_1_), channel_id=1, source_target_pairs={{0,1},{1,0},{2,3},{3,2},{4,5},{5,4},{6,7},{7,6},{8,9},{9,8},{10,11... | collective-permute-start | bytes 3145736 | tf_op jit(solution)/shard_map/ppermute | solution.py:47
  81.4 0.0 collective-permute-done.9
  81.4 3.0 %collective-permute-done.10 = bf16[2,256,512]{2,1,0:T(8,128)(2,1)S(1)} collective-permute-done((bf16[2,256,512]{2,1,0:T(8,128)(2,1)}, bf16[2,256,512]{2,1,0:T(8,128)(2,1)S(1)}, u32[]{:S(2)}, u32[]{:S(2)}) %collective-permute-start.10) | collective-permute-done | bytes 524320 | tf_op jit(solution)/shard_map/ppermute | solution.py:43
  84.4 2.2 %add_convert_fusion.2.refs_3_ = bf16[2,256,512]{2,1,0:T(8,128)(2,1)} fusion(bf16[2,256,512]{2,1,0:T(8,128)(2,1)S(1)} %collective-permute-done.10, f32[2,256,512]{2,1,0:T(8,128)} %get-tuple-element.45, bf16[2,256,512]{2,1,0:T(8,128)(2,1)S(1)} %collective-permute-done.9), kind=kLoop, calls=%fused_computation.2 | loop fusion | flops 1310720 | bytes 2621440 | tf_op jit(solution)/shard_map/convert_element_type | solution.py:469
  86.6 1.2 collective-permute-start.11
  87.9 4.7 %collective-permute-done.12.refs_0_ = bf16[2,256,512]{2,1,0:T(8,128)(2,1)} collective-permute-done((bf16[2,256,512]{2,1,0:T(8,128)(2,1)S(1)}, bf16[2,256,512]{2,1,0:T(8,128)(2,1)}, u32[]{:S(2)}, u32[]{:S(2)}) %collective-permute-start.12) | collective-permute-done | bytes 524320 | tf_op jit(solution)/shard_map/ppermute | solution.py:30
  92.5 4.3 %note_product.3.refs_3_ = f32[2,256,1024]{2,1,0:T(8,128)} custom-call(bf16[2,256,512]{2,1,0:T(8,128)(2,1)} %collective-permute-done.12.refs_0_, bf16[2048,1024]{1,0:T(8,128)(2,1)} %refs_1_.11, bf16[2048,1024]{1,0:T(8,128)(2,1)} %refs_2_.11, bf16[2,256,512]{2,1,0:T(8,128)(2,1)} %add_convert_fusion.2.refs_3_), custom_call_target="tpu_custom_call" | custom-call | tf_op jit(solution)/shard_map/note_product/pallas_call | solution.py:67
  96.8 0.0 collective-permute-done.13.refs_4_.refs_0_
  96.8 6.0 %frame_own.1.refs_4_.refs_2_ = bf16[1024,1024]{1,0:T(8,128)(2,1)} custom-call(bf16[1024,512]{1,0:T(8,128)(2,1)} %get-tuple-element.44.refs_6_.refs_0_, bf16[1024,512]{1,0:T(8,128)(2,1)} %get-tuple-element.57.refs_1_, bf16[2048,1024]{1,0:T(8,128)(2,1)} %refs_2_.9, f32[2,256,1024]{2,1,0:T(8,128)} %note_product.3.refs_3_, ...), custom_call_target="tpu_custom_call" | custom-call | flops 8589934592 | tf_op jit(solution)/shard_map/frame_own/pallas_call | solution.py:67
  102.9 0.1 collective-permute-start.16
  103.0 0.0 collective-permute-done.11.refs_0_
  103.0 3.6 %note_product.4.refs_4_ = bf16[1,256,1024]{2,1,0:T(8,128)(2,1)} custom-call(bf16[2,256,512]{2,1,0:T(8,128)(2,1)} %collective-permute-done.11.refs_0_, bf16[2048,1024]{1,0:T(8,128)(2,1)} %refs_1_.11, bf16[2048,1024]{1,0:T(8,128)(2,1)} %refs_2_.11, f32[2,256,1024]{2,1,0:T(8,128)} %note_product.3.refs_3_, bf16[1024,1024]{1,0:T(8,128)(2,1)} %frame_own.1.refs_4_.refs_2_), custom_call_target="tpu_custom_call" | custom-call | tf_op jit(solution)/shard_map/note_product/pallas_call | solution.py:67
  106.6 1.4 %collective-permute-start.14 = (bf16[1,256,1024]{2,1,0:T(8,128)(2,1)}, bf16[1,256,1024]{2,1,0:T(8,128)(2,1)}, u32[]{:S(2)}, u32[]{:S(2)}) collective-permute-start(bf16[1,256,1024]{2,1,0:T(8,128)(2,1)} %note_product.4.refs_4_), channel_id=1, source_target_pairs={{0,1},{1,0},{2,3},{3,2},{4,5},{5,4},{6,7},{7,6},{8,9},{9,8},{10,11... | collective-permute-start | bytes 1572872 | tf_op jit(solution)/shard_map/ppermute | solution.py:47
  107.9 3.6 %note_product.5.refs_5_ = bf16[1,256,1024]{2,1,0:T(8,128)(2,1)} custom-call(bf16[2,256,512]{2,1,0:T(8,128)(2,1)} %collective-permute-done.11.refs_0_, bf16[2048,1024]{1,0:T(8,128)(2,1)} %refs_1_.11, bf16[2048,1024]{1,0:T(8,128)(2,1)} %refs_2_.11, f32[2,256,1024]{2,1,0:T(8,128)} %note_product.3.refs_3_, bf16[1,256,1024]{2,1,0:T(8,128)(2,1)} %note_product.4.refs_4_), custom_call_target="tpu_custom_call" | custom-call | tf_op jit(solution)/shard_map/note_product/pallas_call | solution.py:67
  111.5 2.7 %collective-permute-done.15.refs_1_ = bf16[1024,512]{1,0:T(8,128)(2,1)} collective-permute-done((bf16[1024,512]{1,0:T(8,128)(2,1)}, bf16[1024,512]{1,0:T(8,128)(2,1)}, u32[]{:S(2)}, u32[]{:S(2)}) %collective-permute-start.15) | collective-permute-done | bytes 1048608 | tf_op jit(solution)/shard_map/ppermute | solution.py:47
  114.2 0.0 collective-permute-done.16.refs_4_
  114.2 6.8 %frame_sum.1 = bf16[1024,1024]{1,0:T(8,128)(2,1)} custom-call(bf16[1024,512]{1,0:T(8,128)(2,1)} %collective-permute-done.13.refs_4_.refs_0_, bf16[1024,512]{1,0:T(8,128)(2,1)} %collective-permute-done.15.refs_1_, bf16[1024,1024]{1,0:T(8,128)(2,1)} %frame_own.1.refs_4_.refs_2_, bf16[512,1024]{1,0:T(8,128)(2,1)} %collective-permute-done.6.refs_3_, ...), custom_call_target="tpu_custom_call" | custom-call | tf_op jit(solution)/shard_map/frame_sum/pallas_call | solution.py:67
  120.9 4.5 %collective-permute-done.14 = bf16[1,256,1024]{2,1,0:T(8,128)(2,1)} collective-permute-done((bf16[1,256,1024]{2,1,0:T(8,128)(2,1)}, bf16[1,256,1024]{2,1,0:T(8,128)(2,1)}, u32[]{:S(2)}, u32[]{:S(2)}) %collective-permute-start.14) | collective-permute-done | bytes 524320 | tf_op jit(solution)/shard_map/ppermute | solution.py:47
  125.4 2.2 %add_convert_fusion = bf16[1,256,1024]{2,1,0:T(8,128)(2,1)} fusion(bf16[1,256,1024]{2,1,0:T(8,128)(2,1)} %collective-permute-done.14, bf16[1,256,1024]{2,1,0:T(8,128)(2,1)} %note_product.5.refs_5_), kind=kLoop, calls=%fused_computation | loop fusion | flops 1048576 | bytes 1572864 | tf_op jit(solution)/shard_map/convert_element_type | solution.py:504
Async XLA Ops:
  4.7 18.0 %collective-permute-start = (bf16[2,256,512]{2,1,0:T(8,128)(2,1)}, bf16[2,256,512]{2,1,0:T(8,128)(2,1)}, u32[]{:S(2)}, u32[]{:S(2)}) collective-permute-start(bf16[2,256,512]{2,1,0:T(8,128)(2,1)} %key_values.1.refs_5_), channel_id=1, source_target_pairs={{0,32},{32,64},{64,96},{96,0},{1,33},{33,65},{65,97},{97,1},{2,34}... | collective-permute-start | bytes 1572872 | tf_op jit(solution)/shard_map/ppermute | solution.py:30
  17.7 18.4 %collective-permute-start.1 = (bf16[2,256,512]{2,1,0:T(8,128)(2,1)}, bf16[2,256,512]{2,1,0:T(8,128)(2,1)}, u32[]{:S(2)}, u32[]{:S(2)}) collective-permute-start(bf16[2,256,512]{2,1,0:T(8,128)(2,1)} %get-tuple-element.34), channel_id=1, source_target_pairs={{0,32},{32,64},{64,96},{96,0},{1,33},{33,65},{65,97},{97,1},{2,34}... | collective-permute-start | bytes 1572872 | tf_op jit(solution)/shard_map/ppermute | solution.py:30
  19.0 36.2 %collective-permute-start.6 = (bf16[512,1024]{1,0:T(8,128)(2,1)}, bf16[512,1024]{1,0:T(8,128)(2,1)}, u32[]{:S(2)}, u32[]{:S(2)}) collective-permute-start(bf16[512,1024]{1,0:T(8,128)(2,1)} %get-tuple-element.42), channel_id=1, source_target_pairs={{0,17},{1,16},{2,19},{3,18},{4,21},{5,20},{6,23},{7,22},{8,25},{9,... | collective-permute-start | bytes 3145736 | tf_op jit(solution)/shard_map/ppermute | solution.py:53
  22.8 17.3 %collective-permute-start.3 = (bf16[2,256,512]{2,1,0:T(8,128)(2,1)}, bf16[2,256,512]{2,1,0:T(8,128)(2,1)}, u32[]{:S(2)}, u32[]{:S(2)}) collective-permute-start(bf16[2,256,512]{2,1,0:T(8,128)(2,1)} %collective-permute-done.refs_3_), channel_id=1, source_target_pairs={{2,4},{6,8},{10,12},{14,16},{18,20},{22,24},{26,28},{4,2},{8,6},{1... | collective-permute-start | bytes 1572872 | tf_op jit(solution)/shard_map/ppermute | solution.py:43
  27.4 12.7 %collective-permute-start.2 = (bf16[2,256,512]{2,1,0:T(8,128)(2,1)}, bf16[2,256,512]{2,1,0:T(8,128)(2,1)}, u32[]{:S(2)}, u32[]{:S(2)}) collective-permute-start(bf16[2,256,512]{2,1,0:T(8,128)(2,1)} %collective-permute-done.refs_3_), channel_id=1, source_target_pairs={{0,2},{2,0},{4,6},{6,4},{8,10},{10,8},{12,14},{14,12},{16,18},{18,... | collective-permute-start | bytes 1572872 | tf_op jit(solution)/shard_map/ppermute | solution.py:37
  36.2 18.1 %collective-permute-start.5 = (bf16[2,256,512]{2,1,0:T(8,128)(2,1)}, bf16[2,256,512]{2,1,0:T(8,128)(2,1)}, u32[]{:S(2)}, u32[]{:S(2)}) collective-permute-start(bf16[2,256,512]{2,1,0:T(8,128)(2,1)} %collective-permute-done.1.refs_3_), channel_id=1, source_target_pairs={{2,4},{6,8},{10,12},{14,16},{18,20},{22,24},{26,28},{4,2},{8,6},{1... | collective-permute-start | bytes 1572872 | tf_op jit(solution)/shard_map/ppermute | solution.py:43
  39.7 14.6 %collective-permute-start.4 = (bf16[2,256,512]{2,1,0:T(8,128)(2,1)}, bf16[2,256,512]{2,1,0:T(8,128)(2,1)}, u32[]{:S(2)}, u32[]{:S(2)}) collective-permute-start(bf16[2,256,512]{2,1,0:T(8,128)(2,1)} %collective-permute-done.1.refs_3_), channel_id=1, source_target_pairs={{0,2},{2,0},{4,6},{6,4},{8,10},{10,8},{12,14},{14,12},{16,18},{18,... | collective-permute-start | bytes 1572872 | tf_op jit(solution)/shard_map/ppermute | solution.py:37
  54.3 42.5 %collective-permute-start.13 = (bf16[1024,512]{1,0:T(8,128)(2,1)}, bf16[1024,512]{1,0:T(8,128)(2,1)}, u32[]{:S(2)}, u32[]{:S(2)}) collective-permute-start(bf16[1024,512]{1,0:T(8,128)(2,1)} %get-tuple-element.44.refs_6_.refs_0_), channel_id=1, source_target_pairs={{0,1},{1,0},{2,3},{3,2},{4,5},{5,4},{6,7},{7,6},{8,9},{9,8},{10,11... | collective-permute-start | bytes 3145736 | tf_op jit(solution)/shard_map/ppermute | solution.py:47
  55.2 18.0 %collective-permute-start.7 = (bf16[2,256,512]{2,1,0:T(8,128)(2,1)}, bf16[2,256,512]{2,1,0:T(8,128)(2,1)}, u32[]{:S(2)}, u32[]{:S(2)}) collective-permute-start(bf16[2,256,512]{2,1,0:T(8,128)(2,1)} %get-tuple-element.46), channel_id=1, source_target_pairs={{0,2},{2,0},{4,6},{6,4},{8,10},{10,8},{12,14},{14,12},{16,18},{18,... | collective-permute-start | bytes 1572872 | tf_op jit(solution)/shard_map/ppermute | solution.py:37
  56.0 17.2 %collective-permute-start.8 = (bf16[2,256,512]{2,1,0:T(8,128)(2,1)}, bf16[2,256,512]{2,1,0:T(8,128)(2,1)}, u32[]{:S(2)}, u32[]{:S(2)}) collective-permute-start(bf16[2,256,512]{2,1,0:T(8,128)(2,1)} %get-tuple-element.47), channel_id=1, source_target_pairs={{2,4},{6,8},{10,12},{14,16},{18,20},{22,24},{26,28},{4,2},{8,6},{1... | collective-permute-start | bytes 1572872 | tf_op jit(solution)/shard_map/ppermute | solution.py:43
  73.2 8.2 %collective-permute-start.9 = (bf16[2,256,512]{2,1,0:T(8,128)(2,1)}, bf16[2,256,512]{2,1,0:T(8,128)(2,1)S(1)}, u32[]{:S(2)}, u32[]{:S(2)}) collective-permute-start(bf16[2,256,512]{2,1,0:T(8,128)(2,1)} %get-tuple-element.50), channel_id=1, source_target_pairs={{0,2},{2,0},{4,6},{6,4},{8,10},{10,8},{12,14},{14,12},{16,18},{18,... | collective-permute-start | bytes 1572872 | tf_op jit(solution)/shard_map/ppermute | solution.py:37
  73.3 11.1 %collective-permute-start.10 = (bf16[2,256,512]{2,1,0:T(8,128)(2,1)}, bf16[2,256,512]{2,1,0:T(8,128)(2,1)S(1)}, u32[]{:S(2)}, u32[]{:S(2)}) collective-permute-start(bf16[2,256,512]{2,1,0:T(8,128)(2,1)} %get-tuple-element.51), channel_id=1, source_target_pairs={{2,4},{6,8},{10,12},{14,16},{18,20},{22,24},{26,28},{4,2},{8,6},{1... | collective-permute-start | bytes 1572872 | tf_op jit(solution)/shard_map/ppermute | solution.py:43
  78.3 14.2 %collective-permute-start.12 = (bf16[2,256,512]{2,1,0:T(8,128)(2,1)S(1)}, bf16[2,256,512]{2,1,0:T(8,128)(2,1)}, u32[]{:S(2)}, u32[]{:S(2)}) collective-permute-start(bf16[2,256,512]{2,1,0:T(8,128)(2,1)S(1)} %add_convert_fusion.1), channel_id=1, source_target_pairs={{0,96},{32,0},{64,32},{96,64},{1,97},{33,1},{65,33},{97,65},{2,98}... | collective-permute-start | bytes 1572872 | tf_op jit(solution)/shard_map/ppermute | solution.py:30
  79.6 34.6 %collective-permute-start.15 = (bf16[1024,512]{1,0:T(8,128)(2,1)}, bf16[1024,512]{1,0:T(8,128)(2,1)}, u32[]{:S(2)}, u32[]{:S(2)}) collective-permute-start(bf16[1024,512]{1,0:T(8,128)(2,1)} %get-tuple-element.57.refs_1_), channel_id=1, source_target_pairs={{0,1},{1,0},{2,3},{3,2},{4,5},{5,4},{6,7},{7,6},{8,9},{9,8},{10,11... | collective-permute-start | bytes 3145736 | tf_op jit(solution)/shard_map/ppermute | solution.py:47
  86.6 16.3 %collective-permute-start.11 = (bf16[2,256,512]{2,1,0:T(8,128)(2,1)}, bf16[2,256,512]{2,1,0:T(8,128)(2,1)}, u32[]{:S(2)}, u32[]{:S(2)}) collective-permute-start(bf16[2,256,512]{2,1,0:T(8,128)(2,1)} %add_convert_fusion.2.refs_3_), channel_id=1, source_target_pairs={{0,96},{32,0},{64,32},{96,64},{1,97},{33,1},{65,33},{97,65},{2,98}... | collective-permute-start | bytes 1572872 | tf_op jit(solution)/shard_map/ppermute | solution.py:30
  102.9 11.3 %collective-permute-start.16 = (bf16[512,1024]{1,0:T(8,128)(2,1)}, bf16[512,1024]{1,0:T(8,128)(2,1)}, u32[]{:S(2)}, u32[]{:S(2)}) collective-permute-start(bf16[512,1024]{1,0:T(8,128)(2,1)} %collective-permute-done.6.refs_3_), channel_id=1, source_target_pairs={{0,2},{2,0},{4,6},{6,4},{8,10},{10,8},{12,14},{14,12},{16,18},{18,... | collective-permute-start | bytes 3145736 | tf_op jit(solution)/shard_map/ppermute | solution.py:37
  106.6 18.8 %collective-permute-start.14 = (bf16[1,256,1024]{2,1,0:T(8,128)(2,1)}, bf16[1,256,1024]{2,1,0:T(8,128)(2,1)}, u32[]{:S(2)}, u32[]{:S(2)}) collective-permute-start(bf16[1,256,1024]{2,1,0:T(8,128)(2,1)} %note_product.4.refs_4_), channel_id=1, source_target_pairs={{0,1},{1,0},{2,3},{3,2},{4,5},{5,4},{6,7},{7,6},{8,9},{9,8},{10,11... | collective-permute-start | bytes 1572872 | tf_op jit(solution)/shard_map/ppermute | solution.py:47
